TPU v7x, 32 devices: a whole 2x2x4 slice. The times are simulated.
32 devices in a mesh: batch: 32 (over z, y, x, core).
Axes of the slice: x: 2, y: 2, z: 4, core: 2. Of those that a mesh axis runs over, the one named last changes fastest.
Arguments:
- tokens: bfloat16 [32, 8, 128, 768], P('batch'), may hold values from -6 to 6
- lengths: int32 [64], replicated, may hold values from 256 to 512, as said below
- cotangent: bfloat16 [32, 8, 64, 768], P('batch'), may hold values from -6 to 6
- query_weight: bfloat16 [768, 768], replicated, may hold values from -0.21875 to 0.21875
- query_bias: float32 [768], replicated, may hold values from -3 to 3
- key_weight: bfloat16 [768, 768], replicated, may hold values from -0.21875 to 0.21875
- value_weight: bfloat16 [768, 768], replicated, may hold values from -0.21875 to 0.21875
- value_bias: float32 [768], replicated, may hold values from -0.3125 to 0.3125
- content_bias: float32 [768], replicated, may hold values from -3 to 3
- position_bias: float32 [768], replicated, may hold values from -3 to 3
- position_weight: float32 [12, 64, 64], replicated, may hold values from -0.75 to 0.75
- out_weight: bfloat16 [768, 768], replicated, may hold values from -1.75 to 1.75
- out_bias: float32 [768], replicated, may hold values from -3 to 3
- inner_gain: float32 [768], replicated, may hold values from 0.5 to 1.5
- inner_shift: float32 [768], replicated, may hold values from -3 to 3
- up_weight: bfloat16 [768, 3072], replicated, may hold values from -0.21875 to 0.21875
- up_bias: float32 [3072], replicated, may hold values from -3 to 3
- down_weight: bfloat16 [3072, 768], replicated, may hold values from -0.109375 to 0.109375
- down_bias: float32 [768], replicated, may hold values from -3 to 3
- outer_gain: float32 [768], replicated, may hold values from 0.5 to 1.5
- outer_shift: float32 [768], replicated, may hold values from -3 to 3
Outputs:
- layer_output: bfloat16 [32, 8, 64, 768], P('batch')
- tokens_grad: float32 [32, 8, 128, 768], P('batch')
- query_weight_grad: float32 [768, 768], replicated
- query_bias_grad: float32 [768], replicated
- key_weight_grad: float32 [768, 768], replicated
- value_weight_grad: float32 [768, 768], replicated
- value_bias_grad: float32 [768], replicated
- content_bias_grad: float32 [768], replicated
- position_bias_grad: float32 [768], replicated
- position_weight_grad: float32 [12, 64, 64], replicated
- out_weight_grad: float32 [768, 768], replicated
- out_bias_grad: float32 [768], replicated
- inner_gain_grad: float32 [768], replicated
- inner_shift_grad: float32 [768], replicated
- up_weight_grad: float32 [768, 3072], replicated
- up_bias_grad: float32 [3072], replicated
- down_weight_grad: float32 [3072, 768], replicated
- down_bias_grad: float32 [768], replicated
- outer_gain_grad: float32 [768], replicated
- outer_shift_grad: float32 [768], replicated
Inputs may be any that keep to these rules, and one draw needn't show every extreme that they name: `lengths`: each entry is 256 or 512; among the 8 rows of each group (rows g * 8 to g * 8 + 7) at least one has 512.
All inputs are finite; a program needn't handle non-finite values.
Results may differ from a plain program's by a relative error of at most 0.014.
The roundings to bfloat16 on the way count: a program that leaves them out, or rounds other values in their place, can miss the bound.
Values may be sent and summed in bfloat16 or wider, within the bound.
No kernel may reach another device: no remote copies, remote signals or barrier semaphores. Data moves between devices by JAX's collectives and lax.ppermute only.
A program may use at most 192 MiB of HBM per device.

v0:
```python
import math

import jax
import jax.numpy as jnp
from jax import lax
from jax.sharding import PartitionSpec as P

G = 4


def from_partner(shard, axis, stride):
    return lax.ppermute(shard, axis, [(i, i ^ 1 << stride) for i in range(lax.axis_size(axis))])


def layer_norm(inputs, norm_gain, norm_shift):
    center = inputs - jnp.mean(inputs, axis=-1, keepdims=True)
    spread = jnp.mean(center * center, axis=-1, keepdims=True)
    return center * lax.rsqrt(spread + 1e-05) * norm_gain + norm_shift


def gelu_exact(hidden):
    return jax.nn.gelu(hidden, approximate=False)


def frequencies(number):
    indices = jnp.arange(number, dtype=jnp.float32)
    return jnp.exp(indices * (-math.log(10000.0) / number))


def query_side(project, cosines, sines):
    middle = project.shape[-1] // 2
    first_half = project[..., :middle]
    second_half = project[..., middle:]
    return jnp.concatenate(
        [first_half * sines + second_half * cosines, second_half * sines - first_half * cosines],
        axis=-1,
    )


def query_back(side_grad, cosines, sines):
    middle = side_grad.shape[-1] // 2
    first_half = side_grad[..., :middle]
    second_half = side_grad[..., middle:]
    return jnp.concatenate(
        [first_half * sines - second_half * cosines, first_half * cosines + second_half * sines],
        axis=-1,
    )


def key_table(length, frequency):
    angles = jnp.arange(length, dtype=jnp.float32)[:, None] * frequency[None, :]
    return jnp.concatenate([jnp.cos(angles), jnp.sin(angles)], axis=-1)


def pair_gather(key_part, value_part):
    device_place = lax.axis_index("batch")
    for bit_level in range(G.bit_length() - 1):
        other_keys, other_values = from_partner((key_part, value_part), "batch", bit_level)
        lower_side = device_place // 2**bit_level % 2 == 0
        key_part = jnp.where(
            lower_side,
            jnp.concatenate([key_part, other_keys], 1),
            jnp.concatenate([other_keys, key_part], 1),
        )
        value_part = jnp.where(
            lower_side,
            jnp.concatenate([value_part, other_values], 1),
            jnp.concatenate([other_values, value_part], 1),
        )
    return (key_part, value_part)


def pair_collect(key_part, value_part):
    device_place = lax.axis_index("batch")
    key_stack = key_part[None]
    value_stack = value_part[None]
    for bit_level in reversed(range(G.bit_length() - 1)):
        middle = key_stack.shape[2] // 2
        lower_side = device_place // 2**bit_level % 2 == 0
        send_keys = jnp.where(lower_side, key_stack[:, :, middle:], key_stack[:, :, :middle])
        send_values = jnp.where(lower_side, value_stack[:, :, middle:], value_stack[:, :, :middle])
        keep_keys = jnp.where(lower_side, key_stack[:, :, :middle], key_stack[:, :, middle:])
        keep_values = jnp.where(lower_side, value_stack[:, :, :middle], value_stack[:, :, middle:])
        got_keys, got_values = from_partner((send_keys, send_values), "batch", bit_level)
        key_stack = jnp.concatenate([keep_keys, got_keys], 0)
        value_stack = jnp.concatenate([keep_values, got_values], 0)
    return (key_stack, value_stack)


def on_device(
    tokens,
    lengths,
    cotangent,
    query_weight,
    query_bias,
    key_weight,
    value_weight,
    value_bias,
    content_bias,
    position_bias,
    position_weight,
    out_weight,
    out_bias,
    inner_gain,
    inner_shift,
    up_weight,
    up_bias,
    down_weight,
    down_bias,
    outer_gain,
    outer_shift,
):
    local_tokens = tokens[0]
    row_count, seg_len, model_width = local_tokens.shape
    pooled_len = seg_len // 2
    head_count = position_weight.shape[0]
    head_dim = position_weight.shape[1]
    full_len = seg_len * G
    device_place = lax.axis_index("batch")
    group_index = device_place // G
    segment = device_place % G
    row_lengths = lax.dynamic_slice_in_dim(lengths, group_index * row_count, row_count)
    frequency = frequencies(head_dim // 2)
    query_places = 2 * (segment * pooled_len + jnp.arange(pooled_len, dtype=jnp.int32))
    angles = query_places.astype(jnp.float32)[:, None] * frequency[None, :]
    cosines = jnp.cos(angles)[:, None, :]
    sines = jnp.sin(angles)[:, None, :]
    key_pos = key_table(full_len, frequency).astype(jnp.bfloat16)
    score_scale = head_dim ** (-0.5)
    allowed = (jnp.arange(full_len, dtype=jnp.int32)[None, :] < row_lengths[:, None])[
        :, None, None, :
    ]
    highest_prec = lax.Precision.HIGHEST
    pooled = (
        local_tokens.astype(jnp.float32).reshape(row_count, pooled_len, 2, model_width).sum(axis=2)
        * 0.5
    )
    pooled_low = pooled.astype(jnp.bfloat16)
    queries = jnp.dot(pooled_low, query_weight, preferred_element_type=jnp.float32) + query_bias
    key_rows = jnp.dot(local_tokens, key_weight, preferred_element_type=jnp.float32).astype(
        jnp.bfloat16
    )
    value_rows = (
        jnp.dot(local_tokens, value_weight, preferred_element_type=jnp.float32) + value_bias
    ).astype(jnp.bfloat16)
    gathered_keys, gathered_values = pair_gather(key_rows, value_rows)
    content = (
        (queries + content_bias)
        .astype(jnp.bfloat16)
        .reshape(row_count, pooled_len, head_count, head_dim)
    )
    shifted = (queries + position_bias).reshape(row_count, pooled_len, head_count, head_dim)
    project = jnp.einsum("rphd,hde->rphe", shifted, position_weight, precision=highest_prec)
    query_pos = query_side(project, cosines, sines).astype(jnp.bfloat16)

    def scores_of(key_heads):
        raw_scores = jnp.einsum(
            "rphd,rkhd->rhpk", content, key_heads, preferred_element_type=jnp.float32
        )
        raw_scores = raw_scores + jnp.einsum(
            "rphd,kd->rhpk", query_pos, key_pos, preferred_element_type=jnp.float32
        )
        return jnp.where(allowed, raw_scores * score_scale, -1000000000.0)

    key_heads = gathered_keys.reshape(row_count, full_len, head_count, head_dim)
    value_heads = gathered_values.reshape(row_count, full_len, head_count, head_dim)
    scores = scores_of(key_heads)
    highest = jnp.max(scores, axis=-1, keepdims=True)
    raised = jnp.exp(scores - highest)
    denominator = jnp.sum(raised, axis=-1, keepdims=True)
    weights = raised / denominator
    log_total = highest + jnp.log(denominator)
    context = jnp.einsum(
        "rhpk,rkhd->rphd",
        weights.astype(jnp.bfloat16),
        value_heads,
        preferred_element_type=jnp.float32,
    )
    context = context.reshape(row_count, pooled_len, model_width).astype(jnp.bfloat16)
    attended = jnp.dot(context, out_weight, preferred_element_type=jnp.float32) + out_bias
    normed, inner_back = jax.vjp(layer_norm, pooled + attended, inner_gain, inner_shift)
    normed_low = normed.astype(jnp.bfloat16)
    hidden = jnp.dot(normed_low, up_weight, preferred_element_type=jnp.float32) + up_bias
    active, gelu_back = jax.vjp(gelu_exact, hidden)
    active_low = active.astype(jnp.bfloat16)
    branch = jnp.dot(active_low, down_weight, preferred_element_type=jnp.float32) + down_bias
    result, outer_back = jax.vjp(layer_norm, normed + branch, outer_gain, outer_shift)
    layer_output = result.astype(jnp.bfloat16)[None]
    outer_grad, outer_gain_grad, outer_shift_grad = outer_back(cotangent[0].astype(jnp.float32))
    branch_grad = outer_grad.astype(jnp.bfloat16)
    down_bias_grad = jnp.sum(branch_grad.astype(jnp.float32), axis=(0, 1))
    down_weight_grad = jnp.einsum(
        "rpf,rpd->fd", active_low, branch_grad, preferred_element_type=jnp.float32
    )
    (hidden_grad,) = gelu_back(
        jnp.einsum("rpd,fd->rpf", branch_grad, down_weight, preferred_element_type=jnp.float32)
    )
    hidden_low = hidden_grad.astype(jnp.bfloat16)
    up_bias_grad = jnp.sum(hidden_low.astype(jnp.float32), axis=(0, 1))
    up_weight_grad = jnp.einsum(
        "rpd,rpf->df", normed_low, hidden_low, preferred_element_type=jnp.float32
    )
    normed_grad = outer_grad + jnp.einsum(
        "rpf,df->rpd", hidden_low, up_weight, preferred_element_type=jnp.float32
    )
    inner_grad, inner_gain_grad, inner_shift_grad = inner_back(normed_grad)
    attended_low = inner_grad.astype(jnp.bfloat16)
    out_bias_grad = jnp.sum(attended_low.astype(jnp.float32), axis=(0, 1))
    out_weight_grad = jnp.einsum(
        "rpc,rpd->cd", context, attended_low, preferred_element_type=jnp.float32
    )
    context_grad = jnp.einsum(
        "rpd,cd->rpc", attended_low, out_weight, preferred_element_type=jnp.float32
    )
    context_grad = context_grad.astype(jnp.bfloat16).reshape(
        row_count, pooled_len, head_count, head_dim
    )
    scores = scores_of(key_heads)
    weights = jnp.exp(scores - log_total)
    weights_grad = jnp.einsum(
        "rphd,rkhd->rhpk", context_grad, value_heads, preferred_element_type=jnp.float32
    )
    inner_sum = jnp.sum(weights * weights_grad, axis=-1, keepdims=True)
    score_grad = (weights * (weights_grad - inner_sum)).astype(jnp.bfloat16)
    key_grad = (
        jnp.einsum("rhpk,rphd->rkhd", score_grad, content, preferred_element_type=jnp.float32)
        * score_scale
    )
    value_grad = jnp.einsum(
        "rhpk,rphd->rkhd",
        weights.astype(jnp.bfloat16),
        context_grad,
        preferred_element_type=jnp.float32,
    )
    content_grad = (
        jnp.einsum("rhpk,rkhd->rphd", score_grad, key_heads, preferred_element_type=jnp.float32)
        * score_scale
    )
    side_grad = (
        jnp.einsum("rhpk,kd->rphd", score_grad, key_pos, preferred_element_type=jnp.float32)
        * score_scale
    )
    project_grad = query_back(side_grad, cosines, sines)
    position_weight_grad = jnp.einsum(
        "rphd,rphe->hde", shifted, project_grad, precision=highest_prec
    )
    shifted_grad = jnp.einsum(
        "rphe,hde->rphd", project_grad, position_weight, precision=highest_prec
    )
    content_bias_grad = jnp.sum(content_grad, axis=(0, 1)).reshape(model_width)
    position_bias_grad = jnp.sum(shifted_grad, axis=(0, 1)).reshape(model_width)
    query_grad = (
        (content_grad + shifted_grad)
        .reshape(row_count, pooled_len, model_width)
        .astype(jnp.bfloat16)
    )
    query_bias_grad = jnp.sum(query_grad.astype(jnp.float32), axis=(0, 1))
    query_weight_grad = jnp.einsum(
        "rpc,rpd->cd", pooled_low, query_grad, preferred_element_type=jnp.float32
    )
    pooled_grad = inner_grad + jnp.einsum(
        "rpd,cd->rpc", query_grad, query_weight, preferred_element_type=jnp.float32
    )
    key_part = key_grad.reshape(row_count, full_len, model_width).astype(jnp.bfloat16)
    value_part = value_grad.reshape(row_count, full_len, model_width).astype(jnp.bfloat16)
    key_stack, value_stack = pair_collect(key_part, value_part)
    value_bias_grad = jnp.sum(value_stack.astype(jnp.float32), axis=(0, 1, 2))
    tiled_tokens = jnp.broadcast_to(local_tokens[None], key_stack.shape)
    key_weight_grad = jnp.einsum(
        "grsc,grsd->cd", tiled_tokens, key_stack, preferred_element_type=jnp.float32
    )
    value_weight_grad = jnp.einsum(
        "grsc,grsd->cd", tiled_tokens, value_stack, preferred_element_type=jnp.float32
    )
    tokens_grad = jnp.sum(
        jnp.einsum("grsd,cd->grsc", key_stack, key_weight, preferred_element_type=jnp.float32),
        axis=0,
    )
    tokens_grad = tokens_grad + jnp.sum(
        jnp.einsum("grsd,cd->grsc", value_stack, value_weight, preferred_element_type=jnp.float32),
        axis=0,
    )
    tokens_grad = tokens_grad + jnp.repeat(0.5 * pooled_grad, 2, axis=1)
    summed = tuple(
        lax.psum(
            (
                query_weight_grad,
                query_bias_grad,
                key_weight_grad,
                value_weight_grad,
                value_bias_grad,
                content_bias_grad,
                position_bias_grad,
                position_weight_grad,
                out_weight_grad,
                out_bias_grad,
                inner_gain_grad,
                inner_shift_grad,
                up_weight_grad,
                up_bias_grad,
                down_weight_grad,
                down_bias_grad,
                outer_gain_grad,
                outer_shift_grad,
            ),
            "batch",
        )
    )
    return (layer_output, tokens_grad[None]) + summed


def solution(mesh):
    in_specs = (
        P("batch", None, None, None),
        P(),
        P("batch", None, None, None),
        P(),
        P(),
        P(),
        P(),
        P(),
        P(),
        P(),
        P(),
        P(),
        P(),
        P(),
        P(),
        P(),
        P(),
        P(),
        P(),
        P(),
        P(),
    )
    out_specs = (
        P("batch", None, None, None),
        P("batch", None, None, None),
        P(),
        P(),
        P(),
        P(),
        P(),
        P(),
        P(),
        P(),
        P(),
        P(),
        P(),
        P(),
        P(),
        P(),
        P(),
        P(),
        P(),
        P(),
    )
    return jax.shard_map(
        on_device, mesh=mesh, in_specs=in_specs, out_specs=out_specs, check_vma=False
    )
```

profile of v0, /device:TPU:0, one launch (start us, length us, event | category | flops | bytes accessed | tf_op | source)
XLA Modules:
  0.0 947.4 jit_solution(15006619427704449964)
XLA Ops:
  8.5 4.0 convolution_convert_fusion
  13.0 2.5 add_convert_fusion.1
  15.6 2.7 reshape.301
  18.2 5.6 reduce_sum.212
  23.9 4.9 maximum_select_fusion.5
  28.8 2.9 collective-permute-start.3
  34.0 2.7 copy.74
  36.7 2.6 copy.77
  39.3 2.5 reshape.296
  41.8 5.3 copy.98
  49.7 4.9 convolution_bitcast_fusion.2
  55.1 6.4 fusion.55
  61.4 4.9 maximum_select_fusion.3
  66.5 2.6 copy.75
  69.1 2.6 copy.78
  71.6 10.5 %maximum_select_fusion.2 = (bf16[8,256,12,64]{1,3,2,0:T(8,128)(2,1)}, bf16[8,256,12,64]{1,3,2,0:T(8,128)(2,1)}) fusion(bf16[8,128,12,64]{1,3,2,0:T(8,128)(2,1)} %bitcast.195, bf16[8,128,12,64]{1,3,2,0:T(8,128)(2,1)} %bitcast.193, pred[]{:T(512)S(6)} %eq.15, bf16[8,128,12,64]{1,3,2,0:T(8,128)(2,1)} %bitcast.194, bf16[8,128,12,64]{1,3,2,0:T(8,128)(2,1)} %bitcast.196), kind=kLoop, calls=%fused_computation.64 | loop fusion | flops 28311552 | bytes 12582913 | tf_op jit(solution)/shard_map/jit(_where)/select_n | solution.py:65
  82.1 18.9 %collective-permute-done.3 = bf16[8,256,768]{2,1,0:T(8,128)(2,1)} collective-permute-done((bf16[8,256,768]{2,1,0:T(8,128)(2,1)}, bf16[8,256,768]{2,1,0:T(8,128)(2,1)}, u32[]{:S(2)}, u32[]{:S(2)}) %collective-permute-start.3) | collective-permute-done | bytes 3145760 | tf_op jit(solution)/shard_map/ppermute | solution.py:12
  101.0 4.6 copy.79
  105.6 15.0 %fusion.103 = (f32[8,12,64]{2,1,0:T(8,128)S(1)}, f32[8,12,64,512]{3,2,1,0:T(8,128)}) fusion(f32[512,8,64,12]{0,2,3,1:T(8,128)} %fusion.55, bf16[8,64,12,64]{1,3,2,0:T(8,128)(2,1)S(1)} %bitcast.189, bf16[8,256,12,64]{1,3,2,0:T(8,128)(2,1)} %bitcast.199, bf16[8,256,12,64]{1,3,2,0:T(8,128)(2,1)} %get-tuple-element.137, pred[]{:T(512)S(6)} %eq.14, ...), kind=kOutput, calls=%fused_computation.192 | convolution fusion | flops 443541504 | bytes 32272384 | tf_op jit(solution)/shard_map/rphd,rkhd->rhpk/dot_general | solution.py:157
  120.7 6.3 fusion.2
  127.6 40.2 %collective-permute-done.1 = bf16[8,256,768]{2,1,0:T(8,128)(2,1)} collective-permute-done((bf16[8,256,768]{2,1,0:T(8,128)(2,1)}, bf16[8,256,768]{2,1,0:T(8,128)(2,1)}, u32[]{:S(2)}, u32[]{:S(2)}) %collective-permute-start.1) | collective-permute-done | bytes 3145760 | tf_op jit(solution)/shard_map/ppermute | solution.py:12
  167.8 4.6 copy.76
  172.4 10.8 %fusion.52 = bf16[8,12,64,64]{3,2,1,0:T(8,128)(2,1)S(1)} fusion(f32[8,12,64,512]{3,2,1,0:T(8,128)} %get-tuple-element.125, f32[8,12,64]{2,1,0:T(8,128)S(1)} %fusion.2, f32[8,12,64]{2,1,0:T(8,128)S(1)} %get-tuple-element.124, bf16[8,256,12,64]{1,3,2,0:T(8,128)(2,1)} %bitcast.201, bf16[8,256,12,64]{1,3,2,0:T(8,128)(2,1)} %get-tuple-element.136, pred[]{:T(512)S(6)} %eq.14), kind=kOutput, calls=%fused_computation.105 | convolution fusion | flops 440795136 | bytes 19709952 | tf_op jit(solution)/shard_map/rhpk,rkhd->rphd/dot_general | solution.py:173
  184.7 7.7 fusion.58
  192.5 15.6 %multiply_convert_fusion.2 = (bf16[8,64,3072]{2,1,0:T(8,128)(2,1)S(1)}, f32[8,64,3072]{2,1,0:T(8,128)}) fusion(f32[8,64,3072]{2,1,0:T(8,128)S(1)} %get-tuple-element.128, f32[3072]{0:T(1024)S(1)} %copy-done.46, u8[64,3072]{1,0:T(8,128)(4,1)S(1)} %get-tuple-element.61, u8[64,3072]{1,0:T(8,128)(4,1)S(1)} %get-tuple-element.60), kind=kLoop, calls=%fused_computation.33 | loop fusion | flops 111673344 | bytes 16134144 | tf_op jit(solution)/shard_map/convert_element_type | solution.py:185
  208.2 2.8 fusion.105
  215.2 8.7 convert_reduce_fusion.1
  223.9 7.4 multiply_reduce_fusion.1
  236.6 16.6 %multiply_reduce_fusion = (f32[8,12,64]{2,1,0:T(8,128)S(1)}, f32[8,12,64,512]{3,2,1,0:T(8,128)}) fusion(f32[8,12,64,512]{3,2,1,0:T(8,128)} %get-tuple-element.125, f32[8,12,64]{2,1,0:T(8,128)} %log_add_fusion, bf16[8,64,12,64]{1,3,2,0:T(8,128)(2,1)} %bitcast.197, bf16[8,256,12,64]{1,3,2,0:T(8,128)(2,1)} %bitcast.202, ...), kind=kOutput, calls=%fused_computation.6 | convolution fusion | flops 440395776 | bytes 32292864 | tf_op jit(solution)/shard_map/rphd,rkhd->rhpk/dot_general | solution.py:220
  253.2 9.8 %fusion.26 = bf16[8,12,64,512]{3,2,1,0:T(8,128)(2,1)} fusion(bf16[8,64,12,64]{1,3,2,0:T(8,128)(2,1)} %bitcast.198, f32[8,12,64,512]{3,2,1,0:T(8,128)} %get-tuple-element.125, f32[8,12,64]{2,1,0:T(8,128)S(1)} %copy-done.33), kind=kOutput, calls=%fused_computation.59 | convolution fusion | flops 412090368 | bytes 19685376 | tf_op jit(solution)/shard_map/rhpk,rphd->rkhd/dot_general | solution.py:229
  263.0 9.4 multiply_convert_fusion.1
  275.1 3.3 fusion.102
  278.4 4.6 copy.124
  283.1 4.8 copy.125
  287.9 6.0 broadcast_select_fusion.3
  295.6 3.4 fusion.101
  299.0 4.7 copy.126
  303.7 5.0 copy.127
  308.7 5.1 broadcast_select_fusion.1
  314.1 3.1 multiply_bitcast_fusion
  321.1 6.7 fusion.32
  327.8 9.0 convert_reduce_fusion.2
  336.8 28.4 %collective-permute-done.4 = bf16[1,8,256,768]{3,2,1,0:T(8,128)(2,1)} collective-permute-done((bf16[1,8,256,768]{3,2,1,0:T(8,128)(2,1)}, bf16[1,8,256,768]{3,2,1,0:T(8,128)(2,1)}, u32[]{:S(2)}, u32[]{:S(2)}) %collective-permute-start.4) | collective-permute-done | bytes 3145760 | tf_op jit(solution)/shard_map/ppermute | solution.py:12
  365.2 5.1 broadcast_select_fusion.7
  370.3 5.2 convolution_bitcast_fusion
  375.5 55.6 %collective-permute-done.6 = bf16[1,8,256,768]{3,2,1,0:T(8,128)(2,1)} collective-permute-done((bf16[1,8,256,768]{3,2,1,0:T(8,128)(2,1)}, bf16[1,8,256,768]{3,2,1,0:T(8,128)(2,1)}, u32[]{:S(2)}, u32[]{:S(2)}) %collective-permute-start.6) | collective-permute-done | bytes 3145760 | tf_op jit(solution)/shard_map/ppermute | solution.py:12
  431.1 5.6 broadcast_select_fusion.5
  436.7 4.0 convolution_bitcast_fusion.5
  443.9 4.0 convolution_bitcast_fusion.4
  447.9 5.5 convolution_bitcast_fusion.1
  453.4 8.0 fusion.49
  461.5 8.0 fusion.46
  471.2 2.3 add_multiply_fusion
  473.5 2.7 broadcast_in_dim.37
  476.3 5.7 reshape.298
  482.2 4.4 convert_reduce_fusion
  486.6 44.0 %all-reduce = (f32[768]{0:T(1024)}, f32[768]{0:T(1024)}, f32[768]{0:T(1024)}, f32[768]{0:T(1024)}, f32[768]{0:T(1024)}, /*index=5*/f32[768]{0:T(1024)}, f32[768]...) all-reduce(f32[768]{0:T(1024)S(1)} %reduce_sum.264, ...), channel_id=1, replica_groups=mesh['batch'=32] {'batch'}, use_global_device_ids=true, to_apply=%region_16.17 | all-reduce | flops 10752 | bytes 86016 | tf_op jit(solution)/shard_map/psum | solution.py:285
  530.7 7.7 fusion.37
  538.4 7.2 convolution_reduce_fusion
  547.9 368.9 %all-reduce.4.cloned.1.call-done = (f32[768,768]{1,0:T(8,128)}, f32[768,768]{0,1:T(8,128)}, f32[768,768]{0,1:T(8,128)}, f32[12,64,64]{2,1,0:T(8,128)}, f32[768,7...) async-done(((f32[768,768]{1,0:T(8,128)}, f32[768,768]{0,1:T(8,128)}, f32[768,768]{0,1:T(8,128)}, f32[12,64,64]{2,1,0:T(8,128)}, f32[768,768]{1,0:T(8,128)}, ...) | async-done | bytes 28508176 | tf_op jit(solution)/shard_map/psum | solution.py:285
  916.8 3.0 copy.101
  919.8 3.2 copy.102
  927.3 9.3 copy.148
  936.6 3.7 copy.149
  (214 shorter events, 38.7 us)
Async XLA Ops:
  7.2 5.8 copy-start.23
  7.2 5.7 copy-start.60
  7.2 909.6 %all-reduce.4.cloned.1.call-start = ((), (), s32[]{:S(2)}) async-start(), calls=%async_computation | async-start | bytes 57409536 | tf_op jit(solution)/shard_map/psum | solution.py:285
  8.5 4.5 copy-start.58
  12.5 11.4 %collective-permute-start.2 = (bf16[8,128,768]{2,1,0:T(8,128)(2,1)}, bf16[8,128,768]{2,1,0:T(8,128)(2,1)}, u32[]{:S(2)}, u32[]{:S(2)}) collective-permute-start(bf16[8,128,768]{2,1,0:T(8,128)(2,1)} %convolution_convert_fusion), channel_id=1, source_target_pairs={{0,1},{1,0},{2,3},{3,2},{4,5},{5,4},{6,7},{7,6},{8,9},{9,8},{10,11... | collective-permute-start | bytes 4718600 | tf_op jit(solution)/shard_map/ppermute | solution.py:12
  15.5 45.9 %collective-permute-start = (bf16[8,128,768]{2,1,0:T(8,128)(2,1)}, bf16[8,128,768]{2,1,0:T(8,128)(2,1)}, u32[]{:S(2)}, u32[]{:S(2)}) collective-permute-start(bf16[8,128,768]{2,1,0:T(8,128)(2,1)} %add_convert_fusion.1), channel_id=1, source_target_pairs={{0,1},{1,0},{2,3},{3,2},{4,5},{5,4},{6,7},{7,6},{8,9},{9,8},{10,11... | collective-permute-start | bytes 4718600 | tf_op jit(solution)/shard_map/ppermute | solution.py:12
  23.9 7.9 copy-start.11
  23.9 7.9 copy-start.57
  23.9 7.9 copy-start.61
  23.9 7.9 copy-start.62
  23.9 7.9 copy-start.63
  28.8 72.2 %collective-permute-start.3 = (bf16[8,256,768]{2,1,0:T(8,128)(2,1)}, bf16[8,256,768]{2,1,0:T(8,128)(2,1)}, u32[]{:S(2)}, u32[]{:S(2)}) collective-permute-start(bf16[8,256,768]{2,1,0:T(8,128)(2,1)} %maximum_select_fusion.5), channel_id=1, source_target_pairs={{0,2},{1,3},{2,0},{3,1},{4,6},{5,7},{6,4},{7,5},{8,10},{9,11},{10,... | collective-permute-start | bytes 9437192 | tf_op jit(solution)/shard_map/ppermute | solution.py:12
  34.0 5.3 copy-start.27
  41.8 7.3 copy-start.67
  41.8 7.9 copy-start.21
  49.4 5.3 copy-start.39
  49.4 5.3 copy-start.41
  49.7 5.4 copy-start.35
  49.7 5.4 copy-start.37
  66.4 101.4 %collective-permute-start.1 = (bf16[8,256,768]{2,1,0:T(8,128)(2,1)}, bf16[8,256,768]{2,1,0:T(8,128)(2,1)}, u32[]{:S(2)}, u32[]{:S(2)}) collective-permute-start(bf16[8,256,768]{2,1,0:T(8,128)(2,1)} %maximum_select_fusion.3), channel_id=1, source_target_pairs={{0,2},{1,3},{2,0},{3,1},{4,6},{5,7},{6,4},{7,5},{8,10},{9,11},{10,... | collective-permute-start | bytes 9437192 | tf_op jit(solution)/shard_map/ppermute | solution.py:12
  172.4 10.8 %copy-start.12 = (f32[8,64,768]{2,1,0:T(8,128)S(1)}, f32[8,64,768]{2,1,0:T(8,128)}, u32[]{:S(2)}) copy-start(f32[8,64,768]{2,1,0:T(8,128)} %copy-done.11) | copy-start | bytes 4718596
  172.4 10.8 %copy-start.28 = (bf16[768,768]{1,0:T(8,128)(2,1)S(1)}, bf16[768,768]{1,0:T(8,128)(2,1)}, u32[]{:S(2)}) copy-start(bf16[768,768]{1,0:T(8,128)(2,1)} %param.32) | copy-start | bytes 3538948
  172.4 10.8 %copy-start.54 = (f32[768]{0:T(1024)S(1)}, f32[768]{0:T(1024)}, u32[]{:S(2)}) copy-start(f32[768]{0:T(1024)} %param.33) | copy-start | bytes 9220
  183.3 24.8 %slice-start.7 = ((s8[4718592]{0:T(1024)(128)(4,1)}), s8[4194304]{0:T(1024)(128)(4,1)S(1)}, s32[]{:S(2)}) async-start(s8[4718592]{0:T(1024)(128)(4,1)} %bitcast.207), calls=%async_computation.8 | async-start | bytes 8388608
  184.4 47.0 %copy-start.3 = (f32[8,64,768]{2,1,0:T(8,128)}, f32[8,64,768]{2,1,0:T(8,128)S(1)}, u32[]{:S(2)}) copy-start(f32[8,64,768]{2,1,0:T(8,128)S(1)} %get-tuple-element.127) | copy-start | bytes 4718596
  184.7 23.4 %slice-start.8 = ((s8[4718592]{0:T(1024)(128)(4,1)}), s8[524288]{0:T(1024)(128)(4,1)S(1)}, s32[]{:S(2)}) async-start(s8[4718592]{0:T(1024)(128)(4,1)} %bitcast.207), calls=%async_computation.9 | async-start | bytes 1048576
  192.5 15.7 %copy-start.64 = (f32[768]{0:T(1024)S(1)}, f32[768]{0:T(1024)}, u32[]{:S(2)}) copy-start(f32[768]{0:T(1024)} %param.39) | copy-start | bytes 9220
  215.2 8.7 copy-start.29
  223.9 7.4 copy-start.68
  236.6 16.6 %copy-start.33 = (f32[8,12,64]{2,1,0:T(8,128)S(1)}, f32[8,12,64]{2,1,0:T(8,128)}, u32[]{:S(2)}) copy-start(f32[8,12,64]{2,1,0:T(8,128)} %log_add_fusion) | copy-start | bytes 73732
  283.1 12.5 %slice-start.2 = ((s8[6291456]{0:T(1024)(128)(4,1)}), s8[2097152]{0:T(1024)(128)(4,1)S(1)}, s32[]{:S(2)}) async-start(s8[6291456]{0:T(1024)(128)(4,1)} %bitcast.186), calls=%async_computation.3 | async-start | bytes 4194304
  287.9 7.7 slice-start.3
  293.8 71.4 %collective-permute-start.4 = (bf16[1,8,256,768]{3,2,1,0:T(8,128)(2,1)}, bf16[1,8,256,768]{3,2,1,0:T(8,128)(2,1)}, u32[]{:S(2)}, u32[]{:S(2)}) collective-permute-start(bf16[1,8,256,768]{3,2,1,0:T(8,128)(2,1)} %get-tuple-element.106), channel_id=1, source_target_pairs={{0,2},{1,3},{2,0},{3,1},{4,6},{5,7},{6,4},{7,5},{8,10},{9,11},{10,... | collective-permute-start | bytes 9437192 | tf_op jit(solution)/shard_map/ppermute | solution.py:12
  303.7 10.4 %slice-start = ((s8[6291456]{0:T(1024)(128)(4,1)}), s8[2097152]{0:T(1024)(128)(4,1)S(1)}, s32[]{:S(2)}) async-start(s8[6291456]{0:T(1024)(128)(4,1)} %bitcast.183), calls=%async_computation.1 | async-start | bytes 4194304
  308.6 5.4 slice-start.1
  308.6 5.4 copy-start.36
  308.7 5.4 copy-start.38
  313.8 117.3 %collective-permute-start.6 = (bf16[1,8,256,768]{3,2,1,0:T(8,128)(2,1)}, bf16[1,8,256,768]{3,2,1,0:T(8,128)(2,1)}, u32[]{:S(2)}, u32[]{:S(2)}) collective-permute-start(bf16[1,8,256,768]{3,2,1,0:T(8,128)(2,1)} %get-tuple-element.100), channel_id=1, source_target_pairs={{0,2},{1,3},{2,0},{3,1},{4,6},{5,7},{6,4},{7,5},{8,10},{9,11},{10,... | collective-permute-start | bytes 9437192 | tf_op jit(solution)/shard_map/ppermute | solution.py:12
  327.8 37.4 %copy-start.8 = (bf16[1,8,256,768]{3,2,1,0:T(8,128)(2,1)S(1)}, bf16[1,8,256,768]{3,2,1,0:T(8,128)(2,1)}, u32[]{:S(2)}) copy-start(bf16[1,8,256,768]{3,2,1,0:T(8,128)(2,1)} %get-tuple-element.105) | copy-start | bytes 9437188
  365.2 5.1 copy-start.16
  365.2 5.1 copy-start.30
  370.3 83.1 %collective-permute-start.5 = (bf16[2,8,128,768]{3,2,1,0:T(8,128)(2,1)}, bf16[2,8,128,768]{3,2,1,0:T(8,128)(2,1)}, u32[]{:S(2)}, u32[]{:S(2)}) collective-permute-start(bf16[2,8,128,768]{3,2,1,0:T(8,128)(2,1)} %get-tuple-element.104), channel_id=1, source_target_pairs={{0,1},{1,0},{2,3},{3,2},{4,5},{5,4},{6,7},{7,6},{8,9},{9,8},{10,11... | collective-permute-start | bytes 9437192 | tf_op jit(solution)/shard_map/ppermute | solution.py:12
  431.1 5.7 copy-start.2
  436.7 4.0 copy-start.20
  436.7 24.8 %collective-permute-start.7 = (bf16[2,8,128,768]{3,2,1,0:T(8,128)(2,1)}, bf16[2,8,128,768]{3,2,1,0:T(8,128)(2,1)}, u32[]{:S(2)}, u32[]{:S(2)}) collective-permute-start(bf16[2,8,128,768]{3,2,1,0:T(8,128)(2,1)} %get-tuple-element.98), channel_id=1, source_target_pairs={{0,1},{1,0},{2,3},{3,2},{4,5},{5,4},{6,7},{7,6},{8,9},{9,8},{10,11... | collective-permute-start | bytes 9437192 | tf_op jit(solution)/shard_map/ppermute | solution.py:12
  443.9 4.0 copy-start.66
  443.9 4.0 copy-start.69
  447.9 5.5 copy-start.17
  447.9 5.5 copy-start.24
  453.4 8.1 copy-start.6
  476.3 5.7 copy-start.50
  476.3 5.8 copy-start.49
  476.3 5.8 copy-start.48
  482.2 4.4 copy-start.44
  482.2 4.4 copy-start.45
  482.2 4.4 copy-start.47
  482.2 4.4 copy-start.52
  482.2 4.4 copy-start.53
  530.6 7.7 copy-start.7
  530.7 7.7 copy-start.59
  538.4 7.2 copy-start.5
  925.8 10.7 %slice-start.4 = ((s8[9437184]{0:T(1024)(128)(4,1)}), s8[4194304]{0:T(1024)(128)(4,1)S(1)}, s32[]{:S(2)}) async-start(s8[9437184]{0:T(1024)(128)(4,1)} %bitcast.191), calls=%async_computation.5 | async-start | bytes 8388608
  927.2 9.3 slice-start.5
  927.2 9.3 slice-start.6
  (24 other events, 52.8 us)
Sparse Core Ops, SparseCore 0:
  469.7 447.0 all-reduce.3
where the time goes:
time: 956 us; the launch traced here: 947 us
  waiting for transfers between devices  512 us (54%)
  matrix products  176 us (18%)
  local copies, waits for them, and re-layouts  102 us (11%)
  other arithmetic  93.3 us (10%)
  blocking collectives  44 us (5%)
  between operations  15.2 us (2%)
    psum x1, waiting for transfers between devices, on_device(): lax.psum((query_weight_grad, query_bias_grad, key_weight_grad, value_weig...  369 us
    ppermute x8, waiting for transfers between devices, from_partner(): lax.ppermute(shard, axis, [(i, i ^ 1 << stride) for i in range(lax.axis_s...  143 us
    unnamed x169, local copies, waits for them, and re-layouts  49.5 us
    psum x1, blocking collectives, on_device(): lax.psum((query_weight_grad, query_bias_grad, key_weight_grad, value_weig...  44 us
  transfers between devices with their start and end apart: 9, of which 5 were waited for; matrix products, arithmetic and copies ran while one was open for 22% of the time, Pallas kernels for 0%

commit v1 on v0

v1 whole, which is shorter than its diff:
```python
import functools
import math

import jax
import jax.numpy as jnp
from jax import lax
from jax.experimental import pallas as pl
from jax.experimental.pallas import tpu as pltpu
from jax.sharding import PartitionSpec as P

G = 4
F32 = jnp.float32
BF = jnp.bfloat16
VM = pl.BlockSpec(memory_space=pltpu.VMEM)
SM = pl.BlockSpec(memory_space=pltpu.SMEM)
BLK = 16
CH = 512


def nn(a, b):
    return lax.dot_general(a, b, (((1,), (0,)), ((), ())), preferred_element_type=F32)


def nt(a, b):
    return lax.dot_general(a, b, (((1,), (1,)), ((), ())), preferred_element_type=F32)


def tn(a, b):
    return lax.dot_general(a, b, (((0,), (0,)), ((), ())), preferred_element_type=F32)


def split(a):
    hi = a.astype(BF)
    return hi, (a - hi.astype(F32)).astype(BF)


def three(dot, a_hi, a_lo, b_hi, b_lo):
    return dot(a_hi, b_hi) + (dot(a_hi, b_lo) + dot(a_lo, b_hi))


def params(mib):
    return pltpu.CompilerParams(vmem_limit_bytes=mib << 20)


def cost(flops, bytes_accessed, transcendentals=0):
    return pl.CostEstimate(
        flops=flops, bytes_accessed=bytes_accessed, transcendentals=transcendentals
    )


def attn_fwd_kernel(
    x0, x1, x2, x3, wq, wk, wv, qb, cb, pb, vb, wph, wpl, sin4, cos4, kfa, kfb,
    k_out, v_out, kt_out, xt_out, qc_out, qf_out, qht_out, qlt_out, pt_out, pooled_out,
    ctx_out, ctxt_out, lse_out,
    x_s, vt_s,
):
    rows = lax.broadcasted_iota(jnp.int32, (64, 128), 0)
    cols = lax.broadcasted_iota(jnp.int32, (64, 128), 1)
    pair = jnp.where(cols // 2 == rows, 0.5, 0.0).astype(BF)
    for d, piece in enumerate((x0, x1, x2, x3)):
        x_s[d * 128 : d * 128 + 128, :] = piece[...]
        pooled_out[d * 64 : d * 64 + 64, :] = nn(pair, piece[...])
    pooled_low = pooled_out[...].astype(BF)
    pt_out[...] = pooled_low.T
    x = x_s[...]
    xt_out[...] = x.T
    q = nn(pooled_low, wq[...]) + qb[...]
    k = nn(x, wk[...]).astype(BF)
    k_out[...] = k
    kt_out[...] = k.T
    v = (nn(x, wv[...]) + vb[...]).astype(BF)
    v_out[...] = v
    vt_s[...] = v.T
    qc_out[...] = (q + cb[...]).astype(BF) * 0.125
    hi, lo = split(q + pb[...])
    qht_out[...] = hi.T
    qlt_out[...] = lo.T
    for g in range(3):
        at = slice(256 * g, 256 * g + 256)
        both = three(nn, hi[:, at], lo[:, at], wph[g], wpl[g])
        side = both[:, :256] * sin4[...] + both[:, 256:] * cos4[...]
        qf_out[:, at] = side.astype(BF) * 0.125
    lane = lax.broadcasted_iota(jnp.int32, (256, 128), 1)
    zero = jnp.zeros((256, 128), BF)
    one_a = (lane == 64).astype(F32).astype(BF)
    one_b = (lane == 0).astype(F32).astype(BF)

    def one_pair(i, carry):
        at = pl.ds(pl.multiple_of(i * 128, 128), 128)
        k_pair = k_out[:, at]
        qc_pair = qc_out[:, at]
        qf_pair = qf_out[:, at]
        for s in range(2):
            mine = (lane < 64) if s == 0 else (lane >= 64)
            left = jnp.concatenate([k_pair, (kfa, kfb)[s][...]], axis=1)
            right = jnp.concatenate(
                [jnp.where(mine, qc_pair, zero), jnp.where(mine, qf_pair, (one_a, one_b)[s])], axis=1
            )
            scores = nt(left, right)
            highest = jnp.max(scores, axis=0, keepdims=True)
            raised = jnp.exp(scores - highest)
            total = jnp.sum(raised, axis=0, keepdims=True)
            weights = (raised * (1.0 / total)).astype(BF)
            head = pl.ds(pl.multiple_of(i * 128 + s * 64, 64), 64)
            ctxt_out[head, :] = nn(vt_s[head, :], weights).astype(BF)
            lse_out[i * 2 + s] = highest + jnp.log(total)
        return carry

    lax.fori_loop(0, 6, one_pair, 0)
    ctx_out[...] = ctxt_out[...].T


def attn_fwd(pieces, w):
    b16 = lambda *s: jax.ShapeDtypeStruct(s, BF)
    f32 = lambda *s: jax.ShapeDtypeStruct(s, F32)
    return pl.pallas_call(
        attn_fwd_kernel,
        out_shape=(
            b16(512, 768), b16(512, 768), b16(768, 512), b16(768, 512), b16(256, 768), b16(256, 768),
            b16(768, 256), b16(768, 256), b16(768, 256), f32(256, 768), b16(256, 768), b16(768, 256),
            f32(12, 1, 256),
        ),
        in_specs=[VM] * 17,
        out_specs=[VM] * 13,
        scratch_shapes=[pltpu.VMEM((512, 768), BF), pltpu.VMEM((768, 512), BF)],
        compiler_params=params(40),
        cost_estimate=cost(4 * 10**9, 12 * 10**6, 12 * 512 * 256),
        name="attn_fwd",
    )(*pieces, *w)


def layer_stats(a):
    center = a - jnp.mean(a, axis=-1, keepdims=True)
    rs = lax.rsqrt(jnp.mean(center * center, axis=-1, keepdims=True) + 1e-05)
    return center * rs, rs


def layer_back(dn, n, rs):
    return rs * (dn - jnp.mean(dn, axis=-1, keepdims=True) - n * jnp.mean(dn * n, axis=-1, keepdims=True))


def ffn_kernel(
    masks, ctx0, ctx1, ctxt0, ctxt1, pooled0, pooled1, c0, c1, c2, c3, wo, wu, wd, ob, ig, ish, ub, db, og, osh,
    out0, out1, out2, out3, d1_out, dctx_out, wog_out, kd_out, sd_out, ku_out, su_out, vec_out, upb_out,
    gp_s, act_s, acc_s, x1_s, n1_s, x1t_s, df_s, rs_s, g_s, u_s,
):
    ctx = jnp.concatenate([ctx0[...], ctx1[...]], axis=0)
    pooled = jnp.concatenate([pooled0[...], pooled1[...]], axis=0)
    n1, rs1 = layer_stats(pooled + (nn(ctx, wo[...]) + ob[...]))
    n1_s[...] = n1
    rs_s[...] = rs1
    x1 = n1 * ig[...] + ish[...]
    x1_s[...] = x1.astype(BF)
    x1t_s[...] = x1.astype(BF).T
    acc_s[...] = x1 + db[...]

    def up_chunk(c, carry):
        at = pl.ds(pl.multiple_of(c * CH, CH), CH)
        z = nn(x1_s[...], wu[:, at]) + ub[:, at]
        phi = 0.5 + 0.5 * lax.erf(z * math.sqrt(0.5))
        gp_s[:, at] = phi + z * (jnp.exp(-0.5 * z * z) * (1.0 / math.sqrt(2.0 * math.pi)))
        act = (z * phi).astype(BF)
        act_s[:, at] = act
        acc_s[...] += nn(act, wd[at, :])
        return carry

    lax.fori_loop(0, 6, up_chunk, 0)
    n2, rs2 = layer_stats(acc_s[...])
    result = (n2 * og[...] + osh[...]).astype(BF)
    for d, out in enumerate((out0, out1, out2, out3)):
        for r in range(2):
            out[r] = result[r * 256 + d * 64 : r * 256 + d * 64 + 64, :]
    cot = jnp.concatenate([c[r] for r in range(2) for c in (c0, c1, c2, c3)], axis=0).astype(F32)
    vec_out[0:1, :] = jnp.sum(cot * n2, axis=0, keepdims=True)
    vec_out[1:2, :] = jnp.sum(cot, axis=0, keepdims=True)
    d2 = layer_back(cot * og[...], n2, rs2)
    df = d2.astype(BF)
    df_s[...] = df
    vec_out[2:3, :] = jnp.sum(df.astype(F32), axis=0, keepdims=True)
    acc_s[...] = d2

    def back_chunk(c, carry):
        at = pl.ds(pl.multiple_of(c * CH, CH), CH)
        df = df_s[...]
        dz = (nt(df, wd[at, :]) * gp_s[:, at]).astype(BF)
        upb_out[:, at] = jnp.sum(dz.astype(F32), axis=0, keepdims=True)
        acc_s[...] += nt(dz, wu[:, at])
        g_s[...] = tn(act_s[:, at], df)
        u_s[...] = nn(x1t_s[...], dz)
        which = c // 3
        slab = (c % 3) * 6
        me = masks[which]
        for r in range(32):
            place = r ^ me
            row = pl.ds(pl.multiple_of(place * 16, 16), 16)
            urow = pl.multiple_of((place // 4) * 96, 32)
            ucol = pl.ds(pl.multiple_of((place % 4) * 128, 128), 128)
            down = (kd_out, sd_out)[r // 16]
            up = (ku_out, su_out)[r // 16]
            for j in range(6):
                down[which, r % 16, slab + j] = g_s[row, j * 128 : j * 128 + 128].astype(BF)
                up[which, r % 16, slab + j] = u_s[pl.ds(urow + 16 * j, 16), ucol].astype(BF)
        return carry

    lax.fori_loop(0, 6, back_chunk, 0)
    dx1 = acc_s[...]
    n1 = n1_s[...]
    vec_out[3:4, :] = jnp.sum(dx1 * n1, axis=0, keepdims=True)
    vec_out[4:5, :] = jnp.sum(dx1, axis=0, keepdims=True)
    d1 = layer_back(dx1 * ig[...], n1, rs_s[...])
    d1_out[...] = d1
    do = d1.astype(BF)
    vec_out[5:6, :] = jnp.sum(do.astype(F32), axis=0, keepdims=True)
    dctx_out[...] = nt(do, wo[...]).astype(BF)
    wog_out[...] = nn(jnp.concatenate([ctxt0[...], ctxt1[...]], axis=1), do)


def ffn(args):
    b16 = lambda *s: jax.ShapeDtypeStruct(s, BF)
    f32 = lambda *s: jax.ShapeDtypeStruct(s, F32)
    grad = b16(2, 16, 18, 16, 128)
    return pl.pallas_call(
        ffn_kernel,
        out_shape=(
            b16(2, 64, 768), b16(2, 64, 768), b16(2, 64, 768), b16(2, 64, 768), f32(512, 768), b16(512, 768),
            f32(768, 768), grad, grad, grad, grad, f32(8, 768), f32(1, 3072),
        ),
        in_specs=[SM] + [VM] * 20,
        out_specs=[VM] * 13,
        scratch_shapes=[
            pltpu.VMEM((512, 3072), F32), pltpu.VMEM((512, 3072), BF), pltpu.VMEM((512, 768), F32),
            pltpu.VMEM((512, 768), BF), pltpu.VMEM((512, 768), F32), pltpu.VMEM((768, 512), BF),
            pltpu.VMEM((512, 768), BF), pltpu.VMEM((512, 1), F32), pltpu.VMEM((512, 768), F32),
            pltpu.VMEM((768, 512), F32),
        ],
        compiler_params=params(60),
        cost_estimate=cost(16 * 10**9, 40 * 10**6, 3 * 10**6),
        name="ffn",
    )(*args)


def attn_bwd_kernel(
    k, v, kt, qc, qf, qht, qlt, lse, dctx, kfa, kfb, kst, sint, cost_t, wph, wpl,
    dk_out, dv_out, dq_out, pwg_out, vec_out,
    dqct_s, dpt_s,
):
    lane = lax.broadcasted_iota(jnp.int32, (256, 128), 1)
    zero = jnp.zeros((256, 128), BF)
    one_a = (lane == 64).astype(F32).astype(BF)
    one_b = (lane == 0).astype(F32).astype(BF)

    def one_pair(i, carry):
        at = pl.ds(pl.multiple_of(i * 128, 128), 128)
        k_pair = k[:, at]
        v_pair = v[:, at]
        qc_pair = qc[:, at]
        qf_pair = qf[:, at]
        dc_pair = dctx[:, at]
        for s in range(2):
            mine = (lane < 64) if s == 0 else (lane >= 64)
            left = jnp.concatenate([k_pair, (kfa, kfb)[s][...]], axis=1)
            qc_mine = jnp.where(mine, qc_pair, zero)
            dc_mine = jnp.where(mine, dc_pair, zero)
            right = jnp.concatenate([qc_mine, jnp.where(mine, qf_pair, (one_a, one_b)[s])], axis=1)
            weights = jnp.exp(nt(left, right) - lse[i * 2 + s])
            dweights = nt(v_pair, dc_mine)
            inner = jnp.sum(weights * dweights, axis=0, keepdims=True)
            dscore = (weights * (dweights - inner)).astype(BF)
            dv_part = nn(weights.astype(BF), dc_mine)
            dk_part = nn(dscore, qc_mine)
            if s == 0:
                dv_first, dk_first = dv_part, dk_part
            head = pl.ds(pl.multiple_of(i * 128 + s * 64, 64), 64)
            side = nn(jnp.concatenate([kt[head, :], kst[...]], axis=0), dscore)
            dqct_s[head, :] = side[0:64] * 0.125
            dpt_s[head, :] = (side[64:128] * sint[...] + side[128:192] * cost_t[...]) * 0.125
        dv_out[:, at] = (dv_first + dv_part).astype(BF)
        dk_out[:, at] = (dk_first + dk_part).astype(BF)
        return carry

    lax.fori_loop(0, 6, one_pair, 0)
    ones = jnp.ones((8, 256), BF)
    for g in range(3):
        at = slice(256 * g, 256 * g + 256)
        hi, lo = split(dpt_s[at, :])
        pwg_out[g] = three(nt, qht[at, :], qlt[at, :], hi, lo)
        shift = three(nn, wph[g][:, :256], wpl[g][:, :256], hi, lo)
        content = dqct_s[at, :]
        dq = (content + shift).T.astype(BF)
        dq_out[:, at] = dq
        shi, slo = split(shift)
        chi, clo = split(content)
        vec_out[0:1, at] = (nt(ones, chi) + nt(ones, clo))[0:1]
        vec_out[1:2, at] = (nt(ones, shi) + nt(ones, slo))[0:1]
        vec_out[2:3, at] = jnp.sum(dq.astype(F32), axis=0, keepdims=True)
    vec_out[3:4, :] = jnp.sum(dv_out[...].astype(F32), axis=0, keepdims=True)


def attn_bwd(args):
    b16 = lambda *s: jax.ShapeDtypeStruct(s, BF)
    f32 = lambda *s: jax.ShapeDtypeStruct(s, F32)
    return pl.pallas_call(
        attn_bwd_kernel,
        out_shape=(b16(512, 768), b16(512, 768), b16(256, 768), f32(3, 256, 256), f32(8, 768)),
        in_specs=[VM] * 16,
        out_specs=[VM] * 5,
        scratch_shapes=[pltpu.VMEM((768, 256), F32), pltpu.VMEM((768, 256), F32)],
        compiler_params=params(40),
        cost_estimate=cost(8 * 10**9, 12 * 10**6, 12 * 512 * 256),
        name="attn_bwd",
    )(*args)


def proj_kernel(
    masks, xt0, xt1, pt0, pt1, dk0, dk1, dv0, dv1, dq0, dq1, d1, wq, wk, wv, wog, smalls,
    t0, t1, t2, t3, ka_out, sa_out, kb_out, sb_out,
    g_s, tok_s,
):
    rows = lax.broadcasted_iota(jnp.int32, (512, 256), 0)
    cols = lax.broadcasted_iota(jnp.int32, (512, 256), 1)
    spread = jnp.where(rows // 2 == cols, 0.5, 0.0).astype(BF)
    for r, (dk, dv, dq) in enumerate(((dk0, dv0, dq0), (dk1, dv1, dq1))):
        hi, lo = split(d1[r * 256 : r * 256 + 256, :] + nt(dq[...], wq[...]))
        tok_s[...] = (nt(dk[...], wk[...]) + nt(dv[...], wv[...])) + (nn(spread, hi) + nn(spread, lo))
        for d, out in enumerate((t0, t1, t2, t3)):
            out[r] = tok_s[d * 128 : d * 128 + 128, :].astype(BF)
    g_s[0:768, :] = wog[...]
    g_s[768:1536, :] = nn(pt0[...], dq0[...]) + nn(pt1[...], dq1[...])
    g_s[1536:2304, :] = nn(xt0[...], dk0[...]) + nn(xt1[...], dk1[...])
    g_s[2304:3072, :] = nn(xt0[...], dv0[...]) + nn(xt1[...], dv1[...])
    me = (masks[0], masks[1])

    def one_block(r, carry):
        for which in range(2):
            place = r ^ me[which]
            near = (ka_out, kb_out)[which]
            far = (sa_out, sb_out)[which]
            for half, out in enumerate((near, far)):
                at = place ^ (16 * half)
                for c in range(3):
                    row = pl.ds(pl.multiple_of((which * 3 + c) * 512 + at * 16, 16), 16)
                    for j in range(6):
                        out[r, c * 6 + j] = g_s[row, j * 128 : j * 128 + 128].astype(BF)
                if which == 1:
                    row = pl.ds(pl.multiple_of(at * 16, 16), 16)
                    out[r, 18] = smalls[row, :].astype(BF)
        return carry

    lax.fori_loop(0, 16, one_block, 0)


def proj(args):
    b16 = lambda *s: jax.ShapeDtypeStruct(s, BF)
    piece = b16(2, 128, 768)
    return pl.pallas_call(
        proj_kernel,
        out_shape=(
            piece, piece, piece, piece, b16(16, 18, 16, 128), b16(16, 18, 16, 128), b16(16, 19, 16, 128),
            b16(16, 19, 16, 128),
        ),
        in_specs=[SM] + [VM] * 16,
        out_specs=[VM] * 8,
        scratch_shapes=[pltpu.VMEM((3072, 768), F32), pltpu.VMEM((512, 768), F32)],
        compiler_params=params(56),
        cost_estimate=cost(9 * 10**9, 25 * 10**6),
        name="proj_back",
    )(*args)


def partner(x, bit):
    size = lax.axis_size("batch")
    return lax.ppermute(x, "batch", [(i, i ^ bit) for i in range(size)])


def plus(a, b):
    return (a.astype(F32) + b.astype(F32)).astype(BF)


def sum_over(keep_a, keep_b, send_a, send_b, bits):
    core, first, second, third, fourth, others = bits
    a = plus(keep_a, partner(send_a, core))
    b = plus(keep_b, partner(send_b, core))
    a, b = plus(a[:8], partner(a[8:], first)), plus(b[:8], partner(b[8:], second))
    a, b = plus(a[:4], partner(a[4:], second)), plus(b[:4], partner(b[4:], first))
    n = a.shape[1]
    both = jnp.concatenate([a, b], axis=1)
    both = plus(both[:2], partner(both[2:], third))
    both = plus(both[:1], partner(both[1:], fourth))
    for bit in others:
        both = plus(both, partner(both, bit))
    both = jnp.concatenate([both, partner(both, fourth)], axis=0)
    both = jnp.concatenate([both, partner(both, third)], axis=0)
    a, b = both[:, :n], both[:, n:]
    a, b = jnp.concatenate([a, partner(a, second)]), jnp.concatenate([b, partner(b, first)])
    a, b = jnp.concatenate([a, partner(a, first)]), jnp.concatenate([b, partner(b, second)])
    return (a, b), (partner(a, core), partner(b, core))


def rows_kernel(masks, a0, b0, a1, b1, out):
    which = pl.program_id(0) // 3
    me = masks[which]
    slab = (pl.program_id(0) % 3) * 6
    for w, halves in enumerate(((a0, a1), (b0, b1))):

        @pl.when(which == w)
        def _():
            for r in range(32):
                row = pl.ds(pl.multiple_of((r ^ me) * 16, 16), 16)
                for j in range(6):
                    out[row, j * 128 : j * 128 + 128] = halves[r // 16][r % 16, slab + j].astype(F32)


def assemble_rows(masks, near, far):
    return pl.pallas_call(
        rows_kernel,
        out_shape=jax.ShapeDtypeStruct((3072, 768), F32),
        grid=(6,),
        in_specs=[SM] + [VM] * 4,
        out_specs=pl.BlockSpec((512, 768), lambda c: (c, 0)),
        compiler_params=params(24),
        cost_estimate=cost(0, 14 * 10**6),
        name="assemble_rows",
    )(masks, *near, *far)


def up_kernel(masks, a0, b0, a1, b1, out):
    which = pl.program_id(0) // 3
    me = masks[which]
    slab = (pl.program_id(0) % 3) * 6
    for w, halves in enumerate(((a0, a1), (b0, b1))):

        @pl.when(which == w)
        def _():
            for r in range(32):
                place = r ^ me
                row = pl.multiple_of((place // 4) * 96, 32)
                col = pl.ds(pl.multiple_of((place % 4) * 128, 128), 128)
                for j in range(6):
                    out[pl.ds(row + 16 * j, 16), col] = halves[r // 16][r % 16, slab + j].astype(F32)


def assemble_up(masks, near, far):
    return pl.pallas_call(
        up_kernel,
        out_shape=jax.ShapeDtypeStruct((768, 3072), F32),
        grid=(6,),
        in_specs=[SM] + [VM] * 4,
        out_specs=pl.BlockSpec((768, 512), lambda c: (0, c)),
        compiler_params=params(24),
        cost_estimate=cost(0, 14 * 10**6),
        name="assemble_up",
    )(masks, *near, *far)


def four_kernel(masks, a0, b0, a1, b1, o_out, q_out, k_out, v_out, s_out):
    outs = (o_out, q_out, k_out, v_out)
    me = (masks[0], masks[1])
    for w, halves in enumerate(((a0, a1), (b0, b1))):
        for r in range(32):
            place = r ^ me[w]
            for c in range(3):
                block = (w * 3 + c) * 32 + place
                source = halves[r // 16]
                matrix = block // 48
                row = pl.ds(pl.multiple_of((block % 48) * 16, 16), 16)
                first = ((w * 3 + c) * 32) // 48
                last = ((w * 3 + c) * 32 + 31) // 48
                for m in range(first, last + 1):

                    def store(m=m):
                        for j in range(6):
                            outs[m][row, j * 128 : j * 128 + 128] = source[r % 16, c * 6 + j].astype(F32)

                    if first == last:
                        store()
                    else:
                        pl.when(matrix == m)(store)
            if w == 1:
                row = pl.ds(pl.multiple_of(place * 16, 16), 16)
                s_out[row, :] = halves[r // 16][r % 16, 18].astype(F32)


def assemble_four(masks, near, far):
    f32 = lambda *s: jax.ShapeDtypeStruct(s, F32)
    return pl.pallas_call(
        four_kernel,
        out_shape=(f32(768, 768),) * 4 + (f32(512, 128),),
        in_specs=[SM] + [VM] * 4,
        out_specs=[VM] * 5,
        compiler_params=params(40),
        cost_estimate=cost(0, 15 * 10**6),
        name="assemble_four",
    )(masks, *near, *far)


def tokens_kernel(place, p0, p1, p2, p3, out):
    j = place[0]
    for d, piece in enumerate((p0, p1, p2, p3)):
        out[j ^ d] = piece[...].astype(F32)


def assemble_tokens(place, pieces):
    return pl.pallas_call(
        tokens_kernel,
        out_shape=jax.ShapeDtypeStruct((4, 2, 128, 768), F32),
        in_specs=[SM] + [VM] * 4,
        out_specs=VM,
        compiler_params=params(16),
        cost_estimate=cost(0, 5 * 10**6),
        name="assemble_tokens",
    )(place, *pieces)


def swapped(table):
    half = table.shape[-1] // 2
    return jnp.concatenate([table[..., half:], table[..., :half]], axis=-1)


def on_device(
    tokens, lengths, cotangent, query_weight, query_bias, key_weight, value_weight, value_bias, content_bias,
    position_bias, position_weight, out_weight, out_bias, inner_gain, inner_shift, up_weight, up_bias, down_weight,
    down_bias, outer_gain, outer_shift,
):
    size = lax.axis_size("batch")
    me = lax.axis_index("batch")
    j = me % G
    group = me // G
    core, first, second, third, fourth = 1, 2, 4, 8, 16
    others = [1 << b for b in range(5, size.bit_length() - 1)]
    bits = (core, first, second, third, fourth, others)
    has = lambda bit: (me // bit) % 2
    low = has(third) * 2 + has(fourth)
    masks = jnp.stack(
        [
            has(core) * 16 + has(first) * 8 + has(second) * 4 + low,
            has(core) * 16 + has(second) * 8 + has(first) * 4 + low,
        ]
    ).astype(jnp.int32)

    by_owner = tokens[0].reshape(4, 2, 128, 768)
    cot_owner = cotangent[0].reshape(4, 2, 64, 768)
    pick = lambda a, d: lax.dynamic_index_in_dim(a, j ^ d, 0, keepdims=False)
    sends = [pick(by_owner, d) for d in range(4)]
    x = [[sends[0][r]] + [None] * 3 for r in range(2)]
    for r in range(2):
        for d in (2, 3, 1):
            x[r][d] = partner(sends[d][r], d)
    cot = [pick(cot_owner, 0)] + [partner(pick(cot_owner, d), d) for d in (1, 2, 3)]

    w = jnp.exp(jnp.arange(32, dtype=F32) * (-math.log(10000.0) / 32))
    segs = j ^ jnp.arange(4, dtype=jnp.int32)
    q_pos = (2 * (segs[:, None] * 64 + jnp.arange(64, dtype=jnp.int32)[None, :])).reshape(256)
    k_pos = (segs[:, None] * 128 + jnp.arange(128, dtype=jnp.int32)[None, :]).reshape(512)
    theta = q_pos.astype(F32)[:, None] * w[None, :]
    sin, cos = jnp.sin(theta), jnp.cos(theta)
    sin4 = jnp.tile(sin, (1, 8))
    cos4 = jnp.tile(jnp.concatenate([cos, -cos], axis=1), (1, 4))
    sint = jnp.concatenate([sin, sin], axis=1).T
    cost_t = jnp.concatenate([-cos, cos], axis=1).T
    angle = k_pos.astype(F32)[:, None] * w[None, :]
    kf = jnp.concatenate([jnp.cos(angle), jnp.sin(angle)], axis=1).astype(BF)
    kst = jnp.concatenate([kf, swapped(kf)], axis=1).T
    kfa, kfb = [], []
    for r in range(2):
        length = lax.dynamic_index_in_dim(lengths, group * 8 + 2 * j + r, 0, keepdims=False)
        bias = jnp.where(k_pos < length, 0.0, -1.0e9).astype(BF)[:, None]
        rest = jnp.concatenate([bias, jnp.zeros((512, 63), BF)], axis=1)
        kfa.append(jnp.concatenate([kf, rest], axis=1))
        kfb.append(jnp.concatenate([rest, kf], axis=1))
    eye = jnp.eye(4, dtype=F32)
    heads = position_weight.reshape(3, 4, 64, 64)
    block = lambda a: (a[:, :, :, None, :] * eye[None, :, None, :, None]).reshape(3, 256, 256)
    wph, wpl = split(jnp.concatenate([block(heads), block(swapped(heads))], axis=2))

    vec = lambda a: a[None, :]
    fwd = []
    for r in range(2):
        fwd.append(
            attn_fwd(
                x[r],
                (
                    query_weight, key_weight, value_weight, vec(query_bias), vec(content_bias), vec(position_bias),
                    vec(value_bias), wph, wpl, sin4, cos4, kfa[r], kfb[r],
                ),
            )
        )
    k, v, kt, xt, qc, qf, qht, qlt, pt, pooled, ctx, ctxt, lse = zip(*fwd)
    (
        out0, out1, out2, out3, d1, dctx, wog, keep_d, send_d, keep_u, send_u, ffn_vec, up_bias_grad,
    ) = ffn(
        (
            masks, *ctx, *ctxt, *pooled, *cot, out_weight, up_weight, down_weight, vec(out_bias), vec(inner_gain),
            vec(inner_shift), vec(up_bias), vec(down_bias), vec(outer_gain), vec(outer_shift),
        )
    )
    back = [out0] + [partner(out, d) for d, out in ((1, out1), (2, out2), (3, out3))]
    stacked = jnp.stack(back)
    order = j ^ jnp.arange(4, dtype=jnp.int32)
    layer_output = jnp.take(stacked, order, axis=0).reshape(1, 8, 64, 768)

    down = sum_over(keep_d[0], keep_d[1], send_d[0], send_d[1], bits)
    up = sum_over(keep_u[0], keep_u[1], send_u[0], send_u[1], bits)

    bwd = []
    for r in range(2):
        bwd.append(
            attn_bwd(
                (
                    k[r], v[r], kt[r], qc[r], qf[r], qht[r], qlt[r], lse[r], dctx[r * 256 : r * 256 + 256], kfa[r],
                    kfb[r], kst, sint, cost_t, wph, wpl,
                )
            )
        )
    dk, dv, dq, pwg, attn_vec = zip(*bwd)
    attn_vec = attn_vec[0] + attn_vec[1]
    pwg = (pwg[0] + pwg[1]).reshape(3, 4, 64, 4, 64)
    pwg = jnp.stack([pwg[:, h, :, h] for h in range(4)], axis=1)
    smalls = jnp.concatenate(
        [ffn_vec[:6].reshape(-1), up_bias_grad.reshape(-1), attn_vec[:4].reshape(-1), pwg.reshape(-1)]
    )
    smalls = jnp.pad(smalls, (0, 65536 - smalls.size)).reshape(512, 128)
    t0, t1, t2, t3, keep_a, send_a, keep_b, send_b = proj(
        (
            masks, *xt, *pt, *[a for pair in (dk, dv, dq) for a in pair], d1, query_weight, key_weight, value_weight,
            wog, smalls,
        )
    )
    pieces = [t0] + [partner(t, d) for d, t in ((1, t1), (2, t2), (3, t3))]
    four = sum_over(keep_a, keep_b, send_a, send_b, bits)

    tokens_grad = assemble_tokens(j.reshape(1).astype(jnp.int32), pieces).reshape(1, 8, 128, 768)
    down_weight_grad = assemble_rows(masks, *down)
    up_weight_grad = assemble_up(masks, *up)
    out_weight_grad, query_weight_grad, key_weight_grad, value_weight_grad, flat = assemble_four(masks, *four)
    flat = flat.reshape(-1)
    line = lambda i: flat[768 * i : 768 * i + 768]
    return (
        layer_output, tokens_grad, query_weight_grad, line(12), key_weight_grad, value_weight_grad, line(13), line(10),
        line(11), flat[10752 : 10752 + 49152].reshape(12, 64, 64), out_weight_grad, line(5), line(3), line(4),
        up_weight_grad, flat[4608 : 4608 + 3072], down_weight_grad, line(2), line(0), line(1),
    )


def solution(mesh):
    in_specs = (P("batch", None, None, None), P(), P("batch", None, None, None)) + (P(),) * 18
    out_specs = (P("batch", None, None, None),) * 2 + (P(),) * 18
    return jax.shard_map(on_device, mesh=mesh, in_specs=in_specs, out_specs=out_specs, check_vma=False)
```

time: 956 us -> 416 us (0.44)
  waiting for transfers between devices: 512 us -> 141 us
  matrix products: 176 us -> 0 us
  Pallas kernels: 0 us -> 112 us
  other arithmetic: 93.3 us -> 18.5 us
  starting transfers between devices: 5.54 us -> 70.3 us
  blocking collectives: 44 us -> 0 us
  local copies, waits for them, and re-layouts: 102 us -> 64.7 us
  between operations: 15.2 us -> 2.41 us
    psum x1 -> x0, waiting for transfers between devices: 369 us -> none  [on_device(): lax.psum((query_weight_grad, query_bias_grad, key_weight_grad, value_weig...]
    dot_general x29 -> x0, matrix products: 176 us -> none  [the longest x1 16.6 us: on_device(): jnp.einsum('rphd,rkhd->rhpk', context_grad, value_heads, preferred_elemen...]
    pallas_call x0 -> x10, Pallas kernels: none -> 112 us  [the longest x1 34.2 us: ffn(): pl.pallas_call(ffn_kernel, out_shape=(b16(2, 64, 768), b16(2, 64, 768), b...]
    ppermute x8 -> x63, starting transfers between devices: 5.5 us -> 70.3 us  [partner(): return lax.ppermute(x, 'batch', [(i, i ^ bit) for i in range(size)])]
    psum x1 -> x0, blocking collectives: 44 us -> none  [on_device(): lax.psum((query_weight_grad, query_bias_grad, key_weight_grad, value_weig...]
    select_n x7 -> x2, other arithmetic: 42.1 us -> 2.23 us  [on_device(): layer_output = jnp.take(stacked, order, axis=0).reshape(1, 8, 64, 768)]
    reduce_sum x10 -> x0, other arithmetic: 21.8 us -> none  [the longest x1 6.3 us: on_device(): denominator = jnp.sum(raised, axis=-1, keepdims=True)]
    convert_element_type x3 -> x27, other arithmetic: 25 us -> 4.01 us  [the longest x22 3.65 us: plus(): return (a.astype(F32) + b.astype(F32)).astype(BF)]
  transfers between devices with their start and end apart: 9 -> 63, of which waited for: 5 -> 29; matrix products, arithmetic and copies ran while one was open for 22% -> 9% of each run, Pallas kernels for 0% -> 9%
where the time goes in v1:
time: 416 us; the launch traced here: 409 us
  waiting for transfers between devices  141 us (34%)
  Pallas kernels  112 us (27%)
  starting transfers between devices  70.3 us (17%)
  local copies, waits for them, and re-layouts  64.7 us (16%)
  other arithmetic  18.5 us (4%)
    ppermute x63, waiting for transfers between devices, partner(): return lax.ppermute(x, 'batch', [(i, i ^ bit) for i in range(size)])  141 us
    ppermute x63, starting transfers between devices, partner(): return lax.ppermute(x, 'batch', [(i, i ^ bit) for i in range(size)])  70.3 us
    unnamed x204, local copies, waits for them, and re-layouts  39.3 us
    pallas_call x1, Pallas kernels, ffn(): pl.pallas_call(ffn_kernel, out_shape=(b16(2, 64, 768), b16(2, 64, 768), b...  34.2 us
    pallas_call x2, Pallas kernels, attn_fwd(): pl.pallas_call(attn_fwd_kernel, out_shape=(b16(512, 768), b16(512, 768),...  21 us
    pallas_call x2, Pallas kernels, attn_bwd(): pl.pallas_call(attn_bwd_kernel, out_shape=(b16(512, 768), b16(512, 768),...  17.9 us
    pallas_call x1, Pallas kernels, proj(): pl.pallas_call(proj_kernel, out_shape=(piece, piece, piece, piece, b16(16...  15.9 us
  transfers between devices with their start and end apart: 63, of which 29 were waited for; matrix products, arithmetic and copies ran while one was open for 9% of the time, Pallas kernels for 9%

profile of v1, /device:TPU:0, one launch (start us, length us, event | category | flops | bytes accessed | tf_op | source)
XLA Modules:
  0.0 408.8 jit_solution(2240112729504822838)
XLA Ops:
  0.7 2.2 dynamic-slice_bitcast_fusion.8
  2.9 2.4 collective-permute-start.8
  20.2 1.8 mul.153
  23.3 1.8 mul.147
  25.0 1.6 broadcast_multiply_fusion.1
  28.8 1.8 collective-permute-start.2
  30.9 11.3 %attn_fwd.3 = (bf16[512,768]{1,0:T(8,128)(2,1)S(1)}, bf16[512,768]{1,0:T(8,128)(2,1)S(1)}, bf16[768,512]{1,0:T(8,128)(2,1)S(1)}, bf16[768,512]{1,0:T(8,128)(2,1)...) custom-call(bf16[128,768]{1,0:T(8,128)(2,1)S(1)} %get-tuple-element., ...), custom_call_target="tpu_custom_call" | custom-call | flops 4000000000 | bytes 12000000 | tf_op jit(solution)/shard_map/attn_fwd/pallas_call | solution.py:116
  50.9 9.7 %attn_fwd.2 = (bf16[512,768]{1,0:T(8,128)(2,1)S(1)}, bf16[512,768]{1,0:T(8,128)(2,1)S(1)}, bf16[768,512]{1,0:T(8,128)(2,1)S(1)}, bf16[768,512]{1,0:T(8,128)(2,1)...) custom-call(bf16[128,768]{1,0:T(8,128)(2,1)S(1)} %get-tuple-element., ...), custom_call_target="tpu_custom_call" | custom-call | flops 4000000000 | bytes 12000000 | tf_op jit(solution)/shard_map/attn_fwd/pallas_call | solution.py:116
  71.1 34.2 %ffn.1 = (bf16[2,64,768]{2,1,0:T(8,128)(2,1)}, bf16[2,64,768]{2,1,0:T(8,128)(2,1)}, bf16[2,64,768]{2,1,0:T(8,128)(2,1)}, bf16[2,64,768]{2,1,0:T(8,128)(2,1)}, f3...) custom-call(s32[2]{0:T(128)} %pad_add_fusion.masks, ...), custom_call_target="tpu_custom_call" | custom-call | flops 16000000000 | bytes 40000000 | tf_op jit(solution)/shard_map/ffn/pallas_call | solution.py:222
  115.3 9.0 %attn_bwd.2 = (bf16[512,768]{1,0:T(8,128)(2,1)S(1)}, bf16[512,768]{1,0:T(8,128)(2,1)S(1)}, bf16[256,768]{1,0:T(8,128)(2,1)S(1)}, f32[3,256,256]{2,1,0:T(8,128)S(1)}, f32[8,768]{1,0:T(8,128)S(1)}) custom-call(bf16[512,768]{1,0:T(8,128)(2,1)S(1)} %copy-done.25, bf16[512,768]{1,0:T(8,128)(2,1)S(1)} %copy-done.27, bf16[768,512]{1,0:T(8,128)(2,1)S(1)} %copy-done.29, ...), custom_call_target="tpu_custom_call" | custom-call | flops 8000000000 | bytes 12000000 | tf_op jit(solution)/shard_map/attn_bwd/pallas_call | solution.py:302
  128.6 8.9 %attn_bwd.3 = (bf16[512,768]{1,0:T(8,128)(2,1)S(1)}, bf16[512,768]{1,0:T(8,128)(2,1)S(1)}, bf16[256,768]{1,0:T(8,128)(2,1)S(1)}, f32[3,256,256]{2,1,0:T(8,128)S(1)}, f32[8,768]{1,0:T(8,128)S(1)}) custom-call(bf16[512,768]{1,0:T(8,128)(2,1)S(1)} %copy-done.18, bf16[512,768]{1,0:T(8,128)(2,1)S(1)} %copy-done.20, bf16[768,512]{1,0:T(8,128)(2,1)S(1)} %copy-done.22, ...), custom_call_target="tpu_custom_call" | custom-call | flops 8000000000 | bytes 12000000 | tf_op jit(solution)/shard_map/attn_bwd/pallas_call | solution.py:302
  142.4 15.9 %proj_back.1 = (bf16[2,128,768]{2,1,0:T(8,128)(2,1)}, bf16[2,128,768]{2,1,0:T(8,128)(2,1)}, bf16[2,128,768]{2,1,0:T(8,128)(2,1)}, bf16[2,128,768]{2,1,0:T(8,128)...) custom-call(s32[2]{0:T(128)} %pad_add_fusion.masks, ...), custom_call_target="tpu_custom_call" | custom-call | flops 8999999488 | bytes 25000000 | tf_op jit(solution)/shard_map/proj_back/pallas_call | solution.py:355
  162.8 1.8 collective-permute-start.16
  165.4 1.8 collective-permute-start.35
  172.5 6.5 %collective-permute-done.16 = bf16[8,18,16,128]{3,2,1,0:T(8,128)(2,1)S(1)} collective-permute-done((bf16[8,18,16,128]{3,2,1,0:T(8,128)(2,1)S(1)}, bf16[8,18,16,128]{3,2,1,0:T(8,128)(2,1)S(1)}, u32[]{:S(2)}, u32[]{:S(2)}) %collective-permute-start.16) | collective-permute-done | bytes 589856 | tf_op jit(solution)/shard_map/ppermute | solution.py:372
  179.0 1.8 collective-permute-start.19
  181.6 1.7 collective-permute-start.17
  183.5 8.1 %collective-permute-done.32 = bf16[8,18,16,128]{3,2,1,0:T(8,128)(2,1)S(1)} collective-permute-done((bf16[8,18,16,128]{3,2,1,0:T(8,128)(2,1)S(1)}, bf16[8,18,16,128]{3,2,1,0:T(8,128)(2,1)S(1)}, u32[]{:S(2)}, u32[]{:S(2)}) %collective-permute-start.32) | collective-permute-done | bytes 589856 | tf_op jit(solution)/shard_map/ppermute | solution.py:372
  191.6 1.8 collective-permute-start.36
  194.3 1.7 collective-permute-start.33
  196.2 8.1 %collective-permute-done.48 = bf16[8,18,16,128]{3,2,1,0:T(8,128)(2,1)S(1)} collective-permute-done((bf16[8,18,16,128]{3,2,1,0:T(8,128)(2,1)S(1)}, bf16[8,18,16,128]{3,2,1,0:T(8,128)(2,1)S(1)}, u32[]{:S(2)}, u32[]{:S(2)}) %collective-permute-start.48) | collective-permute-done | bytes 589856 | tf_op jit(solution)/shard_map/ppermute | solution.py:372
  204.2 1.8 collective-permute-start.52
  207.6 1.7 collective-permute-start.49
  210.6 1.8 collective-permute-start.20
  212.4 7.9 %collective-permute-done.33 = bf16[4,18,16,128]{3,2,1,0:T(8,128)(2,1)S(1)} collective-permute-done((bf16[4,18,16,128]{3,2,1,0:T(8,128)(2,1)S(1)}, bf16[4,18,16,128]{3,2,1,0:T(8,128)(2,1)S(1)}, u32[]{:S(2)}, u32[]{:S(2)}) %collective-permute-start.33) | collective-permute-done | bytes 294944 | tf_op jit(solution)/shard_map/ppermute | solution.py:372
  220.4 1.8 collective-permute-start.37
  222.3 3.5 collective-permute-done.49
  225.8 1.9 collective-permute-start.53
  228.3 2.9 collective-permute-start.38
  231.2 7.8 %collective-permute-done.53 = bf16[2,36,16,128]{3,2,1,0:T(8,128)(2,1)S(1)} collective-permute-done((bf16[2,36,16,128]{3,2,1,0:T(8,128)(2,1)S(1)}, bf16[2,36,16,128]{3,2,1,0:T(8,128)(2,1)S(1)}, u32[]{:S(2)}, u32[]{:S(2)}) %collective-permute-start.53) | collective-permute-done | bytes 294944 | tf_op jit(solution)/shard_map/ppermute | solution.py:372
  239.1 2.0 collective-permute-start.54
  241.1 4.9 %collective-permute-done.21 = bf16[2,37,16,128]{3,2,1,0:T(8,128)(2,1)S(1)} collective-permute-done((bf16[2,37,16,128]{3,2,1,0:T(8,128)(2,1)S(1)}, bf16[2,37,16,128]{3,2,1,0:T(8,128)(2,1)S(1)}, u32[]{:S(2)}, u32[]{:S(2)}) %collective-permute-start.21) | collective-permute-done | bytes 303136 | tf_op jit(solution)/shard_map/ppermute | solution.py:372
  247.4 10.3 %collective-permute-done.54 = bf16[1,36,16,128]{3,2,1,0:T(8,128)(2,1)S(1)} collective-permute-done((bf16[1,36,16,128]{3,2,1,0:T(8,128)(2,1)S(1)}, bf16[1,36,16,128]{3,2,1,0:T(8,128)(2,1)S(1)}, u32[]{:S(2)}, u32[]{:S(2)}) %collective-permute-start.54) | collective-permute-done | bytes 147488 | tf_op jit(solution)/shard_map/ppermute | solution.py:372
  257.8 3.0 collective-permute-start.39
  260.8 7.7 %collective-permute-done.55 = bf16[1,36,16,128]{3,2,1,0:T(8,128)(2,1)S(1)} collective-permute-done((bf16[1,36,16,128]{3,2,1,0:T(8,128)(2,1)S(1)}, bf16[1,36,16,128]{3,2,1,0:T(8,128)(2,1)S(1)}, u32[]{:S(2)}, u32[]{:S(2)}) %collective-permute-start.55) | collective-permute-done | bytes 147488 | tf_op jit(solution)/shard_map/ppermute | solution.py:372
  268.7 2.0 collective-permute-start.23
  270.7 2.1 collective-permute-done.39
  273.0 7.9 %collective-permute-done.56 = bf16[2,36,16,128]{3,2,1,0:T(8,128)(2,1)S(1)} collective-permute-done((bf16[2,36,16,128]{3,2,1,0:T(8,128)(2,1)S(1)}, bf16[2,36,16,128]{3,2,1,0:T(8,128)(2,1)S(1)}, u32[]{:S(2)}, u32[]{:S(2)}) %collective-permute-start.56) | collective-permute-done | bytes 294944 | tf_op jit(solution)/shard_map/ppermute | solution.py:372
  281.0 1.7 collective-permute-start.57
  282.8 4.2 %collective-permute-done.40 = bf16[2,36,16,128]{3,2,1,0:T(8,128)(2,1)S(1)} collective-permute-done((bf16[2,36,16,128]{3,2,1,0:T(8,128)(2,1)S(1)}, bf16[2,36,16,128]{3,2,1,0:T(8,128)(2,1)S(1)}, u32[]{:S(2)}, u32[]{:S(2)}) %collective-permute-start.40) | collective-permute-done | bytes 294944 | tf_op jit(solution)/shard_map/ppermute | solution.py:372
  287.1 3.7 collective-permute-done.57
  291.7 1.7 collective-permute-start.41
  295.6 2.9 collective-permute-done.41
  299.9 15.7 %collective-permute-done.43 = bf16[4,18,16,128]{3,2,1,0:T(8,128)(2,1)S(1)} collective-permute-done((bf16[4,18,16,128]{3,2,1,0:T(8,128)(2,1)S(1)}, bf16[4,18,16,128]{3,2,1,0:T(8,128)(2,1)S(1)}, u32[]{:S(2)}, u32[]{:S(2)}) %collective-permute-start.43) | collective-permute-done | bytes 294944 | tf_op jit(solution)/shard_map/ppermute | solution.py:372
  315.6 3.3 collective-permute-start.25
  319.0 2.0 collective-permute-start.42
  322.3 6.2 %collective-permute-done.59 = bf16[4,18,16,128]{3,2,1,0:T(8,128)(2,1)S(1)} collective-permute-done((bf16[4,18,16,128]{3,2,1,0:T(8,128)(2,1)S(1)}, bf16[4,18,16,128]{3,2,1,0:T(8,128)(2,1)S(1)}, u32[]{:S(2)}, u32[]{:S(2)}) %collective-permute-start.59) | collective-permute-done | bytes 294944 | tf_op jit(solution)/shard_map/ppermute | solution.py:372
  328.6 3.2 collective-permute-start.28
  333.2 3.9 collective-permute-start.26
  337.2 4.0 collective-permute-done.42
  343.5 8.6 %collective-permute-done.11 = bf16[2,64,768]{2,1,0:T(8,128)(2,1)S(1)} collective-permute-done((bf16[2,64,768]{2,1,0:T(8,128)(2,1)S(1)}, bf16[2,64,768]{2,1,0:T(8,128)(2,1)S(1)}, u32[]{:S(2)}, u32[]{:S(2)}) %collective-permute-start.11) | collective-permute-done | bytes 196640 | tf_op jit(solution)/shard_map/ppermute | solution.py:372
  352.1 1.9 collective-permute-start.12
  354.0 2.1 collective-permute-done.60
  356.1 1.8 collective-permute-start.13
  360.0 8.2 %collective-permute-done.13.p2 = bf16[2,128,768]{2,1,0:T(8,128)(2,1)S(1)} collective-permute-done((bf16[2,128,768]{2,1,0:T(8,128)(2,1)S(1)}, bf16[2,128,768]{2,1,0:T(8,128)(2,1)S(1)}, u32[]{:S(2)}, u32[]{:S(2)}) %collective-permute-start.13) | collective-permute-done | bytes 393248 | tf_op jit(solution)/shard_map/ppermute | solution.py:372
  368.1 3.6 collective-permute-done.14.p3
  372.5 1.6 collective-permute-start.46
  375.5 2.1 pad_maximum_fusion.7
  377.6 2.6 gather_fusion
  380.2 2.2 bitcast_select_fusion
  382.5 1.9 assemble_tokens.1
  385.2 6.0 %assemble_rows.1 = f32[3072,768]{1,0:T(8,128)} custom-call(s32[2]{0:T(128)S(1)} %copy-done.11, bf16[16,18,16,128]{3,2,1,0:T(8,128)(2,1)S(1)} %copy-done.1, bf16[16,18,16,128]{3,2,1,0:T(8,128)(2,1)} %pad_maximum_fusion.6.b0, bf16[16,18,16,128]{3,2,1,0:T(8,128)(2,1)S(1)} %copy-done.3, bf16[16,18,16,128]{3,2,1,0:T(8,128)(2,1)} %collective-permute-done.62.b1), custom_call_target="tpu_custom_call" | custom-call | bytes 14000000 | tf_op jit(solution)/shard_map/assemble_rows/pallas_call | solution.py:414
  391.2 7.9 %assemble_up.1 = f32[768,3072]{1,0:T(8,128)} custom-call(s32[2]{0:T(128)S(1)} %copy-done.11, bf16[16,18,16,128]{3,2,1,0:T(8,128)(2,1)} %pad_maximum_fusion.3.a0, bf16[16,18,16,128]{3,2,1,0:T(8,128)(2,1)} %pad_maximum_fusion.4.b0, bf16[16,18,16,128]{3,2,1,0:T(8,128)(2,1)} %collective-permute-done.45.a1, bf16[16,18,16,128]{3,2,1,0:T(8,128)(2,1)} %collective-permute-done.46.b1), custom_call_target="tpu_custom_call" | custom-call | bytes 14000000 | tf_op jit(solution)/shard_map/assemble_up/pallas_call | solution.py:443
  399.1 7.1 %assemble_four.1 = (f32[768,768]{1,0:T(8,128)}, f32[768,768]{1,0:T(8,128)}, f32[768,768]{1,0:T(8,128)}, f32[768,768]{1,0:T(8,128)}, f32[512,128]{1,0:T(8,128)S(1)}) custom-call(s32[2]{0:T(128)S(1)} %copy-done.11, bf16[16,18,16,128]{3,2,1,0:T(8,128)(2,1)S(1)} %pad_maximum_fusion.2.a0, bf16[16,19,16,128]{3,2,1,0:T(8,128)(2,1)S(1)} %pad_maximum_fusion.1.b0, ...), custom_call_target="tpu_custom_call" | custom-call | bytes 15000000 | tf_op jit(solution)/shard_map/assemble_four/pallas_call | solution.py:485
  (406 shorter events, 92.1 us)
Async XLA Ops:
  2.9 67.5 %collective-permute-start.8 = (bf16[2,64,768]{2,1,0:T(8,128)(2,1)}, bf16[2,64,768]{2,1,0:T(8,128)(2,1)}, u32[]{:S(2)}, u32[]{:S(2)}) collective-permute-start(bf16[2,64,768]{2,1,0:T(8,128)(2,1)} %get-tuple-element.166), channel_id=1, source_target_pairs={{0,3},{1,2},{2,1},{3,0},{4,7},{5,6},{6,5},{7,4},{8,11},{9,10},{10,... | collective-permute-start | bytes 589832 | tf_op jit(solution)/shard_map/ppermute | solution.py:372
  5.3 65.1 %collective-permute-start.7 = (bf16[2,64,768]{2,1,0:T(8,128)(2,1)}, bf16[2,64,768]{2,1,0:T(8,128)(2,1)}, u32[]{:S(2)}, u32[]{:S(2)}) collective-permute-start(bf16[2,64,768]{2,1,0:T(8,128)(2,1)} %get-tuple-element.167), channel_id=1, source_target_pairs={{0,2},{1,3},{2,0},{3,1},{4,6},{5,7},{6,4},{7,5},{8,10},{9,11},{10,... | collective-permute-start | bytes 589832 | tf_op jit(solution)/shard_map/ppermute | solution.py:372
  7.0 21.7 %collective-permute-start.5 = (bf16[128,768]{1,0:T(8,128)(2,1)}, bf16[128,768]{1,0:T(8,128)(2,1)S(1)}, u32[]{:S(2)}, u32[]{:S(2)}) collective-permute-start(bf16[128,768]{1,0:T(8,128)(2,1)} %get-tuple-element.156), channel_id=1, source_target_pairs={{0,3},{1,2},{2,1},{3,0},{4,7},{5,6},{6,5},{7,4},{8,11},{9,10},{10,... | collective-permute-start | bytes 589832 | tf_op jit(solution)/shard_map/ppermute | solution.py:372
  8.5 22.1 %collective-permute-start.4 = (bf16[128,768]{1,0:T(8,128)(2,1)}, bf16[128,768]{1,0:T(8,128)(2,1)}, u32[]{:S(2)}, u32[]{:S(2)}) collective-permute-start(bf16[128,768]{1,0:T(8,128)(2,1)} %get-tuple-element.161), channel_id=1, source_target_pairs={{0,2},{1,3},{2,0},{3,1},{4,6},{5,7},{6,4},{7,5},{8,10},{9,11},{10,... | collective-permute-start | bytes 589832 | tf_op jit(solution)/shard_map/ppermute | solution.py:372
  8.8 22.1 %collective-permute-start.3 = (bf16[128,768]{1,0:T(8,128)(2,1)}, bf16[128,768]{1,0:T(8,128)(2,1)}, u32[]{:S(2)}, u32[]{:S(2)}) collective-permute-start(bf16[128,768]{1,0:T(8,128)(2,1)} %get-tuple-element.162), channel_id=1, source_target_pairs={{0,1},{1,0},{2,3},{3,2},{4,5},{5,4},{6,7},{7,6},{8,9},{9,8},{10,11... | collective-permute-start | bytes 589832 | tf_op jit(solution)/shard_map/ppermute | solution.py:372
  16.8 91.1 %copy-start.9 = (f32[64,256]{1,0:T(8,128)}, f32[64,256]{1,0:T(8,128)S(1)}, u32[]{:S(2)}) copy-start(f32[64,256]{1,0:T(8,128)S(1)} %maximum_bitcast_fusion.1.sint) | copy-start | bytes 196612
  28.8 21.5 %collective-permute-start.2 = (bf16[128,768]{1,0:T(8,128)(2,1)S(1)}, bf16[128,768]{1,0:T(8,128)(2,1)S(1)}, u32[]{:S(2)}, u32[]{:S(2)}) collective-permute-start(bf16[128,768]{1,0:T(8,128)(2,1)S(1)} %copy-done.75), channel_id=1, source_target_pairs={{0,3},{1,2},{2,1},{3,0},{4,7},{5,6},{6,5},{7,4},{8,11},{9,10},{10,... | collective-permute-start | bytes 589832 | tf_op jit(solution)/shard_map/ppermute | solution.py:372
  30.6 20.3 %collective-permute-start.1 = (bf16[128,768]{1,0:T(8,128)(2,1)S(1)}, bf16[128,768]{1,0:T(8,128)(2,1)S(1)}, u32[]{:S(2)}, u32[]{:S(2)}) collective-permute-start(bf16[128,768]{1,0:T(8,128)(2,1)S(1)} %copy-done.74), channel_id=1, source_target_pairs={{0,2},{1,3},{2,0},{3,1},{4,6},{5,7},{6,4},{7,5},{8,10},{9,11},{10,... | collective-permute-start | bytes 589832 | tf_op jit(solution)/shard_map/ppermute | solution.py:372
  30.9 20.0 %collective-permute-start = (bf16[128,768]{1,0:T(8,128)(2,1)S(1)}, bf16[128,768]{1,0:T(8,128)(2,1)S(1)}, u32[]{:S(2)}, u32[]{:S(2)}) collective-permute-start(bf16[128,768]{1,0:T(8,128)(2,1)S(1)} %copy-done.73), channel_id=1, source_target_pairs={{0,1},{1,0},{2,3},{3,2},{4,5},{5,4},{6,7},{7,6},{8,9},{9,8},{10,11... | collective-permute-start | bytes 589832 | tf_op jit(solution)/shard_map/ppermute | solution.py:372
  50.3 20.1 %collective-permute-start.6 = (bf16[2,64,768]{2,1,0:T(8,128)(2,1)S(1)}, bf16[2,64,768]{2,1,0:T(8,128)(2,1)S(1)}, u32[]{:S(2)}, u32[]{:S(2)}) collective-permute-start(bf16[2,64,768]{2,1,0:T(8,128)(2,1)S(1)} %copy-done.72), channel_id=1, source_target_pairs={{0,1},{1,0},{2,3},{3,2},{4,5},{5,4},{6,7},{7,6},{8,9},{9,8},{10,11... | collective-permute-start | bytes 589832 | tf_op jit(solution)/shard_map/ppermute | solution.py:372
  158.2 3.1 collective-permute-start.15
  158.7 4.1 collective-permute-start.31
  159.2 5.3 %collective-permute-start.34 = (bf16[16,18,16,128]{3,2,1,0:T(8,128)(2,1)S(1)}, bf16[16,18,16,128]{3,2,1,0:T(8,128)(2,1)S(1)}, u32[]{:S(2)}, u32[]{:S(2)}) collective-permute-start(bf16[16,18,16,128]{3,2,1,0:T(8,128)(2,1)S(1)} %get-tuple-element.151), channel_id=1, source_target_pairs={{0,1},{1,0},{2,3},{3,2},{4,5},{5,4},{6,7},{7,6},{8,9},{9,8},{10,11... | collective-permute-start | bytes 3538952 | tf_op jit(solution)/shard_map/ppermute | solution.py:372
  160.4 6.8 %collective-permute-start.47 = (bf16[16,18,16,128]{3,2,1,0:T(8,128)(2,1)S(1)}, bf16[16,18,16,128]{3,2,1,0:T(8,128)(2,1)S(1)}, u32[]{:S(2)}, u32[]{:S(2)}) collective-permute-start(bf16[16,18,16,128]{3,2,1,0:T(8,128)(2,1)S(1)} %get-tuple-element.146), channel_id=1, source_target_pairs={{0,1},{1,0},{2,3},{3,2},{4,5},{5,4},{6,7},{7,6},{8,9},{9,8},{10,11... | collective-permute-start | bytes 3538952 | tf_op jit(solution)/shard_map/ppermute | solution.py:372
  160.9 7.8 %collective-permute-start.50 = (bf16[16,18,16,128]{3,2,1,0:T(8,128)(2,1)S(1)}, bf16[16,18,16,128]{3,2,1,0:T(8,128)(2,1)S(1)}, u32[]{:S(2)}, u32[]{:S(2)}) collective-permute-start(bf16[16,18,16,128]{3,2,1,0:T(8,128)(2,1)S(1)} %get-tuple-element.147), channel_id=1, source_target_pairs={{0,1},{1,0},{2,3},{3,2},{4,5},{5,4},{6,7},{7,6},{8,9},{9,8},{10,11... | collective-permute-start | bytes 3538952 | tf_op jit(solution)/shard_map/ppermute | solution.py:372
  161.3 9.2 %collective-permute-start.18 = (bf16[16,19,16,128]{3,2,1,0:T(8,128)(2,1)S(1)}, bf16[16,19,16,128]{3,2,1,0:T(8,128)(2,1)S(1)}, u32[]{:S(2)}, u32[]{:S(2)}) collective-permute-start(bf16[16,19,16,128]{3,2,1,0:T(8,128)(2,1)S(1)} %copy-done.92), channel_id=1, source_target_pairs={{0,1},{1,0},{2,3},{3,2},{4,5},{5,4},{6,7},{7,6},{8,9},{9,8},{10,11... | collective-permute-start | bytes 3735560 | tf_op jit(solution)/shard_map/ppermute | solution.py:372
  162.8 16.2 %collective-permute-start.16 = (bf16[8,18,16,128]{3,2,1,0:T(8,128)(2,1)S(1)}, bf16[8,18,16,128]{3,2,1,0:T(8,128)(2,1)S(1)}, u32[]{:S(2)}, u32[]{:S(2)}) collective-permute-start(bf16[8,18,16,128]{3,2,1,0:T(8,128)(2,1)S(1)} %slice.392), channel_id=1, source_target_pairs={{0,2},{1,3},{2,0},{3,1},{4,6},{5,7},{6,4},{7,5},{8,10},{9,11},{10,... | collective-permute-start | bytes 1769480 | tf_op jit(solution)/shard_map/ppermute | solution.py:372
  165.4 16.2 %collective-permute-start.35 = (bf16[8,18,16,128]{3,2,1,0:T(8,128)(2,1)S(1)}, bf16[8,18,16,128]{3,2,1,0:T(8,128)(2,1)S(1)}, u32[]{:S(2)}, u32[]{:S(2)}) collective-permute-start(bf16[8,18,16,128]{3,2,1,0:T(8,128)(2,1)S(1)} %slice.408), channel_id=1, source_target_pairs={{0,4},{1,5},{2,6},{3,7},{4,0},{5,1},{6,2},{7,3},{8,12},{9,13},{10,... | collective-permute-start | bytes 1769480 | tf_op jit(solution)/shard_map/ppermute | solution.py:372
  167.2 24.4 %collective-permute-start.32 = (bf16[8,18,16,128]{3,2,1,0:T(8,128)(2,1)S(1)}, bf16[8,18,16,128]{3,2,1,0:T(8,128)(2,1)S(1)}, u32[]{:S(2)}, u32[]{:S(2)}) collective-permute-start(bf16[8,18,16,128]{3,2,1,0:T(8,128)(2,1)S(1)} %slice.404), channel_id=1, source_target_pairs={{0,2},{1,3},{2,0},{3,1},{4,6},{5,7},{6,4},{7,5},{8,10},{9,11},{10,... | collective-permute-start | bytes 1769480 | tf_op jit(solution)/shard_map/ppermute | solution.py:372
  169.5 24.8 %collective-permute-start.51 = (bf16[8,18,16,128]{3,2,1,0:T(8,128)(2,1)S(1)}, bf16[8,18,16,128]{3,2,1,0:T(8,128)(2,1)S(1)}, u32[]{:S(2)}, u32[]{:S(2)}) collective-permute-start(bf16[8,18,16,128]{3,2,1,0:T(8,128)(2,1)S(1)} %slice.422), channel_id=1, source_target_pairs={{0,4},{1,5},{2,6},{3,7},{4,0},{5,1},{6,2},{7,3},{8,12},{9,13},{10,... | collective-permute-start | bytes 1769480 | tf_op jit(solution)/shard_map/ppermute | solution.py:372
  170.5 33.7 %collective-permute-start.48 = (bf16[8,18,16,128]{3,2,1,0:T(8,128)(2,1)S(1)}, bf16[8,18,16,128]{3,2,1,0:T(8,128)(2,1)S(1)}, u32[]{:S(2)}, u32[]{:S(2)}) collective-permute-start(bf16[8,18,16,128]{3,2,1,0:T(8,128)(2,1)S(1)} %slice.418), channel_id=1, source_target_pairs={{0,2},{1,3},{2,0},{3,1},{4,6},{5,7},{6,4},{7,5},{8,10},{9,11},{10,... | collective-permute-start | bytes 1769480 | tf_op jit(solution)/shard_map/ppermute | solution.py:372
  179.0 28.7 %collective-permute-start.19 = (bf16[8,19,16,128]{3,2,1,0:T(8,128)(2,1)S(1)}, bf16[8,19,16,128]{3,2,1,0:T(8,128)(2,1)S(1)}, u32[]{:S(2)}, u32[]{:S(2)}) collective-permute-start(bf16[8,19,16,128]{3,2,1,0:T(8,128)(2,1)S(1)} %slice.396), channel_id=1, source_target_pairs={{0,4},{1,5},{2,6},{3,7},{4,0},{5,1},{6,2},{7,3},{8,12},{9,13},{10,... | collective-permute-start | bytes 1867784 | tf_op jit(solution)/shard_map/ppermute | solution.py:372
  181.6 46.1 %collective-permute-start.17 = (bf16[4,18,16,128]{3,2,1,0:T(8,128)(2,1)S(1)}, bf16[4,18,16,128]{3,2,1,0:T(8,128)(2,1)S(1)}, u32[]{:S(2)}, u32[]{:S(2)}) collective-permute-start(bf16[4,18,16,128]{3,2,1,0:T(8,128)(2,1)S(1)} %slice.394), channel_id=1, source_target_pairs={{0,4},{1,5},{2,6},{3,7},{4,0},{5,1},{6,2},{7,3},{8,12},{9,13},{10,... | collective-permute-start | bytes 884744 | tf_op jit(solution)/shard_map/ppermute | solution.py:372
  191.6 19.0 %collective-permute-start.36 = (bf16[4,18,16,128]{3,2,1,0:T(8,128)(2,1)S(1)}, bf16[4,18,16,128]{3,2,1,0:T(8,128)(2,1)S(1)}, u32[]{:S(2)}, u32[]{:S(2)}) collective-permute-start(bf16[4,18,16,128]{3,2,1,0:T(8,128)(2,1)S(1)} %slice.410), channel_id=1, source_target_pairs={{0,2},{1,3},{2,0},{3,1},{4,6},{5,7},{6,4},{7,5},{8,10},{9,11},{10,... | collective-permute-start | bytes 884744 | tf_op jit(solution)/shard_map/ppermute | solution.py:372
  194.3 26.0 %collective-permute-start.33 = (bf16[4,18,16,128]{3,2,1,0:T(8,128)(2,1)S(1)}, bf16[4,18,16,128]{3,2,1,0:T(8,128)(2,1)S(1)}, u32[]{:S(2)}, u32[]{:S(2)}) collective-permute-start(bf16[4,18,16,128]{3,2,1,0:T(8,128)(2,1)S(1)} %slice.406), channel_id=1, source_target_pairs={{0,4},{1,5},{2,6},{3,7},{4,0},{5,1},{6,2},{7,3},{8,12},{9,13},{10,... | collective-permute-start | bytes 884744 | tf_op jit(solution)/shard_map/ppermute | solution.py:372
  204.2 18.0 %collective-permute-start.52 = (bf16[4,18,16,128]{3,2,1,0:T(8,128)(2,1)S(1)}, bf16[4,18,16,128]{3,2,1,0:T(8,128)(2,1)S(1)}, u32[]{:S(2)}, u32[]{:S(2)}) collective-permute-start(bf16[4,18,16,128]{3,2,1,0:T(8,128)(2,1)S(1)} %slice.424), channel_id=1, source_target_pairs={{0,2},{1,3},{2,0},{3,1},{4,6},{5,7},{6,4},{7,5},{8,10},{9,11},{10,... | collective-permute-start | bytes 884744 | tf_op jit(solution)/shard_map/ppermute | solution.py:372
  207.6 18.1 %collective-permute-start.49 = (bf16[4,18,16,128]{3,2,1,0:T(8,128)(2,1)S(1)}, bf16[4,18,16,128]{3,2,1,0:T(8,128)(2,1)S(1)}, u32[]{:S(2)}, u32[]{:S(2)}) collective-permute-start(bf16[4,18,16,128]{3,2,1,0:T(8,128)(2,1)S(1)} %slice.420), channel_id=1, source_target_pairs={{0,4},{1,5},{2,6},{3,7},{4,0},{5,1},{6,2},{7,3},{8,12},{9,13},{10,... | collective-permute-start | bytes 884744 | tf_op jit(solution)/shard_map/ppermute | solution.py:372
  210.6 17.2 %collective-permute-start.20 = (bf16[4,19,16,128]{3,2,1,0:T(8,128)(2,1)S(1)}, bf16[4,19,16,128]{3,2,1,0:T(8,128)(2,1)S(1)}, u32[]{:S(2)}, u32[]{:S(2)}) collective-permute-start(bf16[4,19,16,128]{3,2,1,0:T(8,128)(2,1)S(1)} %slice.398), channel_id=1, source_target_pairs={{0,2},{1,3},{2,0},{3,1},{4,6},{5,7},{6,4},{7,5},{8,10},{9,11},{10,... | collective-permute-start | bytes 933896 | tf_op jit(solution)/shard_map/ppermute | solution.py:372
  220.4 7.9 %collective-permute-start.37 = (bf16[2,36,16,128]{3,2,1,0:T(8,128)(2,1)S(1)}, bf16[2,36,16,128]{3,2,1,0:T(8,128)(2,1)S(1)}, u32[]{:S(2)}, u32[]{:S(2)}) collective-permute-start(bf16[2,36,16,128]{3,2,1,0:T(8,128)(2,1)S(1)} %pad_maximum_fusion.23), channel_id=1, source_target_pairs={{0,8},{1,9},{2,10},{3,11},{4,12},{5,13},{6,14},{7,15},{8,0},{9,1},... | collective-permute-start | bytes 884744 | tf_op jit(solution)/shard_map/ppermute | solution.py:372
  225.8 13.2 %collective-permute-start.53 = (bf16[2,36,16,128]{3,2,1,0:T(8,128)(2,1)S(1)}, bf16[2,36,16,128]{3,2,1,0:T(8,128)(2,1)S(1)}, u32[]{:S(2)}, u32[]{:S(2)}) collective-permute-start(bf16[2,36,16,128]{3,2,1,0:T(8,128)(2,1)S(1)} %pad_maximum_fusion.22), channel_id=1, source_target_pairs={{0,8},{1,9},{2,10},{3,11},{4,12},{5,13},{6,14},{7,15},{8,0},{9,1},... | collective-permute-start | bytes 884744 | tf_op jit(solution)/shard_map/ppermute | solution.py:372
  227.9 18.1 %collective-permute-start.21 = (bf16[2,37,16,128]{3,2,1,0:T(8,128)(2,1)S(1)}, bf16[2,37,16,128]{3,2,1,0:T(8,128)(2,1)S(1)}, u32[]{:S(2)}, u32[]{:S(2)}) collective-permute-start(bf16[2,37,16,128]{3,2,1,0:T(8,128)(2,1)S(1)} %pad_maximum_fusion.20), channel_id=1, source_target_pairs={{0,8},{1,9},{2,10},{3,11},{4,12},{5,13},{6,14},{7,15},{8,0},{9,1},... | collective-permute-start | bytes 909320 | tf_op jit(solution)/shard_map/ppermute | solution.py:372
  228.3 29.4 %collective-permute-start.38 = (bf16[1,36,16,128]{3,2,1,0:T(8,128)(2,1)S(1)}, bf16[1,36,16,128]{3,2,1,0:T(8,128)(2,1)S(1)}, u32[]{:S(2)}, u32[]{:S(2)}) collective-permute-start(bf16[1,36,16,128]{3,2,1,0:T(8,128)(2,1)S(1)} %slice.414), channel_id=1, source_target_pairs={{0,16},{1,17},{2,18},{3,19},{4,20},{5,21},{6,22},{7,23},{8,24},{9,... | collective-permute-start | bytes 442376 | tf_op jit(solution)/shard_map/ppermute | solution.py:372
  239.1 18.5 %collective-permute-start.54 = (bf16[1,36,16,128]{3,2,1,0:T(8,128)(2,1)S(1)}, bf16[1,36,16,128]{3,2,1,0:T(8,128)(2,1)S(1)}, u32[]{:S(2)}, u32[]{:S(2)}) collective-permute-start(bf16[1,36,16,128]{3,2,1,0:T(8,128)(2,1)S(1)} %slice.428), channel_id=1, source_target_pairs={{0,16},{1,17},{2,18},{3,19},{4,20},{5,21},{6,22},{7,23},{8,24},{9,... | collective-permute-start | bytes 442376 | tf_op jit(solution)/shard_map/ppermute | solution.py:372
  246.1 22.5 %collective-permute-start.22 = (bf16[1,37,16,128]{3,2,1,0:T(8,128)(2,1)S(1)}, bf16[1,37,16,128]{3,2,1,0:T(8,128)(2,1)S(1)}, u32[]{:S(2)}, u32[]{:S(2)}) collective-permute-start(bf16[1,37,16,128]{3,2,1,0:T(8,128)(2,1)S(1)} %slice.402), channel_id=1, source_target_pairs={{0,16},{1,17},{2,18},{3,19},{4,20},{5,21},{6,22},{7,23},{8,24},{9,... | collective-permute-start | bytes 454664 | tf_op jit(solution)/shard_map/ppermute | solution.py:372
  257.7 10.8 %collective-permute-start.55 = (bf16[1,36,16,128]{3,2,1,0:T(8,128)(2,1)S(1)}, bf16[1,36,16,128]{3,2,1,0:T(8,128)(2,1)S(1)}, u32[]{:S(2)}, u32[]{:S(2)}) collective-permute-start(bf16[1,36,16,128]{3,2,1,0:T(8,128)(2,1)S(1)} %add_convert_fusion.18), channel_id=1, source_target_pairs={{0,16},{1,17},{2,18},{3,19},{4,20},{5,21},{6,22},{7,23},{8,24},{9,... | collective-permute-start | bytes 442376 | tf_op jit(solution)/shard_map/ppermute | solution.py:372
  257.8 15.0 %collective-permute-start.39 = (bf16[1,36,16,128]{3,2,1,0:T(8,128)(2,1)S(1)}, bf16[1,36,16,128]{3,2,1,0:T(8,128)(2,1)S(1)}, u32[]{:S(2)}, u32[]{:S(2)}) collective-permute-start(bf16[1,36,16,128]{3,2,1,0:T(8,128)(2,1)S(1)} %add_convert_fusion.19), channel_id=1, source_target_pairs={{0,16},{1,17},{2,18},{3,19},{4,20},{5,21},{6,22},{7,23},{8,24},{9,... | collective-permute-start | bytes 442376 | tf_op jit(solution)/shard_map/ppermute | solution.py:372
  268.5 12.3 %collective-permute-start.56 = (bf16[2,36,16,128]{3,2,1,0:T(8,128)(2,1)S(1)}, bf16[2,36,16,128]{3,2,1,0:T(8,128)(2,1)S(1)}, u32[]{:S(2)}, u32[]{:S(2)}) collective-permute-start(bf16[2,36,16,128]{3,2,1,0:T(8,128)(2,1)S(1)} %pad_maximum_fusion.26), channel_id=1, source_target_pairs={{0,8},{1,9},{2,10},{3,11},{4,12},{5,13},{6,14},{7,15},{8,0},{9,1},... | collective-permute-start | bytes 884744 | tf_op jit(solution)/shard_map/ppermute | solution.py:372
  268.7 14.0 %collective-permute-start.23 = (bf16[1,37,16,128]{3,2,1,0:T(8,128)(2,1)S(1)}, bf16[1,37,16,128]{3,2,1,0:T(8,128)(2,1)S(1)}, u32[]{:S(2)}, u32[]{:S(2)}) collective-permute-start(bf16[1,37,16,128]{3,2,1,0:T(8,128)(2,1)S(1)} %add_convert_fusion.17), channel_id=1, source_target_pairs={{0,16},{1,17},{2,18},{3,19},{4,20},{5,21},{6,22},{7,23},{8,24},{9,... | collective-permute-start | bytes 454664 | tf_op jit(solution)/shard_map/ppermute | solution.py:372
  272.9 14.1 %collective-permute-start.40 = (bf16[2,36,16,128]{3,2,1,0:T(8,128)(2,1)S(1)}, bf16[2,36,16,128]{3,2,1,0:T(8,128)(2,1)S(1)}, u32[]{:S(2)}, u32[]{:S(2)}) collective-permute-start(bf16[2,36,16,128]{3,2,1,0:T(8,128)(2,1)S(1)} %pad_maximum_fusion.25), channel_id=1, source_target_pairs={{0,8},{1,9},{2,10},{3,11},{4,12},{5,13},{6,14},{7,15},{8,0},{9,1},... | collective-permute-start | bytes 884744 | tf_op jit(solution)/shard_map/ppermute | solution.py:372
  281.0 9.8 %collective-permute-start.57 = (bf16[4,18,16,128]{3,2,1,0:T(8,128)(2,1)S(1)}, bf16[4,18,16,128]{3,2,1,0:T(8,128)(2,1)S(1)}, u32[]{:S(2)}, u32[]{:S(2)}) collective-permute-start(bf16[4,18,16,128]{3,2,1,0:T(8,128)(2,1)S(1)} %get-tuple-element.171), channel_id=1, source_target_pairs={{0,4},{1,5},{2,6},{3,7},{4,0},{5,1},{6,2},{7,3},{8,12},{9,13},{10,... | collective-permute-start | bytes 884744 | tf_op jit(solution)/shard_map/ppermute | solution.py:372
  282.7 12.2 %collective-permute-start.24 = (bf16[2,37,16,128]{3,2,1,0:T(8,128)(2,1)S(1)}, bf16[2,37,16,128]{3,2,1,0:T(8,128)(2,1)S(1)}, u32[]{:S(2)}, u32[]{:S(2)}) collective-permute-start(bf16[2,37,16,128]{3,2,1,0:T(8,128)(2,1)S(1)} %pad_maximum_fusion.21), channel_id=1, source_target_pairs={{0,8},{1,9},{2,10},{3,11},{4,12},{5,13},{6,14},{7,15},{8,0},{9,1},... | collective-permute-start | bytes 909320 | tf_op jit(solution)/shard_map/ppermute | solution.py:372
  290.9 28.1 %collective-permute-start.58 = (bf16[8,18,16,128]{3,2,1,0:T(8,128)(2,1)S(1)}, bf16[8,18,16,128]{3,2,1,0:T(8,128)(2,1)S(1)}, u32[]{:S(2)}, u32[]{:S(2)}) collective-permute-start(bf16[8,18,16,128]{3,2,1,0:T(8,128)(2,1)S(1)} %pad_maximum_fusion.14), channel_id=1, source_target_pairs={{0,2},{1,3},{2,0},{3,1},{4,6},{5,7},{6,4},{7,5},{8,10},{9,11},{10,... | collective-permute-start | bytes 1769480 | tf_op jit(solution)/shard_map/ppermute | solution.py:372
  291.7 6.8 %collective-permute-start.41 = (bf16[4,18,16,128]{3,2,1,0:T(8,128)(2,1)S(1)}, bf16[4,18,16,128]{3,2,1,0:T(8,128)(2,1)S(1)}, u32[]{:S(2)}, u32[]{:S(2)}) collective-permute-start(bf16[4,18,16,128]{3,2,1,0:T(8,128)(2,1)S(1)} %get-tuple-element.173), channel_id=1, source_target_pairs={{0,4},{1,5},{2,6},{3,7},{4,0},{5,1},{6,2},{7,3},{8,12},{9,13},{10,... | collective-permute-start | bytes 884744 | tf_op jit(solution)/shard_map/ppermute | solution.py:372
  293.4 22.2 %collective-permute-start.9 = (bf16[2,64,768]{2,1,0:T(8,128)(2,1)S(1)}, bf16[2,64,768]{2,1,0:T(8,128)(2,1)S(1)}, u32[]{:S(2)}, u32[]{:S(2)}) collective-permute-start(bf16[2,64,768]{2,1,0:T(8,128)(2,1)S(1)} %copy-done.98), channel_id=1, source_target_pairs={{0,1},{1,0},{2,3},{3,2},{4,5},{5,4},{6,7},{7,6},{8,9},{9,8},{10,11... | collective-permute-start | bytes 589832 | tf_op jit(solution)/shard_map/ppermute | solution.py:372
  293.4 25.5 %collective-permute-start.10 = (bf16[2,64,768]{2,1,0:T(8,128)(2,1)S(1)}, bf16[2,64,768]{2,1,0:T(8,128)(2,1)S(1)}, u32[]{:S(2)}, u32[]{:S(2)}) collective-permute-start(bf16[2,64,768]{2,1,0:T(8,128)(2,1)S(1)} %copy-done.97), channel_id=1, source_target_pairs={{0,2},{1,3},{2,0},{3,1},{4,6},{5,7},{6,4},{7,5},{8,10},{9,11},{10,... | collective-permute-start | bytes 589832 | tf_op jit(solution)/shard_map/ppermute | solution.py:372
  294.9 20.6 %collective-permute-start.43 = (bf16[4,18,16,128]{3,2,1,0:T(8,128)(2,1)S(1)}, bf16[4,18,16,128]{3,2,1,0:T(8,128)(2,1)S(1)}, u32[]{:S(2)}, u32[]{:S(2)}) collective-permute-start(bf16[4,18,16,128]{3,2,1,0:T(8,128)(2,1)S(1)} %get-tuple-element.172), channel_id=1, source_target_pairs={{0,2},{1,3},{2,0},{3,1},{4,6},{5,7},{6,4},{7,5},{8,10},{9,11},{10,... | collective-permute-start | bytes 884744 | tf_op jit(solution)/shard_map/ppermute | solution.py:372
  298.5 23.7 %collective-permute-start.27 = (bf16[4,19,16,128]{3,2,1,0:T(8,128)(2,1)S(1)}, bf16[4,19,16,128]{3,2,1,0:T(8,128)(2,1)S(1)}, u32[]{:S(2)}, u32[]{:S(2)}) collective-permute-start(bf16[4,19,16,128]{3,2,1,0:T(8,128)(2,1)S(1)} %pad_maximum_fusion.18), channel_id=1, source_target_pairs={{0,2},{1,3},{2,0},{3,1},{4,6},{5,7},{6,4},{7,5},{8,10},{9,11},{10,... | collective-permute-start | bytes 933896 | tf_op jit(solution)/shard_map/ppermute | solution.py:372
  315.6 13.0 %collective-permute-start.59 = (bf16[4,18,16,128]{3,2,1,0:T(8,128)(2,1)S(1)}, bf16[4,18,16,128]{3,2,1,0:T(8,128)(2,1)S(1)}, u32[]{:S(2)}, u32[]{:S(2)}) collective-permute-start(bf16[4,18,16,128]{3,2,1,0:T(8,128)(2,1)S(1)} %get-tuple-element.170), channel_id=1, source_target_pairs={{0,2},{1,3},{2,0},{3,1},{4,6},{5,7},{6,4},{7,5},{8,10},{9,11},{10,... | collective-permute-start | bytes 884744 | tf_op jit(solution)/shard_map/ppermute | solution.py:372
  315.6 16.2 %collective-permute-start.25 = (bf16[4,18,16,128]{3,2,1,0:T(8,128)(2,1)S(1)}, bf16[4,18,16,128]{3,2,1,0:T(8,128)(2,1)S(1)}, u32[]{:S(2)}, u32[]{:S(2)}) collective-permute-start(bf16[4,18,16,128]{3,2,1,0:T(8,128)(2,1)S(1)} %pad_maximum_fusion.24), channel_id=1, source_target_pairs={{0,4},{1,5},{2,6},{3,7},{4,0},{5,1},{6,2},{7,3},{8,12},{9,13},{10,... | collective-permute-start | bytes 884744 | tf_op jit(solution)/shard_map/ppermute | solution.py:372
  318.9 14.3 %collective-permute-start.44 = (bf16[8,18,16,128]{3,2,1,0:T(8,128)(2,1)S(1)}, bf16[8,18,16,128]{3,2,1,0:T(8,128)(2,1)S(1)}, u32[]{:S(2)}, u32[]{:S(2)}) collective-permute-start(bf16[8,18,16,128]{3,2,1,0:T(8,128)(2,1)S(1)} %pad_maximum_fusion.12), channel_id=1, source_target_pairs={{0,4},{1,5},{2,6},{3,7},{4,0},{5,1},{6,2},{7,3},{8,12},{9,13},{10,... | collective-permute-start | bytes 1769480 | tf_op jit(solution)/shard_map/ppermute | solution.py:372
  319.0 22.2 %collective-permute-start.42 = (bf16[8,18,16,128]{3,2,1,0:T(8,128)(2,1)S(1)}, bf16[8,18,16,128]{3,2,1,0:T(8,128)(2,1)S(1)}, u32[]{:S(2)}, u32[]{:S(2)}) collective-permute-start(bf16[8,18,16,128]{3,2,1,0:T(8,128)(2,1)S(1)} %pad_maximum_fusion.11), channel_id=1, source_target_pairs={{0,2},{1,3},{2,0},{3,1},{4,6},{5,7},{6,4},{7,5},{8,10},{9,11},{10,... | collective-permute-start | bytes 1769480 | tf_op jit(solution)/shard_map/ppermute | solution.py:372
  322.2 51.8 %collective-permute-start.61 = (bf16[16,18,16,128]{3,2,1,0:T(8,128)(2,1)S(1)}, bf16[16,18,16,128]{3,2,1,0:T(8,128)(2,1)S(1)}, u32[]{:S(2)}, u32[]{:S(2)}) collective-permute-start(bf16[16,18,16,128]{3,2,1,0:T(8,128)(2,1)S(1)} %pad_maximum_fusion.5.a0), channel_id=1, source_target_pairs={{0,1},{1,0},{2,3},{3,2},{4,5},{5,4},{6,7},{7,6},{8,9},{9,8},{10,11... | collective-permute-start | bytes 3538952 | tf_op jit(solution)/shard_map/ppermute | solution.py:372
  328.6 29.4 %collective-permute-start.28 = (bf16[8,19,16,128]{3,2,1,0:T(8,128)(2,1)S(1)}, bf16[8,19,16,128]{3,2,1,0:T(8,128)(2,1)S(1)}, u32[]{:S(2)}, u32[]{:S(2)}) collective-permute-start(bf16[8,19,16,128]{3,2,1,0:T(8,128)(2,1)S(1)} %pad_maximum_fusion.8), channel_id=1, source_target_pairs={{0,4},{1,5},{2,6},{3,7},{4,0},{5,1},{6,2},{7,3},{8,12},{9,13},{10,... | collective-permute-start | bytes 1867784 | tf_op jit(solution)/shard_map/ppermute | solution.py:372
  331.8 24.3 %collective-permute-start.60 = (bf16[8,18,16,128]{3,2,1,0:T(8,128)(2,1)S(1)}, bf16[8,18,16,128]{3,2,1,0:T(8,128)(2,1)S(1)}, u32[]{:S(2)}, u32[]{:S(2)}) collective-permute-start(bf16[8,18,16,128]{3,2,1,0:T(8,128)(2,1)S(1)} %pad_maximum_fusion.15), channel_id=1, source_target_pairs={{0,4},{1,5},{2,6},{3,7},{4,0},{5,1},{6,2},{7,3},{8,12},{9,13},{10,... | collective-permute-start | bytes 1769480 | tf_op jit(solution)/shard_map/ppermute | solution.py:372
  333.2 26.0 %collective-permute-start.26 = (bf16[8,18,16,128]{3,2,1,0:T(8,128)(2,1)S(1)}, bf16[8,18,16,128]{3,2,1,0:T(8,128)(2,1)S(1)}, u32[]{:S(2)}, u32[]{:S(2)}) collective-permute-start(bf16[8,18,16,128]{3,2,1,0:T(8,128)(2,1)S(1)} %pad_maximum_fusion.9), channel_id=1, source_target_pairs={{0,2},{1,3},{2,0},{3,1},{4,6},{5,7},{6,4},{7,5},{8,10},{9,11},{10,... | collective-permute-start | bytes 1769480 | tf_op jit(solution)/shard_map/ppermute | solution.py:372
  341.2 10.8 %collective-permute-start.11 = (bf16[2,64,768]{2,1,0:T(8,128)(2,1)S(1)}, bf16[2,64,768]{2,1,0:T(8,128)(2,1)S(1)}, u32[]{:S(2)}, u32[]{:S(2)}) collective-permute-start(bf16[2,64,768]{2,1,0:T(8,128)(2,1)S(1)} %copy-done.96), channel_id=1, source_target_pairs={{0,3},{1,2},{2,1},{3,0},{4,7},{5,6},{6,5},{7,4},{8,11},{9,10},{10,... | collective-permute-start | bytes 589832 | tf_op jit(solution)/shard_map/ppermute | solution.py:372
  352.1 7.7 %collective-permute-start.12 = (bf16[2,128,768]{2,1,0:T(8,128)(2,1)S(1)}, bf16[2,128,768]{2,1,0:T(8,128)(2,1)S(1)}, u32[]{:S(2)}, u32[]{:S(2)}) collective-permute-start(bf16[2,128,768]{2,1,0:T(8,128)(2,1)S(1)} %copy-done.95), channel_id=1, source_target_pairs={{0,1},{1,0},{2,3},{3,2},{4,5},{5,4},{6,7},{7,6},{8,9},{9,8},{10,11... | collective-permute-start | bytes 1179656 | tf_op jit(solution)/shard_map/ppermute | solution.py:372
  356.1 12.1 %collective-permute-start.13 = (bf16[2,128,768]{2,1,0:T(8,128)(2,1)S(1)}, bf16[2,128,768]{2,1,0:T(8,128)(2,1)S(1)}, u32[]{:S(2)}, u32[]{:S(2)}) collective-permute-start(bf16[2,128,768]{2,1,0:T(8,128)(2,1)S(1)} %copy-done.94), channel_id=1, source_target_pairs={{0,2},{1,3},{2,0},{3,1},{4,6},{5,7},{6,4},{7,5},{8,10},{9,11},{10,... | collective-permute-start | bytes 1179656 | tf_op jit(solution)/shard_map/ppermute | solution.py:372
  357.9 13.8 %collective-permute-start.14 = (bf16[2,128,768]{2,1,0:T(8,128)(2,1)S(1)}, bf16[2,128,768]{2,1,0:T(8,128)(2,1)S(1)}, u32[]{:S(2)}, u32[]{:S(2)}) collective-permute-start(bf16[2,128,768]{2,1,0:T(8,128)(2,1)S(1)} %copy-done.93), channel_id=1, source_target_pairs={{0,3},{1,2},{2,1},{3,0},{4,7},{5,6},{6,5},{7,4},{8,11},{9,10},{10,... | collective-permute-start | bytes 1179656 | tf_op jit(solution)/shard_map/ppermute | solution.py:372
  359.2 39.9 %collective-permute-start.30 = (bf16[16,19,16,128]{3,2,1,0:T(8,128)(2,1)S(1)}, bf16[16,19,16,128]{3,2,1,0:T(8,128)(2,1)}, u32[]{:S(2)}, u32[]{:S(2)}) collective-permute-start(bf16[16,19,16,128]{3,2,1,0:T(8,128)(2,1)S(1)} %pad_maximum_fusion.1.b0), channel_id=1, source_target_pairs={{0,1},{1,0},{2,3},{3,2},{4,5},{5,4},{6,7},{7,6},{8,9},{9,8},{10,11... | collective-permute-start | bytes 3735560 | tf_op jit(solution)/shard_map/ppermute | solution.py:372
  359.7 24.6 %collective-permute-start.62 = (bf16[16,18,16,128]{3,2,1,0:T(8,128)(2,1)}, bf16[16,18,16,128]{3,2,1,0:T(8,128)(2,1)}, u32[]{:S(2)}, u32[]{:S(2)}) collective-permute-start(bf16[16,18,16,128]{3,2,1,0:T(8,128)(2,1)} %pad_maximum_fusion.6.b0), channel_id=1, source_target_pairs={{0,1},{1,0},{2,3},{3,2},{4,5},{5,4},{6,7},{7,6},{8,9},{9,8},{10,11... | collective-permute-start | bytes 3538952 | tf_op jit(solution)/shard_map/ppermute | solution.py:372
  368.1 23.1 %collective-permute-start.45 = (bf16[16,18,16,128]{3,2,1,0:T(8,128)(2,1)}, bf16[16,18,16,128]{3,2,1,0:T(8,128)(2,1)}, u32[]{:S(2)}, u32[]{:S(2)}) collective-permute-start(bf16[16,18,16,128]{3,2,1,0:T(8,128)(2,1)} %pad_maximum_fusion.3.a0), channel_id=1, source_target_pairs={{0,1},{1,0},{2,3},{3,2},{4,5},{5,4},{6,7},{7,6},{8,9},{9,8},{10,11... | collective-permute-start | bytes 3538952 | tf_op jit(solution)/shard_map/ppermute | solution.py:372
  372.5 18.8 %collective-permute-start.46 = (bf16[16,18,16,128]{3,2,1,0:T(8,128)(2,1)}, bf16[16,18,16,128]{3,2,1,0:T(8,128)(2,1)}, u32[]{:S(2)}, u32[]{:S(2)}) collective-permute-start(bf16[16,18,16,128]{3,2,1,0:T(8,128)(2,1)} %pad_maximum_fusion.4.b0), channel_id=1, source_target_pairs={{0,1},{1,0},{2,3},{3,2},{4,5},{5,4},{6,7},{7,6},{8,9},{9,8},{10,11... | collective-permute-start | bytes 3538952 | tf_op jit(solution)/shard_map/ppermute | solution.py:372
  375.1 24.0 %collective-permute-start.29 = (bf16[16,18,16,128]{3,2,1,0:T(8,128)(2,1)S(1)}, bf16[16,18,16,128]{3,2,1,0:T(8,128)(2,1)}, u32[]{:S(2)}, u32[]{:S(2)}) collective-permute-start(bf16[16,18,16,128]{3,2,1,0:T(8,128)(2,1)S(1)} %pad_maximum_fusion.2.a0), channel_id=1, source_target_pairs={{0,1},{1,0},{2,3},{3,2},{4,5},{5,4},{6,7},{7,6},{8,9},{9,8},{10,11... | collective-permute-start | bytes 3538952 | tf_op jit(solution)/shard_map/ppermute | solution.py:372
  (99 other events, 512.9 us)

commit v2 on v1

v2 whole, which is shorter than its diff:
```python
import functools
import math

import jax
import jax.numpy as jnp
from jax import lax
from jax.experimental import pallas as pl
from jax.experimental.pallas import tpu as pltpu
from jax.sharding import PartitionSpec as P

G = 4
F32 = jnp.float32
BF = jnp.bfloat16
VM = pl.BlockSpec(memory_space=pltpu.VMEM)
SM = pl.BlockSpec(memory_space=pltpu.SMEM)
ANY = pl.BlockSpec(memory_space=pl.ANY)
HBM = pl.BlockSpec(memory_space=pltpu.HBM)
BLK = 16
NA = 12
CH = 512


def nn(a, b):
    return lax.dot_general(a, b, (((1,), (0,)), ((), ())), preferred_element_type=F32)


def nt(a, b):
    return lax.dot_general(a, b, (((1,), (1,)), ((), ())), preferred_element_type=F32)


def tn(a, b):
    return lax.dot_general(a, b, (((0,), (0,)), ((), ())), preferred_element_type=F32)


def split(a):
    hi = a.astype(BF)
    return hi, (a - hi.astype(F32)).astype(BF)


def three(dot, a_hi, a_lo, b_hi, b_lo):
    return dot(a_hi, b_hi) + (dot(a_hi, b_lo) + dot(a_lo, b_hi))


def params(mib):
    return pltpu.CompilerParams(vmem_limit_bytes=mib << 20)


def cost(flops, bytes_accessed, transcendentals=0):
    return pl.CostEstimate(
        flops=flops, bytes_accessed=bytes_accessed, transcendentals=transcendentals
    )


def b16(*shape):
    return jax.ShapeDtypeStruct(shape, BF)


def f32(*shape):
    return jax.ShapeDtypeStruct(shape, F32)


TOKEN = (8, 128)


def call(
    kernel, name, scalars, args, outs, scratch=(), after=(), mib=16, flops=0, moved=0, far_outs=(), last=False, far_args=(),
    aliases=(),
):
    waits = len(after)
    at = waits + len(scalars) + len(args) + len(outs)

    def body(*refs):
        refs[at][...] = jnp.zeros(TOKEN, F32)
        kernel(*refs[waits:at], *refs[at + 1 :])

    place = lambda i, o: o if last else (pltpu.HBM if i in far_outs else pltpu.VMEM)(o.shape, o.dtype)
    space = lambda i: pltpu.HBM if i in far_args else pltpu.VMEM
    near = [a if last else pltpu.with_memory_space_constraint(a, space(i)) for i, a in enumerate(args)]
    return pl.pallas_call(
        body,
        out_shape=tuple(place(i, o) for i, o in enumerate(outs)) + (pltpu.VMEM(TOKEN, F32),),
        in_specs=[ANY] * waits + [SM] * len(scalars) + [HBM if i in far_args else VM for i in range(len(args))],
        out_specs=tuple(HBM if i in far_outs else VM for i in range(len(outs))) + (VM,),
        scratch_shapes=list(scratch),
        compiler_params=params(mib),
        cost_estimate=cost(flops, moved),
        input_output_aliases={waits + len(scalars) + i: o for i, o in aliases},
        name=name,
    )(*after, *scalars, *near)


def gate(arrays, after):
    n = len(arrays)
    outs = tuple(jax.ShapeDtypeStruct(a.shape, a.dtype) for a in arrays)
    return call(lambda *refs: None, "gate", (), arrays, outs, after=after, mib=4, aliases=[(i, i) for i in range(n)])


def call_grid(kernel, name, steps, scalars, args, outs, out_specs, after, mib, moved):
    waits = len(after)
    at = waits + len(scalars) + len(args) + len(outs)

    def body(*refs):
        refs[at][...] = jnp.zeros(TOKEN, F32)
        kernel(*refs[waits:at])

    return pl.pallas_call(
        body,
        out_shape=(*outs, pltpu.VMEM(TOKEN, F32)),
        grid=(steps,),
        in_specs=[ANY] * waits + [SM] * len(scalars) + [VM] * len(args),
        out_specs=(*out_specs, VM),
        compiler_params=params(mib),
        cost_estimate=cost(0, moved),
        name=name,
    )(*after, *scalars, *args)


def sems(n):
    return pltpu.SemaphoreType.DMA((n,))


def vs(*shape, dtype=F32):
    return pltpu.VMEM(shape, dtype)


def tables_kernel(scalars, lengths, near_q, far_q, kst, kf_out):
    j = scalars[0]
    exponent = -math.log(10000.0) / 32

    def positions(shape, size, step):
        row = lax.broadcasted_iota(jnp.int32, shape, 0)
        return step * (((row // size) ^ j) * size + row % size)

    def angles(shape, size, step):
        lane = lax.broadcasted_iota(jnp.int32, shape, 1)
        w = jnp.exp((lane % 32).astype(F32) * exponent)
        return positions(shape, size, step).astype(F32) * w, lane % 64 < 32

    theta, early = angles((256, 128), 64, 2)
    sin, cos = jnp.sin(theta), jnp.cos(theta)
    signed = jnp.where(early, cos, -cos)
    near_q[:, :128] = sin
    near_q[:, 128:] = signed
    far_q[:64] = sin.T[:64]
    far_q[64:] = -signed.T[:64]
    angle, early = angles((512, 128), 128, 1)
    sin, cos = jnp.sin(angle), jnp.cos(angle)
    kf = jnp.where(early, cos, sin)
    lane = lax.broadcasted_iota(jnp.int32, (512, 128), 1)
    kst[...] = jnp.where(lane < 64, kf, jnp.where(early, sin, cos)).astype(BF).T
    place = positions((512, 128), 128, 1)
    for r in range(2):
        bias = jnp.where(place < lengths[scalars[1] + r], 0.0, -1.0e9)
        kf_out[r, 0] = jnp.where(lane < 64, kf, jnp.where(lane == 64, bias, 0.0)).astype(BF)
        kf_out[r, 1] = jnp.where(lane >= 64, kf, jnp.where(lane == 0, bias, 0.0)).astype(BF)


def tables(scalars, lengths, after):
    outs = (f32(256, 256), f32(128, 256), b16(128, 512), b16(2, 2, 512, 128))
    return call(tables_kernel, "tables", (scalars, lengths), (), outs, after=after)


def spread_heads(weight, high, low, sides):
    for g in range(3):
        high[g] = jnp.zeros((256, 256 * sides), BF)
        low[g] = jnp.zeros((256, 256 * sides), BF)
        for a in range(4):
            hi, lo = split(weight[4 * g + a])
            at = slice(64 * a, 64 * a + 64)
            high[g, at, at] = hi
            low[g, at, at] = lo
            if sides == 2:
                there = slice(256 + 64 * a, 256 + 64 * a + 64)
                high[g, at, there] = jnp.concatenate([hi[:, 32:], hi[:, :32]], axis=1)
                low[g, at, there] = jnp.concatenate([lo[:, 32:], lo[:, :32]], axis=1)


def attn_fwd_kernel(
    r,
    x0, x1, x2, x3, wq, wk, wv, vecs, pw, near_q, kf,
    k_far, v_far, kt_far, xt_far, qc_far, qf_far, qht_far, qlt_far, pt_far, pooled_out, ctx_out, ctxt_out, lse_out,
    x_s, vt_s, wph, wpl, k_out, v_out, kt_out, xt_out, qc_out, qf_out, qht_out, qlt_out, pt_out, sem,
):
    copies = []

    def send(here, there):
        copies.append(pltpu.make_async_copy(here, there, sem.at[len(copies)]))
        copies[-1].start()

    qb, cb, pb, vb = (vecs[i : i + 1, :] for i in range(4))
    spread_heads(pw, wph, wpl, 2)
    rows = lax.broadcasted_iota(jnp.int32, (64, 128), 0)
    cols = lax.broadcasted_iota(jnp.int32, (64, 128), 1)
    pair = jnp.where(cols // 2 == rows, 0.5, 0.0).astype(BF)
    for d, piece in enumerate((x0, x1, x2, x3)):
        x_s[d * 128 : d * 128 + 128, :] = piece[...]
        pooled_out[d * 64 : d * 64 + 64, :] = nn(pair, piece[...])
    pooled_low = pooled_out[...].astype(BF)
    pt_out[...] = pooled_low.T
    send(pt_out, pt_far)
    x = x_s[...]
    xt_out[...] = x.T
    send(xt_out, xt_far)
    q = nn(pooled_low, wq[...]) + qb
    k = nn(x, wk[...]).astype(BF)
    k_out[...] = k
    kt_out[...] = k.T
    send(k_out, k_far)
    send(kt_out, kt_far)
    v = (nn(x, wv[...]) + vb).astype(BF)
    v_out[...] = v
    send(v_out, v_far)
    vt_s[...] = v.T
    qc_out[...] = (q + cb).astype(BF) * 0.125
    hi, lo = split(q + pb)
    qht_out[...] = hi.T
    qlt_out[...] = lo.T
    send(qc_out, qc_far)
    send(qht_out, qht_far)
    send(qlt_out, qlt_far)
    sin4 = jnp.concatenate([near_q[:, :128]] * 2, axis=1)
    cos4 = jnp.concatenate([near_q[:, 128:]] * 2, axis=1)
    for g in range(3):
        at = slice(256 * g, 256 * g + 256)
        both = three(nn, hi[:, at], lo[:, at], wph[g], wpl[g])
        side = both[:, :256] * sin4 + both[:, 256:] * cos4
        qf_out[:, at] = side.astype(BF) * 0.125
    send(qf_out, qf_far)
    lane = lax.broadcasted_iota(jnp.int32, (256, 128), 1)
    zero = jnp.zeros((256, 128), BF)
    one_a = (lane == 64).astype(F32).astype(BF)
    one_b = (lane == 0).astype(F32).astype(BF)

    def one_pair(i, carry):
        at = pl.ds(pl.multiple_of(i * 128, 128), 128)
        k_pair = k_out[:, at]
        qc_pair = qc_out[:, at]
        qf_pair = qf_out[:, at]
        for s in range(2):
            mine = (lane < 64) if s == 0 else (lane >= 64)
            left = jnp.concatenate([k_pair, kf[r, s]], axis=1)
            right = jnp.concatenate(
                [jnp.where(mine, qc_pair, zero), jnp.where(mine, qf_pair, (one_a, one_b)[s])], axis=1
            )
            scores = nt(left, right)
            highest = jnp.max(scores, axis=0, keepdims=True)
            raised = jnp.exp(scores - highest)
            total = jnp.sum(raised, axis=0, keepdims=True)
            weights = (raised * (1.0 / total)).astype(BF)
            head = pl.ds(pl.multiple_of(i * 128 + s * 64, 64), 64)
            ctxt_out[head, :] = nn(vt_s[head, :], weights).astype(BF)
            lse_out[i * 2 + s] = highest + jnp.log(total)
        return carry

    lax.fori_loop(0, 6, one_pair, 0)
    ctx_out[...] = ctxt_out[...].T
    for copy in copies:
        copy.wait()


def attn_fwd(r, args, after=()):
    return call(
        functools.partial(attn_fwd_kernel, r), "attn_fwd", (), args,
        (
            b16(512, 768), b16(512, 768), b16(768, 512), b16(768, 512), b16(256, 768), b16(256, 768),
            b16(768, 256), b16(768, 256), b16(768, 256), f32(256, 768), b16(256, 768), b16(768, 256),
            f32(12, 1, 256),
        ),
        (
            vs(512, 768, dtype=BF), vs(768, 512, dtype=BF), vs(3, 256, 512, dtype=BF), vs(3, 256, 512, dtype=BF),
            vs(512, 768, dtype=BF), vs(512, 768, dtype=BF), vs(768, 512, dtype=BF), vs(768, 512, dtype=BF),
            vs(256, 768, dtype=BF), vs(256, 768, dtype=BF), vs(768, 256, dtype=BF), vs(768, 256, dtype=BF),
            vs(768, 256, dtype=BF), sems(9),
        ),
        after, mib=20, far_outs=range(9), flops=4 * 10**9, moved=12 * 10**6,
    )


def layer_stats(a):
    center = a - jnp.mean(a, axis=-1, keepdims=True)
    rs = lax.rsqrt(jnp.mean(center * center, axis=-1, keepdims=True) + 1e-05)
    return center * rs, rs


def layer_back(dn, n, rs):
    return rs * (dn - jnp.mean(dn, axis=-1, keepdims=True) - n * jnp.mean(dn * n, axis=-1, keepdims=True))


def put_blocks(source, near, far, me, slabs, first):
    for r in range(16):
        for half, out in enumerate((near, far)):
            place = (r ^ me) ^ (16 * half)
            row = pl.multiple_of((place // 2) * 48, 16)
            col = pl.multiple_of((place % 2) * 384, 128)
            for to, s in slabs:
                at = pl.ds(row + (s // 9 * 768 + s % 9 // 3 * 16), 16)
                out[r, first + to] = source[at, pl.ds(col + s % 3 * 128, 128)].astype(BF)


def ffn_down_kernel(
    masks, ctx0, ctx1, pooled0, pooled1, c0, c1, c2, c3, wo, wu, wd, vecs, ub,
    out0, out1, out23, d2_out, df_out, x1t_out, n1_out, rs_out, gp_out, near, far, vec_out,
    act_s, acc_s, x1_s, g_s,
):
    def chunk(c):
        return pl.ds(pl.multiple_of(c * CH, CH), CH)

    ob, ig, ish, db, og, osh = (vecs[i : i + 1, :] for i in range(4, 10))
    ctx = jnp.concatenate([ctx0[...], ctx1[...]], axis=0)
    pooled = jnp.concatenate([pooled0[...], pooled1[...]], axis=0)
    n1, rs1 = layer_stats(pooled + (nn(ctx, wo[...]) + ob))
    n1_out[...] = n1
    rs_out[...] = rs1
    x1 = n1 * ig + ish
    x1_s[...] = x1.astype(BF)
    x1t_out[...] = x1.astype(BF).T
    acc_s[...] = x1 + db

    def up_chunk(c, carry):
        at = chunk(c)
        z = nn(x1_s[...], wu[:, at]) + ub[:, at]
        phi = 0.5 + 0.5 * lax.erf(z * math.sqrt(0.5))
        gp_out[:, at] = phi + z * (jnp.exp(-0.5 * z * z) * (1.0 / math.sqrt(2.0 * math.pi)))
        act = (z * phi).astype(BF)
        act_s[:, at] = act
        acc_s[...] += nn(act, wd[at, :])
        return carry

    lax.fori_loop(0, 6, up_chunk, 0)
    n2, rs2 = layer_stats(acc_s[...])
    result = (n2 * og + osh).astype(BF)
    for d, out in enumerate((out0, out1, out23.at[0], out23.at[1])):
        for r in range(2):
            out[r] = result[r * 256 + d * 64 : r * 256 + d * 64 + 64, :]
    cot = jnp.concatenate([c[r] for r in range(2) for c in (c0, c1, c2, c3)], axis=0).astype(F32)
    vec_out[0:1, :] = jnp.sum(cot * n2, axis=0, keepdims=True)
    vec_out[1:2, :] = jnp.sum(cot, axis=0, keepdims=True)
    d2 = layer_back(cot * og, n2, rs2)
    df = d2.astype(BF)
    df_out[...] = df
    vec_out[2:3, :] = jnp.sum(df.astype(F32), axis=0, keepdims=True)
    d2_out[...] = d2

    def down_chunk(which, i, carry):
        c = which * 3 + i
        g_s[...] = tn(act_s[:, chunk(c)], df_out[...])
        slab = c * 6
        me = masks[2 + which]
        for r in range(32):
            row = pl.ds(pl.multiple_of((r ^ me) * 16, 16), 16)
            for j in range(6):
                (near, far)[r // 16][r % 16, slab + j] = g_s[row, j * 128 : j * 128 + 128].astype(BF)
        return carry

    for which in range(2):
        lax.fori_loop(0, 3, functools.partial(down_chunk, which), 0)


def ffn_down(masks, args, after=()):
    grad = b16(16, 36, 16, 128)
    return call(
        ffn_down_kernel, "ffn_down", (masks,), args,
        (
            b16(2, 64, 768), b16(2, 64, 768), b16(2, 2, 64, 768), f32(512, 768), b16(512, 768),
            b16(768, 512), f32(512, 768), f32(512, 1), f32(512, 3072), grad, grad, f32(8, 768),
        ),
        (vs(512, 3072, dtype=BF), vs(512, 768), vs(512, 768, dtype=BF), vs(512, 768)),
        after, mib=18, flops=8 * 10**9, moved=25 * 10**6,
    )


def hidden_back(masks, which, df_in, gp, x1t, wu, wd, near, far, upb_out, acc_s, u_s):
    me = masks[2 + which]

    def up_chunk(i, carry):
        at = pl.ds(pl.multiple_of((which * 3 + i) * CH, CH), CH)
        dz = (nt(df_in[...], wd[at, :]) * gp[:, at]).astype(BF)
        upb_out[:, pl.ds(pl.multiple_of(i * CH, CH), CH)] = jnp.sum(dz.astype(F32), axis=0, keepdims=True)
        acc_s[...] += nt(dz, wu[:, at])
        u_s[...] = nn(x1t[...], dz)
        slab = (which * 3 + i) * 6
        for r in range(32):
            place = r ^ me
            row = pl.multiple_of((place // 4) * 96, 32)
            col = pl.ds(pl.multiple_of((place % 4) * 128, 128), 128)
            for j in range(6):
                (near, far)[r // 16][r % 16, slab + j] = u_s[pl.ds(row + 16 * j, 16), col].astype(BF)
        return carry

    lax.fori_loop(0, 3, up_chunk, 0)


def ffn_up_a_kernel(masks, df_in, d2, gp, x1t, wu, wd, acc, near, far, upb_out, u_s):
    acc[...] = d2[...]
    hidden_back(masks, 0, df_in, gp, x1t, wu, wd, near, far, upb_out, acc, u_s)


def ffn_up_a(masks, args, after=()):
    return call(
        ffn_up_a_kernel, "ffn_up_a", (masks,), args,
        (f32(512, 768), b16(16, 45, 16, 128), b16(16, 45, 16, 128), f32(1, 1536)),
        (vs(768, 512),), after, mib=14, flops=4 * 10**9, moved=12 * 10**6,
    )


def ffn_up_b_kernel(
    masks, df_in, acc, gp, x1t, n1, rs, ctxt0, ctxt1, wo, wu, wd, vecs, near_in, far_in,
    d1_out, dctx_out, near, far, vec_out, upb_out,
    acc_s, u_s, o_s,
):
    ig = vecs[5:6, :]
    acc_s[...] = acc[...]
    hidden_back(masks, 1, df_in, gp, x1t, wu, wd, near, far, upb_out, acc_s, u_s)
    dx1 = acc_s[...]
    vec_out[0:1, :] = jnp.sum(dx1 * n1[...], axis=0, keepdims=True)
    vec_out[1:2, :] = jnp.sum(dx1, axis=0, keepdims=True)
    d1 = layer_back(dx1 * ig, n1[...], rs[...])
    d1_out[...] = d1
    do = d1.astype(BF)
    vec_out[2:3, :] = jnp.sum(do.astype(F32), axis=0, keepdims=True)
    dctx = nt(do, wo[...]).astype(BF)
    for r in range(2):
        dctx_out[r] = dctx[r * 256 : r * 256 + 256]
    o_s[...] = nn(ctxt0[...], do[:256]) + nn(ctxt1[...], do[256:])
    put_blocks(o_s, near, far, masks[3], [(i, i) for i in range(9)], 36)


def ffn_up_b(masks, args, after=()):
    return call(
        ffn_up_b_kernel, "ffn_up_b", (masks,), args,
        (f32(512, 768), b16(2, 256, 768), b16(16, 45, 16, 128), b16(16, 45, 16, 128), f32(8, 768), f32(1, 1536)),
        (vs(512, 768), vs(768, 512), vs(768, 768)),
        after, mib=16, flops=5 * 10**9, moved=14 * 10**6, aliases=((12, 2), (13, 3)),
    )


def attn_bwd_kernel(
    r,
    k, v, kt, qc, qf, qht, qlt, lse, dctx, kf, kst, far_q, pw,
    dk_out, dv_out, dq_out, pwg_out, vec_out,
    dqct_s, dpt_s, wph, wpl,
):
    spread_heads(pw, wph, wpl, 1)
    lane = lax.broadcasted_iota(jnp.int32, (256, 128), 1)
    zero = jnp.zeros((256, 128), BF)
    one_a = (lane == 64).astype(F32).astype(BF)
    one_b = (lane == 0).astype(F32).astype(BF)

    def one_pair(i, carry):
        at = pl.ds(pl.multiple_of(i * 128, 128), 128)
        k_pair = k[:, at]
        v_pair = v[:, at]
        qc_pair = qc[:, at]
        qf_pair = qf[:, at]
        dc_pair = dctx[r, :, at]
        for s in range(2):
            mine = (lane < 64) if s == 0 else (lane >= 64)
            left = jnp.concatenate([k_pair, kf[r, s]], axis=1)
            qc_mine = jnp.where(mine, qc_pair, zero)
            dc_mine = jnp.where(mine, dc_pair, zero)
            right = jnp.concatenate([qc_mine, jnp.where(mine, qf_pair, (one_a, one_b)[s])], axis=1)
            weights = jnp.exp(nt(left, right) - lse[i * 2 + s])
            dweights = nt(v_pair, dc_mine)
            inner = jnp.sum(weights * dweights, axis=0, keepdims=True)
            dscore = (weights * (dweights - inner)).astype(BF)
            dv_part = nn(weights.astype(BF), dc_mine)
            dk_part = nn(dscore, qc_mine)
            if s == 0:
                dv_first, dk_first = dv_part, dk_part
            head = pl.ds(pl.multiple_of(i * 128 + s * 64, 64), 64)
            side = nn(jnp.concatenate([kt[head, :], kst[...]], axis=0), dscore)
            dqct_s[head, :] = side[0:64] * 0.125
            dpt_s[head, :] = (side[64:128] * far_q[:64] + side[128:192] * far_q[64:]) * 0.125
        dv_out[:, at] = (dv_first + dv_part).astype(BF)
        dk_out[:, at] = (dk_first + dk_part).astype(BF)
        return carry

    lax.fori_loop(0, 6, one_pair, 0)
    ones = jnp.ones((8, 256), BF)
    for g in range(3):
        at = slice(256 * g, 256 * g + 256)
        hi, lo = split(dpt_s[at, :])
        pwg = three(nt, qht[at, :], qlt[at, :], hi, lo)
        early = lax.broadcasted_iota(jnp.int32, (64, 128), 1) < 64
        for i in range(2):
            m = 128 * i
            mixed = jnp.where(early, pwg[m : m + 64, m : m + 128], pwg[m + 64 : m + 128, m : m + 128])
            pwg_out[(2 * g + i) * 64 : (2 * g + i) * 64 + 64, :] = mixed
        shift = three(nn, wph[g], wpl[g], hi, lo)
        content = dqct_s[at, :]
        dq = (content + shift).T.astype(BF)
        dq_out[:, at] = dq
        shi, slo = split(shift)
        chi, clo = split(content)
        vec_out[0:1, at] = (nt(ones, chi) + nt(ones, clo))[0:1]
        vec_out[1:2, at] = (nt(ones, shi) + nt(ones, slo))[0:1]
        vec_out[2:3, at] = jnp.sum(dq.astype(F32), axis=0, keepdims=True)
    vec_out[3:4, :] = jnp.sum(dv_out[...].astype(F32), axis=0, keepdims=True)


def attn_bwd(r, args, after=()):
    return call(
        functools.partial(attn_bwd_kernel, r), "attn_bwd", (), args,
        (b16(512, 768), b16(512, 768), b16(256, 768), f32(384, 128), f32(8, 768)),
        (vs(768, 256), vs(768, 256), vs(3, 256, 256, dtype=BF), vs(3, 256, 256, dtype=BF)),
        after, mib=14, flops=8 * 10**9, moved=12 * 10**6,
    )


def tokens_back_kernel(dk0, dk1, dv0, dv1, dq0, dq1, d1, wq, wk, wv, t0, t1, t23, tok_s):
    rows = lax.broadcasted_iota(jnp.int32, (512, 256), 0)
    cols = lax.broadcasted_iota(jnp.int32, (512, 256), 1)
    spread = jnp.where(rows // 2 == cols, 0.5, 0.0).astype(BF)
    for r, (dk, dv, dq) in enumerate(((dk0, dv0, dq0), (dk1, dv1, dq1))):
        hi, lo = split(d1[r * 256 : r * 256 + 256, :] + nt(dq[...], wq[...]))
        tok_s[...] = (nt(dk[...], wk[...]) + nt(dv[...], wv[...])) + (nn(spread, hi) + nn(spread, lo))
        for d, out in enumerate((t0, t1, t23.at[0], t23.at[1])):
            out[r] = tok_s[d * 128 : d * 128 + 128, :].astype(BF)


def weights_back_kernel(
    masks, xt0, xt1, pt0, pt1, dk0, dk1, dv0, dv1, dq0, dq1, pwg0, pwg1, av0, av1, vec_d, vec_u, upb_a, upb_b,
    near, far, g_s, smalls,
):
    smalls[0:384, :] = pwg0[...] + pwg1[...]
    attn = av0[...] + av1[...]
    lines = [vec_d[i : i + 1, :] for i in range(3)] + [vec_u[i : i + 1, :] for i in range(3)]
    lines += [upb[:, 768 * i : 768 * i + 768] for upb in (upb_a, upb_b) for i in range(2)] + [attn[i : i + 1, :] for i in range(4)]
    for i, line in enumerate(lines):
        for t in range(6):
            row = 384 + 6 * i + t
            smalls[row : row + 1, :] = line[:, 128 * t : 128 * t + 128]
    smalls[468:512, :] = jnp.zeros((44, 128), F32)
    g_s[0:768, :] = nn(pt0[...], dq0[...]) + nn(pt1[...], dq1[...])
    g_s[768:1536, :] = nn(xt0[...], dk0[...]) + nn(xt1[...], dk1[...])
    g_s[1536:2304, :] = nn(xt0[...], dv0[...]) + nn(xt1[...], dv1[...])
    put_blocks(g_s, near, far, masks[2], [(i, i) for i in range(NA)], 0)
    put_blocks(g_s, near, far, masks[3], [(i, i) for i in range(NA, 27)], 0)
    for r in range(16):
        for half, out in enumerate((near, far)):
            row = pl.ds(pl.multiple_of((r ^ masks[3] ^ (16 * half)) * 16, 16), 16)
            out[r, 27] = smalls[row, :].astype(BF)


def last_back_kernel(
    scalars, k, v, kt, qc, qf, qht, qlt, lse, dctx, kf, kst, far_q, pw, xt0, xt1, pt0, pt1, dk0, dv0, dq0, pwg0, av0, vec_d,
    vec_u, upb_a, upb_b, d1, wq, wk, wv,
    near, far, t0, t1, t23,
    dqct_s, dpt_s, wph, wpl, dk1, dv1, dq1, pwg1, av1, g_s, smalls, tok_s,
):
    attn_bwd_kernel(
        1, k, v, kt, qc, qf, qht, qlt, lse, dctx, kf, kst, far_q, pw, dk1, dv1, dq1, pwg1, av1, dqct_s, dpt_s, wph, wpl
    )
    weights_back_kernel(
        scalars, xt0, xt1, pt0, pt1, dk0, dk1, dv0, dv1, dq0, dq1, pwg0, pwg1, av0, av1, vec_d, vec_u, upb_a, upb_b, near, far,
        g_s, smalls,
    )
    tokens_back_kernel(dk0, dk1, dv0, dv1, dq0, dq1, d1, wq, wk, wv, t0, t1, t23, tok_s)


def last_back(scalars, args, after=()):
    grad = b16(16, 28, 16, 128)
    return call(
        last_back_kernel, "last_back", (scalars,), args,
        (grad, grad, b16(2, 128, 768), b16(2, 128, 768), b16(2, 2, 128, 768)),
        (
            vs(768, 256), vs(768, 256), vs(3, 256, 256, dtype=BF), vs(3, 256, 256, dtype=BF), vs(512, 768, dtype=BF),
            vs(512, 768, dtype=BF), vs(256, 768, dtype=BF), vs(384, 128), vs(8, 768), vs(2304, 768), vs(512, 128),
            vs(512, 768),
        ),
        after, mib=28, flops=17 * 10**9, moved=30 * 10**6,
    )


def partner(x, bit):
    size = lax.axis_size("batch")
    return lax.ppermute(x, "batch", [(i, i ^ bit) for i in range(size)])


def add_kernel(step, cuts, parts, *refs):
    here, came, outs = refs[:parts], refs[parts : 2 * parts], refs[2 * parts :]
    if step < 5:
        pieces = 2 if step < 4 else 1
        at = 0
        for p in range(parts):
            rows, slabs = here[p].shape[:2]
            half = rows // pieces

            def add(r, carry, p=p, at=at, half=half, slabs=slabs):
                for h in range(pieces):
                    total = (here[p][h * half + r].astype(F32) + came[p][h * half + r].astype(F32)).astype(BF)
                    if len(outs) == pieces:
                        outs[h][r, at : at + slabs] = total
                    elif parts == 2:
                        outs[pieces * p + h][r] = total
                    else:
                        outs[h][r] = total[:cuts]
                        outs[pieces + h][r] = total[cuts:]
                return carry

            lax.fori_loop(0, half, add, 0)
            at += slabs
    else:
        at = 0
        for p in range(parts):
            rows, slabs = here[p].shape[:2]
            for source, to in ((here[p], slice(0, rows)), (came[p], slice(rows, 2 * rows))):
                if len(outs) == 1:
                    outs[0][to, at : at + slabs] = source[...]
                elif parts == 2:
                    outs[p][to] = source[...]
                else:
                    outs[0][to] = source[:, :cuts]
                    outs[1][to] = source[:, cuts:]
            at += slabs


class Order:
    def __init__(self):
        self.last = ()

    def run(self, function, *args, also=()):
        *results, token = function(*args, (*self.last, *also))
        self.last = (token,)
        return results


class Sum:
    def __init__(self, order, keep, sends, cuts, bits):
        core, first, second, third, fourth, self.others = bits
        self.bits = [(core,) * len(keep), (first, second), (second, first), (third,), (fourth,)]
        self.bits += [(fourth,), (third,), (second, first), (first, second), (core,)]
        self.cuts, self.slabs = cuts, sum(k.shape[1] for k in keep)
        self.order, self.keep, self.sends, self.step = order, keep, sends, 0

    def start(self):
        self.got = [partner(s, b) for s, b in zip(self.sends, self.bits[self.step])]
        return self

    def finish(self):
        step, a, b = self.step, self.cuts, self.slabs - self.cuts
        here = self.keep if step < 5 else self.sends
        if step < 9:
            rows = (8, 4, 2, 1, 1, 2, 4, 8, 16)[step]
            shapes = [(a,), (b,)] if step in (0, 1, 6, 7) else [(a + b,)]
            copies = 2 if step < 4 else 1
            outs = [b16(rows, *s, 16, 128) for s in shapes for _ in range(copies)]

            def add(after):
                return call(
                    functools.partial(add_kernel, step, a, len(here)), "sum_step", (), (*here, *self.got), outs,
                    after=after, mib=8, moved=10**6,
                )

            outs = self.order.run(add)
            if step < 4:
                self.keep, self.sends = outs[::2], outs[1::2]
            else:
                self.sends = outs
            if step == 4:
                for bit in self.others:
                    self.sends = [(s.astype(F32) + partner(s, bit).astype(F32)).astype(BF) for s in self.sends]
        else:
            self.sends = (*self.sends, *self.got)
        self.step += 1
        return self


def get_blocks(me, halves, slabs, outs):
    for half, source in enumerate(halves):
        for r in range(16):
            place = (r ^ me) ^ (16 * half)
            row = pl.multiple_of((place // 2) * 48, 16)
            col = pl.multiple_of((place % 2) * 384, 128)
            for at, s in slabs:
                to = pl.ds(row + s % 9 // 3 * 16, 16)
                outs[s // 9][to, pl.ds(col + s % 3 * 128, 128)] = source[r, at].astype(F32)


def rows_kernel(masks, near, far, out):
    c = pl.program_id(0)
    me = masks[2 + c // 3]
    for r in range(32):
        row = pl.ds(pl.multiple_of((r ^ me) * 16, 16), 16)
        for j in range(6):
            out[row, j * 128 : j * 128 + 128] = (near, far)[r // 16][r % 16, c * 6 + j].astype(F32)


def assemble_rows(masks, halves, after=()):
    return call_grid(
        rows_kernel, "assemble_rows", 6, (masks,), halves, (f32(3072, 768),), (pl.BlockSpec((512, 768), lambda c: (c, 0)),),
        after, 24, 14 * 10**6,
    )


def up_kernel(masks, near, far, out, o_out):
    c = pl.program_id(0)
    me = masks[2 + c // 3]
    for r in range(32):
        place = r ^ me
        row = pl.multiple_of((place // 4) * 96, 32)
        col = pl.ds(pl.multiple_of((place % 4) * 128, 128), 128)
        for j in range(6):
            out[pl.ds(row + 16 * j, 16), col] = (near, far)[r // 16][r % 16, c * 6 + j].astype(F32)

    @pl.when(c == 0)
    def _():
        get_blocks(masks[3], (near, far), [(36 + i, i) for i in range(9)], (o_out,))


def assemble_up(masks, halves, after=()):
    return call_grid(
        up_kernel, "assemble_up", 6, (masks,), halves, (f32(768, 3072), f32(768, 768)),
        (pl.BlockSpec((768, 512), lambda c: (0, c)), VM), after, 28, 18 * 10**6,
    )


def three_kernel(masks, near, far, q_out, k_out, v_out, w_out, l_out, s_out):
    outs = (q_out, k_out, v_out)
    get_blocks(masks[2], (near, far), [(i, i) for i in range(NA)], outs)
    get_blocks(masks[3], (near, far), [(i, i) for i in range(NA, 27)], outs)
    for half, source in enumerate((near, far)):
        for r in range(16):
            row = pl.ds(pl.multiple_of((r ^ masks[3] ^ (16 * half)) * 16, 16), 16)
            s_out[row, :] = source[r, 27].astype(F32)
    for h in range(12):
        w_out[h] = s_out[h // 2 * 64 : h // 2 * 64 + 64, h % 2 * 64 : h % 2 * 64 + 64]
    for i in range(14):
        for t in range(6):
            row = 384 + 6 * i + t
            l_out[i : i + 1, 128 * t : 128 * t + 128] = s_out[row : row + 1, :]


def assemble_three(masks, halves, after=()):
    return call(
        three_kernel, "assemble_three", (masks,), halves, (f32(768, 768),) * 3 + (f32(12, 64, 64), f32(16, 768)),
        (vs(512, 128),), after, mib=36, moved=11 * 10**6, last=True,
    )


def owners_kernel(scalars, p0, p2, p13, out):
    j = scalars[0]
    out[j] = p0[...].astype(out.dtype)
    out[j ^ 2] = p2[0].astype(out.dtype)
    out[j ^ 1] = p13[0].astype(out.dtype)
    out[j ^ 3] = p13[1].astype(out.dtype)


def assemble_owners(name, dtype, scalars, pieces, after=()):
    shape = (4, *pieces[0].shape)
    return call(
        owners_kernel, name, (scalars,), pieces, (jax.ShapeDtypeStruct(shape, dtype),), after=after, moved=5 * 10**6,
        last=True,
    )


def join_pieces(own, came, after=()):
    def kernel(a, b, out):
        out[0] = a[...]
        out[1] = b[1]

    return call(kernel, "join", (), (own, came), (jax.ShapeDtypeStruct(came.shape, came.dtype),), after=after, moved=10**6)


def pick_kernel(row, scalars, blocks, o0, o1, o2, o3, sem):
    copies = []
    for d, out in enumerate((o0, o1, o2, o3)):
        source = blocks.at[scalars[0] ^ d] if row is None else blocks.at[scalars[0] ^ d, row]
        copies.append(pltpu.make_async_copy(source, out, sem.at[d]))
        copies[-1].start()
    for copy in copies:
        copy.wait()


def pick(row, scalars, blocks, after=()):
    shape = blocks.shape[1:] if row is None else blocks.shape[2:]
    return call(
        functools.partial(pick_kernel, row), "pick", (scalars,), (blocks,), (b16(*shape),) * 4, (sems(4),), after=after,
        mib=4, moved=2 * 10**6, far_args=(0,),
    )


def on_device(
    tokens, lengths, cotangent, query_weight, query_bias, key_weight, value_weight, value_bias, content_bias,
    position_bias, position_weight, out_weight, out_bias, inner_gain, inner_shift, up_weight, up_bias, down_weight,
    down_bias, outer_gain, outer_shift,
):
    size = lax.axis_size("batch")
    me = lax.axis_index("batch").astype(jnp.int32)
    j = me % G
    core, first, second, third, fourth = 1, 2, 4, 8, 16
    others = [1 << b for b in range(5, size.bit_length() - 1)]
    bits = (core, first, second, third, fourth, others)
    has = lambda bit: (me // bit) % 2
    low = has(core) * 16 + has(third) * 2 + has(fourth)
    scalars = jnp.stack(
        [j, me // G * 8 + 2 * j, low + has(first) * 8 + has(second) * 4, low + has(second) * 8 + has(first) * 4]
    )
    order = Order()

    by_owner = tokens[0].reshape(4, 2, 128, 768)
    cot_owner = cotangent[0].reshape(4, 2, 64, 768)

    def trade(pieces):
        return [pieces[0]] + [partner(pieces[d], d) for d in (1, 2, 3)]

    x0 = trade(order.run(pick, 0, scalars, by_owner))
    near_q, far_q, kst, kf = order.run(tables, scalars, lengths)
    vecs = jnp.stack(
        [
            query_bias, content_bias, position_bias, value_bias, out_bias, inner_gain, inner_shift, down_bias,
            outer_gain, outer_shift,
        ]
    )
    s1 = order.run(pick, 1, scalars, by_owner)
    sc = order.run(pick, None, scalars, cot_owner)
    x1 = trade(order.run(gate, s1, also=x0[1:]))

    def forward(r, x):
        return order.run(
            attn_fwd, r, (*x, query_weight, key_weight, value_weight, vecs, position_weight, near_q, kf)
        )

    fwd = [forward(0, x0)]
    cot = trade(order.run(gate, sc, also=x1[1:]))
    fwd.append(forward(1, x1))
    k, v, kt, xt, qc, qf, qht, qlt, pt, pooled, ctx, ctxt, lse = zip(*fwd)
    outs = order.run(
        ffn_down, scalars, (*ctx, *pooled, *cot, out_weight, up_weight, down_weight, vecs, up_bias[None, :])
    )
    out0, out1, out23, d2, df, x1t, n1, rs1, gp, near, far, vec_d = outs
    far, out23 = order.run(gate, (far, out23))
    down = Sum(order, (near,), (far,), 18, bits).start()
    back23 = partner(out23, 2)
    acc, near, far, upb_a = order.run(ffn_up_a, scalars, (df, d2, gp, x1t, up_weight, down_weight))
    down.finish().start()
    (out13,) = order.run(join_pieces, out1, back23)
    back13 = partner(out13, 1)
    d1, dctx, near, far, vec_u, upb_b = order.run(
        ffn_up_b, scalars, (df, acc, gp, x1t, n1, rs1, *ctxt, out_weight, up_weight, down_weight, vecs, near, far)
    )
    down.finish().start()
    (far,) = order.run(gate, (far,))
    up = Sum(order, (near,), (far,), 18, bits).start()

    def backward(r):
        return k[r], v[r], kt[r], qc[r], qf[r], qht[r], qlt[r], lse[r], dctx, kf, kst, far_q, position_weight

    dk, dv, dq, pwg, attn_vec = order.run(attn_bwd, 0, backward(0))
    down.finish().start()
    up.finish().start()
    near, far, t0, t1, t23 = order.run(
        last_back, scalars,
        (
            *backward(1), *xt, *pt, dk, dv, dq, pwg, attn_vec, vec_d, vec_u, upb_a, upb_b, d1, query_weight, key_weight,
            value_weight,
        ),
    )
    up.finish().start()
    down.finish().start()
    (far,) = order.run(gate, (far,))
    three = Sum(order, (near,), (far,), NA, bits).start()
    layer_output = order.run(assemble_owners, "layer_output", BF, scalars, (out0, back23, back13))[0]
    three.finish().start()
    down.finish().start()
    up.finish().start()
    down.finish().start()
    (t23,) = order.run(gate, (t23,))
    u23 = partner(t23, 2)
    three.finish().start()
    up.finish().start()
    three.finish().start()
    down.finish().start()
    up.finish().start()
    three.finish().start()
    up.finish().start()
    down.finish().start()
    three.finish().start()
    u13 = partner(order.run(join_pieces, t1, u23)[0], 1)
    up.finish().start()
    three.finish().start()
    down.finish().start()
    up.finish().start()
    three.finish().start()
    down.finish()
    down_weight_grad = order.run(assemble_rows, scalars, down.sends)[0]
    tokens_grad = order.run(assemble_owners, "tokens_grad", F32, scalars, (t0, u23, u13))[0]
    three.finish().start()
    up.finish().start()
    three.finish().start()
    up.finish()
    up_weight_grad, out_weight_grad = order.run(assemble_up, scalars, up.sends)
    three.finish()
    query_weight_grad, key_weight_grad, value_weight_grad, position_weight_grad, lines = order.run(
        assemble_three, scalars, three.sends
    )
    layer_output = layer_output.reshape(1, 8, 64, 768)
    tokens_grad = tokens_grad.reshape(1, 8, 128, 768)
    line = lambda i: lines[i]
    return (
        layer_output, tokens_grad, query_weight_grad, line(12), key_weight_grad, value_weight_grad, line(13), line(10),
        line(11), position_weight_grad, out_weight_grad, line(5), line(3), line(4),
        up_weight_grad, lines[6:10].reshape(3072), down_weight_grad, line(2), line(0), line(1),
    )


def solution(mesh):
    in_specs = (P("batch", None, None, None), P(), P("batch", None, None, None)) + (P(),) * 18
    out_specs = (P("batch", None, None, None),) * 2 + (P(),) * 18
    return jax.shard_map(on_device, mesh=mesh, in_specs=in_specs, out_specs=out_specs, check_vma=False)
```

time: 416 us -> 287 us (0.69)
  waiting for transfers between devices: 141 us -> 90.9 us
  local copies, waits for them, and re-layouts: 64.7 us -> 14.7 us
  other arithmetic: 18.5 us -> 0.08 us
  starting transfers between devices: 70.3 us -> 59.9 us
    ppermute x63 -> x55, waiting for transfers between devices: 141 us -> 90.9 us  [partner(): return lax.ppermute(x, 'batch', [(i, i ^ bit) for i in range(size)])]
    unnamed x204 -> x100, local copies, waits for them, and re-layouts: 39.3 us -> 6.46 us
    ppermute x63 -> x55, starting transfers between devices: 70.3 us -> 59.9 us  [partner(): return lax.ppermute(x, 'batch', [(i, i ^ bit) for i in range(size)])]
    another operation x5 -> x11, local copies, waits for them, and re-layouts: 0.31 us -> 6.97 us  [on_device(): jnp.stack([query_bias, content_bias, position_bias, value_bias, out_bias,...]
    mul x6 -> x0, local copies, waits for them, and re-layouts: 5.52 us -> none  [on_device(): a[:, :, :, None, :] * eye[None, :, None, :, None]]
    concatenate x23 -> x0, other arithmetic: 4.99 us -> none  [the longest x3 2.38 us: sum_over(): jnp.concatenate([b, partner(b, second)])]
    slice x25 -> x2, local copies, waits for them, and re-layouts: 5.5 us -> 0.68 us  [the longest x1 0.68 us: on_device(): line = lambda i: lines[i]]
    pallas_call x10 -> x51, Pallas kernels: 112 us -> 114 us  [the longest x49 102 us: call(): pl.pallas_call(body, out_shape=tuple((place(i, o) for i, o in enumerate(o...]
  transfers between devices with their start and end apart: 63 -> 55, of which waited for: 29 -> 21; matrix products, arithmetic and copies ran while one was open for 9% -> 2% of each run, Pallas kernels for 9% -> 32%
where the time goes in v2:
time: 287 us; the launch traced here: 281 us
  Pallas kernels  114 us (40%)
  waiting for transfers between devices  90.9 us (32%)
  starting transfers between devices  59.9 us (21%)
  local copies, waits for them, and re-layouts  14.7 us (5%)
    pallas_call x49, Pallas kernels, call(): pl.pallas_call(body, out_shape=tuple((place(i, o) for i, o in enumerate(o...  102 us
    ppermute x55, waiting for transfers between devices, partner(): return lax.ppermute(x, 'batch', [(i, i ^ bit) for i in range(size)])  90.9 us
    ppermute x55, starting transfers between devices, partner(): return lax.ppermute(x, 'batch', [(i, i ^ bit) for i in range(size)])  59.9 us
    pallas_call x2, Pallas kernels, call_grid(): pl.pallas_call(body, out_shape=(*outs, pltpu.VMEM(TOKEN, F32)), grid=(ste...  12.2 us
    another operation x11, local copies, waits for them, and re-layouts, on_device(): jnp.stack([query_bias, content_bias, position_bias, value_bias, out_bias,...  6.97 us
    unnamed x100, local copies, waits for them, and re-layouts  6.46 us
  transfers between devices with their start and end apart: 55, of which 21 were waited for; matrix products, arithmetic and copies ran while one was open for 2% of the time, Pallas kernels for 32%

profile of v2, /device:TPU:0, one launch (start us, length us, event | category | flops | bytes accessed | tf_op | source)
XLA Modules:
  0.0 281.3 jit_solution(10137061928797024544)
XLA Ops:
  0.8 2.6 pick.3
  4.0 2.6 collective-permute-start.1
  14.2 2.3 tables.1
  17.2 1.8 pick.4
  19.0 1.8 pick.5
  21.1 1.9 collective-permute-start.4
  23.1 1.3 copy-done.6
  24.3 1.3 copy-done.9
  25.6 1.3 copy-done.12
  27.9 10.2 %attn_fwd.2 = (bf16[512,768]{1,0:T(8,128)(2,1)}, bf16[512,768]{1,0:T(8,128)(2,1)}, bf16[768,512]{1,0:T(8,128)(2,1)}, bf16[768,512]{1,0:T(8,128)(2,1)}, bf16[256,...) custom-call(f32[8,128]{1,0:T(8,128)S(1)} %get-tuple-element.237.refs, ...), custom_call_target="tpu_custom_call" | custom-call | flops 4000000000 | bytes 12000000 | tf_op jit(solution)/shard_map/attn_fwd/pallas_call | solution.py:79
  38.4 1.9 collective-permute-start.7
  40.4 10.1 %attn_fwd.3 = (bf16[512,768]{1,0:T(8,128)(2,1)}, bf16[512,768]{1,0:T(8,128)(2,1)}, bf16[768,512]{1,0:T(8,128)(2,1)}, bf16[768,512]{1,0:T(8,128)(2,1)}, bf16[256,...) custom-call(f32[8,128]{1,0:T(8,128)S(1)} %get-tuple-element.249.refs, ...), custom_call_target="tpu_custom_call" | custom-call | flops 4000000000 | bytes 12000000 | tf_op jit(solution)/shard_map/attn_fwd/pallas_call | solution.py:79
  50.6 15.7 %ffn_down.1 = (bf16[2,64,768]{2,1,0:T(8,128)(2,1)S(1)}, bf16[2,64,768]{2,1,0:T(8,128)(2,1)S(1)}, bf16[2,2,64,768]{3,2,1,0:T(8,128)(2,1)S(1)}, f32[512,768]{1,0:T...) custom-call(f32[8,128]{1,0:T(8,128)S(1)} %get-tuple-element.251.refs, ...), custom_call_target="tpu_custom_call" | custom-call | flops 8000000000 | bytes 25000000 | tf_op jit(solution)/shard_map/ffn_down/pallas_call | solution.py:79
  66.6 1.9 collective-permute-start.10
  68.6 6.6 %ffn_up_a.1 = (f32[512,768]{1,0:T(8,128)S(1)}, bf16[16,45,16,128]{3,2,1,0:T(8,128)(2,1)S(1)}, bf16[16,45,16,128]{3,2,1,0:T(8,128)(2,1)S(1)}, f32[1,1536]{1,0:T(1,128)S(1)}, f32[8,128]{1,0:T(8,128)S(1)}) custom-call(f32[8,128]{1,0:T(8,128)S(1)} %get-tuple-element.263.refs_0_, s32[4]{0:T(128)S(1)} %pad_add_fusion.refs_0_.refs_1_, ...), custom_call_target="tpu_custom_call" | custom-call | flops 4000000000 | bytes 12000000 | tf_op jit(solution)/shard_map/ffn_up_a/pallas_call | solution.py:79
  76.2 1.9 collective-permute-start.12
  78.2 9.3 %ffn_up_b.1 = (f32[512,768]{1,0:T(8,128)S(1)}, bf16[2,256,768]{2,1,0:T(8,128)(2,1)S(1)}, bf16[16,45,16,128]{3,2,1,0:T(8,128)(2,1)S(1)}, bf16[16,45,16,128]{3,2,1...) custom-call(f32[8,128]{1,0:T(8,128)S(1)} %get-tuple-element.274.refs, ...), custom_call_target="tpu_custom_call", output_to_operand_aliasing={{2}: (14, {}), {3}: (15, {})} | custom-call | flops 5000000000 | bytes 14000000 | tf_op jit(solution)/shard_map/ffn_up_b/pallas_call | solution.py:79
  87.5 3.6 %collective-permute-done.11.refs_3_ = bf16[8,18,16,128]{3,2,1,0:T(8,128)(2,1)S(1)} collective-permute-done((bf16[8,18,16,128]{3,2,1,0:T(8,128)(2,1)S(1)}, bf16[8,18,16,128]{3,2,1,0:T(8,128)(2,1)S(1)}, u32[]{:S(2)}, u32[]{:S(2)}) %collective-permute-start.11) | collective-permute-done | bytes 589856 | tf_op jit(solution)/shard_map/ppermute | solution.py:577
  91.7 1.8 collective-permute-start.13
  93.4 1.5 collective-permute-start.14
  95.2 9.1 %attn_bwd.1 = (bf16[512,768]{1,0:T(8,128)(2,1)S(1)}, bf16[512,768]{1,0:T(8,128)(2,1)S(1)}, bf16[256,768]{1,0:T(8,128)(2,1)S(1)}, f32[384,128]{1,0:T(8,128)S(1)},...) custom-call(f32[8,128]{1,0:T(8,128)S(1)} %get-tuple-element.289.refs_0_, bf16[512,768]{1,0:T(8,128)(2,1)S(1)} %copy-done.33, ...), custom_call_target="tpu_custom_call" | custom-call | flops 8000000000 | bytes 12000000 | tf_op jit(solution)/shard_map/attn_bwd/pallas_call | solution.py:79
  104.4 1.7 collective-permute-start.18
  107.4 1.0 collective-permute-start.17
  108.7 18.7 %last_back.1 = (bf16[16,28,16,128]{3,2,1,0:T(8,128)(2,1)S(1)}, bf16[16,28,16,128]{3,2,1,0:T(8,128)(2,1)S(1)}, bf16[2,128,768]{2,1,0:T(8,128)(2,1)S(1)}, bf16[2,1...) custom-call(f32[8,128]{1,0:T(8,128)S(1)} %get-tuple-element.309.refs_0_, ...), custom_call_target="tpu_custom_call" | custom-call | flops 16999999488 | bytes 30000000 | tf_op jit(solution)/shard_map/last_back/pallas_call | solution.py:79
  129.3 1.5 collective-permute-start.23
  130.8 2.3 collective-permute-done.19.refs_4_
  133.2 1.5 layer_output.1
  135.7 1.5 collective-permute-start.22
  137.2 1.5 collective-permute-start.25
  138.7 2.6 collective-permute-start.21
  141.3 6.4 %collective-permute-done.21.refs_2_ = bf16[1,36,16,128]{3,2,1,0:T(8,128)(2,1)S(1)} collective-permute-done((bf16[1,36,16,128]{3,2,1,0:T(8,128)(2,1)S(1)}, bf16[1,36,16,128]{3,2,1,0:T(8,128)(2,1)S(1)}, u32[]{:S(2)}, u32[]{:S(2)}) %collective-permute-start.21) | collective-permute-done | bytes 147488 | tf_op jit(solution)/shard_map/ppermute | solution.py:577
  147.7 7.7 %collective-permute-done.22.refs_3_ = bf16[4,18,16,128]{3,2,1,0:T(8,128)(2,1)S(1)} collective-permute-done((bf16[4,18,16,128]{3,2,1,0:T(8,128)(2,1)S(1)}, bf16[4,18,16,128]{3,2,1,0:T(8,128)(2,1)S(1)}, u32[]{:S(2)}, u32[]{:S(2)}) %collective-permute-start.22) | collective-permute-done | bytes 294944 | tf_op jit(solution)/shard_map/ppermute | solution.py:577
  156.2 2.6 collective-permute-start.24
  158.8 7.9 %collective-permute-done.24.refs_2_ = bf16[1,36,16,128]{3,2,1,0:T(8,128)(2,1)S(1)} collective-permute-done((bf16[1,36,16,128]{3,2,1,0:T(8,128)(2,1)S(1)}, bf16[1,36,16,128]{3,2,1,0:T(8,128)(2,1)S(1)}, u32[]{:S(2)}, u32[]{:S(2)}) %collective-permute-start.24) | collective-permute-done | bytes 147488 | tf_op jit(solution)/shard_map/ppermute | solution.py:577
  166.7 5.0 %collective-permute-start.30 = (bf16[2,36,16,128]{3,2,1,0:T(8,128)(2,1)S(1)}, bf16[2,36,16,128]{3,2,1,0:T(8,128)(2,1)S(1)}, u32[]{:S(2)}, u32[]{:S(2)}) collective-permute-start(bf16[2,36,16,128]{3,2,1,0:T(8,128)(2,1)S(1)} %get-tuple-element.375.refs_1_), channel_id=1, source_target_pairs={{0,8},{1,9},{2,10},{3,11},{4,12},{5,13},{6,14},{7,15},{8,0},{9,1},... | collective-permute-start | bytes 884744 | tf_op jit(solution)/shard_map/ppermute | solution.py:577
  172.0 1.7 collective-permute-start.29
  174.3 5.8 %collective-permute-done.28.refs_3_ = bf16[4,12,16,128]{3,2,1,0:T(8,128)(2,1)S(1)} collective-permute-done((bf16[4,12,16,128]{3,2,1,0:T(8,128)(2,1)S(1)}, bf16[4,12,16,128]{3,2,1,0:T(8,128)(2,1)S(1)}, u32[]{:S(2)}, u32[]{:S(2)}) %collective-permute-start.28) | collective-permute-done | bytes 196640 | tf_op jit(solution)/shard_map/ppermute | solution.py:577
  180.8 1.6 collective-permute-start.35
  183.2 2.5 collective-permute-start.33
  185.7 4.6 %collective-permute-done.32.refs_2_ = bf16[2,28,16,128]{3,2,1,0:T(8,128)(2,1)S(1)} collective-permute-done((bf16[2,28,16,128]{3,2,1,0:T(8,128)(2,1)S(1)}, bf16[2,28,16,128]{3,2,1,0:T(8,128)(2,1)S(1)}, u32[]{:S(2)}, u32[]{:S(2)}) %collective-permute-start.32) | collective-permute-done | bytes 229408 | tf_op jit(solution)/shard_map/ppermute | solution.py:577
  190.4 1.5 collective-permute-done.33.refs_2_
  192.0 2.2 collective-permute-start.40
  194.1 2.6 collective-permute-start.41
  196.7 7.1 %collective-permute-done.36.refs_2_ = bf16[1,28,16,128]{3,2,1,0:T(8,128)(2,1)S(1)} collective-permute-done((bf16[1,28,16,128]{3,2,1,0:T(8,128)(2,1)S(1)}, bf16[1,28,16,128]{3,2,1,0:T(8,128)(2,1)S(1)}, u32[]{:S(2)}, u32[]{:S(2)}) %collective-permute-start.36) | collective-permute-done | bytes 114720 | tf_op jit(solution)/shard_map/ppermute | solution.py:577
  203.8 3.4 %collective-permute-start.39 = (bf16[1,28,16,128]{3,2,1,0:T(8,128)(2,1)S(1)}, bf16[1,28,16,128]{3,2,1,0:T(8,128)(2,1)S(1)}, u32[]{:S(2)}, u32[]{:S(2)}) collective-permute-start(bf16[1,28,16,128]{3,2,1,0:T(8,128)(2,1)S(1)} %get-tuple-element.396.refs_1_), channel_id=1, source_target_pairs={{0,16},{1,17},{2,18},{3,19},{4,20},{5,21},{6,22},{7,23},{8,24},{9,... | collective-permute-start | bytes 344072 | tf_op jit(solution)/shard_map/ppermute | solution.py:577
  207.7 2.3 collective-permute-done.39.refs_2_
  210.0 4.5 %collective-permute-done.40.refs_3_ = bf16[8,18,16,128]{3,2,1,0:T(8,128)(2,1)S(1)} collective-permute-done((bf16[8,18,16,128]{3,2,1,0:T(8,128)(2,1)S(1)}, bf16[8,18,16,128]{3,2,1,0:T(8,128)(2,1)S(1)}, u32[]{:S(2)}, u32[]{:S(2)}) %collective-permute-start.40) | collective-permute-done | bytes 589856 | tf_op jit(solution)/shard_map/ppermute | solution.py:577
  214.8 1.3 collective-permute-start.43
  216.2 1.3 collective-permute-start.42
  217.4 7.8 %collective-permute-done.42.refs_3_ = bf16[4,18,16,128]{3,2,1,0:T(8,128)(2,1)S(1)} collective-permute-done((bf16[4,18,16,128]{3,2,1,0:T(8,128)(2,1)S(1)}, bf16[4,18,16,128]{3,2,1,0:T(8,128)(2,1)S(1)}, u32[]{:S(2)}, u32[]{:S(2)}) %collective-permute-start.42) | collective-permute-done | bytes 294944 | tf_op jit(solution)/shard_map/ppermute | solution.py:577
  225.2 2.2 collective-permute-done.43.refs_4_
  227.5 1.6 collective-permute-start.50
  229.1 1.0 collective-permute-start.49
  230.1 7.7 %collective-permute-done.44.refs_2_ = bf16[2,28,16,128]{3,2,1,0:T(8,128)(2,1)S(1)} collective-permute-done((bf16[2,28,16,128]{3,2,1,0:T(8,128)(2,1)S(1)}, bf16[2,28,16,128]{3,2,1,0:T(8,128)(2,1)S(1)}, u32[]{:S(2)}, u32[]{:S(2)}) %collective-permute-start.44) | collective-permute-done | bytes 229408 | tf_op jit(solution)/shard_map/ppermute | solution.py:577
  237.9 1.1 collective-permute-start.48
  239.5 4.8 %assemble_rows.1 = (f32[3072,768]{1,0:T(8,128)}, f32[8,128]{1,0:T(8,128)S(1)}) custom-call(f32[8,128]{1,0:T(8,128)S(1)} %get-tuple-element.405.refs_0_, s32[4]{0:T(128)S(1)} %pad_add_fusion.refs_0_.refs_1_, bf16[16,36,16,128]{3,2,1,0:T(8,128)(2,1)S(1)} %get-tuple-element.406.refs_2_, bf16[16,36,16,128]{3,2,1,0:T(8,128)(2,1)S(1)} %collective-permute-done.45.refs_3_), custom_call_target="tpu_custom_call" | custom-call | bytes 14000000 | tf_op jit(solution)/shard_map/assemble_rows/pallas_call | solution.py:106
  244.3 2.4 tokens_grad.1
  246.7 6.3 %collective-permute-done.47.refs_3_ = bf16[4,12,16,128]{3,2,1,0:T(8,128)(2,1)S(1)} collective-permute-done((bf16[4,12,16,128]{3,2,1,0:T(8,128)(2,1)S(1)}, bf16[4,12,16,128]{3,2,1,0:T(8,128)(2,1)S(1)}, u32[]{:S(2)}, u32[]{:S(2)}) %collective-permute-start.47) | collective-permute-done | bytes 196640 | tf_op jit(solution)/shard_map/ppermute | solution.py:577
  253.4 1.6 collective-permute-start.52
  255.0 1.0 collective-permute-start.51
  256.0 10.2 %collective-permute-done.51.refs_3_ = bf16[8,12,16,128]{3,2,1,0:T(8,128)(2,1)S(1)} collective-permute-done((bf16[8,12,16,128]{3,2,1,0:T(8,128)(2,1)S(1)}, bf16[8,12,16,128]{3,2,1,0:T(8,128)(2,1)S(1)}, u32[]{:S(2)}, u32[]{:S(2)}) %collective-permute-start.51) | collective-permute-done | bytes 393248 | tf_op jit(solution)/shard_map/ppermute | solution.py:577
  266.2 1.5 collective-permute-done.52.refs_4_
  267.9 7.3 %assemble_up.1 = (f32[768,3072]{1,0:T(8,128)}, f32[768,768]{1,0:T(8,128)}, f32[8,128]{1,0:T(8,128)S(1)}) custom-call(f32[8,128]{1,0:T(8,128)S(1)} %get-tuple-element.420.refs_0_, s32[4]{0:T(128)S(1)} %pad_add_fusion.refs_0_.refs_1_, bf16[16,45,16,128]{3,2,1,0:T(8,128)(2,1)S(1)} %get-tuple-element.421.refs_2_, ...), custom_call_target="tpu_custom_call" | custom-call | bytes 18000000 | tf_op jit(solution)/shard_map/assemble_up/pallas_call | solution.py:106
  275.3 4.6 %assemble_three.1 = (f32[768,768]{1,0:T(8,128)}, f32[768,768]{1,0:T(8,128)}, f32[768,768]{1,0:T(8,128)}, f32[12,64,64]{2,1,0:T(8,128)}, f32[16,768]{1,0:T(8,128)S(1)}, /*index=5*/f32[8,128]{1,0:T(8,128)}) custom-call(f32[8,128]{1,0:T(8,128)S(1)} %get-tuple-element.422.refs_0_, s32[4]{0:T(128)S(1)} %pad_add_fusion.refs_0_.refs_1_, ...), custom_call_target="tpu_custom_call" | custom-call | bytes 11000000 | tf_op jit(solution)/shard_map/assemble_three/pallas_call | solution.py:79
  (214 shorter events, 23.3 us)
Async XLA Ops:
  0.8 22.2 %copy-start.17 = (f32[12,64,64]{2,1,0:T(8,128)S(1)}, f32[12,64,64]{2,1,0:T(8,128)}, u32[]{:S(2)}) copy-start(f32[12,64,64]{2,1,0:T(8,128)} %refs_14_.1) | copy-start | bytes 589828
  3.5 17.4 %collective-permute-start = (bf16[128,768]{1,0:T(8,128)(2,1)}, bf16[128,768]{1,0:T(8,128)(2,1)S(1)}, u32[]{:S(2)}, u32[]{:S(2)}) collective-permute-start(bf16[128,768]{1,0:T(8,128)(2,1)} %get-tuple-element.230), channel_id=1, source_target_pairs={{0,1},{1,0},{2,3},{3,2},{4,5},{5,4},{6,7},{7,6},{8,9},{9,8},{10,11... | collective-permute-start | bytes 589832 | tf_op jit(solution)/shard_map/ppermute | solution.py:577
  4.0 16.9 %collective-permute-start.1 = (bf16[128,768]{1,0:T(8,128)(2,1)}, bf16[128,768]{1,0:T(8,128)(2,1)S(1)}, u32[]{:S(2)}, u32[]{:S(2)}) collective-permute-start(bf16[128,768]{1,0:T(8,128)(2,1)} %get-tuple-element.231), channel_id=1, source_target_pairs={{0,2},{1,3},{2,0},{3,1},{4,6},{5,7},{6,4},{7,5},{8,10},{9,11},{10,... | collective-permute-start | bytes 589832 | tf_op jit(solution)/shard_map/ppermute | solution.py:577
  6.5 14.4 %collective-permute-start.2 = (bf16[128,768]{1,0:T(8,128)(2,1)}, bf16[128,768]{1,0:T(8,128)(2,1)S(1)}, u32[]{:S(2)}, u32[]{:S(2)}) collective-permute-start(bf16[128,768]{1,0:T(8,128)(2,1)} %get-tuple-element.232), channel_id=1, source_target_pairs={{0,3},{1,2},{2,1},{3,0},{4,7},{5,6},{6,5},{7,4},{8,11},{9,10},{10,... | collective-permute-start | bytes 589832 | tf_op jit(solution)/shard_map/ppermute | solution.py:577
  20.9 17.2 %collective-permute-start.3 = (bf16[128,768]{1,0:T(8,128)(2,1)S(1)}, bf16[128,768]{1,0:T(8,128)(2,1)S(1)}, u32[]{:S(2)}, u32[]{:S(2)}) collective-permute-start(bf16[128,768]{1,0:T(8,128)(2,1)S(1)} %get-tuple-element.242), channel_id=1, source_target_pairs={{0,1},{1,0},{2,3},{3,2},{4,5},{5,4},{6,7},{7,6},{8,9},{9,8},{10,11... | collective-permute-start | bytes 589832 | tf_op jit(solution)/shard_map/ppermute | solution.py:577
  21.1 17.0 %collective-permute-start.4 = (bf16[128,768]{1,0:T(8,128)(2,1)S(1)}, bf16[128,768]{1,0:T(8,128)(2,1)S(1)}, u32[]{:S(2)}, u32[]{:S(2)}) collective-permute-start(bf16[128,768]{1,0:T(8,128)(2,1)S(1)} %get-tuple-element.243), channel_id=1, source_target_pairs={{0,2},{1,3},{2,0},{3,1},{4,6},{5,7},{6,4},{7,5},{8,10},{9,11},{10,... | collective-permute-start | bytes 589832 | tf_op jit(solution)/shard_map/ppermute | solution.py:577
  23.1 15.0 %collective-permute-start.5 = (bf16[128,768]{1,0:T(8,128)(2,1)S(1)}, bf16[128,768]{1,0:T(8,128)(2,1)S(1)}, u32[]{:S(2)}, u32[]{:S(2)}) collective-permute-start(bf16[128,768]{1,0:T(8,128)(2,1)S(1)} %get-tuple-element.244), channel_id=1, source_target_pairs={{0,3},{1,2},{2,1},{3,0},{4,7},{5,6},{6,5},{7,4},{8,11},{9,10},{10,... | collective-permute-start | bytes 589832 | tf_op jit(solution)/shard_map/ppermute | solution.py:577
  38.1 12.4 %collective-permute-start.6 = (bf16[2,64,768]{2,1,0:T(8,128)(2,1)S(1)}, bf16[2,64,768]{2,1,0:T(8,128)(2,1)S(1)}, u32[]{:S(2)}, u32[]{:S(2)}) collective-permute-start(bf16[2,64,768]{2,1,0:T(8,128)(2,1)S(1)} %get-tuple-element.257), channel_id=1, source_target_pairs={{0,1},{1,0},{2,3},{3,2},{4,5},{5,4},{6,7},{7,6},{8,9},{9,8},{10,11... | collective-permute-start | bytes 589832 | tf_op jit(solution)/shard_map/ppermute | solution.py:577
  38.4 12.1 %collective-permute-start.7 = (bf16[2,64,768]{2,1,0:T(8,128)(2,1)S(1)}, bf16[2,64,768]{2,1,0:T(8,128)(2,1)S(1)}, u32[]{:S(2)}, u32[]{:S(2)}) collective-permute-start(bf16[2,64,768]{2,1,0:T(8,128)(2,1)S(1)} %get-tuple-element.258), channel_id=1, source_target_pairs={{0,2},{1,3},{2,0},{3,1},{4,6},{5,7},{6,4},{7,5},{8,10},{9,11},{10,... | collective-permute-start | bytes 589832 | tf_op jit(solution)/shard_map/ppermute | solution.py:577
  40.4 10.2 %collective-permute-start.8 = (bf16[2,64,768]{2,1,0:T(8,128)(2,1)S(1)}, bf16[2,64,768]{2,1,0:T(8,128)(2,1)S(1)}, u32[]{:S(2)}, u32[]{:S(2)}) collective-permute-start(bf16[2,64,768]{2,1,0:T(8,128)(2,1)S(1)} %get-tuple-element.259), channel_id=1, source_target_pairs={{0,3},{1,2},{2,1},{3,0},{4,7},{5,6},{6,5},{7,4},{8,11},{9,10},{10,... | collective-permute-start | bytes 589832 | tf_op jit(solution)/shard_map/ppermute | solution.py:577
  66.4 8.8 %collective-permute-start.9 = (bf16[16,36,16,128]{3,2,1,0:T(8,128)(2,1)S(1)}, bf16[16,36,16,128]{3,2,1,0:T(8,128)(2,1)S(1)}, u32[]{:S(2)}, u32[]{:S(2)}) collective-permute-start(bf16[16,36,16,128]{3,2,1,0:T(8,128)(2,1)S(1)} %get-tuple-element.270), channel_id=1, source_target_pairs={{0,1},{1,0},{2,3},{3,2},{4,5},{5,4},{6,7},{7,6},{8,9},{9,8},{10,11... | collective-permute-start | bytes 7077896 | tf_op jit(solution)/shard_map/ppermute | solution.py:577
  66.6 11.5 %collective-permute-start.10 = (bf16[2,2,64,768]{3,2,1,0:T(8,128)(2,1)S(1)}, bf16[2,2,64,768]{3,2,1,0:T(8,128)(2,1)S(1)}, u32[]{:S(2)}, u32[]{:S(2)}) collective-permute-start(bf16[2,2,64,768]{3,2,1,0:T(8,128)(2,1)S(1)} %get-tuple-element.273), channel_id=1, source_target_pairs={{0,2},{1,3},{2,0},{3,1},{4,6},{5,7},{6,4},{7,5},{8,10},{9,11},{10,... | collective-permute-start | bytes 1179656 | tf_op jit(solution)/shard_map/ppermute | solution.py:577
  76.0 15.1 %collective-permute-start.11 = (bf16[8,18,16,128]{3,2,1,0:T(8,128)(2,1)S(1)}, bf16[8,18,16,128]{3,2,1,0:T(8,128)(2,1)S(1)}, u32[]{:S(2)}, u32[]{:S(2)}) collective-permute-start(bf16[8,18,16,128]{3,2,1,0:T(8,128)(2,1)S(1)} %get-tuple-element.285), channel_id=1, source_target_pairs={{0,2},{1,3},{2,0},{3,1},{4,6},{5,7},{6,4},{7,5},{8,10},{9,11},{10,... | collective-permute-start | bytes 1769480 | tf_op jit(solution)/shard_map/ppermute | solution.py:577
  76.2 15.0 %collective-permute-start.12 = (bf16[8,18,16,128]{3,2,1,0:T(8,128)(2,1)S(1)}, bf16[8,18,16,128]{3,2,1,0:T(8,128)(2,1)S(1)}, u32[]{:S(2)}, u32[]{:S(2)}) collective-permute-start(bf16[8,18,16,128]{3,2,1,0:T(8,128)(2,1)S(1)} %get-tuple-element.286), channel_id=1, source_target_pairs={{0,4},{1,5},{2,6},{3,7},{4,0},{5,1},{6,2},{7,3},{8,12},{9,13},{10,... | collective-permute-start | bytes 1769480 | tf_op jit(solution)/shard_map/ppermute | solution.py:577
  91.6 14.5 %collective-permute-start.15 = (bf16[16,45,16,128]{3,2,1,0:T(8,128)(2,1)S(1)}, bf16[16,45,16,128]{3,2,1,0:T(8,128)(2,1)S(1)}, u32[]{:S(2)}, u32[]{:S(2)}) collective-permute-start(bf16[16,45,16,128]{3,2,1,0:T(8,128)(2,1)S(1)} %get-tuple-element.308), channel_id=1, source_target_pairs={{0,1},{1,0},{2,3},{3,2},{4,5},{5,4},{6,7},{7,6},{8,9},{9,8},{10,11... | collective-permute-start | bytes 8847368 | tf_op jit(solution)/shard_map/ppermute | solution.py:577
  91.7 12.5 %collective-permute-start.13 = (bf16[4,18,16,128]{3,2,1,0:T(8,128)(2,1)S(1)}, bf16[4,18,16,128]{3,2,1,0:T(8,128)(2,1)S(1)}, u32[]{:S(2)}, u32[]{:S(2)}) collective-permute-start(bf16[4,18,16,128]{3,2,1,0:T(8,128)(2,1)S(1)} %get-tuple-element.304), channel_id=1, source_target_pairs={{0,4},{1,5},{2,6},{3,7},{4,0},{5,1},{6,2},{7,3},{8,12},{9,13},{10,... | collective-permute-start | bytes 884744 | tf_op jit(solution)/shard_map/ppermute | solution.py:577
  93.4 10.8 %collective-permute-start.14 = (bf16[4,18,16,128]{3,2,1,0:T(8,128)(2,1)S(1)}, bf16[4,18,16,128]{3,2,1,0:T(8,128)(2,1)S(1)}, u32[]{:S(2)}, u32[]{:S(2)}) collective-permute-start(bf16[4,18,16,128]{3,2,1,0:T(8,128)(2,1)S(1)} %get-tuple-element.305), channel_id=1, source_target_pairs={{0,2},{1,3},{2,0},{3,1},{4,6},{5,7},{6,4},{7,5},{8,10},{9,11},{10,... | collective-permute-start | bytes 884744 | tf_op jit(solution)/shard_map/ppermute | solution.py:577
  95.0 13.4 %copy-start.19 = (f32[12,64,64]{2,1,0:T(8,128)S(1)}, f32[12,64,64]{2,1,0:T(8,128)}, u32[]{:S(2)}) copy-start(f32[12,64,64]{2,1,0:T(8,128)} %refs_14_.1) | copy-start | bytes 589828
  95.0 13.4 %copy-start.28 = (bf16[768,512]{1,0:T(8,128)(2,1)S(1)}, bf16[768,512]{1,0:T(8,128)(2,1)}, u32[]{:S(2)}) copy-start(bf16[768,512]{1,0:T(8,128)(2,1)} %get-tuple-element.318.refs_15_) | copy-start | bytes 2359300
  95.0 13.4 %copy-start.29 = (bf16[512,768]{1,0:T(8,128)(2,1)S(1)}, bf16[512,768]{1,0:T(8,128)(2,1)}, u32[]{:S(2)}) copy-start(bf16[512,768]{1,0:T(8,128)(2,1)} %get-tuple-element.310.refs_2_) | copy-start | bytes 2359300
  95.1 13.4 %copy-start.30 = (bf16[512,768]{1,0:T(8,128)(2,1)S(1)}, bf16[512,768]{1,0:T(8,128)(2,1)}, u32[]{:S(2)}) copy-start(bf16[512,768]{1,0:T(8,128)(2,1)} %get-tuple-element.311.refs_3_) | copy-start | bytes 2359300
  95.1 13.4 %copy-start.31 = (bf16[768,512]{1,0:T(8,128)(2,1)S(1)}, bf16[768,512]{1,0:T(8,128)(2,1)}, u32[]{:S(2)}) copy-start(bf16[768,512]{1,0:T(8,128)(2,1)} %get-tuple-element.312.refs_4_) | copy-start | bytes 2359300
  95.1 13.4 %copy-start.32 = (bf16[768,512]{1,0:T(8,128)(2,1)S(1)}, bf16[768,512]{1,0:T(8,128)(2,1)}, u32[]{:S(2)}) copy-start(bf16[768,512]{1,0:T(8,128)(2,1)} %get-tuple-element.319.refs_16_) | copy-start | bytes 2359300
  95.1 13.4 %copy-start.36 = (bf16[768,256]{1,0:T(8,128)(2,1)S(1)}, bf16[768,256]{1,0:T(8,128)(2,1)}, u32[]{:S(2)}) copy-start(bf16[768,256]{1,0:T(8,128)(2,1)} %get-tuple-element.320.refs_17_) | copy-start | bytes 1179652
  95.1 13.4 %copy-start.37 = (bf16[256,768]{1,0:T(8,128)(2,1)S(1)}, bf16[256,768]{1,0:T(8,128)(2,1)}, u32[]{:S(2)}) copy-start(bf16[256,768]{1,0:T(8,128)(2,1)} %get-tuple-element.313.refs_5_) | copy-start | bytes 1179652
  104.4 24.3 %collective-permute-start.18 = (bf16[2,36,16,128]{3,2,1,0:T(8,128)(2,1)S(1)}, bf16[2,36,16,128]{3,2,1,0:T(8,128)(2,1)S(1)}, u32[]{:S(2)}, u32[]{:S(2)}) collective-permute-start(bf16[2,36,16,128]{3,2,1,0:T(8,128)(2,1)S(1)} %get-tuple-element.339), channel_id=1, source_target_pairs={{0,8},{1,9},{2,10},{3,11},{4,12},{5,13},{6,14},{7,15},{8,0},{9,1},... | collective-permute-start | bytes 884744 | tf_op jit(solution)/shard_map/ppermute | solution.py:577
  106.8 20.6 %collective-permute-start.16 = (bf16[8,18,16,128]{3,2,1,0:T(8,128)(2,1)S(1)}, bf16[8,18,16,128]{3,2,1,0:T(8,128)(2,1)S(1)}, u32[]{:S(2)}, u32[]{:S(2)}) collective-permute-start(bf16[8,18,16,128]{3,2,1,0:T(8,128)(2,1)S(1)} %get-tuple-element.335), channel_id=1, source_target_pairs={{0,2},{1,3},{2,0},{3,1},{4,6},{5,7},{6,4},{7,5},{8,10},{9,11},{10,... | collective-permute-start | bytes 1769480 | tf_op jit(solution)/shard_map/ppermute | solution.py:577
  107.4 20.9 %collective-permute-start.17 = (bf16[8,27,16,128]{3,2,1,0:T(8,128)(2,1)S(1)}, bf16[8,27,16,128]{3,2,1,0:T(8,128)(2,1)S(1)}, u32[]{:S(2)}, u32[]{:S(2)}) collective-permute-start(bf16[8,27,16,128]{3,2,1,0:T(8,128)(2,1)S(1)} %get-tuple-element.336), channel_id=1, source_target_pairs={{0,4},{1,5},{2,6},{3,7},{4,0},{5,1},{6,2},{7,3},{8,12},{9,13},{10,... | collective-permute-start | bytes 2654216 | tf_op jit(solution)/shard_map/ppermute | solution.py:577
  128.8 5.9 %collective-permute-start.20 = (bf16[16,28,16,128]{3,2,1,0:T(8,128)(2,1)S(1)}, bf16[16,28,16,128]{3,2,1,0:T(8,128)(2,1)S(1)}, u32[]{:S(2)}, u32[]{:S(2)}) collective-permute-start(bf16[16,28,16,128]{3,2,1,0:T(8,128)(2,1)S(1)} %get-tuple-element.348), channel_id=1, source_target_pairs={{0,1},{1,0},{2,3},{3,2},{4,5},{5,4},{6,7},{7,6},{8,9},{9,8},{10,11... | collective-permute-start | bytes 5505032 | tf_op jit(solution)/shard_map/ppermute | solution.py:577
  128.8 4.3 %collective-permute-start.19 = (bf16[2,2,64,768]{3,2,1,0:T(8,128)(2,1)S(1)}, bf16[2,2,64,768]{3,2,1,0:T(8,128)(2,1)S(1)}, u32[]{:S(2)}, u32[]{:S(2)}) collective-permute-start(bf16[2,2,64,768]{3,2,1,0:T(8,128)(2,1)S(1)} %get-tuple-element.344), channel_id=1, source_target_pairs={{0,1},{1,0},{2,3},{3,2},{4,5},{5,4},{6,7},{7,6},{8,9},{9,8},{10,11... | collective-permute-start | bytes 1179656 | tf_op jit(solution)/shard_map/ppermute | solution.py:577
  129.3 26.1 %collective-permute-start.23 = (bf16[4,27,16,128]{3,2,1,0:T(8,128)(2,1)S(1)}, bf16[4,27,16,128]{3,2,1,0:T(8,128)(2,1)S(1)}, u32[]{:S(2)}, u32[]{:S(2)}) collective-permute-start(bf16[4,27,16,128]{3,2,1,0:T(8,128)(2,1)S(1)} %get-tuple-element.356), channel_id=1, source_target_pairs={{0,2},{1,3},{2,0},{3,1},{4,6},{5,7},{6,4},{7,5},{8,10},{9,11},{10,... | collective-permute-start | bytes 1327112 | tf_op jit(solution)/shard_map/ppermute | solution.py:577
  135.1 36.6 %collective-permute-start.26 = (bf16[8,16,16,128]{3,2,1,0:T(8,128)(2,1)S(1)}, bf16[8,16,16,128]{3,2,1,0:T(8,128)(2,1)S(1)}, u32[]{:S(2)}, u32[]{:S(2)}) collective-permute-start(bf16[8,16,16,128]{3,2,1,0:T(8,128)(2,1)S(1)} %get-tuple-element.365), channel_id=1, source_target_pairs={{0,4},{1,5},{2,6},{3,7},{4,0},{5,1},{6,2},{7,3},{8,12},{9,13},{10,... | collective-permute-start | bytes 1572872 | tf_op jit(solution)/shard_map/ppermute | solution.py:577
  135.7 19.8 %collective-permute-start.22 = (bf16[4,18,16,128]{3,2,1,0:T(8,128)(2,1)S(1)}, bf16[4,18,16,128]{3,2,1,0:T(8,128)(2,1)S(1)}, u32[]{:S(2)}, u32[]{:S(2)}) collective-permute-start(bf16[4,18,16,128]{3,2,1,0:T(8,128)(2,1)S(1)} %get-tuple-element.355), channel_id=1, source_target_pairs={{0,4},{1,5},{2,6},{3,7},{4,0},{5,1},{6,2},{7,3},{8,12},{9,13},{10,... | collective-permute-start | bytes 884744 | tf_op jit(solution)/shard_map/ppermute | solution.py:577
  137.2 34.5 %collective-permute-start.25 = (bf16[8,12,16,128]{3,2,1,0:T(8,128)(2,1)S(1)}, bf16[8,12,16,128]{3,2,1,0:T(8,128)(2,1)S(1)}, u32[]{:S(2)}, u32[]{:S(2)}) collective-permute-start(bf16[8,12,16,128]{3,2,1,0:T(8,128)(2,1)S(1)} %get-tuple-element.364), channel_id=1, source_target_pairs={{0,2},{1,3},{2,0},{3,1},{4,6},{5,7},{6,4},{7,5},{8,10},{9,11},{10,... | collective-permute-start | bytes 1179656 | tf_op jit(solution)/shard_map/ppermute | solution.py:577
  138.7 9.0 %collective-permute-start.21 = (bf16[1,36,16,128]{3,2,1,0:T(8,128)(2,1)S(1)}, bf16[1,36,16,128]{3,2,1,0:T(8,128)(2,1)S(1)}, u32[]{:S(2)}, u32[]{:S(2)}) collective-permute-start(bf16[1,36,16,128]{3,2,1,0:T(8,128)(2,1)S(1)} %get-tuple-element.351), channel_id=1, source_target_pairs={{0,16},{1,17},{2,18},{3,19},{4,20},{5,21},{6,22},{7,23},{8,24},{9,... | collective-permute-start | bytes 442376 | tf_op jit(solution)/shard_map/ppermute | solution.py:577
  155.7 18.4 %collective-permute-start.27 = (bf16[2,45,16,128]{3,2,1,0:T(8,128)(2,1)S(1)}, bf16[2,45,16,128]{3,2,1,0:T(8,128)(2,1)S(1)}, u32[]{:S(2)}, u32[]{:S(2)}) collective-permute-start(bf16[2,45,16,128]{3,2,1,0:T(8,128)(2,1)S(1)} %get-tuple-element.368), channel_id=1, source_target_pairs={{0,8},{1,9},{2,10},{3,11},{4,12},{5,13},{6,14},{7,15},{8,0},{9,1},... | collective-permute-start | bytes 1105928 | tf_op jit(solution)/shard_map/ppermute | solution.py:577
  156.2 10.5 %collective-permute-start.24 = (bf16[1,36,16,128]{3,2,1,0:T(8,128)(2,1)S(1)}, bf16[1,36,16,128]{3,2,1,0:T(8,128)(2,1)S(1)}, u32[]{:S(2)}, u32[]{:S(2)}) collective-permute-start(bf16[1,36,16,128]{3,2,1,0:T(8,128)(2,1)S(1)} %get-tuple-element.358.refs_1_), channel_id=1, source_target_pairs={{0,16},{1,17},{2,18},{3,19},{4,20},{5,21},{6,22},{7,23},{8,24},{9,... | collective-permute-start | bytes 442376 | tf_op jit(solution)/shard_map/ppermute | solution.py:577
  166.7 13.7 %collective-permute-start.30 = (bf16[2,36,16,128]{3,2,1,0:T(8,128)(2,1)S(1)}, bf16[2,36,16,128]{3,2,1,0:T(8,128)(2,1)S(1)}, u32[]{:S(2)}, u32[]{:S(2)}) collective-permute-start(bf16[2,36,16,128]{3,2,1,0:T(8,128)(2,1)S(1)} %get-tuple-element.375.refs_1_), channel_id=1, source_target_pairs={{0,8},{1,9},{2,10},{3,11},{4,12},{5,13},{6,14},{7,15},{8,0},{9,1},... | collective-permute-start | bytes 884744 | tf_op jit(solution)/shard_map/ppermute | solution.py:577
  172.0 8.1 %collective-permute-start.29 = (bf16[4,16,16,128]{3,2,1,0:T(8,128)(2,1)S(1)}, bf16[4,16,16,128]{3,2,1,0:T(8,128)(2,1)S(1)}, u32[]{:S(2)}, u32[]{:S(2)}) collective-permute-start(bf16[4,16,16,128]{3,2,1,0:T(8,128)(2,1)S(1)} %get-tuple-element.373), channel_id=1, source_target_pairs={{0,2},{1,3},{2,0},{3,1},{4,6},{5,7},{6,4},{7,5},{8,10},{9,11},{10,... | collective-permute-start | bytes 786440 | tf_op jit(solution)/shard_map/ppermute | solution.py:577
  173.7 6.4 %collective-permute-start.28 = (bf16[4,12,16,128]{3,2,1,0:T(8,128)(2,1)S(1)}, bf16[4,12,16,128]{3,2,1,0:T(8,128)(2,1)S(1)}, u32[]{:S(2)}, u32[]{:S(2)}) collective-permute-start(bf16[4,12,16,128]{3,2,1,0:T(8,128)(2,1)S(1)} %get-tuple-element.372), channel_id=1, source_target_pairs={{0,4},{1,5},{2,6},{3,7},{4,0},{5,1},{6,2},{7,3},{8,12},{9,13},{10,... | collective-permute-start | bytes 589832 | tf_op jit(solution)/shard_map/ppermute | solution.py:577
  174.2 9.0 %collective-permute-start.31 = (bf16[1,45,16,128]{3,2,1,0:T(8,128)(2,1)S(1)}, bf16[1,45,16,128]{3,2,1,0:T(8,128)(2,1)S(1)}, u32[]{:S(2)}, u32[]{:S(2)}) collective-permute-start(bf16[1,45,16,128]{3,2,1,0:T(8,128)(2,1)S(1)} %get-tuple-element.378), channel_id=1, source_target_pairs={{0,16},{1,17},{2,18},{3,19},{4,20},{5,21},{6,22},{7,23},{8,24},{9,... | collective-permute-start | bytes 552968 | tf_op jit(solution)/shard_map/ppermute | solution.py:577
  180.4 11.5 %collective-permute-start.34 = (bf16[4,18,16,128]{3,2,1,0:T(8,128)(2,1)S(1)}, bf16[4,18,16,128]{3,2,1,0:T(8,128)(2,1)S(1)}, u32[]{:S(2)}, u32[]{:S(2)}) collective-permute-start(bf16[4,18,16,128]{3,2,1,0:T(8,128)(2,1)S(1)} %get-tuple-element.385.refs_1_), channel_id=1, source_target_pairs={{0,4},{1,5},{2,6},{3,7},{4,0},{5,1},{6,2},{7,3},{8,12},{9,13},{10,... | collective-permute-start | bytes 884744 | tf_op jit(solution)/shard_map/ppermute | solution.py:577
  180.8 11.1 %collective-permute-start.35 = (bf16[4,18,16,128]{3,2,1,0:T(8,128)(2,1)S(1)}, bf16[4,18,16,128]{3,2,1,0:T(8,128)(2,1)S(1)}, u32[]{:S(2)}, u32[]{:S(2)}) collective-permute-start(bf16[4,18,16,128]{3,2,1,0:T(8,128)(2,1)S(1)} %get-tuple-element.386.refs_2_), channel_id=1, source_target_pairs={{0,2},{1,3},{2,0},{3,1},{4,6},{5,7},{6,4},{7,5},{8,10},{9,11},{10,... | collective-permute-start | bytes 884744 | tf_op jit(solution)/shard_map/ppermute | solution.py:577
  182.4 7.9 %collective-permute-start.32 = (bf16[2,28,16,128]{3,2,1,0:T(8,128)(2,1)S(1)}, bf16[2,28,16,128]{3,2,1,0:T(8,128)(2,1)S(1)}, u32[]{:S(2)}, u32[]{:S(2)}) collective-permute-start(bf16[2,28,16,128]{3,2,1,0:T(8,128)(2,1)S(1)} %get-tuple-element.381), channel_id=1, source_target_pairs={{0,8},{1,9},{2,10},{3,11},{4,12},{5,13},{6,14},{7,15},{8,0},{9,1},... | collective-permute-start | bytes 688136 | tf_op jit(solution)/shard_map/ppermute | solution.py:577
  183.0 24.6 %collective-permute-start.37 = (bf16[2,2,128,768]{3,2,1,0:T(8,128)(2,1)S(1)}, bf16[2,2,128,768]{3,2,1,0:T(8,128)(2,1)S(1)}, u32[]{:S(2)}, u32[]{:S(2)}) collective-permute-start(bf16[2,2,128,768]{3,2,1,0:T(8,128)(2,1)S(1)} %get-tuple-element.392), channel_id=1, source_target_pairs={{0,2},{1,3},{2,0},{3,1},{4,6},{5,7},{6,4},{7,5},{8,10},{9,11},{10,... | collective-permute-start | bytes 2359304 | tf_op jit(solution)/shard_map/ppermute | solution.py:577
  183.2 8.6 %collective-permute-start.33 = (bf16[1,45,16,128]{3,2,1,0:T(8,128)(2,1)S(1)}, bf16[1,45,16,128]{3,2,1,0:T(8,128)(2,1)S(1)}, u32[]{:S(2)}, u32[]{:S(2)}) collective-permute-start(bf16[1,45,16,128]{3,2,1,0:T(8,128)(2,1)S(1)} %get-tuple-element.383.refs_1_), channel_id=1, source_target_pairs={{0,16},{1,17},{2,18},{3,19},{4,20},{5,21},{6,22},{7,23},{8,24},{9,... | collective-permute-start | bytes 552968 | tf_op jit(solution)/shard_map/ppermute | solution.py:577
  192.0 22.6 %collective-permute-start.40 = (bf16[8,18,16,128]{3,2,1,0:T(8,128)(2,1)S(1)}, bf16[8,18,16,128]{3,2,1,0:T(8,128)(2,1)S(1)}, u32[]{:S(2)}, u32[]{:S(2)}) collective-permute-start(bf16[8,18,16,128]{3,2,1,0:T(8,128)(2,1)S(1)} %get-tuple-element.398.refs_1_), channel_id=1, source_target_pairs={{0,2},{1,3},{2,0},{3,1},{4,6},{5,7},{6,4},{7,5},{8,10},{9,11},{10,... | collective-permute-start | bytes 1769480 | tf_op jit(solution)/shard_map/ppermute | solution.py:577
  194.1 20.5 %collective-permute-start.41 = (bf16[8,18,16,128]{3,2,1,0:T(8,128)(2,1)S(1)}, bf16[8,18,16,128]{3,2,1,0:T(8,128)(2,1)S(1)}, u32[]{:S(2)}, u32[]{:S(2)}) collective-permute-start(bf16[8,18,16,128]{3,2,1,0:T(8,128)(2,1)S(1)} %get-tuple-element.399.refs_2_), channel_id=1, source_target_pairs={{0,4},{1,5},{2,6},{3,7},{4,0},{5,1},{6,2},{7,3},{8,12},{9,13},{10,... | collective-permute-start | bytes 1769480 | tf_op jit(solution)/shard_map/ppermute | solution.py:577
  196.7 11.0 %collective-permute-start.38 = (bf16[2,45,16,128]{3,2,1,0:T(8,128)(2,1)S(1)}, bf16[2,45,16,128]{3,2,1,0:T(8,128)(2,1)S(1)}, u32[]{:S(2)}, u32[]{:S(2)}) collective-permute-start(bf16[2,45,16,128]{3,2,1,0:T(8,128)(2,1)S(1)} %get-tuple-element.394.refs_1_), channel_id=1, source_target_pairs={{0,8},{1,9},{2,10},{3,11},{4,12},{5,13},{6,14},{7,15},{8,0},{9,1},... | collective-permute-start | bytes 1105928 | tf_op jit(solution)/shard_map/ppermute | solution.py:577
  196.7 7.1 %collective-permute-start.36 = (bf16[1,28,16,128]{3,2,1,0:T(8,128)(2,1)S(1)}, bf16[1,28,16,128]{3,2,1,0:T(8,128)(2,1)S(1)}, u32[]{:S(2)}, u32[]{:S(2)}) collective-permute-start(bf16[1,28,16,128]{3,2,1,0:T(8,128)(2,1)S(1)} %get-tuple-element.389), channel_id=1, source_target_pairs={{0,16},{1,17},{2,18},{3,19},{4,20},{5,21},{6,22},{7,23},{8,24},{9,... | collective-permute-start | bytes 344072 | tf_op jit(solution)/shard_map/ppermute | solution.py:577
  203.8 6.2 %collective-permute-start.39 = (bf16[1,28,16,128]{3,2,1,0:T(8,128)(2,1)S(1)}, bf16[1,28,16,128]{3,2,1,0:T(8,128)(2,1)S(1)}, u32[]{:S(2)}, u32[]{:S(2)}) collective-permute-start(bf16[1,28,16,128]{3,2,1,0:T(8,128)(2,1)S(1)} %get-tuple-element.396.refs_1_), channel_id=1, source_target_pairs={{0,16},{1,17},{2,18},{3,19},{4,20},{5,21},{6,22},{7,23},{8,24},{9,... | collective-permute-start | bytes 344072 | tf_op jit(solution)/shard_map/ppermute | solution.py:577
  214.8 24.2 %collective-permute-start.45 = (bf16[16,36,16,128]{3,2,1,0:T(8,128)(2,1)S(1)}, bf16[16,36,16,128]{3,2,1,0:T(8,128)(2,1)S(1)}, u32[]{:S(2)}, u32[]{:S(2)}) collective-permute-start(bf16[16,36,16,128]{3,2,1,0:T(8,128)(2,1)S(1)} %get-tuple-element.406.refs_2_), channel_id=1, source_target_pairs={{0,1},{1,0},{2,3},{3,2},{4,5},{5,4},{6,7},{7,6},{8,9},{9,8},{10,11... | collective-permute-start | bytes 7077896 | tf_op jit(solution)/shard_map/ppermute | solution.py:577
  214.8 12.6 %collective-permute-start.43 = (bf16[4,27,16,128]{3,2,1,0:T(8,128)(2,1)S(1)}, bf16[4,27,16,128]{3,2,1,0:T(8,128)(2,1)S(1)}, u32[]{:S(2)}, u32[]{:S(2)}) collective-permute-start(bf16[4,27,16,128]{3,2,1,0:T(8,128)(2,1)S(1)} %get-tuple-element.402.refs_2_), channel_id=1, source_target_pairs={{0,2},{1,3},{2,0},{3,1},{4,6},{5,7},{6,4},{7,5},{8,10},{9,11},{10,... | collective-permute-start | bytes 1327112 | tf_op jit(solution)/shard_map/ppermute | solution.py:577
  216.2 9.1 %collective-permute-start.42 = (bf16[4,18,16,128]{3,2,1,0:T(8,128)(2,1)S(1)}, bf16[4,18,16,128]{3,2,1,0:T(8,128)(2,1)S(1)}, u32[]{:S(2)}, u32[]{:S(2)}) collective-permute-start(bf16[4,18,16,128]{3,2,1,0:T(8,128)(2,1)S(1)} %get-tuple-element.401.refs_1_), channel_id=1, source_target_pairs={{0,4},{1,5},{2,6},{3,7},{4,0},{5,1},{6,2},{7,3},{8,12},{9,13},{10,... | collective-permute-start | bytes 884744 | tf_op jit(solution)/shard_map/ppermute | solution.py:577
  227.5 25.6 %collective-permute-start.50 = (bf16[8,27,16,128]{3,2,1,0:T(8,128)(2,1)S(1)}, bf16[8,27,16,128]{3,2,1,0:T(8,128)(2,1)S(1)}, u32[]{:S(2)}, u32[]{:S(2)}) collective-permute-start(bf16[8,27,16,128]{3,2,1,0:T(8,128)(2,1)S(1)} %get-tuple-element.416.refs_2_), channel_id=1, source_target_pairs={{0,4},{1,5},{2,6},{3,7},{4,0},{5,1},{6,2},{7,3},{8,12},{9,13},{10,... | collective-permute-start | bytes 2654216 | tf_op jit(solution)/shard_map/ppermute | solution.py:577
  229.1 15.2 %collective-permute-start.46 = (bf16[2,2,128,768]{3,2,1,0:T(8,128)(2,1)S(1)}, bf16[2,2,128,768]{3,2,1,0:T(8,128)(2,1)S(1)}, u32[]{:S(2)}, u32[]{:S(2)}) collective-permute-start(bf16[2,2,128,768]{3,2,1,0:T(8,128)(2,1)S(1)} %get-tuple-element.409), channel_id=1, source_target_pairs={{0,1},{1,0},{2,3},{3,2},{4,5},{5,4},{6,7},{7,6},{8,9},{9,8},{10,11... | collective-permute-start | bytes 2359304 | tf_op jit(solution)/shard_map/ppermute | solution.py:577
  229.1 24.0 %collective-permute-start.49 = (bf16[8,18,16,128]{3,2,1,0:T(8,128)(2,1)S(1)}, bf16[8,18,16,128]{3,2,1,0:T(8,128)(2,1)S(1)}, u32[]{:S(2)}, u32[]{:S(2)}) collective-permute-start(bf16[8,18,16,128]{3,2,1,0:T(8,128)(2,1)S(1)} %get-tuple-element.415.refs_1_), channel_id=1, source_target_pairs={{0,2},{1,3},{2,0},{3,1},{4,6},{5,7},{6,4},{7,5},{8,10},{9,11},{10,... | collective-permute-start | bytes 1769480 | tf_op jit(solution)/shard_map/ppermute | solution.py:577
  230.1 7.7 %collective-permute-start.44 = (bf16[2,28,16,128]{3,2,1,0:T(8,128)(2,1)S(1)}, bf16[2,28,16,128]{3,2,1,0:T(8,128)(2,1)S(1)}, u32[]{:S(2)}, u32[]{:S(2)}) collective-permute-start(bf16[2,28,16,128]{3,2,1,0:T(8,128)(2,1)S(1)} %get-tuple-element.404.refs_1_), channel_id=1, source_target_pairs={{0,8},{1,9},{2,10},{3,11},{4,12},{5,13},{6,14},{7,15},{8,0},{9,1},... | collective-permute-start | bytes 688136 | tf_op jit(solution)/shard_map/ppermute | solution.py:577
  237.9 15.1 %collective-permute-start.48 = (bf16[4,16,16,128]{3,2,1,0:T(8,128)(2,1)S(1)}, bf16[4,16,16,128]{3,2,1,0:T(8,128)(2,1)S(1)}, u32[]{:S(2)}, u32[]{:S(2)}) collective-permute-start(bf16[4,16,16,128]{3,2,1,0:T(8,128)(2,1)S(1)} %get-tuple-element.413.refs_2_), channel_id=1, source_target_pairs={{0,2},{1,3},{2,0},{3,1},{4,6},{5,7},{6,4},{7,5},{8,10},{9,11},{10,... | collective-permute-start | bytes 786440 | tf_op jit(solution)/shard_map/ppermute | solution.py:577
  239.0 14.0 %collective-permute-start.47 = (bf16[4,12,16,128]{3,2,1,0:T(8,128)(2,1)S(1)}, bf16[4,12,16,128]{3,2,1,0:T(8,128)(2,1)S(1)}, u32[]{:S(2)}, u32[]{:S(2)}) collective-permute-start(bf16[4,12,16,128]{3,2,1,0:T(8,128)(2,1)S(1)} %get-tuple-element.412.refs_1_), channel_id=1, source_target_pairs={{0,4},{1,5},{2,6},{3,7},{4,0},{5,1},{6,2},{7,3},{8,12},{9,13},{10,... | collective-permute-start | bytes 589832 | tf_op jit(solution)/shard_map/ppermute | solution.py:577
  253.3 14.6 %collective-permute-start.53 = (bf16[16,45,16,128]{3,2,1,0:T(8,128)(2,1)S(1)}, bf16[16,45,16,128]{3,2,1,0:T(8,128)(2,1)S(1)}, u32[]{:S(2)}, u32[]{:S(2)}) collective-permute-start(bf16[16,45,16,128]{3,2,1,0:T(8,128)(2,1)S(1)} %get-tuple-element.421.refs_2_), channel_id=1, source_target_pairs={{0,1},{1,0},{2,3},{3,2},{4,5},{5,4},{6,7},{7,6},{8,9},{9,8},{10,11... | collective-permute-start | bytes 8847368 | tf_op jit(solution)/shard_map/ppermute | solution.py:577
  253.4 14.3 %collective-permute-start.52 = (bf16[8,16,16,128]{3,2,1,0:T(8,128)(2,1)S(1)}, bf16[8,16,16,128]{3,2,1,0:T(8,128)(2,1)S(1)}, u32[]{:S(2)}, u32[]{:S(2)}) collective-permute-start(bf16[8,16,16,128]{3,2,1,0:T(8,128)(2,1)S(1)} %get-tuple-element.419.refs_2_), channel_id=1, source_target_pairs={{0,4},{1,5},{2,6},{3,7},{4,0},{5,1},{6,2},{7,3},{8,12},{9,13},{10,... | collective-permute-start | bytes 1572872 | tf_op jit(solution)/shard_map/ppermute | solution.py:577
  255.0 11.2 %collective-permute-start.51 = (bf16[8,12,16,128]{3,2,1,0:T(8,128)(2,1)S(1)}, bf16[8,12,16,128]{3,2,1,0:T(8,128)(2,1)S(1)}, u32[]{:S(2)}, u32[]{:S(2)}) collective-permute-start(bf16[8,12,16,128]{3,2,1,0:T(8,128)(2,1)S(1)} %get-tuple-element.418.refs_1_), channel_id=1, source_target_pairs={{0,2},{1,3},{2,0},{3,1},{4,6},{5,7},{6,4},{7,5},{8,10},{9,11},{10,... | collective-permute-start | bytes 1179656 | tf_op jit(solution)/shard_map/ppermute | solution.py:577
  267.8 7.4 %collective-permute-start.54 = (bf16[16,28,16,128]{3,2,1,0:T(8,128)(2,1)S(1)}, bf16[16,28,16,128]{3,2,1,0:T(8,128)(2,1)S(1)}, u32[]{:S(2)}, u32[]{:S(2)}) collective-permute-start(bf16[16,28,16,128]{3,2,1,0:T(8,128)(2,1)S(1)} %get-tuple-element.423.refs_2_), channel_id=1, source_target_pairs={{0,1},{1,0},{2,3},{3,2},{4,5},{5,4},{6,7},{7,6},{8,9},{9,8},{10,11... | collective-permute-start | bytes 5505032 | tf_op jit(solution)/shard_map/ppermute | solution.py:577
  (41 other events, 264.3 us)

commit v3 on v2

--- a/solution.py
+++ b/solution.py
@@ -64,7 +64,7 @@
 
 def call(
     kernel, name, scalars, args, outs, scratch=(), after=(), mib=16, flops=0, moved=0, far_outs=(), last=False, far_args=(),
-    aliases=(),
+    aliases=(), free=(),
 ):
     waits = len(after)
     at = waits + len(scalars) + len(args) + len(outs)
@@ -75,7 +75,7 @@
 
     place = lambda i, o: o if last else (pltpu.HBM if i in far_outs else pltpu.VMEM)(o.shape, o.dtype)
     space = lambda i: pltpu.HBM if i in far_args else pltpu.VMEM
-    near = [a if last else pltpu.with_memory_space_constraint(a, space(i)) for i, a in enumerate(args)]
+    near = [a if last or i in free else pltpu.with_memory_space_constraint(a, space(i)) for i, a in enumerate(args)]
     return pl.pallas_call(
         body,
         out_shape=tuple(place(i, o) for i, o in enumerate(outs)) + (pltpu.VMEM(TOKEN, F32),),
@@ -123,7 +123,10 @@
     return pltpu.VMEM(shape, dtype)
 
 
-def tables_kernel(scalars, lengths, near_q, far_q, kst, kf_out):
+def tables_kernel(count, scalars, lengths, *refs):
+    lines, (near_q, far_q, kst, kf_out, vecs) = refs[:10], refs[count:]
+    for i, line in enumerate(lines):
+        vecs[i : i + 1, :] = line[...].reshape(1, 768)
     j = scalars[0]
     exponent = -math.log(10000.0) / 32
 
@@ -155,9 +158,10 @@
         kf_out[r, 1] = jnp.where(lane >= 64, kf, jnp.where(lane == 0, bias, 0.0)).astype(BF)
 
 
-def tables(scalars, lengths, after):
-    outs = (f32(256, 256), f32(128, 256), b16(128, 512), b16(2, 2, 512, 128))
-    return call(tables_kernel, "tables", (scalars, lengths), (), outs, after=after)
+def tables(scalars, lengths, lines, weights, after):
+    outs = (f32(256, 256), f32(128, 256), b16(128, 512), b16(2, 2, 512, 128), f32(10, 768))
+    kernel = functools.partial(tables_kernel, 10 + len(weights))
+    return call(kernel, "tables", (scalars, lengths), (*lines, *weights), outs, after=after, free=range(10))
 
 
 def spread_heads(weight, high, low, sides):
@@ -507,14 +511,14 @@
     )
 
 
-def tokens_back_kernel(dk0, dk1, dv0, dv1, dq0, dq1, d1, wq, wk, wv, t0, t1, t23, tok_s):
+def tokens_back_kernel(dk0, dk1, dv0, dv1, dq0, dq1, d1, wq, wk, wv, t0, t1, t2, t3, tok_s):
     rows = lax.broadcasted_iota(jnp.int32, (512, 256), 0)
     cols = lax.broadcasted_iota(jnp.int32, (512, 256), 1)
     spread = jnp.where(rows // 2 == cols, 0.5, 0.0).astype(BF)
     for r, (dk, dv, dq) in enumerate(((dk0, dv0, dq0), (dk1, dv1, dq1))):
         hi, lo = split(d1[r * 256 : r * 256 + 256, :] + nt(dq[...], wq[...]))
         tok_s[...] = (nt(dk[...], wk[...]) + nt(dv[...], wv[...])) + (nn(spread, hi) + nn(spread, lo))
-        for d, out in enumerate((t0, t1, t23.at[0], t23.at[1])):
+        for d, out in enumerate((t0, t1, t2, t3)):
             out[r] = tok_s[d * 128 : d * 128 + 128, :].astype(BF)
 
 
@@ -545,7 +549,7 @@
 def last_back_kernel(
     scalars, k, v, kt, qc, qf, qht, qlt, lse, dctx, kf, kst, far_q, pw, xt0, xt1, pt0, pt1, dk0, dv0, dq0, pwg0, av0, vec_d,
     vec_u, upb_a, upb_b, d1, wq, wk, wv,
-    near, far, t0, t1, t23,
+    near, far, t0, t1, t2, t3,
     dqct_s, dpt_s, wph, wpl, dk1, dv1, dq1, pwg1, av1, g_s, smalls, tok_s,
 ):
     attn_bwd_kernel(
@@ -555,14 +559,14 @@
         scalars, xt0, xt1, pt0, pt1, dk0, dk1, dv0, dv1, dq0, dq1, pwg0, pwg1, av0, av1, vec_d, vec_u, upb_a, upb_b, near, far,
         g_s, smalls,
     )
-    tokens_back_kernel(dk0, dk1, dv0, dv1, dq0, dq1, d1, wq, wk, wv, t0, t1, t23, tok_s)
+    tokens_back_kernel(dk0, dk1, dv0, dv1, dq0, dq1, d1, wq, wk, wv, t0, t1, t2, t3, tok_s)
 
 
 def last_back(scalars, args, after=()):
     grad = b16(16, 28, 16, 128)
     return call(
         last_back_kernel, "last_back", (scalars,), args,
-        (grad, grad, b16(2, 128, 768), b16(2, 128, 768), b16(2, 2, 128, 768)),
+        (grad, grad) + (b16(2, 128, 768),) * 4,
         (
             vs(768, 256), vs(768, 256), vs(3, 256, 256, dtype=BF), vs(3, 256, 256, dtype=BF), vs(512, 768, dtype=BF),
             vs(512, 768, dtype=BF), vs(256, 768, dtype=BF), vs(384, 128), vs(8, 768), vs(2304, 768), vs(512, 128),
@@ -637,33 +641,52 @@
         self.got = [partner(s, b) for s, b in zip(self.sends, self.bits[self.step])]
         return self
 
-    def finish(self):
+    def plan(self):
         step, a, b = self.step, self.cuts, self.slabs - self.cuts
         here = self.keep if step < 5 else self.sends
-        if step < 9:
-            rows = (8, 4, 2, 1, 1, 2, 4, 8, 16)[step]
-            shapes = [(a,), (b,)] if step in (0, 1, 6, 7) else [(a + b,)]
-            copies = 2 if step < 4 else 1
-            outs = [b16(rows, *s, 16, 128) for s in shapes for _ in range(copies)]
-
-            def add(after):
-                return call(
-                    functools.partial(add_kernel, step, a, len(here)), "sum_step", (), (*here, *self.got), outs,
-                    after=after, mib=8, moved=10**6,
-                )
-
-            outs = self.order.run(add)
-            if step < 4:
-                self.keep, self.sends = outs[::2], outs[1::2]
-            else:
-                self.sends = outs
-            if step == 4:
-                for bit in self.others:
-                    self.sends = [(s.astype(F32) + partner(s, bit).astype(F32)).astype(BF) for s in self.sends]
+        rows = (8, 4, 2, 1, 1, 2, 4, 8, 16)[step]
+        shapes = [(a,), (b,)] if step in (0, 1, 6, 7) else [(a + b,)]
+        outs = [b16(rows, *s, 16, 128) for s in shapes for _ in range(2 if step < 4 else 1)]
+        kernel = functools.partial(add_kernel, step, a, len(here))
+        return kernel, (*here, *self.got), outs
+
+    def take(self, outs):
+        step = self.step
+        if step < 4:
+            self.keep, self.sends = outs[::2], outs[1::2]
+        else:
+            self.sends = outs
+        if step == 4:
+            for bit in self.others:
+                self.sends = [(s.astype(F32) + partner(s, bit).astype(F32)).astype(BF) for s in self.sends]
+        self.step += 1
+
+    def finish(self):
+        if self.step < 9:
+            finish_together(self.order, (self,))
         else:
             self.sends = (*self.sends, *self.got)
-        self.step += 1
+            self.step += 1
         return self
+
+
+def finish_together(order, sums, also=()):
+    plans = [s.plan() for s in sums]
+    args = [a for p in plans for a in p[1]]
+    outs = [o for p in plans for o in p[2]]
+
+    def kernel(*refs):
+        here, there = 0, len(args)
+        for step, taken, given in plans:
+            step(*refs[here : here + len(taken)], *refs[there : there + len(given)])
+            here, there = here + len(taken), there + len(given)
+
+    results = order.run(
+        lambda after: call(kernel, "sum_step", (), args, outs, after=after, mib=8, moved=10**6), also=also
+    )
+    for s, (_, _, given) in zip(sums, plans):
+        s.take(results[: len(given)])
+        results = results[len(given) :]
 
 
 def get_blocks(me, halves, slabs, outs):
@@ -741,7 +764,7 @@
 def owners_kernel(scalars, p0, p2, p13, out):
     j = scalars[0]
     out[j] = p0[...].astype(out.dtype)
-    out[j ^ 2] = p2[0].astype(out.dtype)
+    out[j ^ 2] = (p2[0] if len(p2.shape) > len(p0.shape) else p2[...]).astype(out.dtype)
     out[j ^ 1] = p13[0].astype(out.dtype)
     out[j ^ 3] = p13[1].astype(out.dtype)
 
@@ -757,9 +780,10 @@
 def join_pieces(own, came, after=()):
     def kernel(a, b, out):
         out[0] = a[...]
-        out[1] = b[1]
-
-    return call(kernel, "join", (), (own, came), (jax.ShapeDtypeStruct(came.shape, came.dtype),), after=after, moved=10**6)
+        out[1] = b[1] if len(b.shape) > len(a.shape) else b[...]
+
+    shape = (2, *own.shape)
+    return call(kernel, "join", (), (own, came), (jax.ShapeDtypeStruct(shape, own.dtype),), after=after, moved=10**6)
 
 
 def pick_kernel(row, scalars, blocks, o0, o1, o2, o3, sem):
@@ -805,13 +829,11 @@
         return [pieces[0]] + [partner(pieces[d], d) for d in (1, 2, 3)]
 
     x0 = trade(order.run(pick, 0, scalars, by_owner))
-    near_q, far_q, kst, kf = order.run(tables, scalars, lengths)
-    vecs = jnp.stack(
-        [
-            query_bias, content_bias, position_bias, value_bias, out_bias, inner_gain, inner_shift, down_bias,
-            outer_gain, outer_shift,
-        ]
-    )
+    lines = (
+        query_bias, content_bias, position_bias, value_bias, out_bias, inner_gain, inner_shift, down_bias, outer_gain,
+        outer_shift,
+    )
+    near_q, far_q, kst, kf, vecs = order.run(tables, scalars, lengths, lines, ())
     s1 = order.run(pick, 1, scalars, by_owner)
     sc = order.run(pick, None, scalars, cot_owner)
     x1 = trade(order.run(gate, s1, also=x0[1:]))
@@ -847,49 +869,52 @@
         return k[r], v[r], kt[r], qc[r], qf[r], qht[r], qlt[r], lse[r], dctx, kf, kst, far_q, position_weight
 
     dk, dv, dq, pwg, attn_vec = order.run(attn_bwd, 0, backward(0))
-    down.finish().start()
-    up.finish().start()
-    near, far, t0, t1, t23 = order.run(
+    finish_together(order, (down, up))
+    down.start(), up.start()
+    near, far, t0, t1, t2, t3 = order.run(
         last_back, scalars,
         (
             *backward(1), *xt, *pt, dk, dv, dq, pwg, attn_vec, vec_d, vec_u, upb_a, upb_b, d1, query_weight, key_weight,
             value_weight,
         ),
     )
-    up.finish().start()
-    down.finish().start()
+
+    finish_together(order, (up, down))
+    up.start(), down.start()
     (far,) = order.run(gate, (far,))
     three = Sum(order, (near,), (far,), NA, bits).start()
+    finish_together(order, (up, down, three))
+    up.start(), down.start(), three.start()
+    finish_together(order, (up, down, three))
+    up.start(), down.start(), three.start()
+    (t3,) = order.run(gate, (t3,))
+    u3 = partner(t3, 2)
+    finish_together(order, (up, down, three), also=(u3,))
+    up.start(), down.start(), three.start()
+    (t2,) = order.run(gate, (t2,))
+    u2 = partner(t2, 2)
+    finish_together(order, (up, down, three), also=(u2,))
+    up.start(), down.start(), three.start()
+    (t13,) = order.run(join_pieces, t1, u3)
+    u13 = partner(t13, 1)
     layer_output = order.run(assemble_owners, "layer_output", BF, scalars, (out0, back23, back13))[0]
-    three.finish().start()
-    down.finish().start()
-    up.finish().start()
-    down.finish().start()
-    (t23,) = order.run(gate, (t23,))
-    u23 = partner(t23, 2)
-    three.finish().start()
-    up.finish().start()
-    three.finish().start()
-    down.finish().start()
-    up.finish().start()
-    three.finish().start()
-    up.finish().start()
-    down.finish().start()
-    three.finish().start()
-    u13 = partner(order.run(join_pieces, t1, u23)[0], 1)
-    up.finish().start()
-    three.finish().start()
-    down.finish().start()
-    up.finish().start()
-    three.finish().start()
+    finish_together(order, (up, three, down))
+    up.start(), three.start(), down.start()
+    finish_together(order, (up, three))
+    up.start(), three.start()
     down.finish()
     down_weight_grad = order.run(assemble_rows, scalars, down.sends)[0]
-    tokens_grad = order.run(assemble_owners, "tokens_grad", F32, scalars, (t0, u23, u13))[0]
-    three.finish().start()
-    up.finish().start()
-    three.finish().start()
+    finish_together(order, (three,))
+    three.start()
+    tokens_grad = order.run(assemble_owners, "tokens_grad", F32, scalars, (t0, u2, u13))[0]
+    finish_together(order, (three,))
+    three.start()
+    finish_together(order, (up,))
+    up.start()
     up.finish()
     up_weight_grad, out_weight_grad = order.run(assemble_up, scalars, up.sends)
+    finish_together(order, (three,))
+    three.start()
     three.finish()
     query_weight_grad, key_weight_grad, value_weight_grad, position_weight_grad, lines = order.run(
         assemble_three, scalars, three.sends

time: 287 us -> 266 us (0.927)
  waiting for transfers between devices: 90.9 us -> 79.9 us
  local copies, waits for them, and re-layouts: 14.7 us -> 9.05 us
    ppermute x55 -> x56, waiting for transfers between devices: 90.9 us -> 79.9 us  [partner(): return lax.ppermute(x, 'batch', [(i, i ^ bit) for i in range(size)])]
    another operation x11 -> x0, local copies, waits for them, and re-layouts: 6.97 us -> none  [on_device(): jnp.stack([query_bias, content_bias, position_bias, value_bias, out_bias,...]
    ppermute x55 -> x56, starting transfers between devices: 59.9 us -> 57.3 us  [partner(): return lax.ppermute(x, 'batch', [(i, i ^ bit) for i in range(size)])]
    unnamed x100 -> x126, local copies, waits for them, and re-layouts: 6.46 us -> 7.76 us
    pallas_call x49 -> x37, Pallas kernels: 102 us -> 101 us  [call(): pl.pallas_call(body, out_shape=tuple((place(i, o) for i, o in enumerate(o...]
  transfers between devices with their start and end apart: 55 -> 56, of which waited for: 21 -> 21; matrix products, arithmetic and copies ran while one was open for 2% -> 0% of each run, Pallas kernels for 32% -> 33%
where the time goes in v3:
time: 266 us; the launch traced here: 261 us
  Pallas kernels  113 us (42%)
  waiting for transfers between devices  79.9 us (30%)
  starting transfers between devices  57.3 us (22%)
  local copies, waits for them, and re-layouts  9.05 us (3%)
    pallas_call x37, Pallas kernels, call(): pl.pallas_call(body, out_shape=tuple((place(i, o) for i, o in enumerate(o...  101 us
    ppermute x56, waiting for transfers between devices, partner(): return lax.ppermute(x, 'batch', [(i, i ^ bit) for i in range(size)])  79.9 us
    ppermute x56, starting transfers between devices, partner(): return lax.ppermute(x, 'batch', [(i, i ^ bit) for i in range(size)])  57.3 us
    pallas_call x2, Pallas kernels, call_grid(): pl.pallas_call(body, out_shape=(*outs, pltpu.VMEM(TOKEN, F32)), grid=(ste...  12.2 us
    unnamed x126, local copies, waits for them, and re-layouts  7.76 us
  transfers between devices with their start and end apart: 56, of which 21 were waited for; matrix products, arithmetic and copies ran while one was open for 0% of the time, Pallas kernels for 33%

profile of v3, /device:TPU:0, one launch (start us, length us, event | category | flops | bytes accessed | tf_op | source)
XLA Modules:
  0.0 261.5 jit_solution(11469575824414928936)
XLA Ops:
  0.8 1.8 pick.3
  3.2 2.6 collective-permute-start.1
  13.3 2.4 tables.1
  15.7 1.8 pick.4
  17.5 1.8 pick.5
  19.6 1.9 collective-permute-start.4
  21.6 10.2 %attn_fwd.2 = (bf16[512,768]{1,0:T(8,128)(2,1)}, bf16[512,768]{1,0:T(8,128)(2,1)}, bf16[768,512]{1,0:T(8,128)(2,1)}, bf16[768,512]{1,0:T(8,128)(2,1)}, bf16[256,...) custom-call(f32[8,128]{1,0:T(8,128)S(1)} %get-tuple-element.228.refs, ...), custom_call_target="tpu_custom_call" | custom-call | flops 4000000000 | bytes 12000000 | tf_op jit(solution)/shard_map/attn_fwd/pallas_call | solution.py:79
  32.1 1.9 collective-permute-start.7
  34.1 10.1 %attn_fwd.3 = (bf16[512,768]{1,0:T(8,128)(2,1)}, bf16[512,768]{1,0:T(8,128)(2,1)}, bf16[768,512]{1,0:T(8,128)(2,1)}, bf16[768,512]{1,0:T(8,128)(2,1)}, bf16[256,...) custom-call(f32[8,128]{1,0:T(8,128)S(1)} %get-tuple-element.241.refs, ...), custom_call_target="tpu_custom_call" | custom-call | flops 4000000000 | bytes 12000000 | tf_op jit(solution)/shard_map/attn_fwd/pallas_call | solution.py:79
  44.3 15.7 %ffn_down.1 = (bf16[2,64,768]{2,1,0:T(8,128)(2,1)S(1)}, bf16[2,64,768]{2,1,0:T(8,128)(2,1)S(1)}, bf16[2,2,64,768]{3,2,1,0:T(8,128)(2,1)S(1)}, f32[512,768]{1,0:T...) custom-call(f32[8,128]{1,0:T(8,128)S(1)} %get-tuple-element.243.refs, ...), custom_call_target="tpu_custom_call" | custom-call | flops 8000000000 | bytes 25000000 | tf_op jit(solution)/shard_map/ffn_down/pallas_call | solution.py:79
  60.3 1.9 collective-permute-start.10
  62.2 6.6 %ffn_up_a.1 = (f32[512,768]{1,0:T(8,128)S(1)}, bf16[16,45,16,128]{3,2,1,0:T(8,128)(2,1)S(1)}, bf16[16,45,16,128]{3,2,1,0:T(8,128)(2,1)S(1)}, f32[1,1536]{1,0:T(1,128)S(1)}, f32[8,128]{1,0:T(8,128)S(1)}) custom-call(f32[8,128]{1,0:T(8,128)S(1)} %get-tuple-element.255.refs_0_, s32[4]{0:T(128)S(1)} %pad_add_fusion.refs_0_.refs_1_, ...), custom_call_target="tpu_custom_call" | custom-call | flops 4000000000 | bytes 12000000 | tf_op jit(solution)/shard_map/ffn_up_a/pallas_call | solution.py:79
  69.9 1.9 collective-permute-start.12
  71.9 9.3 %ffn_up_b.1 = (f32[512,768]{1,0:T(8,128)S(1)}, bf16[2,256,768]{2,1,0:T(8,128)(2,1)S(1)}, bf16[16,45,16,128]{3,2,1,0:T(8,128)(2,1)S(1)}, bf16[16,45,16,128]{3,2,1...) custom-call(f32[8,128]{1,0:T(8,128)S(1)} %get-tuple-element.266.refs, ...), custom_call_target="tpu_custom_call", output_to_operand_aliasing={{2}: (14, {}), {3}: (15, {})} | custom-call | flops 5000000000 | bytes 14000000 | tf_op jit(solution)/shard_map/ffn_up_b/pallas_call | solution.py:79
  81.3 3.6 %collective-permute-done.11.refs_3_ = bf16[8,18,16,128]{3,2,1,0:T(8,128)(2,1)S(1)} collective-permute-done((bf16[8,18,16,128]{3,2,1,0:T(8,128)(2,1)S(1)}, bf16[8,18,16,128]{3,2,1,0:T(8,128)(2,1)S(1)}, u32[]{:S(2)}, u32[]{:S(2)}) %collective-permute-start.11) | collective-permute-done | bytes 589856 | tf_op jit(solution)/shard_map/ppermute | solution.py:581
  85.4 1.8 collective-permute-start.13
  87.1 1.5 collective-permute-start.14
  88.8 9.1 %attn_bwd.1 = (bf16[512,768]{1,0:T(8,128)(2,1)S(1)}, bf16[512,768]{1,0:T(8,128)(2,1)S(1)}, bf16[256,768]{1,0:T(8,128)(2,1)S(1)}, f32[384,128]{1,0:T(8,128)S(1)},...) custom-call(f32[8,128]{1,0:T(8,128)S(1)} %get-tuple-element.281.refs_0_, bf16[512,768]{1,0:T(8,128)(2,1)S(1)} %copy-done.42, ...), custom_call_target="tpu_custom_call" | custom-call | flops 8000000000 | bytes 12000000 | tf_op jit(solution)/shard_map/attn_bwd/pallas_call | solution.py:79
  98.1 0.9 sum_step.16
  99.0 1.6 collective-permute-start.18
  101.1 0.9 collective-permute-start.17
  102.2 18.8 %last_back.1 = (bf16[16,28,16,128]{3,2,1,0:T(8,128)(2,1)S(1)}, bf16[16,28,16,128]{3,2,1,0:T(8,128)(2,1)S(1)}, bf16[2,128,768]{2,1,0:T(8,128)(2,1)S(1)}, bf16[2,1...) custom-call(f32[8,128]{1,0:T(8,128)S(1)} %get-tuple-element.300.refs, ...), custom_call_target="tpu_custom_call" | custom-call | flops 16999999488 | bytes 30000000 | tf_op jit(solution)/shard_map/last_back/pallas_call | solution.py:79
  121.0 1.0 collective-permute-done.17.refs_4_
  122.5 1.5 collective-permute-start.20
  124.6 2.6 collective-permute-start.21
  127.2 7.0 %collective-permute-done.21.refs_6_ = bf16[1,36,16,128]{3,2,1,0:T(8,128)(2,1)S(1)} collective-permute-done((bf16[1,36,16,128]{3,2,1,0:T(8,128)(2,1)S(1)}, bf16[1,36,16,128]{3,2,1,0:T(8,128)(2,1)S(1)}, u32[]{:S(2)}, u32[]{:S(2)}) %collective-permute-start.21) | collective-permute-done | bytes 147488 | tf_op jit(solution)/shard_map/ppermute | solution.py:581
  134.2 0.9 collective-permute-done.20.refs_4_
  136.5 1.4 collective-permute-start.25
  138.4 2.6 collective-permute-start.24
  141.0 7.7 %collective-permute-done.24.refs_4_ = bf16[1,36,16,128]{3,2,1,0:T(8,128)(2,1)S(1)} collective-permute-done((bf16[1,36,16,128]{3,2,1,0:T(8,128)(2,1)S(1)}, bf16[1,36,16,128]{3,2,1,0:T(8,128)(2,1)S(1)}, u32[]{:S(2)}, u32[]{:S(2)}) %collective-permute-start.24) | collective-permute-done | bytes 147488 | tf_op jit(solution)/shard_map/ppermute | solution.py:581
  148.6 2.0 collective-permute-done.23.refs_2_
  151.0 1.1 collective-permute-start.27
  152.1 2.1 collective-permute-start.29
  154.2 1.5 collective-permute-start.31
  155.7 1.5 collective-permute-start.30
  157.7 8.2 %collective-permute-done.28.refs_3_ = bf16[1,45,16,128]{3,2,1,0:T(8,128)(2,1)S(1)} collective-permute-done((bf16[1,45,16,128]{3,2,1,0:T(8,128)(2,1)S(1)}, bf16[1,45,16,128]{3,2,1,0:T(8,128)(2,1)S(1)}, u32[]{:S(2)}, u32[]{:S(2)}) %collective-permute-start.28) | collective-permute-done | bytes 184352 | tf_op jit(solution)/shard_map/ppermute | solution.py:581
  167.0 1.2 collective-permute-start.32
  168.2 0.9 collective-permute-start.34
  169.1 1.5 collective-permute-start.35
  170.6 1.6 collective-permute-start.36
  173.0 7.7 %collective-permute-done.33.refs_3_ = bf16[1,45,16,128]{3,2,1,0:T(8,128)(2,1)S(1)} collective-permute-done((bf16[1,45,16,128]{3,2,1,0:T(8,128)(2,1)S(1)}, bf16[1,45,16,128]{3,2,1,0:T(8,128)(2,1)S(1)}, u32[]{:S(2)}, u32[]{:S(2)}) %collective-permute-start.33) | collective-permute-done | bytes 184352 | tf_op jit(solution)/shard_map/ppermute | solution.py:581
  180.7 1.8 collective-permute-done.35.refs_7_
  182.6 1.3 collective-permute-start.40
  184.8 1.6 collective-permute-start.38
  187.2 1.5 layer_output.1
  188.6 8.7 %collective-permute-done.39.refs_4_ = bf16[1,28,16,128]{3,2,1,0:T(8,128)(2,1)S(1)} collective-permute-done((bf16[1,28,16,128]{3,2,1,0:T(8,128)(2,1)S(1)}, bf16[1,28,16,128]{3,2,1,0:T(8,128)(2,1)S(1)}, u32[]{:S(2)}, u32[]{:S(2)}) %collective-permute-start.39) | collective-permute-done | bytes 114720 | tf_op jit(solution)/shard_map/ppermute | solution.py:581
  197.3 0.9 collective-permute-done.38.refs_2_
  198.5 1.5 collective-permute-start.43
  200.6 2.5 collective-permute-start.44
  203.1 5.8 %collective-permute-done.44.refs_6_ = bf16[1,28,16,128]{3,2,1,0:T(8,128)(2,1)S(1)} collective-permute-done((bf16[1,28,16,128]{3,2,1,0:T(8,128)(2,1)S(1)}, bf16[1,28,16,128]{3,2,1,0:T(8,128)(2,1)S(1)}, u32[]{:S(2)}, u32[]{:S(2)}) %collective-permute-start.44) | collective-permute-done | bytes 114720 | tf_op jit(solution)/shard_map/ppermute | solution.py:581
  209.1 2.0 collective-permute-done.43.refs_4_
  211.2 1.3 collective-permute-start.51
  213.3 1.2 collective-permute-start.46
  214.5 4.8 %assemble_rows.1 = (f32[3072,768]{1,0:T(8,128)}, f32[8,128]{1,0:T(8,128)S(1)}) custom-call(f32[8,128]{1,0:T(8,128)S(1)} %get-tuple-element.385.refs_0_, s32[4]{0:T(128)S(1)} %pad_add_fusion.refs_0_.refs_1_, bf16[16,36,16,128]{3,2,1,0:T(8,128)(2,1)S(1)} %get-tuple-element.386.refs_2_, bf16[16,36,16,128]{3,2,1,0:T(8,128)(2,1)S(1)} %collective-permute-done.45.refs_3_), custom_call_target="tpu_custom_call" | custom-call | bytes 14000000 | tf_op jit(solution)/shard_map/assemble_rows/pallas_call | solution.py:106
  219.3 1.7 collective-permute-done.46.refs_2_
  221.1 1.3 collective-permute-start.49
  223.2 2.4 tokens_grad.1
  225.6 11.1 %collective-permute-done.48.refs_3_ = bf16[4,12,16,128]{3,2,1,0:T(8,128)(2,1)S(1)} collective-permute-done((bf16[4,12,16,128]{3,2,1,0:T(8,128)(2,1)S(1)}, bf16[4,12,16,128]{3,2,1,0:T(8,128)(2,1)S(1)}, u32[]{:S(2)}, u32[]{:S(2)}) %collective-permute-start.48) | collective-permute-done | bytes 196640 | tf_op jit(solution)/shard_map/ppermute | solution.py:581
  237.1 1.3 collective-permute-start.54
  239.1 3.3 %collective-permute-done.52.refs_3_ = bf16[16,45,16,128]{3,2,1,0:T(8,128)(2,1)S(1)} collective-permute-done((bf16[16,45,16,128]{3,2,1,0:T(8,128)(2,1)S(1)}, bf16[16,45,16,128]{3,2,1,0:T(8,128)(2,1)S(1)}, u32[]{:S(2)}, u32[]{:S(2)}) %collective-permute-start.52) | collective-permute-done | bytes 2949152 | tf_op jit(solution)/shard_map/ppermute | solution.py:581
  242.4 7.3 %assemble_up.1 = (f32[768,3072]{1,0:T(8,128)}, f32[768,768]{1,0:T(8,128)}, f32[8,128]{1,0:T(8,128)S(1)}) custom-call(f32[8,128]{1,0:T(8,128)S(1)} %get-tuple-element.399.refs_0_, s32[4]{0:T(128)S(1)} %pad_add_fusion.refs_0_.refs_1_, bf16[16,45,16,128]{3,2,1,0:T(8,128)(2,1)S(1)} %get-tuple-element.400.refs_2_, ...), custom_call_target="tpu_custom_call" | custom-call | bytes 18000000 | tf_op jit(solution)/shard_map/assemble_up/pallas_call | solution.py:106
  249.8 1.7 collective-permute-done.54.refs_4_
  251.6 3.8 %collective-permute-done.55.refs_3_ = bf16[16,28,16,128]{3,2,1,0:T(8,128)(2,1)S(1)} collective-permute-done((bf16[16,28,16,128]{3,2,1,0:T(8,128)(2,1)S(1)}, bf16[16,28,16,128]{3,2,1,0:T(8,128)(2,1)S(1)}, u32[]{:S(2)}, u32[]{:S(2)}) %collective-permute-start.55) | collective-permute-done | bytes 1835040 | tf_op jit(solution)/shard_map/ppermute | solution.py:581
  255.4 4.6 %assemble_three.1 = (f32[768,768]{1,0:T(8,128)}, f32[768,768]{1,0:T(8,128)}, f32[768,768]{1,0:T(8,128)}, f32[12,64,64]{2,1,0:T(8,128)}, f32[16,768]{1,0:T(8,128)S(1)}, /*index=5*/f32[8,128]{1,0:T(8,128)}) custom-call(f32[8,128]{1,0:T(8,128)S(1)} %get-tuple-element.404.refs_0_, s32[4]{0:T(128)S(1)} %pad_add_fusion.refs_0_.refs_1_, ...), custom_call_target="tpu_custom_call" | custom-call | bytes 11000000 | tf_op jit(solution)/shard_map/assemble_three/pallas_call | solution.py:79
  (219 shorter events, 23.8 us)
Async XLA Ops:
  0.8 20.7 %copy-start.16 = (bf16[768,768]{1,0:T(8,128)(2,1)S(1)}, bf16[768,768]{1,0:T(8,128)(2,1)}, u32[]{:S(2)}) copy-start(bf16[768,768]{1,0:T(8,128)(2,1)} %refs_29_.1) | copy-start | bytes 3538948
  0.8 20.7 %copy-start.24 = (f32[12,64,64]{2,1,0:T(8,128)S(1)}, f32[12,64,64]{2,1,0:T(8,128)}, u32[]{:S(2)}) copy-start(f32[12,64,64]{2,1,0:T(8,128)} %refs_14_.1) | copy-start | bytes 589828
  2.7 16.7 %collective-permute-start = (bf16[128,768]{1,0:T(8,128)(2,1)S(1)}, bf16[128,768]{1,0:T(8,128)(2,1)S(1)}, u32[]{:S(2)}, u32[]{:S(2)}) collective-permute-start(bf16[128,768]{1,0:T(8,128)(2,1)S(1)} %get-tuple-element.221), channel_id=1, source_target_pairs={{0,1},{1,0},{2,3},{3,2},{4,5},{5,4},{6,7},{7,6},{8,9},{9,8},{10,11... | collective-permute-start | bytes 589832 | tf_op jit(solution)/shard_map/ppermute | solution.py:581
  3.2 16.2 %collective-permute-start.1 = (bf16[128,768]{1,0:T(8,128)(2,1)S(1)}, bf16[128,768]{1,0:T(8,128)(2,1)S(1)}, u32[]{:S(2)}, u32[]{:S(2)}) collective-permute-start(bf16[128,768]{1,0:T(8,128)(2,1)S(1)} %get-tuple-element.222), channel_id=1, source_target_pairs={{0,2},{1,3},{2,0},{3,1},{4,6},{5,7},{6,4},{7,5},{8,10},{9,11},{10,... | collective-permute-start | bytes 589832 | tf_op jit(solution)/shard_map/ppermute | solution.py:581
  5.7 13.6 %collective-permute-start.2 = (bf16[128,768]{1,0:T(8,128)(2,1)S(1)}, bf16[128,768]{1,0:T(8,128)(2,1)S(1)}, u32[]{:S(2)}, u32[]{:S(2)}) collective-permute-start(bf16[128,768]{1,0:T(8,128)(2,1)S(1)} %get-tuple-element.223), channel_id=1, source_target_pairs={{0,3},{1,2},{2,1},{3,0},{4,7},{5,6},{6,5},{7,4},{8,11},{9,10},{10,... | collective-permute-start | bytes 589832 | tf_op jit(solution)/shard_map/ppermute | solution.py:581
  15.7 72.9 %copy-start.22 = (bf16[2,2,512,128]{3,2,1,0:T(8,128)(2,1)}, bf16[2,2,512,128]{3,2,1,0:T(8,128)(2,1)S(1)}, u32[]{:S(2)}) copy-start(bf16[2,2,512,128]{3,2,1,0:T(8,128)(2,1)S(1)} %get-tuple-element.232.refs_11_.refs_10_) | copy-start | bytes 1572868
  15.7 72.9 %copy-start.28 = (f32[128,256]{1,0:T(8,128)}, f32[128,256]{1,0:T(8,128)S(1)}, u32[]{:S(2)}) copy-start(f32[128,256]{1,0:T(8,128)S(1)} %get-tuple-element.292.refs_12_.refs_13_) | copy-start | bytes 393220
  15.7 72.9 %copy-start.30 = (bf16[128,512]{1,0:T(8,128)(2,1)}, bf16[128,512]{1,0:T(8,128)(2,1)S(1)}, u32[]{:S(2)}) copy-start(bf16[128,512]{1,0:T(8,128)(2,1)S(1)} %get-tuple-element.291.refs_11_.refs_12_) | copy-start | bytes 393220
  19.4 12.4 %collective-permute-start.3 = (bf16[128,768]{1,0:T(8,128)(2,1)S(1)}, bf16[128,768]{1,0:T(8,128)(2,1)S(1)}, u32[]{:S(2)}, u32[]{:S(2)}) collective-permute-start(bf16[128,768]{1,0:T(8,128)(2,1)S(1)} %get-tuple-element.234), channel_id=1, source_target_pairs={{0,1},{1,0},{2,3},{3,2},{4,5},{5,4},{6,7},{7,6},{8,9},{9,8},{10,11... | collective-permute-start | bytes 589832 | tf_op jit(solution)/shard_map/ppermute | solution.py:581
  19.6 12.2 %collective-permute-start.4 = (bf16[128,768]{1,0:T(8,128)(2,1)S(1)}, bf16[128,768]{1,0:T(8,128)(2,1)S(1)}, u32[]{:S(2)}, u32[]{:S(2)}) collective-permute-start(bf16[128,768]{1,0:T(8,128)(2,1)S(1)} %get-tuple-element.235), channel_id=1, source_target_pairs={{0,2},{1,3},{2,0},{3,1},{4,6},{5,7},{6,4},{7,5},{8,10},{9,11},{10,... | collective-permute-start | bytes 589832 | tf_op jit(solution)/shard_map/ppermute | solution.py:581
  21.5 10.3 %collective-permute-start.5 = (bf16[128,768]{1,0:T(8,128)(2,1)S(1)}, bf16[128,768]{1,0:T(8,128)(2,1)S(1)}, u32[]{:S(2)}, u32[]{:S(2)}) collective-permute-start(bf16[128,768]{1,0:T(8,128)(2,1)S(1)} %get-tuple-element.236), channel_id=1, source_target_pairs={{0,3},{1,2},{2,1},{3,0},{4,7},{5,6},{6,5},{7,4},{8,11},{9,10},{10,... | collective-permute-start | bytes 589832 | tf_op jit(solution)/shard_map/ppermute | solution.py:581
  31.9 12.3 %collective-permute-start.6 = (bf16[2,64,768]{2,1,0:T(8,128)(2,1)S(1)}, bf16[2,64,768]{2,1,0:T(8,128)(2,1)S(1)}, u32[]{:S(2)}, u32[]{:S(2)}) collective-permute-start(bf16[2,64,768]{2,1,0:T(8,128)(2,1)S(1)} %get-tuple-element.249), channel_id=1, source_target_pairs={{0,1},{1,0},{2,3},{3,2},{4,5},{5,4},{6,7},{7,6},{8,9},{9,8},{10,11... | collective-permute-start | bytes 589832 | tf_op jit(solution)/shard_map/ppermute | solution.py:581
  32.1 12.0 %collective-permute-start.7 = (bf16[2,64,768]{2,1,0:T(8,128)(2,1)S(1)}, bf16[2,64,768]{2,1,0:T(8,128)(2,1)S(1)}, u32[]{:S(2)}, u32[]{:S(2)}) collective-permute-start(bf16[2,64,768]{2,1,0:T(8,128)(2,1)S(1)} %get-tuple-element.250), channel_id=1, source_target_pairs={{0,2},{1,3},{2,0},{3,1},{4,6},{5,7},{6,4},{7,5},{8,10},{9,11},{10,... | collective-permute-start | bytes 589832 | tf_op jit(solution)/shard_map/ppermute | solution.py:581
  34.0 10.1 %collective-permute-start.8 = (bf16[2,64,768]{2,1,0:T(8,128)(2,1)S(1)}, bf16[2,64,768]{2,1,0:T(8,128)(2,1)S(1)}, u32[]{:S(2)}, u32[]{:S(2)}) collective-permute-start(bf16[2,64,768]{2,1,0:T(8,128)(2,1)S(1)} %get-tuple-element.251), channel_id=1, source_target_pairs={{0,3},{1,2},{2,1},{3,0},{4,7},{5,6},{6,5},{7,4},{8,11},{9,10},{10,... | collective-permute-start | bytes 589832 | tf_op jit(solution)/shard_map/ppermute | solution.py:581
  44.1 15.9 %copy-start.55 = (f32[12,1,256]{2,1,0:T(1,128)}, f32[12,1,256]{2,1,0:T(1,128)S(1)}, u32[]{:S(2)}) copy-start(f32[12,1,256]{2,1,0:T(1,128)S(1)} %get-tuple-element.308.refs_9_) | copy-start | bytes 36868
  60.0 8.9 %collective-permute-start.9 = (bf16[16,36,16,128]{3,2,1,0:T(8,128)(2,1)S(1)}, bf16[16,36,16,128]{3,2,1,0:T(8,128)(2,1)S(1)}, u32[]{:S(2)}, u32[]{:S(2)}) collective-permute-start(bf16[16,36,16,128]{3,2,1,0:T(8,128)(2,1)S(1)} %get-tuple-element.262), channel_id=1, source_target_pairs={{0,1},{1,0},{2,3},{3,2},{4,5},{5,4},{6,7},{7,6},{8,9},{9,8},{10,11... | collective-permute-start | bytes 7077896 | tf_op jit(solution)/shard_map/ppermute | solution.py:581
  60.3 11.5 %collective-permute-start.10 = (bf16[2,2,64,768]{3,2,1,0:T(8,128)(2,1)S(1)}, bf16[2,2,64,768]{3,2,1,0:T(8,128)(2,1)S(1)}, u32[]{:S(2)}, u32[]{:S(2)}) collective-permute-start(bf16[2,2,64,768]{3,2,1,0:T(8,128)(2,1)S(1)} %get-tuple-element.265), channel_id=1, source_target_pairs={{0,2},{1,3},{2,0},{3,1},{4,6},{5,7},{6,4},{7,5},{8,10},{9,11},{10,... | collective-permute-start | bytes 1179656 | tf_op jit(solution)/shard_map/ppermute | solution.py:581
  69.7 15.1 %collective-permute-start.11 = (bf16[8,18,16,128]{3,2,1,0:T(8,128)(2,1)S(1)}, bf16[8,18,16,128]{3,2,1,0:T(8,128)(2,1)S(1)}, u32[]{:S(2)}, u32[]{:S(2)}) collective-permute-start(bf16[8,18,16,128]{3,2,1,0:T(8,128)(2,1)S(1)} %get-tuple-element.277), channel_id=1, source_target_pairs={{0,2},{1,3},{2,0},{3,1},{4,6},{5,7},{6,4},{7,5},{8,10},{9,11},{10,... | collective-permute-start | bytes 1769480 | tf_op jit(solution)/shard_map/ppermute | solution.py:581
  69.9 15.0 %collective-permute-start.12 = (bf16[8,18,16,128]{3,2,1,0:T(8,128)(2,1)S(1)}, bf16[8,18,16,128]{3,2,1,0:T(8,128)(2,1)S(1)}, u32[]{:S(2)}, u32[]{:S(2)}) collective-permute-start(bf16[8,18,16,128]{3,2,1,0:T(8,128)(2,1)S(1)} %get-tuple-element.278), channel_id=1, source_target_pairs={{0,4},{1,5},{2,6},{3,7},{4,0},{5,1},{6,2},{7,3},{8,12},{9,13},{10,... | collective-permute-start | bytes 1769480 | tf_op jit(solution)/shard_map/ppermute | solution.py:581
  85.3 12.6 %collective-permute-start.15 = (bf16[16,45,16,128]{3,2,1,0:T(8,128)(2,1)S(1)}, bf16[16,45,16,128]{3,2,1,0:T(8,128)(2,1)S(1)}, u32[]{:S(2)}, u32[]{:S(2)}) collective-permute-start(bf16[16,45,16,128]{3,2,1,0:T(8,128)(2,1)S(1)} %get-tuple-element.299), channel_id=1, source_target_pairs={{0,1},{1,0},{2,3},{3,2},{4,5},{5,4},{6,7},{7,6},{8,9},{9,8},{10,11... | collective-permute-start | bytes 8847368 | tf_op jit(solution)/shard_map/ppermute | solution.py:581
  85.4 12.5 %collective-permute-start.13 = (bf16[4,18,16,128]{3,2,1,0:T(8,128)(2,1)S(1)}, bf16[4,18,16,128]{3,2,1,0:T(8,128)(2,1)S(1)}, u32[]{:S(2)}, u32[]{:S(2)}) collective-permute-start(bf16[4,18,16,128]{3,2,1,0:T(8,128)(2,1)S(1)} %get-tuple-element.296), channel_id=1, source_target_pairs={{0,4},{1,5},{2,6},{3,7},{4,0},{5,1},{6,2},{7,3},{8,12},{9,13},{10,... | collective-permute-start | bytes 884744 | tf_op jit(solution)/shard_map/ppermute | solution.py:581
  87.1 10.8 %collective-permute-start.14 = (bf16[4,18,16,128]{3,2,1,0:T(8,128)(2,1)S(1)}, bf16[4,18,16,128]{3,2,1,0:T(8,128)(2,1)S(1)}, u32[]{:S(2)}, u32[]{:S(2)}) collective-permute-start(bf16[4,18,16,128]{3,2,1,0:T(8,128)(2,1)S(1)} %get-tuple-element.297), channel_id=1, source_target_pairs={{0,2},{1,3},{2,0},{3,1},{4,6},{5,7},{6,4},{7,5},{8,10},{9,11},{10,... | collective-permute-start | bytes 884744 | tf_op jit(solution)/shard_map/ppermute | solution.py:581
  88.7 13.3 %copy-start.40 = (bf16[768,512]{1,0:T(8,128)(2,1)S(1)}, bf16[768,512]{1,0:T(8,128)(2,1)}, u32[]{:S(2)}) copy-start(bf16[768,512]{1,0:T(8,128)(2,1)} %get-tuple-element.303.refs_4_) | copy-start | bytes 2359300
  99.0 22.0 %collective-permute-start.18 = (bf16[2,36,16,128]{3,2,1,0:T(8,128)(2,1)S(1)}, bf16[2,36,16,128]{3,2,1,0:T(8,128)(2,1)S(1)}, u32[]{:S(2)}, u32[]{:S(2)}) collective-permute-start(bf16[2,36,16,128]{3,2,1,0:T(8,128)(2,1)S(1)} %get-tuple-element.329), channel_id=1, source_target_pairs={{0,8},{1,9},{2,10},{3,11},{4,12},{5,13},{6,14},{7,15},{8,0},{9,1},... | collective-permute-start | bytes 884744 | tf_op jit(solution)/shard_map/ppermute | solution.py:581
  100.6 20.4 %collective-permute-start.16 = (bf16[8,18,16,128]{3,2,1,0:T(8,128)(2,1)S(1)}, bf16[8,18,16,128]{3,2,1,0:T(8,128)(2,1)S(1)}, u32[]{:S(2)}, u32[]{:S(2)}) collective-permute-start(bf16[8,18,16,128]{3,2,1,0:T(8,128)(2,1)S(1)} %get-tuple-element.326), channel_id=1, source_target_pairs={{0,2},{1,3},{2,0},{3,1},{4,6},{5,7},{6,4},{7,5},{8,10},{9,11},{10,... | collective-permute-start | bytes 1769480 | tf_op jit(solution)/shard_map/ppermute | solution.py:581
  101.1 20.9 %collective-permute-start.17 = (bf16[8,27,16,128]{3,2,1,0:T(8,128)(2,1)S(1)}, bf16[8,27,16,128]{3,2,1,0:T(8,128)(2,1)S(1)}, u32[]{:S(2)}, u32[]{:S(2)}) collective-permute-start(bf16[8,27,16,128]{3,2,1,0:T(8,128)(2,1)S(1)} %get-tuple-element.327), channel_id=1, source_target_pairs={{0,4},{1,5},{2,6},{3,7},{4,0},{5,1},{6,2},{7,3},{8,12},{9,13},{10,... | collective-permute-start | bytes 2654216 | tf_op jit(solution)/shard_map/ppermute | solution.py:581
  122.5 12.7 %collective-permute-start.22 = (bf16[16,28,16,128]{3,2,1,0:T(8,128)(2,1)S(1)}, bf16[16,28,16,128]{3,2,1,0:T(8,128)(2,1)S(1)}, u32[]{:S(2)}, u32[]{:S(2)}) collective-permute-start(bf16[16,28,16,128]{3,2,1,0:T(8,128)(2,1)S(1)} %get-tuple-element.340), channel_id=1, source_target_pairs={{0,1},{1,0},{2,3},{3,2},{4,5},{5,4},{6,7},{7,6},{8,9},{9,8},{10,11... | collective-permute-start | bytes 5505032 | tf_op jit(solution)/shard_map/ppermute | solution.py:581
  122.5 12.6 %collective-permute-start.20 = (bf16[4,27,16,128]{3,2,1,0:T(8,128)(2,1)S(1)}, bf16[4,27,16,128]{3,2,1,0:T(8,128)(2,1)S(1)}, u32[]{:S(2)}, u32[]{:S(2)}) collective-permute-start(bf16[4,27,16,128]{3,2,1,0:T(8,128)(2,1)S(1)} %get-tuple-element.336), channel_id=1, source_target_pairs={{0,2},{1,3},{2,0},{3,1},{4,6},{5,7},{6,4},{7,5},{8,10},{9,11},{10,... | collective-permute-start | bytes 1327112 | tf_op jit(solution)/shard_map/ppermute | solution.py:581
  124.1 10.1 %collective-permute-start.19 = (bf16[4,18,16,128]{3,2,1,0:T(8,128)(2,1)S(1)}, bf16[4,18,16,128]{3,2,1,0:T(8,128)(2,1)S(1)}, u32[]{:S(2)}, u32[]{:S(2)}) collective-permute-start(bf16[4,18,16,128]{3,2,1,0:T(8,128)(2,1)S(1)} %get-tuple-element.335), channel_id=1, source_target_pairs={{0,4},{1,5},{2,6},{3,7},{4,0},{5,1},{6,2},{7,3},{8,12},{9,13},{10,... | collective-permute-start | bytes 884744 | tf_op jit(solution)/shard_map/ppermute | solution.py:581
  124.6 9.6 %collective-permute-start.21 = (bf16[1,36,16,128]{3,2,1,0:T(8,128)(2,1)S(1)}, bf16[1,36,16,128]{3,2,1,0:T(8,128)(2,1)S(1)}, u32[]{:S(2)}, u32[]{:S(2)}) collective-permute-start(bf16[1,36,16,128]{3,2,1,0:T(8,128)(2,1)S(1)} %get-tuple-element.338), channel_id=1, source_target_pairs={{0,16},{1,17},{2,18},{3,19},{4,20},{5,21},{6,22},{7,23},{8,24},{9,... | collective-permute-start | bytes 442376 | tf_op jit(solution)/shard_map/ppermute | solution.py:581
  135.9 14.8 %collective-permute-start.26 = (bf16[8,16,16,128]{3,2,1,0:T(8,128)(2,1)S(1)}, bf16[8,16,16,128]{3,2,1,0:T(8,128)(2,1)S(1)}, u32[]{:S(2)}, u32[]{:S(2)}) collective-permute-start(bf16[8,16,16,128]{3,2,1,0:T(8,128)(2,1)S(1)} %get-tuple-element.348), channel_id=1, source_target_pairs={{0,4},{1,5},{2,6},{3,7},{4,0},{5,1},{6,2},{7,3},{8,12},{9,13},{10,... | collective-permute-start | bytes 1572872 | tf_op jit(solution)/shard_map/ppermute | solution.py:581
  136.5 14.2 %collective-permute-start.25 = (bf16[8,12,16,128]{3,2,1,0:T(8,128)(2,1)S(1)}, bf16[8,12,16,128]{3,2,1,0:T(8,128)(2,1)S(1)}, u32[]{:S(2)}, u32[]{:S(2)}) collective-permute-start(bf16[8,12,16,128]{3,2,1,0:T(8,128)(2,1)S(1)} %get-tuple-element.347), channel_id=1, source_target_pairs={{0,2},{1,3},{2,0},{3,1},{4,6},{5,7},{6,4},{7,5},{8,10},{9,11},{10,... | collective-permute-start | bytes 1179656 | tf_op jit(solution)/shard_map/ppermute | solution.py:581
  137.9 12.8 %collective-permute-start.23 = (bf16[2,45,16,128]{3,2,1,0:T(8,128)(2,1)S(1)}, bf16[2,45,16,128]{3,2,1,0:T(8,128)(2,1)S(1)}, u32[]{:S(2)}, u32[]{:S(2)}) collective-permute-start(bf16[2,45,16,128]{3,2,1,0:T(8,128)(2,1)S(1)} %get-tuple-element.343), channel_id=1, source_target_pairs={{0,8},{1,9},{2,10},{3,11},{4,12},{5,13},{6,14},{7,15},{8,0},{9,1},... | collective-permute-start | bytes 1105928 | tf_op jit(solution)/shard_map/ppermute | solution.py:581
  138.4 10.3 %collective-permute-start.24 = (bf16[1,36,16,128]{3,2,1,0:T(8,128)(2,1)S(1)}, bf16[1,36,16,128]{3,2,1,0:T(8,128)(2,1)S(1)}, u32[]{:S(2)}, u32[]{:S(2)}) collective-permute-start(bf16[1,36,16,128]{3,2,1,0:T(8,128)(2,1)S(1)} %get-tuple-element.344.refs_3_), channel_id=1, source_target_pairs={{0,16},{1,17},{2,18},{3,19},{4,20},{5,21},{6,22},{7,23},{8,24},{9,... | collective-permute-start | bytes 442376 | tf_op jit(solution)/shard_map/ppermute | solution.py:581
  151.0 15.6 %collective-permute-start.27 = (bf16[2,128,768]{2,1,0:T(8,128)(2,1)S(1)}, bf16[2,128,768]{2,1,0:T(8,128)(2,1)S(1)}, u32[]{:S(2)}, u32[]{:S(2)}) collective-permute-start(bf16[2,128,768]{2,1,0:T(8,128)(2,1)S(1)} %get-tuple-element.352), channel_id=1, source_target_pairs={{0,2},{1,3},{2,0},{3,1},{4,6},{5,7},{6,4},{7,5},{8,10},{9,11},{10,... | collective-permute-start | bytes 1179656 | tf_op jit(solution)/shard_map/ppermute | solution.py:581
  152.1 14.5 %collective-permute-start.29 = (bf16[2,36,16,128]{3,2,1,0:T(8,128)(2,1)S(1)}, bf16[2,36,16,128]{3,2,1,0:T(8,128)(2,1)S(1)}, u32[]{:S(2)}, u32[]{:S(2)}) collective-permute-start(bf16[2,36,16,128]{3,2,1,0:T(8,128)(2,1)S(1)} %get-tuple-element.355.refs_4_), channel_id=1, source_target_pairs={{0,8},{1,9},{2,10},{3,11},{4,12},{5,13},{6,14},{7,15},{8,0},{9,1},... | collective-permute-start | bytes 884744 | tf_op jit(solution)/shard_map/ppermute | solution.py:581
  154.2 12.4 %collective-permute-start.31 = (bf16[4,16,16,128]{3,2,1,0:T(8,128)(2,1)S(1)}, bf16[4,16,16,128]{3,2,1,0:T(8,128)(2,1)S(1)}, u32[]{:S(2)}, u32[]{:S(2)}) collective-permute-start(bf16[4,16,16,128]{3,2,1,0:T(8,128)(2,1)S(1)} %get-tuple-element.359), channel_id=1, source_target_pairs={{0,2},{1,3},{2,0},{3,1},{4,6},{5,7},{6,4},{7,5},{8,10},{9,11},{10,... | collective-permute-start | bytes 786440 | tf_op jit(solution)/shard_map/ppermute | solution.py:581
  155.7 10.2 %collective-permute-start.30 = (bf16[4,12,16,128]{3,2,1,0:T(8,128)(2,1)S(1)}, bf16[4,12,16,128]{3,2,1,0:T(8,128)(2,1)S(1)}, u32[]{:S(2)}, u32[]{:S(2)}) collective-permute-start(bf16[4,12,16,128]{3,2,1,0:T(8,128)(2,1)S(1)} %get-tuple-element.358), channel_id=1, source_target_pairs={{0,4},{1,5},{2,6},{3,7},{4,0},{5,1},{6,2},{7,3},{8,12},{9,13},{10,... | collective-permute-start | bytes 589832 | tf_op jit(solution)/shard_map/ppermute | solution.py:581
  157.3 8.6 %collective-permute-start.28 = (bf16[1,45,16,128]{3,2,1,0:T(8,128)(2,1)S(1)}, bf16[1,45,16,128]{3,2,1,0:T(8,128)(2,1)S(1)}, u32[]{:S(2)}, u32[]{:S(2)}) collective-permute-start(bf16[1,45,16,128]{3,2,1,0:T(8,128)(2,1)S(1)} %get-tuple-element.354), channel_id=1, source_target_pairs={{0,16},{1,17},{2,18},{3,19},{4,20},{5,21},{6,22},{7,23},{8,24},{9,... | collective-permute-start | bytes 552968 | tf_op jit(solution)/shard_map/ppermute | solution.py:581
  166.6 18.1 %copy-start.27 = (bf16[2,2,64,768]{3,2,1,0:T(8,128)(2,1)S(1)}, bf16[2,2,64,768]{3,2,1,0:T(8,128)(2,1)}, u32[]{:S(2)}) copy-start(bf16[2,2,64,768]{3,2,1,0:T(8,128)(2,1)} %copy-done.26) | copy-start | bytes 1179652
  167.0 15.4 %collective-permute-start.32 = (bf16[2,128,768]{2,1,0:T(8,128)(2,1)S(1)}, bf16[2,128,768]{2,1,0:T(8,128)(2,1)S(1)}, u32[]{:S(2)}, u32[]{:S(2)}) collective-permute-start(bf16[2,128,768]{2,1,0:T(8,128)(2,1)S(1)} %get-tuple-element.363), channel_id=1, source_target_pairs={{0,2},{1,3},{2,0},{3,1},{4,6},{5,7},{6,4},{7,5},{8,10},{9,11},{10,... | collective-permute-start | bytes 1179656 | tf_op jit(solution)/shard_map/ppermute | solution.py:581
  168.2 12.4 %collective-permute-start.34 = (bf16[4,18,16,128]{3,2,1,0:T(8,128)(2,1)S(1)}, bf16[4,18,16,128]{3,2,1,0:T(8,128)(2,1)S(1)}, u32[]{:S(2)}, u32[]{:S(2)}) collective-permute-start(bf16[4,18,16,128]{3,2,1,0:T(8,128)(2,1)S(1)} %get-tuple-element.365.refs_4_), channel_id=1, source_target_pairs={{0,4},{1,5},{2,6},{3,7},{4,0},{5,1},{6,2},{7,3},{8,12},{9,13},{10,... | collective-permute-start | bytes 884744 | tf_op jit(solution)/shard_map/ppermute | solution.py:581
  169.1 13.3 %collective-permute-start.35 = (bf16[4,18,16,128]{3,2,1,0:T(8,128)(2,1)S(1)}, bf16[4,18,16,128]{3,2,1,0:T(8,128)(2,1)S(1)}, u32[]{:S(2)}, u32[]{:S(2)}) collective-permute-start(bf16[4,18,16,128]{3,2,1,0:T(8,128)(2,1)S(1)} %get-tuple-element.366.refs_5_), channel_id=1, source_target_pairs={{0,2},{1,3},{2,0},{3,1},{4,6},{5,7},{6,4},{7,5},{8,10},{9,11},{10,... | collective-permute-start | bytes 884744 | tf_op jit(solution)/shard_map/ppermute | solution.py:581
  170.6 10.1 %collective-permute-start.36 = (bf16[2,28,16,128]{3,2,1,0:T(8,128)(2,1)S(1)}, bf16[2,28,16,128]{3,2,1,0:T(8,128)(2,1)S(1)}, u32[]{:S(2)}, u32[]{:S(2)}) collective-permute-start(bf16[2,28,16,128]{3,2,1,0:T(8,128)(2,1)S(1)} %get-tuple-element.368), channel_id=1, source_target_pairs={{0,8},{1,9},{2,10},{3,11},{4,12},{5,13},{6,14},{7,15},{8,0},{9,1},... | collective-permute-start | bytes 688136 | tf_op jit(solution)/shard_map/ppermute | solution.py:581
  172.3 8.4 %collective-permute-start.33 = (bf16[1,45,16,128]{3,2,1,0:T(8,128)(2,1)S(1)}, bf16[1,45,16,128]{3,2,1,0:T(8,128)(2,1)S(1)}, u32[]{:S(2)}, u32[]{:S(2)}) collective-permute-start(bf16[1,45,16,128]{3,2,1,0:T(8,128)(2,1)S(1)} %get-tuple-element.364.refs_2_), channel_id=1, source_target_pairs={{0,16},{1,17},{2,18},{3,19},{4,20},{5,21},{6,22},{7,23},{8,24},{9,... | collective-permute-start | bytes 552968 | tf_op jit(solution)/shard_map/ppermute | solution.py:581
  182.6 15.6 %collective-permute-start.40 = (bf16[8,18,16,128]{3,2,1,0:T(8,128)(2,1)S(1)}, bf16[8,18,16,128]{3,2,1,0:T(8,128)(2,1)S(1)}, u32[]{:S(2)}, u32[]{:S(2)}) collective-permute-start(bf16[8,18,16,128]{3,2,1,0:T(8,128)(2,1)S(1)} %get-tuple-element.379.refs_5_), channel_id=1, source_target_pairs={{0,2},{1,3},{2,0},{3,1},{4,6},{5,7},{6,4},{7,5},{8,10},{9,11},{10,... | collective-permute-start | bytes 1769480 | tf_op jit(solution)/shard_map/ppermute | solution.py:581
  183.9 14.3 %collective-permute-start.41 = (bf16[8,18,16,128]{3,2,1,0:T(8,128)(2,1)S(1)}, bf16[8,18,16,128]{3,2,1,0:T(8,128)(2,1)S(1)}, u32[]{:S(2)}, u32[]{:S(2)}) collective-permute-start(bf16[8,18,16,128]{3,2,1,0:T(8,128)(2,1)S(1)} %get-tuple-element.380.refs_6_), channel_id=1, source_target_pairs={{0,4},{1,5},{2,6},{3,7},{4,0},{5,1},{6,2},{7,3},{8,12},{9,13},{10,... | collective-permute-start | bytes 1769480 | tf_op jit(solution)/shard_map/ppermute | solution.py:581
  184.7 2.4 collective-permute-start.37
  184.8 13.5 %collective-permute-start.38 = (bf16[2,45,16,128]{3,2,1,0:T(8,128)(2,1)S(1)}, bf16[2,45,16,128]{3,2,1,0:T(8,128)(2,1)S(1)}, u32[]{:S(2)}, u32[]{:S(2)}) collective-permute-start(bf16[2,45,16,128]{3,2,1,0:T(8,128)(2,1)S(1)} %get-tuple-element.376.refs_1_), channel_id=1, source_target_pairs={{0,8},{1,9},{2,10},{3,11},{4,12},{5,13},{6,14},{7,15},{8,0},{9,1},... | collective-permute-start | bytes 1105928 | tf_op jit(solution)/shard_map/ppermute | solution.py:581
  186.3 11.0 %collective-permute-start.39 = (bf16[1,28,16,128]{3,2,1,0:T(8,128)(2,1)S(1)}, bf16[1,28,16,128]{3,2,1,0:T(8,128)(2,1)S(1)}, u32[]{:S(2)}, u32[]{:S(2)}) collective-permute-start(bf16[1,28,16,128]{3,2,1,0:T(8,128)(2,1)S(1)} %get-tuple-element.378), channel_id=1, source_target_pairs={{0,16},{1,17},{2,18},{3,19},{4,20},{5,21},{6,22},{7,23},{8,24},{9,... | collective-permute-start | bytes 344072 | tf_op jit(solution)/shard_map/ppermute | solution.py:581
  198.4 16.1 %collective-permute-start.45 = (bf16[16,36,16,128]{3,2,1,0:T(8,128)(2,1)S(1)}, bf16[16,36,16,128]{3,2,1,0:T(8,128)(2,1)S(1)}, u32[]{:S(2)}, u32[]{:S(2)}) collective-permute-start(bf16[16,36,16,128]{3,2,1,0:T(8,128)(2,1)S(1)} %get-tuple-element.386.refs_2_), channel_id=1, source_target_pairs={{0,1},{1,0},{2,3},{3,2},{4,5},{5,4},{6,7},{7,6},{8,9},{9,8},{10,11... | collective-permute-start | bytes 7077896 | tf_op jit(solution)/shard_map/ppermute | solution.py:581
  198.5 12.6 %collective-permute-start.43 = (bf16[4,27,16,128]{3,2,1,0:T(8,128)(2,1)S(1)}, bf16[4,27,16,128]{3,2,1,0:T(8,128)(2,1)S(1)}, u32[]{:S(2)}, u32[]{:S(2)}) collective-permute-start(bf16[4,27,16,128]{3,2,1,0:T(8,128)(2,1)S(1)} %get-tuple-element.383.refs_2_), channel_id=1, source_target_pairs={{0,2},{1,3},{2,0},{3,1},{4,6},{5,7},{6,4},{7,5},{8,10},{9,11},{10,... | collective-permute-start | bytes 1327112 | tf_op jit(solution)/shard_map/ppermute | solution.py:581
  200.1 9.1 %collective-permute-start.42 = (bf16[4,18,16,128]{3,2,1,0:T(8,128)(2,1)S(1)}, bf16[4,18,16,128]{3,2,1,0:T(8,128)(2,1)S(1)}, u32[]{:S(2)}, u32[]{:S(2)}) collective-permute-start(bf16[4,18,16,128]{3,2,1,0:T(8,128)(2,1)S(1)} %get-tuple-element.382.refs_1_), channel_id=1, source_target_pairs={{0,4},{1,5},{2,6},{3,7},{4,0},{5,1},{6,2},{7,3},{8,12},{9,13},{10,... | collective-permute-start | bytes 884744 | tf_op jit(solution)/shard_map/ppermute | solution.py:581
  200.6 8.3 %collective-permute-start.44 = (bf16[1,28,16,128]{3,2,1,0:T(8,128)(2,1)S(1)}, bf16[1,28,16,128]{3,2,1,0:T(8,128)(2,1)S(1)}, u32[]{:S(2)}, u32[]{:S(2)}) collective-permute-start(bf16[1,28,16,128]{3,2,1,0:T(8,128)(2,1)S(1)} %get-tuple-element.384.refs_5_), channel_id=1, source_target_pairs={{0,16},{1,17},{2,18},{3,19},{4,20},{5,21},{6,22},{7,23},{8,24},{9,... | collective-permute-start | bytes 344072 | tf_op jit(solution)/shard_map/ppermute | solution.py:581
  211.2 25.6 %collective-permute-start.51 = (bf16[8,27,16,128]{3,2,1,0:T(8,128)(2,1)S(1)}, bf16[8,27,16,128]{3,2,1,0:T(8,128)(2,1)S(1)}, u32[]{:S(2)}, u32[]{:S(2)}) collective-permute-start(bf16[8,27,16,128]{3,2,1,0:T(8,128)(2,1)S(1)} %get-tuple-element.398.refs_2_), channel_id=1, source_target_pairs={{0,4},{1,5},{2,6},{3,7},{4,0},{5,1},{6,2},{7,3},{8,12},{9,13},{10,... | collective-permute-start | bytes 2654216 | tf_op jit(solution)/shard_map/ppermute | solution.py:581
  212.5 10.7 %collective-permute-start.47 = (bf16[2,2,128,768]{3,2,1,0:T(8,128)(2,1)S(1)}, bf16[2,2,128,768]{3,2,1,0:T(8,128)(2,1)S(1)}, u32[]{:S(2)}, u32[]{:S(2)}) collective-permute-start(bf16[2,2,128,768]{3,2,1,0:T(8,128)(2,1)S(1)} %get-tuple-element.391), channel_id=1, source_target_pairs={{0,1},{1,0},{2,3},{3,2},{4,5},{5,4},{6,7},{7,6},{8,9},{9,8},{10,11... | collective-permute-start | bytes 2359304 | tf_op jit(solution)/shard_map/ppermute | solution.py:581
  212.5 24.3 %collective-permute-start.50 = (bf16[8,18,16,128]{3,2,1,0:T(8,128)(2,1)S(1)}, bf16[8,18,16,128]{3,2,1,0:T(8,128)(2,1)S(1)}, u32[]{:S(2)}, u32[]{:S(2)}) collective-permute-start(bf16[8,18,16,128]{3,2,1,0:T(8,128)(2,1)S(1)} %get-tuple-element.397.refs_1_), channel_id=1, source_target_pairs={{0,2},{1,3},{2,0},{3,1},{4,6},{5,7},{6,4},{7,5},{8,10},{9,11},{10,... | collective-permute-start | bytes 1769480 | tf_op jit(solution)/shard_map/ppermute | solution.py:581
  213.3 7.7 %collective-permute-start.46 = (bf16[2,28,16,128]{3,2,1,0:T(8,128)(2,1)S(1)}, bf16[2,28,16,128]{3,2,1,0:T(8,128)(2,1)S(1)}, u32[]{:S(2)}, u32[]{:S(2)}) collective-permute-start(bf16[2,28,16,128]{3,2,1,0:T(8,128)(2,1)S(1)} %get-tuple-element.388.refs_1_), channel_id=1, source_target_pairs={{0,8},{1,9},{2,10},{3,11},{4,12},{5,13},{6,14},{7,15},{8,0},{9,1},... | collective-permute-start | bytes 688136 | tf_op jit(solution)/shard_map/ppermute | solution.py:581
  221.1 15.7 %collective-permute-start.49 = (bf16[4,16,16,128]{3,2,1,0:T(8,128)(2,1)S(1)}, bf16[4,16,16,128]{3,2,1,0:T(8,128)(2,1)S(1)}, u32[]{:S(2)}, u32[]{:S(2)}) collective-permute-start(bf16[4,16,16,128]{3,2,1,0:T(8,128)(2,1)S(1)} %get-tuple-element.395.refs_2_), channel_id=1, source_target_pairs={{0,2},{1,3},{2,0},{3,1},{4,6},{5,7},{6,4},{7,5},{8,10},{9,11},{10,... | collective-permute-start | bytes 786440 | tf_op jit(solution)/shard_map/ppermute | solution.py:581
  222.4 14.3 %collective-permute-start.48 = (bf16[4,12,16,128]{3,2,1,0:T(8,128)(2,1)S(1)}, bf16[4,12,16,128]{3,2,1,0:T(8,128)(2,1)S(1)}, u32[]{:S(2)}, u32[]{:S(2)}) collective-permute-start(bf16[4,12,16,128]{3,2,1,0:T(8,128)(2,1)S(1)} %get-tuple-element.394.refs_1_), channel_id=1, source_target_pairs={{0,4},{1,5},{2,6},{3,7},{4,0},{5,1},{6,2},{7,3},{8,12},{9,13},{10,... | collective-permute-start | bytes 589832 | tf_op jit(solution)/shard_map/ppermute | solution.py:581
  237.0 5.4 %collective-permute-start.52 = (bf16[16,45,16,128]{3,2,1,0:T(8,128)(2,1)S(1)}, bf16[16,45,16,128]{3,2,1,0:T(8,128)(2,1)S(1)}, u32[]{:S(2)}, u32[]{:S(2)}) collective-permute-start(bf16[16,45,16,128]{3,2,1,0:T(8,128)(2,1)S(1)} %get-tuple-element.400.refs_2_), channel_id=1, source_target_pairs={{0,1},{1,0},{2,3},{3,2},{4,5},{5,4},{6,7},{7,6},{8,9},{9,8},{10,11... | collective-permute-start | bytes 8847368 | tf_op jit(solution)/shard_map/ppermute | solution.py:581
  237.1 14.3 %collective-permute-start.54 = (bf16[8,16,16,128]{3,2,1,0:T(8,128)(2,1)S(1)}, bf16[8,16,16,128]{3,2,1,0:T(8,128)(2,1)S(1)}, u32[]{:S(2)}, u32[]{:S(2)}) collective-permute-start(bf16[8,16,16,128]{3,2,1,0:T(8,128)(2,1)S(1)} %get-tuple-element.403.refs_2_), channel_id=1, source_target_pairs={{0,4},{1,5},{2,6},{3,7},{4,0},{5,1},{6,2},{7,3},{8,12},{9,13},{10,... | collective-permute-start | bytes 1572872 | tf_op jit(solution)/shard_map/ppermute | solution.py:581
  238.4 11.4 %collective-permute-start.53 = (bf16[8,12,16,128]{3,2,1,0:T(8,128)(2,1)S(1)}, bf16[8,12,16,128]{3,2,1,0:T(8,128)(2,1)S(1)}, u32[]{:S(2)}, u32[]{:S(2)}) collective-permute-start(bf16[8,12,16,128]{3,2,1,0:T(8,128)(2,1)S(1)} %get-tuple-element.402.refs_1_), channel_id=1, source_target_pairs={{0,2},{1,3},{2,0},{3,1},{4,6},{5,7},{6,4},{7,5},{8,10},{9,11},{10,... | collective-permute-start | bytes 1179656 | tf_op jit(solution)/shard_map/ppermute | solution.py:581
  251.5 3.9 %collective-permute-start.55 = (bf16[16,28,16,128]{3,2,1,0:T(8,128)(2,1)S(1)}, bf16[16,28,16,128]{3,2,1,0:T(8,128)(2,1)S(1)}, u32[]{:S(2)}, u32[]{:S(2)}) collective-permute-start(bf16[16,28,16,128]{3,2,1,0:T(8,128)(2,1)S(1)} %get-tuple-element.405.refs_2_), channel_id=1, source_target_pairs={{0,1},{1,0},{2,3},{3,2},{4,5},{5,4},{6,7},{7,6},{8,9},{9,8},{10,11... | collective-permute-start | bytes 5505032 | tf_op jit(solution)/shard_map/ppermute | solution.py:581
  (55 other events, 313.9 us)

commit v4 on v3

--- a/solution.py
+++ b/solution.py
@@ -16,7 +16,7 @@
 ANY = pl.BlockSpec(memory_space=pl.ANY)
 HBM = pl.BlockSpec(memory_space=pltpu.HBM)
 BLK = 16
-NA = 12
+NA = 18
 CH = 512
 
 
@@ -124,9 +124,10 @@
 
 
 def tables_kernel(count, scalars, lengths, *refs):
-    lines, (near_q, far_q, kst, kf_out, vecs) = refs[:10], refs[count:]
-    for i, line in enumerate(lines):
-        vecs[i : i + 1, :] = line[...].reshape(1, 768)
+    lines, (near_q, far_q, kst, kf_out, vecs), near = refs[:10], refs[count : count + 5], refs[count + 5 : count + 15]
+    copies = [pltpu.make_async_copy(a, b, refs[-1].at[i]) for i, (a, b) in enumerate(zip(lines, near))]
+    for copy in copies:
+        copy.start()
     j = scalars[0]
     exponent = -math.log(10000.0) / 32
 
@@ -156,12 +157,16 @@
         bias = jnp.where(place < lengths[scalars[1] + r], 0.0, -1.0e9)
         kf_out[r, 0] = jnp.where(lane < 64, kf, jnp.where(lane == 64, bias, 0.0)).astype(BF)
         kf_out[r, 1] = jnp.where(lane >= 64, kf, jnp.where(lane == 0, bias, 0.0)).astype(BF)
+    for i, copy in enumerate(copies):
+        copy.wait()
+        vecs[i : i + 1, :] = near[i][...].reshape(1, 768)
 
 
 def tables(scalars, lengths, lines, weights, after):
     outs = (f32(256, 256), f32(128, 256), b16(128, 512), b16(2, 2, 512, 128), f32(10, 768))
     kernel = functools.partial(tables_kernel, 10 + len(weights))
-    return call(kernel, "tables", (scalars, lengths), (*lines, *weights), outs, after=after, free=range(10))
+    scratch = [vs(768) for _ in range(10)] + [sems(10)]
+    return call(kernel, "tables", (scalars, lengths), (*lines, *weights), outs, scratch, after, far_args=range(10))
 
 
 def spread_heads(weight, high, low, sides):
@@ -256,7 +261,7 @@
             lse_out[i * 2 + s] = highest + jnp.log(total)
         return carry
 
-    lax.fori_loop(0, 6, one_pair, 0)
+    lax.fori_loop(0, 6, one_pair, 0, unroll=2)
     ctx_out[...] = ctxt_out[...].T
     for copy in copies:
         copy.wait()
@@ -330,7 +335,7 @@
         acc_s[...] += nn(act, wd[at, :])
         return carry
 
-    lax.fori_loop(0, 6, up_chunk, 0)
+    lax.fori_loop(0, 6, up_chunk, 0, unroll=2)
     n2, rs2 = layer_stats(acc_s[...])
     result = (n2 * og + osh).astype(BF)
     for d, out in enumerate((out0, out1, out23.at[0], out23.at[1])):
@@ -357,7 +362,7 @@
         return carry
 
     for which in range(2):
-        lax.fori_loop(0, 3, functools.partial(down_chunk, which), 0)
+        lax.fori_loop(0, 3, functools.partial(down_chunk, which), 0, unroll=3)
 
 
 def ffn_down(masks, args, after=()):
@@ -391,7 +396,7 @@
                 (near, far)[r // 16][r % 16, slab + j] = u_s[pl.ds(row + 16 * j, 16), col].astype(BF)
         return carry
 
-    lax.fori_loop(0, 3, up_chunk, 0)
+    lax.fori_loop(0, 3, up_chunk, 0, unroll=3)
 
 
 def ffn_up_a_kernel(masks, df_in, d2, gp, x1t, wu, wd, acc, near, far, upb_out, u_s):
@@ -479,7 +484,7 @@
         dk_out[:, at] = (dk_first + dk_part).astype(BF)
         return carry
 
-    lax.fori_loop(0, 6, one_pair, 0)
+    lax.fori_loop(0, 6, one_pair, 0, unroll=2)
     ones = jnp.ones((8, 256), BF)
     for g in range(3):
         at = slice(256 * g, 256 * g + 256)

time: 266 us -> 258 us (0.970)
  Pallas kernels: 113 us -> 105 us
  waiting for transfers between devices: 79.9 us -> 87.4 us
  local copies, waits for them, and re-layouts: 9.05 us -> 2.19 us
    pallas_call x37, Pallas kernels: 101 us -> 92.4 us  [call(): pl.pallas_call(body, out_shape=tuple((place(i, o) for i, o in enumerate(o...]
    ppermute x56, waiting for transfers between devices: 79.9 us -> 87.4 us  [partner(): return lax.ppermute(x, 'batch', [(i, i ^ bit) for i in range(size)])]
    unnamed x126 -> x106, local copies, waits for them, and re-layouts: 7.76 us -> 0.89 us
  transfers between devices with their start and end apart: 56 -> 56, of which waited for: 21 -> 25; matrix products, arithmetic and copies ran while one was open for 0% -> 0% of each run, Pallas kernels for 33% -> 32%
where the time goes in v4:
time: 258 us; the launch traced here: 254 us
  Pallas kernels  105 us (41%)
  waiting for transfers between devices  87.4 us (34%)
  starting transfers between devices  57.3 us (22%)
    pallas_call x37, Pallas kernels, call(): pl.pallas_call(body, out_shape=tuple((place(i, o) for i, o in enumerate(o...  92.4 us
    ppermute x56, waiting for transfers between devices, partner(): return lax.ppermute(x, 'batch', [(i, i ^ bit) for i in range(size)])  87.4 us
    ppermute x56, starting transfers between devices, partner(): return lax.ppermute(x, 'batch', [(i, i ^ bit) for i in range(size)])  57.3 us
    pallas_call x2, Pallas kernels, call_grid(): pl.pallas_call(body, out_shape=(*outs, pltpu.VMEM(TOKEN, F32)), grid=(ste...  12.2 us
  transfers between devices with their start and end apart: 56, of which 25 were waited for; matrix products, arithmetic and copies ran while one was open for 0% of the time, Pallas kernels for 32%

profile of v4, /device:TPU:0, one launch (start us, length us, event | category | flops | bytes accessed | tf_op | source)
XLA Modules:
  0.0 253.6 jit_solution(15026091664242180717)
XLA Ops:
  0.8 1.8 pick.3
  3.2 2.6 %collective-permute-start.1 = (bf16[128,768]{1,0:T(8,128)(2,1)S(1)}, bf16[128,768]{1,0:T(8,128)(2,1)S(1)}, u32[]{:S(2)}, u32[]{:S(2)}) collective-permute-start(bf16[128,768]{1,0:T(8,128)(2,1)S(1)} %get-tuple-element.222), channel_id=1, source_target_pairs={{0,2},{1,3},{2,0},{3,1},{4,6},{5,7},{6,4},{7,5},{8,10},{9,11},{10,... | collective-permute-start | bytes 589832 | tf_op jit(solution)/shard_map/ppermute | solution.py:586
  6.5 3.0 %tables.1 = (f32[256,256]{1,0:T(8,128)S(1)}, f32[128,256]{1,0:T(8,128)S(1)}, bf16[128,512]{1,0:T(8,128)(2,1)S(1)}, bf16[2,2,512,128]{3,2,1,0:T(8,128)(2,1)S(1)},...) custom-call(f32[8,128]{1,0:T(8,128)S(1)} %get-tuple-element.217.refs_0_, s32[4]{0:T(128)S(1)} %pad_add_fusion.refs_0_.refs_1_, ...), custom_call_target="tpu_custom_call" | custom-call | tf_op jit(solution)/shard_map/tables/pallas_call | solution.py:79
  9.5 1.8 pick.4
  11.3 1.8 pick.5
  13.1 2.1 collective-permute-done.2.refs_3_.refs_4_
  15.3 1.7 collective-permute-start.4
  17.1 8.8 %attn_fwd.2 = (bf16[512,768]{1,0:T(8,128)(2,1)}, bf16[512,768]{1,0:T(8,128)(2,1)}, bf16[768,512]{1,0:T(8,128)(2,1)}, bf16[768,512]{1,0:T(8,128)(2,1)}, bf16[256,...) custom-call(f32[8,128]{1,0:T(8,128)S(1)} %get-tuple-element.228.refs, ...), custom_call_target="tpu_custom_call" | custom-call | flops 4000000000 | bytes 12000000 | tf_op jit(solution)/shard_map/attn_fwd/pallas_call | solution.py:79
  26.5 1.6 collective-permute-start.7
  28.2 8.5 %attn_fwd.3 = (bf16[512,768]{1,0:T(8,128)(2,1)}, bf16[512,768]{1,0:T(8,128)(2,1)}, bf16[768,512]{1,0:T(8,128)(2,1)}, bf16[768,512]{1,0:T(8,128)(2,1)}, bf16[256,...) custom-call(f32[8,128]{1,0:T(8,128)S(1)} %get-tuple-element.241.refs, ...), custom_call_target="tpu_custom_call" | custom-call | flops 4000000000 | bytes 12000000 | tf_op jit(solution)/shard_map/attn_fwd/pallas_call | solution.py:79
  36.9 14.6 %ffn_down.1 = (bf16[2,64,768]{2,1,0:T(8,128)(2,1)S(1)}, bf16[2,64,768]{2,1,0:T(8,128)(2,1)S(1)}, bf16[2,2,64,768]{3,2,1,0:T(8,128)(2,1)S(1)}, f32[512,768]{1,0:T...) custom-call(f32[8,128]{1,0:T(8,128)S(1)} %get-tuple-element.243.refs, ...), custom_call_target="tpu_custom_call" | custom-call | flops 8000000000 | bytes 25000000 | tf_op jit(solution)/shard_map/ffn_down/pallas_call | solution.py:79
  52.2 1.5 collective-permute-start.10
  53.8 5.4 %ffn_up_a.1 = (f32[512,768]{1,0:T(8,128)S(1)}, bf16[16,45,16,128]{3,2,1,0:T(8,128)(2,1)S(1)}, bf16[16,45,16,128]{3,2,1,0:T(8,128)(2,1)S(1)}, f32[1,1536]{1,0:T(1,128)S(1)}, f32[8,128]{1,0:T(8,128)S(1)}) custom-call(f32[8,128]{1,0:T(8,128)S(1)} %get-tuple-element.255.refs_0_, s32[4]{0:T(128)S(1)} %pad_add_fusion.refs_0_.refs_1_, ...), custom_call_target="tpu_custom_call" | custom-call | flops 4000000000 | bytes 12000000 | tf_op jit(solution)/shard_map/ffn_up_a/pallas_call | solution.py:79
  60.5 1.6 collective-permute-start.12
  62.1 2.2 collective-permute-done.10.refs_2_.refs_3_
  64.2 7.5 %ffn_up_b.1 = (f32[512,768]{1,0:T(8,128)S(1)}, bf16[2,256,768]{2,1,0:T(8,128)(2,1)S(1)}, bf16[16,45,16,128]{3,2,1,0:T(8,128)(2,1)S(1)}, bf16[16,45,16,128]{3,2,1...) custom-call(f32[8,128]{1,0:T(8,128)S(1)} %get-tuple-element.266.refs, ...), custom_call_target="tpu_custom_call", output_to_operand_aliasing={{2}: (14, {}), {3}: (15, {})} | custom-call | flops 5000000000 | bytes 14000000 | tf_op jit(solution)/shard_map/ffn_up_b/pallas_call | solution.py:79
  71.8 4.2 %collective-permute-done.11.refs_3_ = bf16[8,18,16,128]{3,2,1,0:T(8,128)(2,1)S(1)} collective-permute-done((bf16[8,18,16,128]{3,2,1,0:T(8,128)(2,1)S(1)}, bf16[8,18,16,128]{3,2,1,0:T(8,128)(2,1)S(1)}, u32[]{:S(2)}, u32[]{:S(2)}) %collective-permute-start.11) | collective-permute-done | bytes 589856 | tf_op jit(solution)/shard_map/ppermute | solution.py:586
  76.5 1.6 collective-permute-start.13
  78.1 1.5 collective-permute-start.14
  79.8 8.4 %attn_bwd.1 = (bf16[512,768]{1,0:T(8,128)(2,1)S(1)}, bf16[512,768]{1,0:T(8,128)(2,1)S(1)}, bf16[256,768]{1,0:T(8,128)(2,1)S(1)}, f32[384,128]{1,0:T(8,128)S(1)},...) custom-call(f32[8,128]{1,0:T(8,128)S(1)} %get-tuple-element.281.refs_0_, bf16[512,768]{1,0:T(8,128)(2,1)S(1)} %copy-done.32, ...), custom_call_target="tpu_custom_call" | custom-call | flops 8000000000 | bytes 12000000 | tf_op jit(solution)/shard_map/attn_bwd/pallas_call | solution.py:79
  89.2 1.6 collective-permute-start.18
  91.4 0.9 collective-permute-start.17
  92.4 17.9 %last_back.1 = (bf16[16,28,16,128]{3,2,1,0:T(8,128)(2,1)S(1)}, bf16[16,28,16,128]{3,2,1,0:T(8,128)(2,1)S(1)}, bf16[2,128,768]{2,1,0:T(8,128)(2,1)S(1)}, bf16[2,1...) custom-call(f32[8,128]{1,0:T(8,128)S(1)} %get-tuple-element.300.refs, ...), custom_call_target="tpu_custom_call" | custom-call | flops 16999999488 | bytes 30000000 | tf_op jit(solution)/shard_map/last_back/pallas_call | solution.py:79
  110.3 1.9 collective-permute-done.17.refs_4_
  112.8 1.6 collective-permute-start.20
  114.8 2.6 %collective-permute-start.21 = (bf16[1,36,16,128]{3,2,1,0:T(8,128)(2,1)S(1)}, bf16[1,36,16,128]{3,2,1,0:T(8,128)(2,1)S(1)}, u32[]{:S(2)}, u32[]{:S(2)}) collective-permute-start(bf16[1,36,16,128]{3,2,1,0:T(8,128)(2,1)S(1)} %get-tuple-element.338), channel_id=1, source_target_pairs={{0,16},{1,17},{2,18},{3,19},{4,20},{5,21},{6,22},{7,23},{8,24},{9,... | collective-permute-start | bytes 442376 | tf_op jit(solution)/shard_map/ppermute | solution.py:586
  117.4 7.0 %collective-permute-done.21.refs_6_ = bf16[1,36,16,128]{3,2,1,0:T(8,128)(2,1)S(1)} collective-permute-done((bf16[1,36,16,128]{3,2,1,0:T(8,128)(2,1)S(1)}, bf16[1,36,16,128]{3,2,1,0:T(8,128)(2,1)S(1)}, u32[]{:S(2)}, u32[]{:S(2)}) %collective-permute-start.21) | collective-permute-done | bytes 147488 | tf_op jit(solution)/shard_map/ppermute | solution.py:586
  124.4 0.9 collective-permute-done.20.refs_4_
  126.1 1.6 collective-permute-start.25
  128.6 2.6 %collective-permute-start.24 = (bf16[1,36,16,128]{3,2,1,0:T(8,128)(2,1)S(1)}, bf16[1,36,16,128]{3,2,1,0:T(8,128)(2,1)S(1)}, u32[]{:S(2)}, u32[]{:S(2)}) collective-permute-start(bf16[1,36,16,128]{3,2,1,0:T(8,128)(2,1)S(1)} %get-tuple-element.344.refs_3_), channel_id=1, source_target_pairs={{0,16},{1,17},{2,18},{3,19},{4,20},{5,21},{6,22},{7,23},{8,24},{9,... | collective-permute-start | bytes 442376 | tf_op jit(solution)/shard_map/ppermute | solution.py:586
  131.2 7.5 %collective-permute-done.24.refs_4_ = bf16[1,36,16,128]{3,2,1,0:T(8,128)(2,1)S(1)} collective-permute-done((bf16[1,36,16,128]{3,2,1,0:T(8,128)(2,1)S(1)}, bf16[1,36,16,128]{3,2,1,0:T(8,128)(2,1)S(1)}, u32[]{:S(2)}, u32[]{:S(2)}) %collective-permute-start.24) | collective-permute-done | bytes 147488 | tf_op jit(solution)/shard_map/ppermute | solution.py:586
  138.6 2.0 collective-permute-done.23.refs_2_
  141.7 1.6 collective-permute-start.27
  143.7 1.3 collective-permute-start.29
  145.0 1.8 collective-permute-start.28
  147.3 7.7 %collective-permute-done.31.refs_9_ = bf16[4,10,16,128]{3,2,1,0:T(8,128)(2,1)S(1)} collective-permute-done((bf16[4,10,16,128]{3,2,1,0:T(8,128)(2,1)S(1)}, bf16[4,10,16,128]{3,2,1,0:T(8,128)(2,1)S(1)}, u32[]{:S(2)}, u32[]{:S(2)}) %collective-permute-start.31) | collective-permute-done | bytes 163872 | tf_op jit(solution)/shard_map/ppermute | solution.py:586
  155.3 1.6 collective-permute-start.32
  157.3 1.4 collective-permute-start.35
  158.7 2.5 %collective-permute-start.36 = (bf16[2,28,16,128]{3,2,1,0:T(8,128)(2,1)S(1)}, bf16[2,28,16,128]{3,2,1,0:T(8,128)(2,1)S(1)}, u32[]{:S(2)}, u32[]{:S(2)}) collective-permute-start(bf16[2,28,16,128]{3,2,1,0:T(8,128)(2,1)S(1)} %get-tuple-element.368), channel_id=1, source_target_pairs={{0,8},{1,9},{2,10},{3,11},{4,12},{5,13},{6,14},{7,15},{8,0},{9,1},... | collective-permute-start | bytes 688136 | tf_op jit(solution)/shard_map/ppermute | solution.py:586
  161.7 8.0 %collective-permute-done.33.refs_3_ = bf16[1,45,16,128]{3,2,1,0:T(8,128)(2,1)S(1)} collective-permute-done((bf16[1,45,16,128]{3,2,1,0:T(8,128)(2,1)S(1)}, bf16[1,45,16,128]{3,2,1,0:T(8,128)(2,1)S(1)}, u32[]{:S(2)}, u32[]{:S(2)}) %collective-permute-start.33) | collective-permute-done | bytes 184352 | tf_op jit(solution)/shard_map/ppermute | solution.py:586
  169.7 1.4 collective-permute-done.35.refs_7_
  171.2 1.2 collective-permute-start.40
  173.1 2.2 collective-permute-start.38
  176.0 1.5 layer_output.1
  177.5 8.8 %collective-permute-done.39.refs_4_ = bf16[1,28,16,128]{3,2,1,0:T(8,128)(2,1)S(1)} collective-permute-done((bf16[1,28,16,128]{3,2,1,0:T(8,128)(2,1)S(1)}, bf16[1,28,16,128]{3,2,1,0:T(8,128)(2,1)S(1)}, u32[]{:S(2)}, u32[]{:S(2)}) %collective-permute-start.39) | collective-permute-done | bytes 114720 | tf_op jit(solution)/shard_map/ppermute | solution.py:586
  187.4 1.6 collective-permute-start.43
  189.4 2.6 %collective-permute-start.44 = (bf16[1,28,16,128]{3,2,1,0:T(8,128)(2,1)S(1)}, bf16[1,28,16,128]{3,2,1,0:T(8,128)(2,1)S(1)}, u32[]{:S(2)}, u32[]{:S(2)}) collective-permute-start(bf16[1,28,16,128]{3,2,1,0:T(8,128)(2,1)S(1)} %get-tuple-element.384.refs_5_), channel_id=1, source_target_pairs={{0,16},{1,17},{2,18},{3,19},{4,20},{5,21},{6,22},{7,23},{8,24},{9,... | collective-permute-start | bytes 344072 | tf_op jit(solution)/shard_map/ppermute | solution.py:586
  192.1 5.7 %collective-permute-done.44.refs_6_ = bf16[1,28,16,128]{3,2,1,0:T(8,128)(2,1)S(1)} collective-permute-done((bf16[1,28,16,128]{3,2,1,0:T(8,128)(2,1)S(1)}, bf16[1,28,16,128]{3,2,1,0:T(8,128)(2,1)S(1)}, u32[]{:S(2)}, u32[]{:S(2)}) %collective-permute-start.44) | collective-permute-done | bytes 114720 | tf_op jit(solution)/shard_map/ppermute | solution.py:586
  198.0 1.9 collective-permute-done.43.refs_4_
  200.1 0.9 collective-permute-start.51
  201.0 1.1 collective-permute-start.50
  202.1 2.0 collective-permute-start.46
  204.1 4.8 %assemble_rows.1 = (f32[3072,768]{1,0:T(8,128)}, f32[8,128]{1,0:T(8,128)S(1)}) custom-call(f32[8,128]{1,0:T(8,128)S(1)} %get-tuple-element.385.refs_0_, s32[4]{0:T(128)S(1)} %pad_add_fusion.refs_0_.refs_1_, bf16[16,36,16,128]{3,2,1,0:T(8,128)(2,1)S(1)} %get-tuple-element.386.refs_2_, bf16[16,36,16,128]{3,2,1,0:T(8,128)(2,1)S(1)} %collective-permute-done.45.refs_3_), custom_call_target="tpu_custom_call" | custom-call | bytes 14000000 | tf_op jit(solution)/shard_map/assemble_rows/pallas_call | solution.py:106
  209.0 1.1 collective-permute-done.46.refs_2_
  210.1 1.4 collective-permute-start.48
  212.2 2.4 tokens_grad.1
  214.6 5.6 %collective-permute-done.49.refs_4_ = bf16[4,10,16,128]{3,2,1,0:T(8,128)(2,1)S(1)} collective-permute-done((bf16[4,10,16,128]{3,2,1,0:T(8,128)(2,1)S(1)}, bf16[4,10,16,128]{3,2,1,0:T(8,128)(2,1)S(1)}, u32[]{:S(2)}, u32[]{:S(2)}) %collective-permute-start.49) | collective-permute-done | bytes 163872 | tf_op jit(solution)/shard_map/ppermute | solution.py:586
  220.2 7.4 %collective-permute-done.48.refs_3_ = bf16[4,18,16,128]{3,2,1,0:T(8,128)(2,1)S(1)} collective-permute-done((bf16[4,18,16,128]{3,2,1,0:T(8,128)(2,1)S(1)}, bf16[4,18,16,128]{3,2,1,0:T(8,128)(2,1)S(1)}, u32[]{:S(2)}, u32[]{:S(2)}) %collective-permute-start.48) | collective-permute-done | bytes 294944 | tf_op jit(solution)/shard_map/ppermute | solution.py:586
  228.0 1.6 collective-permute-start.53
  230.1 3.3 %collective-permute-done.52.refs_3_ = bf16[16,45,16,128]{3,2,1,0:T(8,128)(2,1)S(1)} collective-permute-done((bf16[16,45,16,128]{3,2,1,0:T(8,128)(2,1)S(1)}, bf16[16,45,16,128]{3,2,1,0:T(8,128)(2,1)S(1)}, u32[]{:S(2)}, u32[]{:S(2)}) %collective-permute-start.52) | collective-permute-done | bytes 2949152 | tf_op jit(solution)/shard_map/ppermute | solution.py:586
  233.4 7.3 %assemble_up.1 = (f32[768,3072]{1,0:T(8,128)}, f32[768,768]{1,0:T(8,128)}, f32[8,128]{1,0:T(8,128)S(1)}) custom-call(f32[8,128]{1,0:T(8,128)S(1)} %get-tuple-element.399.refs_0_, s32[4]{0:T(128)S(1)} %pad_add_fusion.refs_0_.refs_1_, bf16[16,45,16,128]{3,2,1,0:T(8,128)(2,1)S(1)} %get-tuple-element.400.refs_2_, ...), custom_call_target="tpu_custom_call" | custom-call | bytes 18000000 | tf_op jit(solution)/shard_map/assemble_up/pallas_call | solution.py:106
  240.7 3.1 %collective-permute-done.53.refs_3_ = bf16[8,18,16,128]{3,2,1,0:T(8,128)(2,1)S(1)} collective-permute-done((bf16[8,18,16,128]{3,2,1,0:T(8,128)(2,1)S(1)}, bf16[8,18,16,128]{3,2,1,0:T(8,128)(2,1)S(1)}, u32[]{:S(2)}, u32[]{:S(2)}) %collective-permute-start.53) | collective-permute-done | bytes 589856 | tf_op jit(solution)/shard_map/ppermute | solution.py:586
  244.0 3.8 %collective-permute-done.55.refs_3_ = bf16[16,28,16,128]{3,2,1,0:T(8,128)(2,1)S(1)} collective-permute-done((bf16[16,28,16,128]{3,2,1,0:T(8,128)(2,1)S(1)}, bf16[16,28,16,128]{3,2,1,0:T(8,128)(2,1)S(1)}, u32[]{:S(2)}, u32[]{:S(2)}) %collective-permute-start.55) | collective-permute-done | bytes 1835040 | tf_op jit(solution)/shard_map/ppermute | solution.py:586
  247.7 4.3 %assemble_three.1 = (f32[768,768]{1,0:T(8,128)}, f32[768,768]{1,0:T(8,128)}, f32[768,768]{1,0:T(8,128)}, f32[12,64,64]{2,1,0:T(8,128)}, f32[16,768]{1,0:T(8,128)S(1)}, /*index=5*/f32[8,128]{1,0:T(8,128)}) custom-call(f32[8,128]{1,0:T(8,128)S(1)} %get-tuple-element.404.refs_0_, s32[4]{0:T(128)S(1)} %pad_add_fusion.refs_0_.refs_1_, ...), custom_call_target="tpu_custom_call" | custom-call | bytes 11000000 | tf_op jit(solution)/shard_map/assemble_three/pallas_call | solution.py:79
  (199 shorter events, 18.6 us)
Async XLA Ops:
  0.8 16.2 %copy-start.6 = (bf16[768,768]{1,0:T(8,128)(2,1)S(1)}, bf16[768,768]{1,0:T(8,128)(2,1)}, u32[]{:S(2)}) copy-start(bf16[768,768]{1,0:T(8,128)(2,1)} %refs_29_.1) | copy-start | bytes 3538948
  0.8 16.2 %copy-start.14 = (f32[12,64,64]{2,1,0:T(8,128)S(1)}, f32[12,64,64]{2,1,0:T(8,128)}, u32[]{:S(2)}) copy-start(f32[12,64,64]{2,1,0:T(8,128)} %refs_14_.1) | copy-start | bytes 589828
  2.7 10.4 %collective-permute-start = (bf16[128,768]{1,0:T(8,128)(2,1)S(1)}, bf16[128,768]{1,0:T(8,128)(2,1)S(1)}, u32[]{:S(2)}, u32[]{:S(2)}) collective-permute-start(bf16[128,768]{1,0:T(8,128)(2,1)S(1)} %get-tuple-element.221), channel_id=1, source_target_pairs={{0,1},{1,0},{2,3},{3,2},{4,5},{5,4},{6,7},{7,6},{8,9},{9,8},{10,11... | collective-permute-start | bytes 589832 | tf_op jit(solution)/shard_map/ppermute | solution.py:586
  3.2 9.9 %collective-permute-start.1 = (bf16[128,768]{1,0:T(8,128)(2,1)S(1)}, bf16[128,768]{1,0:T(8,128)(2,1)S(1)}, u32[]{:S(2)}, u32[]{:S(2)}) collective-permute-start(bf16[128,768]{1,0:T(8,128)(2,1)S(1)} %get-tuple-element.222), channel_id=1, source_target_pairs={{0,2},{1,3},{2,0},{3,1},{4,6},{5,7},{6,4},{7,5},{8,10},{9,11},{10,... | collective-permute-start | bytes 589832 | tf_op jit(solution)/shard_map/ppermute | solution.py:586
  5.7 9.4 %collective-permute-start.2 = (bf16[128,768]{1,0:T(8,128)(2,1)S(1)}, bf16[128,768]{1,0:T(8,128)(2,1)S(1)}, u32[]{:S(2)}, u32[]{:S(2)}) collective-permute-start(bf16[128,768]{1,0:T(8,128)(2,1)S(1)} %get-tuple-element.223), channel_id=1, source_target_pairs={{0,3},{1,2},{2,1},{3,0},{4,7},{5,6},{6,5},{7,4},{8,11},{9,10},{10,... | collective-permute-start | bytes 589832 | tf_op jit(solution)/shard_map/ppermute | solution.py:586
  9.4 70.2 %copy-start.12 = (bf16[2,2,512,128]{3,2,1,0:T(8,128)(2,1)}, bf16[2,2,512,128]{3,2,1,0:T(8,128)(2,1)S(1)}, u32[]{:S(2)}) copy-start(bf16[2,2,512,128]{3,2,1,0:T(8,128)(2,1)S(1)} %get-tuple-element.232.refs_11_.refs_10_) | copy-start | bytes 1572868
  9.4 70.1 %copy-start.18 = (f32[128,256]{1,0:T(8,128)}, f32[128,256]{1,0:T(8,128)S(1)}, u32[]{:S(2)}) copy-start(f32[128,256]{1,0:T(8,128)S(1)} %get-tuple-element.292.refs_12_.refs_13_) | copy-start | bytes 393220
  9.5 70.1 %copy-start.20 = (bf16[128,512]{1,0:T(8,128)(2,1)}, bf16[128,512]{1,0:T(8,128)(2,1)S(1)}, u32[]{:S(2)}) copy-start(bf16[128,512]{1,0:T(8,128)(2,1)S(1)} %get-tuple-element.291.refs_11_.refs_12_) | copy-start | bytes 393220
  15.2 10.7 %collective-permute-start.3 = (bf16[128,768]{1,0:T(8,128)(2,1)S(1)}, bf16[128,768]{1,0:T(8,128)(2,1)S(1)}, u32[]{:S(2)}, u32[]{:S(2)}) collective-permute-start(bf16[128,768]{1,0:T(8,128)(2,1)S(1)} %get-tuple-element.234), channel_id=1, source_target_pairs={{0,1},{1,0},{2,3},{3,2},{4,5},{5,4},{6,7},{7,6},{8,9},{9,8},{10,11... | collective-permute-start | bytes 589832 | tf_op jit(solution)/shard_map/ppermute | solution.py:586
  15.3 10.6 %collective-permute-start.4 = (bf16[128,768]{1,0:T(8,128)(2,1)S(1)}, bf16[128,768]{1,0:T(8,128)(2,1)S(1)}, u32[]{:S(2)}, u32[]{:S(2)}) collective-permute-start(bf16[128,768]{1,0:T(8,128)(2,1)S(1)} %get-tuple-element.235), channel_id=1, source_target_pairs={{0,2},{1,3},{2,0},{3,1},{4,6},{5,7},{6,4},{7,5},{8,10},{9,11},{10,... | collective-permute-start | bytes 589832 | tf_op jit(solution)/shard_map/ppermute | solution.py:586
  17.0 9.1 %collective-permute-start.5 = (bf16[128,768]{1,0:T(8,128)(2,1)S(1)}, bf16[128,768]{1,0:T(8,128)(2,1)S(1)}, u32[]{:S(2)}, u32[]{:S(2)}) collective-permute-start(bf16[128,768]{1,0:T(8,128)(2,1)S(1)} %get-tuple-element.236), channel_id=1, source_target_pairs={{0,3},{1,2},{2,1},{3,0},{4,7},{5,6},{6,5},{7,4},{8,11},{9,10},{10,... | collective-permute-start | bytes 589832 | tf_op jit(solution)/shard_map/ppermute | solution.py:586
  26.2 10.6 %collective-permute-start.6 = (bf16[2,64,768]{2,1,0:T(8,128)(2,1)S(1)}, bf16[2,64,768]{2,1,0:T(8,128)(2,1)S(1)}, u32[]{:S(2)}, u32[]{:S(2)}) collective-permute-start(bf16[2,64,768]{2,1,0:T(8,128)(2,1)S(1)} %get-tuple-element.249), channel_id=1, source_target_pairs={{0,1},{1,0},{2,3},{3,2},{4,5},{5,4},{6,7},{7,6},{8,9},{9,8},{10,11... | collective-permute-start | bytes 589832 | tf_op jit(solution)/shard_map/ppermute | solution.py:586
  26.5 10.2 %collective-permute-start.7 = (bf16[2,64,768]{2,1,0:T(8,128)(2,1)S(1)}, bf16[2,64,768]{2,1,0:T(8,128)(2,1)S(1)}, u32[]{:S(2)}, u32[]{:S(2)}) collective-permute-start(bf16[2,64,768]{2,1,0:T(8,128)(2,1)S(1)} %get-tuple-element.250), channel_id=1, source_target_pairs={{0,2},{1,3},{2,0},{3,1},{4,6},{5,7},{6,4},{7,5},{8,10},{9,11},{10,... | collective-permute-start | bytes 589832 | tf_op jit(solution)/shard_map/ppermute | solution.py:586
  28.2 8.7 %collective-permute-start.8 = (bf16[2,64,768]{2,1,0:T(8,128)(2,1)S(1)}, bf16[2,64,768]{2,1,0:T(8,128)(2,1)S(1)}, u32[]{:S(2)}, u32[]{:S(2)}) collective-permute-start(bf16[2,64,768]{2,1,0:T(8,128)(2,1)S(1)} %get-tuple-element.251), channel_id=1, source_target_pairs={{0,3},{1,2},{2,1},{3,0},{4,7},{5,6},{6,5},{7,4},{8,11},{9,10},{10,... | collective-permute-start | bytes 589832 | tf_op jit(solution)/shard_map/ppermute | solution.py:586
  36.7 14.8 %copy-start.45 = (f32[12,1,256]{2,1,0:T(1,128)}, f32[12,1,256]{2,1,0:T(1,128)S(1)}, u32[]{:S(2)}) copy-start(f32[12,1,256]{2,1,0:T(1,128)S(1)} %get-tuple-element.308.refs_9_) | copy-start | bytes 36868
  51.5 7.6 %collective-permute-start.9 = (bf16[16,36,16,128]{3,2,1,0:T(8,128)(2,1)S(1)}, bf16[16,36,16,128]{3,2,1,0:T(8,128)(2,1)S(1)}, u32[]{:S(2)}, u32[]{:S(2)}) collective-permute-start(bf16[16,36,16,128]{3,2,1,0:T(8,128)(2,1)S(1)} %get-tuple-element.262), channel_id=1, source_target_pairs={{0,1},{1,0},{2,3},{3,2},{4,5},{5,4},{6,7},{7,6},{8,9},{9,8},{10,11... | collective-permute-start | bytes 7077896 | tf_op jit(solution)/shard_map/ppermute | solution.py:586
  52.2 12.0 %collective-permute-start.10 = (bf16[2,2,64,768]{3,2,1,0:T(8,128)(2,1)S(1)}, bf16[2,2,64,768]{3,2,1,0:T(8,128)(2,1)S(1)}, u32[]{:S(2)}, u32[]{:S(2)}) collective-permute-start(bf16[2,2,64,768]{3,2,1,0:T(8,128)(2,1)S(1)} %get-tuple-element.265), channel_id=1, source_target_pairs={{0,2},{1,3},{2,0},{3,1},{4,6},{5,7},{6,4},{7,5},{8,10},{9,11},{10,... | collective-permute-start | bytes 1179656 | tf_op jit(solution)/shard_map/ppermute | solution.py:586
  59.9 16.0 %collective-permute-start.11 = (bf16[8,18,16,128]{3,2,1,0:T(8,128)(2,1)S(1)}, bf16[8,18,16,128]{3,2,1,0:T(8,128)(2,1)S(1)}, u32[]{:S(2)}, u32[]{:S(2)}) collective-permute-start(bf16[8,18,16,128]{3,2,1,0:T(8,128)(2,1)S(1)} %get-tuple-element.277), channel_id=1, source_target_pairs={{0,2},{1,3},{2,0},{3,1},{4,6},{5,7},{6,4},{7,5},{8,10},{9,11},{10,... | collective-permute-start | bytes 1769480 | tf_op jit(solution)/shard_map/ppermute | solution.py:586
  60.5 15.5 %collective-permute-start.12 = (bf16[8,18,16,128]{3,2,1,0:T(8,128)(2,1)S(1)}, bf16[8,18,16,128]{3,2,1,0:T(8,128)(2,1)S(1)}, u32[]{:S(2)}, u32[]{:S(2)}) collective-permute-start(bf16[8,18,16,128]{3,2,1,0:T(8,128)(2,1)S(1)} %get-tuple-element.278), channel_id=1, source_target_pairs={{0,4},{1,5},{2,6},{3,7},{4,0},{5,1},{6,2},{7,3},{8,12},{9,13},{10,... | collective-permute-start | bytes 1769480 | tf_op jit(solution)/shard_map/ppermute | solution.py:586
  76.4 11.8 %collective-permute-start.15 = (bf16[16,45,16,128]{3,2,1,0:T(8,128)(2,1)S(1)}, bf16[16,45,16,128]{3,2,1,0:T(8,128)(2,1)S(1)}, u32[]{:S(2)}, u32[]{:S(2)}) collective-permute-start(bf16[16,45,16,128]{3,2,1,0:T(8,128)(2,1)S(1)} %get-tuple-element.299), channel_id=1, source_target_pairs={{0,1},{1,0},{2,3},{3,2},{4,5},{5,4},{6,7},{7,6},{8,9},{9,8},{10,11... | collective-permute-start | bytes 8847368 | tf_op jit(solution)/shard_map/ppermute | solution.py:586
  76.5 11.7 %collective-permute-start.13 = (bf16[4,18,16,128]{3,2,1,0:T(8,128)(2,1)S(1)}, bf16[4,18,16,128]{3,2,1,0:T(8,128)(2,1)S(1)}, u32[]{:S(2)}, u32[]{:S(2)}) collective-permute-start(bf16[4,18,16,128]{3,2,1,0:T(8,128)(2,1)S(1)} %get-tuple-element.296), channel_id=1, source_target_pairs={{0,4},{1,5},{2,6},{3,7},{4,0},{5,1},{6,2},{7,3},{8,12},{9,13},{10,... | collective-permute-start | bytes 884744 | tf_op jit(solution)/shard_map/ppermute | solution.py:586
  78.1 10.0 %collective-permute-start.14 = (bf16[4,18,16,128]{3,2,1,0:T(8,128)(2,1)S(1)}, bf16[4,18,16,128]{3,2,1,0:T(8,128)(2,1)S(1)}, u32[]{:S(2)}, u32[]{:S(2)}) collective-permute-start(bf16[4,18,16,128]{3,2,1,0:T(8,128)(2,1)S(1)} %get-tuple-element.297), channel_id=1, source_target_pairs={{0,2},{1,3},{2,0},{3,1},{4,6},{5,7},{6,4},{7,5},{8,10},{9,11},{10,... | collective-permute-start | bytes 884744 | tf_op jit(solution)/shard_map/ppermute | solution.py:586
  79.7 12.5 %copy-start.30 = (bf16[768,512]{1,0:T(8,128)(2,1)S(1)}, bf16[768,512]{1,0:T(8,128)(2,1)}, u32[]{:S(2)}) copy-start(bf16[768,512]{1,0:T(8,128)(2,1)} %get-tuple-element.303.refs_4_) | copy-start | bytes 2359300
  89.2 21.1 %collective-permute-start.18 = (bf16[2,36,16,128]{3,2,1,0:T(8,128)(2,1)S(1)}, bf16[2,36,16,128]{3,2,1,0:T(8,128)(2,1)S(1)}, u32[]{:S(2)}, u32[]{:S(2)}) collective-permute-start(bf16[2,36,16,128]{3,2,1,0:T(8,128)(2,1)S(1)} %get-tuple-element.329), channel_id=1, source_target_pairs={{0,8},{1,9},{2,10},{3,11},{4,12},{5,13},{6,14},{7,15},{8,0},{9,1},... | collective-permute-start | bytes 884744 | tf_op jit(solution)/shard_map/ppermute | solution.py:586
  90.8 19.5 %collective-permute-start.16 = (bf16[8,18,16,128]{3,2,1,0:T(8,128)(2,1)S(1)}, bf16[8,18,16,128]{3,2,1,0:T(8,128)(2,1)S(1)}, u32[]{:S(2)}, u32[]{:S(2)}) collective-permute-start(bf16[8,18,16,128]{3,2,1,0:T(8,128)(2,1)S(1)} %get-tuple-element.326), channel_id=1, source_target_pairs={{0,2},{1,3},{2,0},{3,1},{4,6},{5,7},{6,4},{7,5},{8,10},{9,11},{10,... | collective-permute-start | bytes 1769480 | tf_op jit(solution)/shard_map/ppermute | solution.py:586
  91.4 20.9 %collective-permute-start.17 = (bf16[8,27,16,128]{3,2,1,0:T(8,128)(2,1)S(1)}, bf16[8,27,16,128]{3,2,1,0:T(8,128)(2,1)S(1)}, u32[]{:S(2)}, u32[]{:S(2)}) collective-permute-start(bf16[8,27,16,128]{3,2,1,0:T(8,128)(2,1)S(1)} %get-tuple-element.327), channel_id=1, source_target_pairs={{0,4},{1,5},{2,6},{3,7},{4,0},{5,1},{6,2},{7,3},{8,12},{9,13},{10,... | collective-permute-start | bytes 2654216 | tf_op jit(solution)/shard_map/ppermute | solution.py:586
  112.7 12.7 %collective-permute-start.22 = (bf16[16,28,16,128]{3,2,1,0:T(8,128)(2,1)S(1)}, bf16[16,28,16,128]{3,2,1,0:T(8,128)(2,1)S(1)}, u32[]{:S(2)}, u32[]{:S(2)}) collective-permute-start(bf16[16,28,16,128]{3,2,1,0:T(8,128)(2,1)S(1)} %get-tuple-element.340), channel_id=1, source_target_pairs={{0,1},{1,0},{2,3},{3,2},{4,5},{5,4},{6,7},{7,6},{8,9},{9,8},{10,11... | collective-permute-start | bytes 5505032 | tf_op jit(solution)/shard_map/ppermute | solution.py:586
  112.8 12.6 %collective-permute-start.20 = (bf16[4,27,16,128]{3,2,1,0:T(8,128)(2,1)S(1)}, bf16[4,27,16,128]{3,2,1,0:T(8,128)(2,1)S(1)}, u32[]{:S(2)}, u32[]{:S(2)}) collective-permute-start(bf16[4,27,16,128]{3,2,1,0:T(8,128)(2,1)S(1)} %get-tuple-element.336), channel_id=1, source_target_pairs={{0,2},{1,3},{2,0},{3,1},{4,6},{5,7},{6,4},{7,5},{8,10},{9,11},{10,... | collective-permute-start | bytes 1327112 | tf_op jit(solution)/shard_map/ppermute | solution.py:586
  114.3 10.1 %collective-permute-start.19 = (bf16[4,18,16,128]{3,2,1,0:T(8,128)(2,1)S(1)}, bf16[4,18,16,128]{3,2,1,0:T(8,128)(2,1)S(1)}, u32[]{:S(2)}, u32[]{:S(2)}) collective-permute-start(bf16[4,18,16,128]{3,2,1,0:T(8,128)(2,1)S(1)} %get-tuple-element.335), channel_id=1, source_target_pairs={{0,4},{1,5},{2,6},{3,7},{4,0},{5,1},{6,2},{7,3},{8,12},{9,13},{10,... | collective-permute-start | bytes 884744 | tf_op jit(solution)/shard_map/ppermute | solution.py:586
  114.8 9.6 %collective-permute-start.21 = (bf16[1,36,16,128]{3,2,1,0:T(8,128)(2,1)S(1)}, bf16[1,36,16,128]{3,2,1,0:T(8,128)(2,1)S(1)}, u32[]{:S(2)}, u32[]{:S(2)}) collective-permute-start(bf16[1,36,16,128]{3,2,1,0:T(8,128)(2,1)S(1)} %get-tuple-element.338), channel_id=1, source_target_pairs={{0,16},{1,17},{2,18},{3,19},{4,20},{5,21},{6,22},{7,23},{8,24},{9,... | collective-permute-start | bytes 442376 | tf_op jit(solution)/shard_map/ppermute | solution.py:586
  126.1 15.0 %collective-permute-start.25 = (bf16[8,18,16,128]{3,2,1,0:T(8,128)(2,1)S(1)}, bf16[8,18,16,128]{3,2,1,0:T(8,128)(2,1)S(1)}, u32[]{:S(2)}, u32[]{:S(2)}) collective-permute-start(bf16[8,18,16,128]{3,2,1,0:T(8,128)(2,1)S(1)} %get-tuple-element.347), channel_id=1, source_target_pairs={{0,2},{1,3},{2,0},{3,1},{4,6},{5,7},{6,4},{7,5},{8,10},{9,11},{10,... | collective-permute-start | bytes 1769480 | tf_op jit(solution)/shard_map/ppermute | solution.py:586
  127.6 13.0 %collective-permute-start.23 = (bf16[2,45,16,128]{3,2,1,0:T(8,128)(2,1)S(1)}, bf16[2,45,16,128]{3,2,1,0:T(8,128)(2,1)S(1)}, u32[]{:S(2)}, u32[]{:S(2)}) collective-permute-start(bf16[2,45,16,128]{3,2,1,0:T(8,128)(2,1)S(1)} %get-tuple-element.343), channel_id=1, source_target_pairs={{0,8},{1,9},{2,10},{3,11},{4,12},{5,13},{6,14},{7,15},{8,0},{9,1},... | collective-permute-start | bytes 1105928 | tf_op jit(solution)/shard_map/ppermute | solution.py:586
  128.1 10.6 %collective-permute-start.26 = (bf16[8,10,16,128]{3,2,1,0:T(8,128)(2,1)S(1)}, bf16[8,10,16,128]{3,2,1,0:T(8,128)(2,1)S(1)}, u32[]{:S(2)}, u32[]{:S(2)}) collective-permute-start(bf16[8,10,16,128]{3,2,1,0:T(8,128)(2,1)S(1)} %get-tuple-element.348), channel_id=1, source_target_pairs={{0,4},{1,5},{2,6},{3,7},{4,0},{5,1},{6,2},{7,3},{8,12},{9,13},{10,... | collective-permute-start | bytes 983048 | tf_op jit(solution)/shard_map/ppermute | solution.py:586
  128.6 10.0 %collective-permute-start.24 = (bf16[1,36,16,128]{3,2,1,0:T(8,128)(2,1)S(1)}, bf16[1,36,16,128]{3,2,1,0:T(8,128)(2,1)S(1)}, u32[]{:S(2)}, u32[]{:S(2)}) collective-permute-start(bf16[1,36,16,128]{3,2,1,0:T(8,128)(2,1)S(1)} %get-tuple-element.344.refs_3_), channel_id=1, source_target_pairs={{0,16},{1,17},{2,18},{3,19},{4,20},{5,21},{6,22},{7,23},{8,24},{9,... | collective-permute-start | bytes 442376 | tf_op jit(solution)/shard_map/ppermute | solution.py:586
  141.7 13.4 %collective-permute-start.27 = (bf16[2,128,768]{2,1,0:T(8,128)(2,1)S(1)}, bf16[2,128,768]{2,1,0:T(8,128)(2,1)S(1)}, u32[]{:S(2)}, u32[]{:S(2)}) collective-permute-start(bf16[2,128,768]{2,1,0:T(8,128)(2,1)S(1)} %get-tuple-element.352), channel_id=1, source_target_pairs={{0,2},{1,3},{2,0},{3,1},{4,6},{5,7},{6,4},{7,5},{8,10},{9,11},{10,... | collective-permute-start | bytes 1179656 | tf_op jit(solution)/shard_map/ppermute | solution.py:586
  143.2 11.8 %collective-permute-start.30 = (bf16[4,18,16,128]{3,2,1,0:T(8,128)(2,1)S(1)}, bf16[4,18,16,128]{3,2,1,0:T(8,128)(2,1)S(1)}, u32[]{:S(2)}, u32[]{:S(2)}) collective-permute-start(bf16[4,18,16,128]{3,2,1,0:T(8,128)(2,1)S(1)} %get-tuple-element.358), channel_id=1, source_target_pairs={{0,4},{1,5},{2,6},{3,7},{4,0},{5,1},{6,2},{7,3},{8,12},{9,13},{10,... | collective-permute-start | bytes 884744 | tf_op jit(solution)/shard_map/ppermute | solution.py:586
  143.7 11.3 %collective-permute-start.29 = (bf16[2,36,16,128]{3,2,1,0:T(8,128)(2,1)S(1)}, bf16[2,36,16,128]{3,2,1,0:T(8,128)(2,1)S(1)}, u32[]{:S(2)}, u32[]{:S(2)}) collective-permute-start(bf16[2,36,16,128]{3,2,1,0:T(8,128)(2,1)S(1)} %get-tuple-element.355.refs_4_), channel_id=1, source_target_pairs={{0,8},{1,9},{2,10},{3,11},{4,12},{5,13},{6,14},{7,15},{8,0},{9,1},... | collective-permute-start | bytes 884744 | tf_op jit(solution)/shard_map/ppermute | solution.py:586
  145.0 10.0 %collective-permute-start.28 = (bf16[1,45,16,128]{3,2,1,0:T(8,128)(2,1)S(1)}, bf16[1,45,16,128]{3,2,1,0:T(8,128)(2,1)S(1)}, u32[]{:S(2)}, u32[]{:S(2)}) collective-permute-start(bf16[1,45,16,128]{3,2,1,0:T(8,128)(2,1)S(1)} %get-tuple-element.354), channel_id=1, source_target_pairs={{0,16},{1,17},{2,18},{3,19},{4,20},{5,21},{6,22},{7,23},{8,24},{9,... | collective-permute-start | bytes 552968 | tf_op jit(solution)/shard_map/ppermute | solution.py:586
  146.8 8.3 %collective-permute-start.31 = (bf16[4,10,16,128]{3,2,1,0:T(8,128)(2,1)S(1)}, bf16[4,10,16,128]{3,2,1,0:T(8,128)(2,1)S(1)}, u32[]{:S(2)}, u32[]{:S(2)}) collective-permute-start(bf16[4,10,16,128]{3,2,1,0:T(8,128)(2,1)S(1)} %get-tuple-element.359), channel_id=1, source_target_pairs={{0,2},{1,3},{2,0},{3,1},{4,6},{5,7},{6,4},{7,5},{8,10},{9,11},{10,... | collective-permute-start | bytes 491528 | tf_op jit(solution)/shard_map/ppermute | solution.py:586
  155.0 18.1 %copy-start.17 = (bf16[2,2,64,768]{3,2,1,0:T(8,128)(2,1)S(1)}, bf16[2,2,64,768]{3,2,1,0:T(8,128)(2,1)}, u32[]{:S(2)}) copy-start(bf16[2,2,64,768]{3,2,1,0:T(8,128)(2,1)} %copy-done.16) | copy-start | bytes 1179652
  155.3 15.8 %collective-permute-start.32 = (bf16[2,128,768]{2,1,0:T(8,128)(2,1)S(1)}, bf16[2,128,768]{2,1,0:T(8,128)(2,1)S(1)}, u32[]{:S(2)}, u32[]{:S(2)}) collective-permute-start(bf16[2,128,768]{2,1,0:T(8,128)(2,1)S(1)} %get-tuple-element.363), channel_id=1, source_target_pairs={{0,2},{1,3},{2,0},{3,1},{4,6},{5,7},{6,4},{7,5},{8,10},{9,11},{10,... | collective-permute-start | bytes 1179656 | tf_op jit(solution)/shard_map/ppermute | solution.py:586
  156.8 12.8 %collective-permute-start.34 = (bf16[4,18,16,128]{3,2,1,0:T(8,128)(2,1)S(1)}, bf16[4,18,16,128]{3,2,1,0:T(8,128)(2,1)S(1)}, u32[]{:S(2)}, u32[]{:S(2)}) collective-permute-start(bf16[4,18,16,128]{3,2,1,0:T(8,128)(2,1)S(1)} %get-tuple-element.365.refs_4_), channel_id=1, source_target_pairs={{0,4},{1,5},{2,6},{3,7},{4,0},{5,1},{6,2},{7,3},{8,12},{9,13},{10,... | collective-permute-start | bytes 884744 | tf_op jit(solution)/shard_map/ppermute | solution.py:586
  157.3 13.7 %collective-permute-start.35 = (bf16[4,18,16,128]{3,2,1,0:T(8,128)(2,1)S(1)}, bf16[4,18,16,128]{3,2,1,0:T(8,128)(2,1)S(1)}, u32[]{:S(2)}, u32[]{:S(2)}) collective-permute-start(bf16[4,18,16,128]{3,2,1,0:T(8,128)(2,1)S(1)} %get-tuple-element.366.refs_5_), channel_id=1, source_target_pairs={{0,2},{1,3},{2,0},{3,1},{4,6},{5,7},{6,4},{7,5},{8,10},{9,11},{10,... | collective-permute-start | bytes 884744 | tf_op jit(solution)/shard_map/ppermute | solution.py:586
  158.7 11.0 %collective-permute-start.36 = (bf16[2,28,16,128]{3,2,1,0:T(8,128)(2,1)S(1)}, bf16[2,28,16,128]{3,2,1,0:T(8,128)(2,1)S(1)}, u32[]{:S(2)}, u32[]{:S(2)}) collective-permute-start(bf16[2,28,16,128]{3,2,1,0:T(8,128)(2,1)S(1)} %get-tuple-element.368), channel_id=1, source_target_pairs={{0,8},{1,9},{2,10},{3,11},{4,12},{5,13},{6,14},{7,15},{8,0},{9,1},... | collective-permute-start | bytes 688136 | tf_op jit(solution)/shard_map/ppermute | solution.py:586
  161.3 8.4 %collective-permute-start.33 = (bf16[1,45,16,128]{3,2,1,0:T(8,128)(2,1)S(1)}, bf16[1,45,16,128]{3,2,1,0:T(8,128)(2,1)S(1)}, u32[]{:S(2)}, u32[]{:S(2)}) collective-permute-start(bf16[1,45,16,128]{3,2,1,0:T(8,128)(2,1)S(1)} %get-tuple-element.364.refs_2_), channel_id=1, source_target_pairs={{0,16},{1,17},{2,18},{3,19},{4,20},{5,21},{6,22},{7,23},{8,24},{9,... | collective-permute-start | bytes 552968 | tf_op jit(solution)/shard_map/ppermute | solution.py:586
  171.2 15.8 %collective-permute-start.40 = (bf16[8,18,16,128]{3,2,1,0:T(8,128)(2,1)S(1)}, bf16[8,18,16,128]{3,2,1,0:T(8,128)(2,1)S(1)}, u32[]{:S(2)}, u32[]{:S(2)}) collective-permute-start(bf16[8,18,16,128]{3,2,1,0:T(8,128)(2,1)S(1)} %get-tuple-element.379.refs_5_), channel_id=1, source_target_pairs={{0,2},{1,3},{2,0},{3,1},{4,6},{5,7},{6,4},{7,5},{8,10},{9,11},{10,... | collective-permute-start | bytes 1769480 | tf_op jit(solution)/shard_map/ppermute | solution.py:586
  172.4 14.6 %collective-permute-start.41 = (bf16[8,18,16,128]{3,2,1,0:T(8,128)(2,1)S(1)}, bf16[8,18,16,128]{3,2,1,0:T(8,128)(2,1)S(1)}, u32[]{:S(2)}, u32[]{:S(2)}) collective-permute-start(bf16[8,18,16,128]{3,2,1,0:T(8,128)(2,1)S(1)} %get-tuple-element.380.refs_6_), channel_id=1, source_target_pairs={{0,4},{1,5},{2,6},{3,7},{4,0},{5,1},{6,2},{7,3},{8,12},{9,13},{10,... | collective-permute-start | bytes 1769480 | tf_op jit(solution)/shard_map/ppermute | solution.py:586
  173.1 2.9 %collective-permute-start.37 = (bf16[2,2,64,768]{3,2,1,0:T(8,128)(2,1)S(1)}, bf16[2,2,64,768]{3,2,1,0:T(8,128)(2,1)S(1)}, u32[]{:S(2)}, u32[]{:S(2)}) collective-permute-start(bf16[2,2,64,768]{3,2,1,0:T(8,128)(2,1)S(1)} %copy-done.17), channel_id=1, source_target_pairs={{0,1},{1,0},{2,3},{3,2},{4,5},{5,4},{6,7},{7,6},{8,9},{9,8},{10,11... | collective-permute-start | bytes 1179656 | tf_op jit(solution)/shard_map/ppermute | solution.py:586
  173.1 14.0 %collective-permute-start.38 = (bf16[2,45,16,128]{3,2,1,0:T(8,128)(2,1)S(1)}, bf16[2,45,16,128]{3,2,1,0:T(8,128)(2,1)S(1)}, u32[]{:S(2)}, u32[]{:S(2)}) collective-permute-start(bf16[2,45,16,128]{3,2,1,0:T(8,128)(2,1)S(1)} %get-tuple-element.376.refs_1_), channel_id=1, source_target_pairs={{0,8},{1,9},{2,10},{3,11},{4,12},{5,13},{6,14},{7,15},{8,0},{9,1},... | collective-permute-start | bytes 1105928 | tf_op jit(solution)/shard_map/ppermute | solution.py:586
  175.3 11.0 %collective-permute-start.39 = (bf16[1,28,16,128]{3,2,1,0:T(8,128)(2,1)S(1)}, bf16[1,28,16,128]{3,2,1,0:T(8,128)(2,1)S(1)}, u32[]{:S(2)}, u32[]{:S(2)}) collective-permute-start(bf16[1,28,16,128]{3,2,1,0:T(8,128)(2,1)S(1)} %get-tuple-element.378), channel_id=1, source_target_pairs={{0,16},{1,17},{2,18},{3,19},{4,20},{5,21},{6,22},{7,23},{8,24},{9,... | collective-permute-start | bytes 344072 | tf_op jit(solution)/shard_map/ppermute | solution.py:586
  187.3 16.8 %collective-permute-start.45 = (bf16[16,36,16,128]{3,2,1,0:T(8,128)(2,1)S(1)}, bf16[16,36,16,128]{3,2,1,0:T(8,128)(2,1)S(1)}, u32[]{:S(2)}, u32[]{:S(2)}) collective-permute-start(bf16[16,36,16,128]{3,2,1,0:T(8,128)(2,1)S(1)} %get-tuple-element.386.refs_2_), channel_id=1, source_target_pairs={{0,1},{1,0},{2,3},{3,2},{4,5},{5,4},{6,7},{7,6},{8,9},{9,8},{10,11... | collective-permute-start | bytes 7077896 | tf_op jit(solution)/shard_map/ppermute | solution.py:586
  187.4 12.6 %collective-permute-start.43 = (bf16[4,27,16,128]{3,2,1,0:T(8,128)(2,1)S(1)}, bf16[4,27,16,128]{3,2,1,0:T(8,128)(2,1)S(1)}, u32[]{:S(2)}, u32[]{:S(2)}) collective-permute-start(bf16[4,27,16,128]{3,2,1,0:T(8,128)(2,1)S(1)} %get-tuple-element.383.refs_2_), channel_id=1, source_target_pairs={{0,2},{1,3},{2,0},{3,1},{4,6},{5,7},{6,4},{7,5},{8,10},{9,11},{10,... | collective-permute-start | bytes 1327112 | tf_op jit(solution)/shard_map/ppermute | solution.py:586
  188.9 9.1 %collective-permute-start.42 = (bf16[4,18,16,128]{3,2,1,0:T(8,128)(2,1)S(1)}, bf16[4,18,16,128]{3,2,1,0:T(8,128)(2,1)S(1)}, u32[]{:S(2)}, u32[]{:S(2)}) collective-permute-start(bf16[4,18,16,128]{3,2,1,0:T(8,128)(2,1)S(1)} %get-tuple-element.382.refs_1_), channel_id=1, source_target_pairs={{0,4},{1,5},{2,6},{3,7},{4,0},{5,1},{6,2},{7,3},{8,12},{9,13},{10,... | collective-permute-start | bytes 884744 | tf_op jit(solution)/shard_map/ppermute | solution.py:586
  189.4 8.3 %collective-permute-start.44 = (bf16[1,28,16,128]{3,2,1,0:T(8,128)(2,1)S(1)}, bf16[1,28,16,128]{3,2,1,0:T(8,128)(2,1)S(1)}, u32[]{:S(2)}, u32[]{:S(2)}) collective-permute-start(bf16[1,28,16,128]{3,2,1,0:T(8,128)(2,1)S(1)} %get-tuple-element.384.refs_5_), channel_id=1, source_target_pairs={{0,16},{1,17},{2,18},{3,19},{4,20},{5,21},{6,22},{7,23},{8,24},{9,... | collective-permute-start | bytes 344072 | tf_op jit(solution)/shard_map/ppermute | solution.py:586
  200.1 27.7 %collective-permute-start.51 = (bf16[8,27,16,128]{3,2,1,0:T(8,128)(2,1)S(1)}, bf16[8,27,16,128]{3,2,1,0:T(8,128)(2,1)S(1)}, u32[]{:S(2)}, u32[]{:S(2)}) collective-permute-start(bf16[8,27,16,128]{3,2,1,0:T(8,128)(2,1)S(1)} %get-tuple-element.398.refs_2_), channel_id=1, source_target_pairs={{0,4},{1,5},{2,6},{3,7},{4,0},{5,1},{6,2},{7,3},{8,12},{9,13},{10,... | collective-permute-start | bytes 2654216 | tf_op jit(solution)/shard_map/ppermute | solution.py:586
  201.0 11.2 %collective-permute-start.47 = (bf16[2,2,128,768]{3,2,1,0:T(8,128)(2,1)S(1)}, bf16[2,2,128,768]{3,2,1,0:T(8,128)(2,1)S(1)}, u32[]{:S(2)}, u32[]{:S(2)}) collective-permute-start(bf16[2,2,128,768]{3,2,1,0:T(8,128)(2,1)S(1)} %get-tuple-element.391), channel_id=1, source_target_pairs={{0,1},{1,0},{2,3},{3,2},{4,5},{5,4},{6,7},{7,6},{8,9},{9,8},{10,11... | collective-permute-start | bytes 2359304 | tf_op jit(solution)/shard_map/ppermute | solution.py:586
  201.0 26.7 %collective-permute-start.50 = (bf16[8,18,16,128]{3,2,1,0:T(8,128)(2,1)S(1)}, bf16[8,18,16,128]{3,2,1,0:T(8,128)(2,1)S(1)}, u32[]{:S(2)}, u32[]{:S(2)}) collective-permute-start(bf16[8,18,16,128]{3,2,1,0:T(8,128)(2,1)S(1)} %get-tuple-element.397.refs_1_), channel_id=1, source_target_pairs={{0,2},{1,3},{2,0},{3,1},{4,6},{5,7},{6,4},{7,5},{8,10},{9,11},{10,... | collective-permute-start | bytes 1769480 | tf_op jit(solution)/shard_map/ppermute | solution.py:586
  202.1 8.0 %collective-permute-start.46 = (bf16[2,28,16,128]{3,2,1,0:T(8,128)(2,1)S(1)}, bf16[2,28,16,128]{3,2,1,0:T(8,128)(2,1)S(1)}, u32[]{:S(2)}, u32[]{:S(2)}) collective-permute-start(bf16[2,28,16,128]{3,2,1,0:T(8,128)(2,1)S(1)} %get-tuple-element.388.refs_1_), channel_id=1, source_target_pairs={{0,8},{1,9},{2,10},{3,11},{4,12},{5,13},{6,14},{7,15},{8,0},{9,1},... | collective-permute-start | bytes 688136 | tf_op jit(solution)/shard_map/ppermute | solution.py:586
  210.1 17.5 %collective-permute-start.48 = (bf16[4,18,16,128]{3,2,1,0:T(8,128)(2,1)S(1)}, bf16[4,18,16,128]{3,2,1,0:T(8,128)(2,1)S(1)}, u32[]{:S(2)}, u32[]{:S(2)}) collective-permute-start(bf16[4,18,16,128]{3,2,1,0:T(8,128)(2,1)S(1)} %get-tuple-element.394.refs_1_), channel_id=1, source_target_pairs={{0,4},{1,5},{2,6},{3,7},{4,0},{5,1},{6,2},{7,3},{8,12},{9,13},{10,... | collective-permute-start | bytes 884744 | tf_op jit(solution)/shard_map/ppermute | solution.py:586
  211.5 8.7 %collective-permute-start.49 = (bf16[4,10,16,128]{3,2,1,0:T(8,128)(2,1)S(1)}, bf16[4,10,16,128]{3,2,1,0:T(8,128)(2,1)S(1)}, u32[]{:S(2)}, u32[]{:S(2)}) collective-permute-start(bf16[4,10,16,128]{3,2,1,0:T(8,128)(2,1)S(1)} %get-tuple-element.395.refs_2_), channel_id=1, source_target_pairs={{0,2},{1,3},{2,0},{3,1},{4,6},{5,7},{6,4},{7,5},{8,10},{9,11},{10,... | collective-permute-start | bytes 491528 | tf_op jit(solution)/shard_map/ppermute | solution.py:586
  227.9 5.4 %collective-permute-start.52 = (bf16[16,45,16,128]{3,2,1,0:T(8,128)(2,1)S(1)}, bf16[16,45,16,128]{3,2,1,0:T(8,128)(2,1)S(1)}, u32[]{:S(2)}, u32[]{:S(2)}) collective-permute-start(bf16[16,45,16,128]{3,2,1,0:T(8,128)(2,1)S(1)} %get-tuple-element.400.refs_2_), channel_id=1, source_target_pairs={{0,1},{1,0},{2,3},{3,2},{4,5},{5,4},{6,7},{7,6},{8,9},{9,8},{10,11... | collective-permute-start | bytes 8847368 | tf_op jit(solution)/shard_map/ppermute | solution.py:586
  228.0 15.7 %collective-permute-start.53 = (bf16[8,18,16,128]{3,2,1,0:T(8,128)(2,1)S(1)}, bf16[8,18,16,128]{3,2,1,0:T(8,128)(2,1)S(1)}, u32[]{:S(2)}, u32[]{:S(2)}) collective-permute-start(bf16[8,18,16,128]{3,2,1,0:T(8,128)(2,1)S(1)} %get-tuple-element.402.refs_1_), channel_id=1, source_target_pairs={{0,2},{1,3},{2,0},{3,1},{4,6},{5,7},{6,4},{7,5},{8,10},{9,11},{10,... | collective-permute-start | bytes 1769480 | tf_op jit(solution)/shard_map/ppermute | solution.py:586
  229.6 11.1 %collective-permute-start.54 = (bf16[8,10,16,128]{3,2,1,0:T(8,128)(2,1)S(1)}, bf16[8,10,16,128]{3,2,1,0:T(8,128)(2,1)S(1)}, u32[]{:S(2)}, u32[]{:S(2)}) collective-permute-start(bf16[8,10,16,128]{3,2,1,0:T(8,128)(2,1)S(1)} %get-tuple-element.403.refs_2_), channel_id=1, source_target_pairs={{0,4},{1,5},{2,6},{3,7},{4,0},{5,1},{6,2},{7,3},{8,12},{9,13},{10,... | collective-permute-start | bytes 983048 | tf_op jit(solution)/shard_map/ppermute | solution.py:586
  243.9 3.9 %collective-permute-start.55 = (bf16[16,28,16,128]{3,2,1,0:T(8,128)(2,1)S(1)}, bf16[16,28,16,128]{3,2,1,0:T(8,128)(2,1)S(1)}, u32[]{:S(2)}, u32[]{:S(2)}) collective-permute-start(bf16[16,28,16,128]{3,2,1,0:T(8,128)(2,1)S(1)} %get-tuple-element.405.refs_2_), channel_id=1, source_target_pairs={{0,1},{1,0},{2,3},{3,2},{4,5},{5,4},{6,7},{7,6},{8,9},{9,8},{10,11... | collective-permute-start | bytes 5505032 | tf_op jit(solution)/shard_map/ppermute | solution.py:586
  (45 other events, 295.0 us)

commit v5 on v4

--- a/solution.py
+++ b/solution.py
@@ -907,10 +907,10 @@
     up.start(), three.start(), down.start()
     finish_together(order, (up, three))
     up.start(), three.start()
+    finish_together(order, (three,))
+    three.start()
     down.finish()
     down_weight_grad = order.run(assemble_rows, scalars, down.sends)[0]
-    finish_together(order, (three,))
-    three.start()
     tokens_grad = order.run(assemble_owners, "tokens_grad", F32, scalars, (t0, u2, u13))[0]
     finish_together(order, (three,))
     three.start()

time: 258 us -> 258 us (level)
  no operation moved by 1% of the time
where the time goes in v5:
time: 258 us; the launch traced here: 254 us
  Pallas kernels  105 us (41%)
  waiting for transfers between devices  87.4 us (34%)
  starting transfers between devices  57.3 us (22%)
    pallas_call x37, Pallas kernels, call(): pl.pallas_call(body, out_shape=tuple((place(i, o) for i, o in enumerate(o...  92.4 us
    ppermute x56, waiting for transfers between devices, partner(): return lax.ppermute(x, 'batch', [(i, i ^ bit) for i in range(size)])  87.4 us
    ppermute x56, starting transfers between devices, partner(): return lax.ppermute(x, 'batch', [(i, i ^ bit) for i in range(size)])  57.3 us
    pallas_call x2, Pallas kernels, call_grid(): pl.pallas_call(body, out_shape=(*outs, pltpu.VMEM(TOKEN, F32)), grid=(ste...  12.2 us
  transfers between devices with their start and end apart: 56, of which 25 were waited for; matrix products, arithmetic and copies ran while one was open for 0% of the time, Pallas kernels for 32%

profile of v5, /device:TPU:0, one launch (start us, length us, event | category | flops | bytes accessed | tf_op | source)
XLA Modules:
  0.0 253.6 jit_solution(14638778466164455414)
XLA Ops:
  0.8 1.8 pick.3
  3.2 2.6 %collective-permute-start.1 = (bf16[128,768]{1,0:T(8,128)(2,1)S(1)}, bf16[128,768]{1,0:T(8,128)(2,1)S(1)}, u32[]{:S(2)}, u32[]{:S(2)}) collective-permute-start(bf16[128,768]{1,0:T(8,128)(2,1)S(1)} %get-tuple-element.222), channel_id=1, source_target_pairs={{0,2},{1,3},{2,0},{3,1},{4,6},{5,7},{6,4},{7,5},{8,10},{9,11},{10,... | collective-permute-start | bytes 589832 | tf_op jit(solution)/shard_map/ppermute | solution.py:586
  6.5 3.0 %tables.1 = (f32[256,256]{1,0:T(8,128)S(1)}, f32[128,256]{1,0:T(8,128)S(1)}, bf16[128,512]{1,0:T(8,128)(2,1)S(1)}, bf16[2,2,512,128]{3,2,1,0:T(8,128)(2,1)S(1)},...) custom-call(f32[8,128]{1,0:T(8,128)S(1)} %get-tuple-element.217.refs_0_, s32[4]{0:T(128)S(1)} %pad_add_fusion.refs_0_.refs_1_, ...), custom_call_target="tpu_custom_call" | custom-call | tf_op jit(solution)/shard_map/tables/pallas_call | solution.py:79
  9.5 1.8 pick.4
  11.3 1.8 pick.5
  13.1 2.1 collective-permute-done.2.refs_3_.refs_4_
  15.3 1.7 collective-permute-start.4
  17.1 8.8 %attn_fwd.2 = (bf16[512,768]{1,0:T(8,128)(2,1)}, bf16[512,768]{1,0:T(8,128)(2,1)}, bf16[768,512]{1,0:T(8,128)(2,1)}, bf16[768,512]{1,0:T(8,128)(2,1)}, bf16[256,...) custom-call(f32[8,128]{1,0:T(8,128)S(1)} %get-tuple-element.228.refs, ...), custom_call_target="tpu_custom_call" | custom-call | flops 4000000000 | bytes 12000000 | tf_op jit(solution)/shard_map/attn_fwd/pallas_call | solution.py:79
  26.5 1.6 collective-permute-start.7
  28.2 8.5 %attn_fwd.3 = (bf16[512,768]{1,0:T(8,128)(2,1)}, bf16[512,768]{1,0:T(8,128)(2,1)}, bf16[768,512]{1,0:T(8,128)(2,1)}, bf16[768,512]{1,0:T(8,128)(2,1)}, bf16[256,...) custom-call(f32[8,128]{1,0:T(8,128)S(1)} %get-tuple-element.241.refs, ...), custom_call_target="tpu_custom_call" | custom-call | flops 4000000000 | bytes 12000000 | tf_op jit(solution)/shard_map/attn_fwd/pallas_call | solution.py:79
  36.9 14.6 %ffn_down.1 = (bf16[2,64,768]{2,1,0:T(8,128)(2,1)S(1)}, bf16[2,64,768]{2,1,0:T(8,128)(2,1)S(1)}, bf16[2,2,64,768]{3,2,1,0:T(8,128)(2,1)S(1)}, f32[512,768]{1,0:T...) custom-call(f32[8,128]{1,0:T(8,128)S(1)} %get-tuple-element.243.refs, ...), custom_call_target="tpu_custom_call" | custom-call | flops 8000000000 | bytes 25000000 | tf_op jit(solution)/shard_map/ffn_down/pallas_call | solution.py:79
  52.2 1.5 collective-permute-start.10
  53.8 5.4 %ffn_up_a.1 = (f32[512,768]{1,0:T(8,128)S(1)}, bf16[16,45,16,128]{3,2,1,0:T(8,128)(2,1)S(1)}, bf16[16,45,16,128]{3,2,1,0:T(8,128)(2,1)S(1)}, f32[1,1536]{1,0:T(1,128)S(1)}, f32[8,128]{1,0:T(8,128)S(1)}) custom-call(f32[8,128]{1,0:T(8,128)S(1)} %get-tuple-element.255.refs_0_, s32[4]{0:T(128)S(1)} %pad_add_fusion.refs_0_.refs_1_, ...), custom_call_target="tpu_custom_call" | custom-call | flops 4000000000 | bytes 12000000 | tf_op jit(solution)/shard_map/ffn_up_a/pallas_call | solution.py:79
  60.5 1.6 collective-permute-start.12
  62.1 2.2 collective-permute-done.10.refs_2_.refs_3_
  64.2 7.5 %ffn_up_b.1 = (f32[512,768]{1,0:T(8,128)S(1)}, bf16[2,256,768]{2,1,0:T(8,128)(2,1)S(1)}, bf16[16,45,16,128]{3,2,1,0:T(8,128)(2,1)S(1)}, bf16[16,45,16,128]{3,2,1...) custom-call(f32[8,128]{1,0:T(8,128)S(1)} %get-tuple-element.266.refs, ...), custom_call_target="tpu_custom_call", output_to_operand_aliasing={{2}: (14, {}), {3}: (15, {})} | custom-call | flops 5000000000 | bytes 14000000 | tf_op jit(solution)/shard_map/ffn_up_b/pallas_call | solution.py:79
  71.8 4.2 %collective-permute-done.11.refs_3_ = bf16[8,18,16,128]{3,2,1,0:T(8,128)(2,1)S(1)} collective-permute-done((bf16[8,18,16,128]{3,2,1,0:T(8,128)(2,1)S(1)}, bf16[8,18,16,128]{3,2,1,0:T(8,128)(2,1)S(1)}, u32[]{:S(2)}, u32[]{:S(2)}) %collective-permute-start.11) | collective-permute-done | bytes 589856 | tf_op jit(solution)/shard_map/ppermute | solution.py:586
  76.5 1.6 collective-permute-start.13
  78.1 1.5 collective-permute-start.14
  79.8 8.4 %attn_bwd.1 = (bf16[512,768]{1,0:T(8,128)(2,1)S(1)}, bf16[512,768]{1,0:T(8,128)(2,1)S(1)}, bf16[256,768]{1,0:T(8,128)(2,1)S(1)}, f32[384,128]{1,0:T(8,128)S(1)},...) custom-call(f32[8,128]{1,0:T(8,128)S(1)} %get-tuple-element.281.refs_0_, bf16[512,768]{1,0:T(8,128)(2,1)S(1)} %copy-done.32, ...), custom_call_target="tpu_custom_call" | custom-call | flops 8000000000 | bytes 12000000 | tf_op jit(solution)/shard_map/attn_bwd/pallas_call | solution.py:79
  88.3 0.9 sum_step.16
  89.2 1.6 collective-permute-start.18
  91.4 0.9 collective-permute-start.17
  92.4 17.9 %last_back.1 = (bf16[16,28,16,128]{3,2,1,0:T(8,128)(2,1)S(1)}, bf16[16,28,16,128]{3,2,1,0:T(8,128)(2,1)S(1)}, bf16[2,128,768]{2,1,0:T(8,128)(2,1)S(1)}, bf16[2,1...) custom-call(f32[8,128]{1,0:T(8,128)S(1)} %get-tuple-element.300.refs, ...), custom_call_target="tpu_custom_call" | custom-call | flops 16999999488 | bytes 30000000 | tf_op jit(solution)/shard_map/last_back/pallas_call | solution.py:79
  110.3 1.9 collective-permute-done.17.refs_4_
  112.8 1.6 collective-permute-start.20
  114.8 2.6 %collective-permute-start.21 = (bf16[1,36,16,128]{3,2,1,0:T(8,128)(2,1)S(1)}, bf16[1,36,16,128]{3,2,1,0:T(8,128)(2,1)S(1)}, u32[]{:S(2)}, u32[]{:S(2)}) collective-permute-start(bf16[1,36,16,128]{3,2,1,0:T(8,128)(2,1)S(1)} %get-tuple-element.338), channel_id=1, source_target_pairs={{0,16},{1,17},{2,18},{3,19},{4,20},{5,21},{6,22},{7,23},{8,24},{9,... | collective-permute-start | bytes 442376 | tf_op jit(solution)/shard_map/ppermute | solution.py:586
  117.4 7.0 %collective-permute-done.21.refs_6_ = bf16[1,36,16,128]{3,2,1,0:T(8,128)(2,1)S(1)} collective-permute-done((bf16[1,36,16,128]{3,2,1,0:T(8,128)(2,1)S(1)}, bf16[1,36,16,128]{3,2,1,0:T(8,128)(2,1)S(1)}, u32[]{:S(2)}, u32[]{:S(2)}) %collective-permute-start.21) | collective-permute-done | bytes 147488 | tf_op jit(solution)/shard_map/ppermute | solution.py:586
  124.4 0.9 collective-permute-done.20.refs_4_
  126.1 1.6 collective-permute-start.25
  128.6 2.6 %collective-permute-start.24 = (bf16[1,36,16,128]{3,2,1,0:T(8,128)(2,1)S(1)}, bf16[1,36,16,128]{3,2,1,0:T(8,128)(2,1)S(1)}, u32[]{:S(2)}, u32[]{:S(2)}) collective-permute-start(bf16[1,36,16,128]{3,2,1,0:T(8,128)(2,1)S(1)} %get-tuple-element.344.refs_3_), channel_id=1, source_target_pairs={{0,16},{1,17},{2,18},{3,19},{4,20},{5,21},{6,22},{7,23},{8,24},{9,... | collective-permute-start | bytes 442376 | tf_op jit(solution)/shard_map/ppermute | solution.py:586
  131.2 7.5 %collective-permute-done.24.refs_4_ = bf16[1,36,16,128]{3,2,1,0:T(8,128)(2,1)S(1)} collective-permute-done((bf16[1,36,16,128]{3,2,1,0:T(8,128)(2,1)S(1)}, bf16[1,36,16,128]{3,2,1,0:T(8,128)(2,1)S(1)}, u32[]{:S(2)}, u32[]{:S(2)}) %collective-permute-start.24) | collective-permute-done | bytes 147488 | tf_op jit(solution)/shard_map/ppermute | solution.py:586
  138.6 2.0 collective-permute-done.23.refs_2_
  141.7 1.6 collective-permute-start.27
  143.7 1.3 collective-permute-start.29
  145.0 1.8 collective-permute-start.28
  147.3 7.7 %collective-permute-done.31.refs_9_ = bf16[4,10,16,128]{3,2,1,0:T(8,128)(2,1)S(1)} collective-permute-done((bf16[4,10,16,128]{3,2,1,0:T(8,128)(2,1)S(1)}, bf16[4,10,16,128]{3,2,1,0:T(8,128)(2,1)S(1)}, u32[]{:S(2)}, u32[]{:S(2)}) %collective-permute-start.31) | collective-permute-done | bytes 163872 | tf_op jit(solution)/shard_map/ppermute | solution.py:586
  155.3 1.6 collective-permute-start.32
  157.3 1.4 collective-permute-start.35
  158.7 2.5 %collective-permute-start.36 = (bf16[2,28,16,128]{3,2,1,0:T(8,128)(2,1)S(1)}, bf16[2,28,16,128]{3,2,1,0:T(8,128)(2,1)S(1)}, u32[]{:S(2)}, u32[]{:S(2)}) collective-permute-start(bf16[2,28,16,128]{3,2,1,0:T(8,128)(2,1)S(1)} %get-tuple-element.368), channel_id=1, source_target_pairs={{0,8},{1,9},{2,10},{3,11},{4,12},{5,13},{6,14},{7,15},{8,0},{9,1},... | collective-permute-start | bytes 688136 | tf_op jit(solution)/shard_map/ppermute | solution.py:586
  161.7 8.0 %collective-permute-done.33.refs_3_ = bf16[1,45,16,128]{3,2,1,0:T(8,128)(2,1)S(1)} collective-permute-done((bf16[1,45,16,128]{3,2,1,0:T(8,128)(2,1)S(1)}, bf16[1,45,16,128]{3,2,1,0:T(8,128)(2,1)S(1)}, u32[]{:S(2)}, u32[]{:S(2)}) %collective-permute-start.33) | collective-permute-done | bytes 184352 | tf_op jit(solution)/shard_map/ppermute | solution.py:586
  169.7 1.4 collective-permute-done.35.refs_7_
  171.2 1.2 collective-permute-start.40
  173.1 2.2 collective-permute-start.38
  176.0 1.5 layer_output.1
  177.5 8.8 %collective-permute-done.39.refs_4_ = bf16[1,28,16,128]{3,2,1,0:T(8,128)(2,1)S(1)} collective-permute-done((bf16[1,28,16,128]{3,2,1,0:T(8,128)(2,1)S(1)}, bf16[1,28,16,128]{3,2,1,0:T(8,128)(2,1)S(1)}, u32[]{:S(2)}, u32[]{:S(2)}) %collective-permute-start.39) | collective-permute-done | bytes 114720 | tf_op jit(solution)/shard_map/ppermute | solution.py:586
  187.4 1.6 collective-permute-start.43
  189.4 2.6 %collective-permute-start.44 = (bf16[1,28,16,128]{3,2,1,0:T(8,128)(2,1)S(1)}, bf16[1,28,16,128]{3,2,1,0:T(8,128)(2,1)S(1)}, u32[]{:S(2)}, u32[]{:S(2)}) collective-permute-start(bf16[1,28,16,128]{3,2,1,0:T(8,128)(2,1)S(1)} %get-tuple-element.384.refs_5_), channel_id=1, source_target_pairs={{0,16},{1,17},{2,18},{3,19},{4,20},{5,21},{6,22},{7,23},{8,24},{9,... | collective-permute-start | bytes 344072 | tf_op jit(solution)/shard_map/ppermute | solution.py:586
  192.1 5.7 %collective-permute-done.44.refs_6_ = bf16[1,28,16,128]{3,2,1,0:T(8,128)(2,1)S(1)} collective-permute-done((bf16[1,28,16,128]{3,2,1,0:T(8,128)(2,1)S(1)}, bf16[1,28,16,128]{3,2,1,0:T(8,128)(2,1)S(1)}, u32[]{:S(2)}, u32[]{:S(2)}) %collective-permute-start.44) | collective-permute-done | bytes 114720 | tf_op jit(solution)/shard_map/ppermute | solution.py:586
  198.0 1.9 collective-permute-done.43.refs_4_
  200.1 0.9 collective-permute-start.51
  201.0 1.1 collective-permute-start.50
  202.1 2.0 collective-permute-start.45
  204.1 6.0 %collective-permute-done.45.refs_2_ = bf16[2,28,16,128]{3,2,1,0:T(8,128)(2,1)S(1)} collective-permute-done((bf16[2,28,16,128]{3,2,1,0:T(8,128)(2,1)S(1)}, bf16[2,28,16,128]{3,2,1,0:T(8,128)(2,1)S(1)}, u32[]{:S(2)}, u32[]{:S(2)}) %collective-permute-start.45) | collective-permute-done | bytes 229408 | tf_op jit(solution)/shard_map/ppermute | solution.py:586
  210.1 1.4 collective-permute-start.48
  212.2 4.8 %assemble_rows.1 = (f32[3072,768]{1,0:T(8,128)}, f32[8,128]{1,0:T(8,128)S(1)}) custom-call(f32[8,128]{1,0:T(8,128)S(1)} %get-tuple-element.387.refs_0_, s32[4]{0:T(128)S(1)} %pad_add_fusion.refs_0_.refs_1_, bf16[16,36,16,128]{3,2,1,0:T(8,128)(2,1)S(1)} %get-tuple-element.388.refs_2_, bf16[16,36,16,128]{3,2,1,0:T(8,128)(2,1)S(1)} %collective-permute-done.46.refs_3_), custom_call_target="tpu_custom_call" | custom-call | bytes 14000000 | tf_op jit(solution)/shard_map/assemble_rows/pallas_call | solution.py:106
  217.1 2.4 tokens_grad.1
  220.2 7.4 %collective-permute-done.48.refs_3_ = bf16[4,18,16,128]{3,2,1,0:T(8,128)(2,1)S(1)} collective-permute-done((bf16[4,18,16,128]{3,2,1,0:T(8,128)(2,1)S(1)}, bf16[4,18,16,128]{3,2,1,0:T(8,128)(2,1)S(1)}, u32[]{:S(2)}, u32[]{:S(2)}) %collective-permute-start.48) | collective-permute-done | bytes 294944 | tf_op jit(solution)/shard_map/ppermute | solution.py:586
  228.0 1.6 collective-permute-start.53
  230.1 3.3 %collective-permute-done.52.refs_3_ = bf16[16,45,16,128]{3,2,1,0:T(8,128)(2,1)S(1)} collective-permute-done((bf16[16,45,16,128]{3,2,1,0:T(8,128)(2,1)S(1)}, bf16[16,45,16,128]{3,2,1,0:T(8,128)(2,1)S(1)}, u32[]{:S(2)}, u32[]{:S(2)}) %collective-permute-start.52) | collective-permute-done | bytes 2949152 | tf_op jit(solution)/shard_map/ppermute | solution.py:586
  233.4 7.3 %assemble_up.1 = (f32[768,3072]{1,0:T(8,128)}, f32[768,768]{1,0:T(8,128)}, f32[8,128]{1,0:T(8,128)S(1)}) custom-call(f32[8,128]{1,0:T(8,128)S(1)} %get-tuple-element.399.refs_0_, s32[4]{0:T(128)S(1)} %pad_add_fusion.refs_0_.refs_1_, bf16[16,45,16,128]{3,2,1,0:T(8,128)(2,1)S(1)} %get-tuple-element.400.refs_2_, ...), custom_call_target="tpu_custom_call" | custom-call | bytes 18000000 | tf_op jit(solution)/shard_map/assemble_up/pallas_call | solution.py:106
  240.7 3.1 %collective-permute-done.53.refs_3_ = bf16[8,18,16,128]{3,2,1,0:T(8,128)(2,1)S(1)} collective-permute-done((bf16[8,18,16,128]{3,2,1,0:T(8,128)(2,1)S(1)}, bf16[8,18,16,128]{3,2,1,0:T(8,128)(2,1)S(1)}, u32[]{:S(2)}, u32[]{:S(2)}) %collective-permute-start.53) | collective-permute-done | bytes 589856 | tf_op jit(solution)/shard_map/ppermute | solution.py:586
  244.0 3.8 %collective-permute-done.55.refs_3_ = bf16[16,28,16,128]{3,2,1,0:T(8,128)(2,1)S(1)} collective-permute-done((bf16[16,28,16,128]{3,2,1,0:T(8,128)(2,1)S(1)}, bf16[16,28,16,128]{3,2,1,0:T(8,128)(2,1)S(1)}, u32[]{:S(2)}, u32[]{:S(2)}) %collective-permute-start.55) | collective-permute-done | bytes 1835040 | tf_op jit(solution)/shard_map/ppermute | solution.py:586
  247.7 4.3 %assemble_three.1 = (f32[768,768]{1,0:T(8,128)}, f32[768,768]{1,0:T(8,128)}, f32[768,768]{1,0:T(8,128)}, f32[12,64,64]{2,1,0:T(8,128)}, f32[16,768]{1,0:T(8,128)S(1)}, /*index=5*/f32[8,128]{1,0:T(8,128)}) custom-call(f32[8,128]{1,0:T(8,128)S(1)} %get-tuple-element.404.refs_0_, s32[4]{0:T(128)S(1)} %pad_add_fusion.refs_0_.refs_1_, ...), custom_call_target="tpu_custom_call" | custom-call | bytes 11000000 | tf_op jit(solution)/shard_map/assemble_three/pallas_call | solution.py:79
  (199 shorter events, 18.5 us)
Async XLA Ops:
  0.8 16.2 %copy-start.6 = (bf16[768,768]{1,0:T(8,128)(2,1)S(1)}, bf16[768,768]{1,0:T(8,128)(2,1)}, u32[]{:S(2)}) copy-start(bf16[768,768]{1,0:T(8,128)(2,1)} %refs_29_.1) | copy-start | bytes 3538948
  0.8 16.2 %copy-start.14 = (f32[12,64,64]{2,1,0:T(8,128)S(1)}, f32[12,64,64]{2,1,0:T(8,128)}, u32[]{:S(2)}) copy-start(f32[12,64,64]{2,1,0:T(8,128)} %refs_14_.1) | copy-start | bytes 589828
  2.7 10.4 %collective-permute-start = (bf16[128,768]{1,0:T(8,128)(2,1)S(1)}, bf16[128,768]{1,0:T(8,128)(2,1)S(1)}, u32[]{:S(2)}, u32[]{:S(2)}) collective-permute-start(bf16[128,768]{1,0:T(8,128)(2,1)S(1)} %get-tuple-element.221), channel_id=1, source_target_pairs={{0,1},{1,0},{2,3},{3,2},{4,5},{5,4},{6,7},{7,6},{8,9},{9,8},{10,11... | collective-permute-start | bytes 589832 | tf_op jit(solution)/shard_map/ppermute | solution.py:586
  3.2 9.9 %collective-permute-start.1 = (bf16[128,768]{1,0:T(8,128)(2,1)S(1)}, bf16[128,768]{1,0:T(8,128)(2,1)S(1)}, u32[]{:S(2)}, u32[]{:S(2)}) collective-permute-start(bf16[128,768]{1,0:T(8,128)(2,1)S(1)} %get-tuple-element.222), channel_id=1, source_target_pairs={{0,2},{1,3},{2,0},{3,1},{4,6},{5,7},{6,4},{7,5},{8,10},{9,11},{10,... | collective-permute-start | bytes 589832 | tf_op jit(solution)/shard_map/ppermute | solution.py:586
  5.7 9.4 %collective-permute-start.2 = (bf16[128,768]{1,0:T(8,128)(2,1)S(1)}, bf16[128,768]{1,0:T(8,128)(2,1)S(1)}, u32[]{:S(2)}, u32[]{:S(2)}) collective-permute-start(bf16[128,768]{1,0:T(8,128)(2,1)S(1)} %get-tuple-element.223), channel_id=1, source_target_pairs={{0,3},{1,2},{2,1},{3,0},{4,7},{5,6},{6,5},{7,4},{8,11},{9,10},{10,... | collective-permute-start | bytes 589832 | tf_op jit(solution)/shard_map/ppermute | solution.py:586
  9.4 70.2 %copy-start.12 = (bf16[2,2,512,128]{3,2,1,0:T(8,128)(2,1)}, bf16[2,2,512,128]{3,2,1,0:T(8,128)(2,1)S(1)}, u32[]{:S(2)}) copy-start(bf16[2,2,512,128]{3,2,1,0:T(8,128)(2,1)S(1)} %get-tuple-element.232.refs_11_.refs_10_) | copy-start | bytes 1572868
  9.4 70.1 %copy-start.18 = (f32[128,256]{1,0:T(8,128)}, f32[128,256]{1,0:T(8,128)S(1)}, u32[]{:S(2)}) copy-start(f32[128,256]{1,0:T(8,128)S(1)} %get-tuple-element.292.refs_12_.refs_13_) | copy-start | bytes 393220
  9.5 70.1 %copy-start.20 = (bf16[128,512]{1,0:T(8,128)(2,1)}, bf16[128,512]{1,0:T(8,128)(2,1)S(1)}, u32[]{:S(2)}) copy-start(bf16[128,512]{1,0:T(8,128)(2,1)S(1)} %get-tuple-element.291.refs_11_.refs_12_) | copy-start | bytes 393220
  15.2 10.7 %collective-permute-start.3 = (bf16[128,768]{1,0:T(8,128)(2,1)S(1)}, bf16[128,768]{1,0:T(8,128)(2,1)S(1)}, u32[]{:S(2)}, u32[]{:S(2)}) collective-permute-start(bf16[128,768]{1,0:T(8,128)(2,1)S(1)} %get-tuple-element.234), channel_id=1, source_target_pairs={{0,1},{1,0},{2,3},{3,2},{4,5},{5,4},{6,7},{7,6},{8,9},{9,8},{10,11... | collective-permute-start | bytes 589832 | tf_op jit(solution)/shard_map/ppermute | solution.py:586
  15.3 10.6 %collective-permute-start.4 = (bf16[128,768]{1,0:T(8,128)(2,1)S(1)}, bf16[128,768]{1,0:T(8,128)(2,1)S(1)}, u32[]{:S(2)}, u32[]{:S(2)}) collective-permute-start(bf16[128,768]{1,0:T(8,128)(2,1)S(1)} %get-tuple-element.235), channel_id=1, source_target_pairs={{0,2},{1,3},{2,0},{3,1},{4,6},{5,7},{6,4},{7,5},{8,10},{9,11},{10,... | collective-permute-start | bytes 589832 | tf_op jit(solution)/shard_map/ppermute | solution.py:586
  17.0 9.1 %collective-permute-start.5 = (bf16[128,768]{1,0:T(8,128)(2,1)S(1)}, bf16[128,768]{1,0:T(8,128)(2,1)S(1)}, u32[]{:S(2)}, u32[]{:S(2)}) collective-permute-start(bf16[128,768]{1,0:T(8,128)(2,1)S(1)} %get-tuple-element.236), channel_id=1, source_target_pairs={{0,3},{1,2},{2,1},{3,0},{4,7},{5,6},{6,5},{7,4},{8,11},{9,10},{10,... | collective-permute-start | bytes 589832 | tf_op jit(solution)/shard_map/ppermute | solution.py:586
  26.2 10.6 %collective-permute-start.6 = (bf16[2,64,768]{2,1,0:T(8,128)(2,1)S(1)}, bf16[2,64,768]{2,1,0:T(8,128)(2,1)S(1)}, u32[]{:S(2)}, u32[]{:S(2)}) collective-permute-start(bf16[2,64,768]{2,1,0:T(8,128)(2,1)S(1)} %get-tuple-element.249), channel_id=1, source_target_pairs={{0,1},{1,0},{2,3},{3,2},{4,5},{5,4},{6,7},{7,6},{8,9},{9,8},{10,11... | collective-permute-start | bytes 589832 | tf_op jit(solution)/shard_map/ppermute | solution.py:586
  26.5 10.2 %collective-permute-start.7 = (bf16[2,64,768]{2,1,0:T(8,128)(2,1)S(1)}, bf16[2,64,768]{2,1,0:T(8,128)(2,1)S(1)}, u32[]{:S(2)}, u32[]{:S(2)}) collective-permute-start(bf16[2,64,768]{2,1,0:T(8,128)(2,1)S(1)} %get-tuple-element.250), channel_id=1, source_target_pairs={{0,2},{1,3},{2,0},{3,1},{4,6},{5,7},{6,4},{7,5},{8,10},{9,11},{10,... | collective-permute-start | bytes 589832 | tf_op jit(solution)/shard_map/ppermute | solution.py:586
  28.2 8.7 %collective-permute-start.8 = (bf16[2,64,768]{2,1,0:T(8,128)(2,1)S(1)}, bf16[2,64,768]{2,1,0:T(8,128)(2,1)S(1)}, u32[]{:S(2)}, u32[]{:S(2)}) collective-permute-start(bf16[2,64,768]{2,1,0:T(8,128)(2,1)S(1)} %get-tuple-element.251), channel_id=1, source_target_pairs={{0,3},{1,2},{2,1},{3,0},{4,7},{5,6},{6,5},{7,4},{8,11},{9,10},{10,... | collective-permute-start | bytes 589832 | tf_op jit(solution)/shard_map/ppermute | solution.py:586
  36.7 14.8 %copy-start.45 = (f32[12,1,256]{2,1,0:T(1,128)}, f32[12,1,256]{2,1,0:T(1,128)S(1)}, u32[]{:S(2)}) copy-start(f32[12,1,256]{2,1,0:T(1,128)S(1)} %get-tuple-element.308.refs_9_) | copy-start | bytes 36868
  51.5 7.6 %collective-permute-start.9 = (bf16[16,36,16,128]{3,2,1,0:T(8,128)(2,1)S(1)}, bf16[16,36,16,128]{3,2,1,0:T(8,128)(2,1)S(1)}, u32[]{:S(2)}, u32[]{:S(2)}) collective-permute-start(bf16[16,36,16,128]{3,2,1,0:T(8,128)(2,1)S(1)} %get-tuple-element.262), channel_id=1, source_target_pairs={{0,1},{1,0},{2,3},{3,2},{4,5},{5,4},{6,7},{7,6},{8,9},{9,8},{10,11... | collective-permute-start | bytes 7077896 | tf_op jit(solution)/shard_map/ppermute | solution.py:586
  52.2 12.0 %collective-permute-start.10 = (bf16[2,2,64,768]{3,2,1,0:T(8,128)(2,1)S(1)}, bf16[2,2,64,768]{3,2,1,0:T(8,128)(2,1)S(1)}, u32[]{:S(2)}, u32[]{:S(2)}) collective-permute-start(bf16[2,2,64,768]{3,2,1,0:T(8,128)(2,1)S(1)} %get-tuple-element.265), channel_id=1, source_target_pairs={{0,2},{1,3},{2,0},{3,1},{4,6},{5,7},{6,4},{7,5},{8,10},{9,11},{10,... | collective-permute-start | bytes 1179656 | tf_op jit(solution)/shard_map/ppermute | solution.py:586
  59.9 16.0 %collective-permute-start.11 = (bf16[8,18,16,128]{3,2,1,0:T(8,128)(2,1)S(1)}, bf16[8,18,16,128]{3,2,1,0:T(8,128)(2,1)S(1)}, u32[]{:S(2)}, u32[]{:S(2)}) collective-permute-start(bf16[8,18,16,128]{3,2,1,0:T(8,128)(2,1)S(1)} %get-tuple-element.277), channel_id=1, source_target_pairs={{0,2},{1,3},{2,0},{3,1},{4,6},{5,7},{6,4},{7,5},{8,10},{9,11},{10,... | collective-permute-start | bytes 1769480 | tf_op jit(solution)/shard_map/ppermute | solution.py:586
  60.5 15.5 %collective-permute-start.12 = (bf16[8,18,16,128]{3,2,1,0:T(8,128)(2,1)S(1)}, bf16[8,18,16,128]{3,2,1,0:T(8,128)(2,1)S(1)}, u32[]{:S(2)}, u32[]{:S(2)}) collective-permute-start(bf16[8,18,16,128]{3,2,1,0:T(8,128)(2,1)S(1)} %get-tuple-element.278), channel_id=1, source_target_pairs={{0,4},{1,5},{2,6},{3,7},{4,0},{5,1},{6,2},{7,3},{8,12},{9,13},{10,... | collective-permute-start | bytes 1769480 | tf_op jit(solution)/shard_map/ppermute | solution.py:586
  76.4 11.8 %collective-permute-start.15 = (bf16[16,45,16,128]{3,2,1,0:T(8,128)(2,1)S(1)}, bf16[16,45,16,128]{3,2,1,0:T(8,128)(2,1)S(1)}, u32[]{:S(2)}, u32[]{:S(2)}) collective-permute-start(bf16[16,45,16,128]{3,2,1,0:T(8,128)(2,1)S(1)} %get-tuple-element.299), channel_id=1, source_target_pairs={{0,1},{1,0},{2,3},{3,2},{4,5},{5,4},{6,7},{7,6},{8,9},{9,8},{10,11... | collective-permute-start | bytes 8847368 | tf_op jit(solution)/shard_map/ppermute | solution.py:586
  76.5 11.7 %collective-permute-start.13 = (bf16[4,18,16,128]{3,2,1,0:T(8,128)(2,1)S(1)}, bf16[4,18,16,128]{3,2,1,0:T(8,128)(2,1)S(1)}, u32[]{:S(2)}, u32[]{:S(2)}) collective-permute-start(bf16[4,18,16,128]{3,2,1,0:T(8,128)(2,1)S(1)} %get-tuple-element.296), channel_id=1, source_target_pairs={{0,4},{1,5},{2,6},{3,7},{4,0},{5,1},{6,2},{7,3},{8,12},{9,13},{10,... | collective-permute-start | bytes 884744 | tf_op jit(solution)/shard_map/ppermute | solution.py:586
  78.1 10.0 %collective-permute-start.14 = (bf16[4,18,16,128]{3,2,1,0:T(8,128)(2,1)S(1)}, bf16[4,18,16,128]{3,2,1,0:T(8,128)(2,1)S(1)}, u32[]{:S(2)}, u32[]{:S(2)}) collective-permute-start(bf16[4,18,16,128]{3,2,1,0:T(8,128)(2,1)S(1)} %get-tuple-element.297), channel_id=1, source_target_pairs={{0,2},{1,3},{2,0},{3,1},{4,6},{5,7},{6,4},{7,5},{8,10},{9,11},{10,... | collective-permute-start | bytes 884744 | tf_op jit(solution)/shard_map/ppermute | solution.py:586
  79.7 12.5 %copy-start.30 = (bf16[768,512]{1,0:T(8,128)(2,1)S(1)}, bf16[768,512]{1,0:T(8,128)(2,1)}, u32[]{:S(2)}) copy-start(bf16[768,512]{1,0:T(8,128)(2,1)} %get-tuple-element.303.refs_4_) | copy-start | bytes 2359300
  89.2 21.1 %collective-permute-start.18 = (bf16[2,36,16,128]{3,2,1,0:T(8,128)(2,1)S(1)}, bf16[2,36,16,128]{3,2,1,0:T(8,128)(2,1)S(1)}, u32[]{:S(2)}, u32[]{:S(2)}) collective-permute-start(bf16[2,36,16,128]{3,2,1,0:T(8,128)(2,1)S(1)} %get-tuple-element.329), channel_id=1, source_target_pairs={{0,8},{1,9},{2,10},{3,11},{4,12},{5,13},{6,14},{7,15},{8,0},{9,1},... | collective-permute-start | bytes 884744 | tf_op jit(solution)/shard_map/ppermute | solution.py:586
  90.8 19.5 %collective-permute-start.16 = (bf16[8,18,16,128]{3,2,1,0:T(8,128)(2,1)S(1)}, bf16[8,18,16,128]{3,2,1,0:T(8,128)(2,1)S(1)}, u32[]{:S(2)}, u32[]{:S(2)}) collective-permute-start(bf16[8,18,16,128]{3,2,1,0:T(8,128)(2,1)S(1)} %get-tuple-element.326), channel_id=1, source_target_pairs={{0,2},{1,3},{2,0},{3,1},{4,6},{5,7},{6,4},{7,5},{8,10},{9,11},{10,... | collective-permute-start | bytes 1769480 | tf_op jit(solution)/shard_map/ppermute | solution.py:586
  91.4 20.9 %collective-permute-start.17 = (bf16[8,27,16,128]{3,2,1,0:T(8,128)(2,1)S(1)}, bf16[8,27,16,128]{3,2,1,0:T(8,128)(2,1)S(1)}, u32[]{:S(2)}, u32[]{:S(2)}) collective-permute-start(bf16[8,27,16,128]{3,2,1,0:T(8,128)(2,1)S(1)} %get-tuple-element.327), channel_id=1, source_target_pairs={{0,4},{1,5},{2,6},{3,7},{4,0},{5,1},{6,2},{7,3},{8,12},{9,13},{10,... | collective-permute-start | bytes 2654216 | tf_op jit(solution)/shard_map/ppermute | solution.py:586
  112.7 12.7 %collective-permute-start.22 = (bf16[16,28,16,128]{3,2,1,0:T(8,128)(2,1)S(1)}, bf16[16,28,16,128]{3,2,1,0:T(8,128)(2,1)S(1)}, u32[]{:S(2)}, u32[]{:S(2)}) collective-permute-start(bf16[16,28,16,128]{3,2,1,0:T(8,128)(2,1)S(1)} %get-tuple-element.340), channel_id=1, source_target_pairs={{0,1},{1,0},{2,3},{3,2},{4,5},{5,4},{6,7},{7,6},{8,9},{9,8},{10,11... | collective-permute-start | bytes 5505032 | tf_op jit(solution)/shard_map/ppermute | solution.py:586
  112.8 12.6 %collective-permute-start.20 = (bf16[4,27,16,128]{3,2,1,0:T(8,128)(2,1)S(1)}, bf16[4,27,16,128]{3,2,1,0:T(8,128)(2,1)S(1)}, u32[]{:S(2)}, u32[]{:S(2)}) collective-permute-start(bf16[4,27,16,128]{3,2,1,0:T(8,128)(2,1)S(1)} %get-tuple-element.336), channel_id=1, source_target_pairs={{0,2},{1,3},{2,0},{3,1},{4,6},{5,7},{6,4},{7,5},{8,10},{9,11},{10,... | collective-permute-start | bytes 1327112 | tf_op jit(solution)/shard_map/ppermute | solution.py:586
  114.3 10.1 %collective-permute-start.19 = (bf16[4,18,16,128]{3,2,1,0:T(8,128)(2,1)S(1)}, bf16[4,18,16,128]{3,2,1,0:T(8,128)(2,1)S(1)}, u32[]{:S(2)}, u32[]{:S(2)}) collective-permute-start(bf16[4,18,16,128]{3,2,1,0:T(8,128)(2,1)S(1)} %get-tuple-element.335), channel_id=1, source_target_pairs={{0,4},{1,5},{2,6},{3,7},{4,0},{5,1},{6,2},{7,3},{8,12},{9,13},{10,... | collective-permute-start | bytes 884744 | tf_op jit(solution)/shard_map/ppermute | solution.py:586
  114.8 9.6 %collective-permute-start.21 = (bf16[1,36,16,128]{3,2,1,0:T(8,128)(2,1)S(1)}, bf16[1,36,16,128]{3,2,1,0:T(8,128)(2,1)S(1)}, u32[]{:S(2)}, u32[]{:S(2)}) collective-permute-start(bf16[1,36,16,128]{3,2,1,0:T(8,128)(2,1)S(1)} %get-tuple-element.338), channel_id=1, source_target_pairs={{0,16},{1,17},{2,18},{3,19},{4,20},{5,21},{6,22},{7,23},{8,24},{9,... | collective-permute-start | bytes 442376 | tf_op jit(solution)/shard_map/ppermute | solution.py:586
  126.1 15.0 %collective-permute-start.25 = (bf16[8,18,16,128]{3,2,1,0:T(8,128)(2,1)S(1)}, bf16[8,18,16,128]{3,2,1,0:T(8,128)(2,1)S(1)}, u32[]{:S(2)}, u32[]{:S(2)}) collective-permute-start(bf16[8,18,16,128]{3,2,1,0:T(8,128)(2,1)S(1)} %get-tuple-element.347), channel_id=1, source_target_pairs={{0,2},{1,3},{2,0},{3,1},{4,6},{5,7},{6,4},{7,5},{8,10},{9,11},{10,... | collective-permute-start | bytes 1769480 | tf_op jit(solution)/shard_map/ppermute | solution.py:586
  127.6 13.0 %collective-permute-start.23 = (bf16[2,45,16,128]{3,2,1,0:T(8,128)(2,1)S(1)}, bf16[2,45,16,128]{3,2,1,0:T(8,128)(2,1)S(1)}, u32[]{:S(2)}, u32[]{:S(2)}) collective-permute-start(bf16[2,45,16,128]{3,2,1,0:T(8,128)(2,1)S(1)} %get-tuple-element.343), channel_id=1, source_target_pairs={{0,8},{1,9},{2,10},{3,11},{4,12},{5,13},{6,14},{7,15},{8,0},{9,1},... | collective-permute-start | bytes 1105928 | tf_op jit(solution)/shard_map/ppermute | solution.py:586
  128.1 10.6 %collective-permute-start.26 = (bf16[8,10,16,128]{3,2,1,0:T(8,128)(2,1)S(1)}, bf16[8,10,16,128]{3,2,1,0:T(8,128)(2,1)S(1)}, u32[]{:S(2)}, u32[]{:S(2)}) collective-permute-start(bf16[8,10,16,128]{3,2,1,0:T(8,128)(2,1)S(1)} %get-tuple-element.348), channel_id=1, source_target_pairs={{0,4},{1,5},{2,6},{3,7},{4,0},{5,1},{6,2},{7,3},{8,12},{9,13},{10,... | collective-permute-start | bytes 983048 | tf_op jit(solution)/shard_map/ppermute | solution.py:586
  128.6 10.0 %collective-permute-start.24 = (bf16[1,36,16,128]{3,2,1,0:T(8,128)(2,1)S(1)}, bf16[1,36,16,128]{3,2,1,0:T(8,128)(2,1)S(1)}, u32[]{:S(2)}, u32[]{:S(2)}) collective-permute-start(bf16[1,36,16,128]{3,2,1,0:T(8,128)(2,1)S(1)} %get-tuple-element.344.refs_3_), channel_id=1, source_target_pairs={{0,16},{1,17},{2,18},{3,19},{4,20},{5,21},{6,22},{7,23},{8,24},{9,... | collective-permute-start | bytes 442376 | tf_op jit(solution)/shard_map/ppermute | solution.py:586
  141.7 13.4 %collective-permute-start.27 = (bf16[2,128,768]{2,1,0:T(8,128)(2,1)S(1)}, bf16[2,128,768]{2,1,0:T(8,128)(2,1)S(1)}, u32[]{:S(2)}, u32[]{:S(2)}) collective-permute-start(bf16[2,128,768]{2,1,0:T(8,128)(2,1)S(1)} %get-tuple-element.352), channel_id=1, source_target_pairs={{0,2},{1,3},{2,0},{3,1},{4,6},{5,7},{6,4},{7,5},{8,10},{9,11},{10,... | collective-permute-start | bytes 1179656 | tf_op jit(solution)/shard_map/ppermute | solution.py:586
  143.2 11.8 %collective-permute-start.30 = (bf16[4,18,16,128]{3,2,1,0:T(8,128)(2,1)S(1)}, bf16[4,18,16,128]{3,2,1,0:T(8,128)(2,1)S(1)}, u32[]{:S(2)}, u32[]{:S(2)}) collective-permute-start(bf16[4,18,16,128]{3,2,1,0:T(8,128)(2,1)S(1)} %get-tuple-element.358), channel_id=1, source_target_pairs={{0,4},{1,5},{2,6},{3,7},{4,0},{5,1},{6,2},{7,3},{8,12},{9,13},{10,... | collective-permute-start | bytes 884744 | tf_op jit(solution)/shard_map/ppermute | solution.py:586
  143.7 11.3 %collective-permute-start.29 = (bf16[2,36,16,128]{3,2,1,0:T(8,128)(2,1)S(1)}, bf16[2,36,16,128]{3,2,1,0:T(8,128)(2,1)S(1)}, u32[]{:S(2)}, u32[]{:S(2)}) collective-permute-start(bf16[2,36,16,128]{3,2,1,0:T(8,128)(2,1)S(1)} %get-tuple-element.355.refs_4_), channel_id=1, source_target_pairs={{0,8},{1,9},{2,10},{3,11},{4,12},{5,13},{6,14},{7,15},{8,0},{9,1},... | collective-permute-start | bytes 884744 | tf_op jit(solution)/shard_map/ppermute | solution.py:586
  145.0 10.0 %collective-permute-start.28 = (bf16[1,45,16,128]{3,2,1,0:T(8,128)(2,1)S(1)}, bf16[1,45,16,128]{3,2,1,0:T(8,128)(2,1)S(1)}, u32[]{:S(2)}, u32[]{:S(2)}) collective-permute-start(bf16[1,45,16,128]{3,2,1,0:T(8,128)(2,1)S(1)} %get-tuple-element.354), channel_id=1, source_target_pairs={{0,16},{1,17},{2,18},{3,19},{4,20},{5,21},{6,22},{7,23},{8,24},{9,... | collective-permute-start | bytes 552968 | tf_op jit(solution)/shard_map/ppermute | solution.py:586
  146.8 8.3 %collective-permute-start.31 = (bf16[4,10,16,128]{3,2,1,0:T(8,128)(2,1)S(1)}, bf16[4,10,16,128]{3,2,1,0:T(8,128)(2,1)S(1)}, u32[]{:S(2)}, u32[]{:S(2)}) collective-permute-start(bf16[4,10,16,128]{3,2,1,0:T(8,128)(2,1)S(1)} %get-tuple-element.359), channel_id=1, source_target_pairs={{0,2},{1,3},{2,0},{3,1},{4,6},{5,7},{6,4},{7,5},{8,10},{9,11},{10,... | collective-permute-start | bytes 491528 | tf_op jit(solution)/shard_map/ppermute | solution.py:586
  155.0 18.1 %copy-start.17 = (bf16[2,2,64,768]{3,2,1,0:T(8,128)(2,1)S(1)}, bf16[2,2,64,768]{3,2,1,0:T(8,128)(2,1)}, u32[]{:S(2)}) copy-start(bf16[2,2,64,768]{3,2,1,0:T(8,128)(2,1)} %copy-done.16) | copy-start | bytes 1179652
  155.3 15.8 %collective-permute-start.32 = (bf16[2,128,768]{2,1,0:T(8,128)(2,1)S(1)}, bf16[2,128,768]{2,1,0:T(8,128)(2,1)S(1)}, u32[]{:S(2)}, u32[]{:S(2)}) collective-permute-start(bf16[2,128,768]{2,1,0:T(8,128)(2,1)S(1)} %get-tuple-element.363), channel_id=1, source_target_pairs={{0,2},{1,3},{2,0},{3,1},{4,6},{5,7},{6,4},{7,5},{8,10},{9,11},{10,... | collective-permute-start | bytes 1179656 | tf_op jit(solution)/shard_map/ppermute | solution.py:586
  156.8 12.8 %collective-permute-start.34 = (bf16[4,18,16,128]{3,2,1,0:T(8,128)(2,1)S(1)}, bf16[4,18,16,128]{3,2,1,0:T(8,128)(2,1)S(1)}, u32[]{:S(2)}, u32[]{:S(2)}) collective-permute-start(bf16[4,18,16,128]{3,2,1,0:T(8,128)(2,1)S(1)} %get-tuple-element.365.refs_4_), channel_id=1, source_target_pairs={{0,4},{1,5},{2,6},{3,7},{4,0},{5,1},{6,2},{7,3},{8,12},{9,13},{10,... | collective-permute-start | bytes 884744 | tf_op jit(solution)/shard_map/ppermute | solution.py:586
  157.3 13.7 %collective-permute-start.35 = (bf16[4,18,16,128]{3,2,1,0:T(8,128)(2,1)S(1)}, bf16[4,18,16,128]{3,2,1,0:T(8,128)(2,1)S(1)}, u32[]{:S(2)}, u32[]{:S(2)}) collective-permute-start(bf16[4,18,16,128]{3,2,1,0:T(8,128)(2,1)S(1)} %get-tuple-element.366.refs_5_), channel_id=1, source_target_pairs={{0,2},{1,3},{2,0},{3,1},{4,6},{5,7},{6,4},{7,5},{8,10},{9,11},{10,... | collective-permute-start | bytes 884744 | tf_op jit(solution)/shard_map/ppermute | solution.py:586
  158.7 11.0 %collective-permute-start.36 = (bf16[2,28,16,128]{3,2,1,0:T(8,128)(2,1)S(1)}, bf16[2,28,16,128]{3,2,1,0:T(8,128)(2,1)S(1)}, u32[]{:S(2)}, u32[]{:S(2)}) collective-permute-start(bf16[2,28,16,128]{3,2,1,0:T(8,128)(2,1)S(1)} %get-tuple-element.368), channel_id=1, source_target_pairs={{0,8},{1,9},{2,10},{3,11},{4,12},{5,13},{6,14},{7,15},{8,0},{9,1},... | collective-permute-start | bytes 688136 | tf_op jit(solution)/shard_map/ppermute | solution.py:586
  161.3 8.4 %collective-permute-start.33 = (bf16[1,45,16,128]{3,2,1,0:T(8,128)(2,1)S(1)}, bf16[1,45,16,128]{3,2,1,0:T(8,128)(2,1)S(1)}, u32[]{:S(2)}, u32[]{:S(2)}) collective-permute-start(bf16[1,45,16,128]{3,2,1,0:T(8,128)(2,1)S(1)} %get-tuple-element.364.refs_2_), channel_id=1, source_target_pairs={{0,16},{1,17},{2,18},{3,19},{4,20},{5,21},{6,22},{7,23},{8,24},{9,... | collective-permute-start | bytes 552968 | tf_op jit(solution)/shard_map/ppermute | solution.py:586
  171.2 15.8 %collective-permute-start.40 = (bf16[8,18,16,128]{3,2,1,0:T(8,128)(2,1)S(1)}, bf16[8,18,16,128]{3,2,1,0:T(8,128)(2,1)S(1)}, u32[]{:S(2)}, u32[]{:S(2)}) collective-permute-start(bf16[8,18,16,128]{3,2,1,0:T(8,128)(2,1)S(1)} %get-tuple-element.379.refs_5_), channel_id=1, source_target_pairs={{0,2},{1,3},{2,0},{3,1},{4,6},{5,7},{6,4},{7,5},{8,10},{9,11},{10,... | collective-permute-start | bytes 1769480 | tf_op jit(solution)/shard_map/ppermute | solution.py:586
  172.4 14.6 %collective-permute-start.41 = (bf16[8,18,16,128]{3,2,1,0:T(8,128)(2,1)S(1)}, bf16[8,18,16,128]{3,2,1,0:T(8,128)(2,1)S(1)}, u32[]{:S(2)}, u32[]{:S(2)}) collective-permute-start(bf16[8,18,16,128]{3,2,1,0:T(8,128)(2,1)S(1)} %get-tuple-element.380.refs_6_), channel_id=1, source_target_pairs={{0,4},{1,5},{2,6},{3,7},{4,0},{5,1},{6,2},{7,3},{8,12},{9,13},{10,... | collective-permute-start | bytes 1769480 | tf_op jit(solution)/shard_map/ppermute | solution.py:586
  173.1 2.9 %collective-permute-start.37 = (bf16[2,2,64,768]{3,2,1,0:T(8,128)(2,1)S(1)}, bf16[2,2,64,768]{3,2,1,0:T(8,128)(2,1)S(1)}, u32[]{:S(2)}, u32[]{:S(2)}) collective-permute-start(bf16[2,2,64,768]{3,2,1,0:T(8,128)(2,1)S(1)} %copy-done.17), channel_id=1, source_target_pairs={{0,1},{1,0},{2,3},{3,2},{4,5},{5,4},{6,7},{7,6},{8,9},{9,8},{10,11... | collective-permute-start | bytes 1179656 | tf_op jit(solution)/shard_map/ppermute | solution.py:586
  173.1 14.0 %collective-permute-start.38 = (bf16[2,45,16,128]{3,2,1,0:T(8,128)(2,1)S(1)}, bf16[2,45,16,128]{3,2,1,0:T(8,128)(2,1)S(1)}, u32[]{:S(2)}, u32[]{:S(2)}) collective-permute-start(bf16[2,45,16,128]{3,2,1,0:T(8,128)(2,1)S(1)} %get-tuple-element.376.refs_1_), channel_id=1, source_target_pairs={{0,8},{1,9},{2,10},{3,11},{4,12},{5,13},{6,14},{7,15},{8,0},{9,1},... | collective-permute-start | bytes 1105928 | tf_op jit(solution)/shard_map/ppermute | solution.py:586
  175.3 11.0 %collective-permute-start.39 = (bf16[1,28,16,128]{3,2,1,0:T(8,128)(2,1)S(1)}, bf16[1,28,16,128]{3,2,1,0:T(8,128)(2,1)S(1)}, u32[]{:S(2)}, u32[]{:S(2)}) collective-permute-start(bf16[1,28,16,128]{3,2,1,0:T(8,128)(2,1)S(1)} %get-tuple-element.378), channel_id=1, source_target_pairs={{0,16},{1,17},{2,18},{3,19},{4,20},{5,21},{6,22},{7,23},{8,24},{9,... | collective-permute-start | bytes 344072 | tf_op jit(solution)/shard_map/ppermute | solution.py:586
  187.3 24.2 %collective-permute-start.46 = (bf16[16,36,16,128]{3,2,1,0:T(8,128)(2,1)S(1)}, bf16[16,36,16,128]{3,2,1,0:T(8,128)(2,1)S(1)}, u32[]{:S(2)}, u32[]{:S(2)}) collective-permute-start(bf16[16,36,16,128]{3,2,1,0:T(8,128)(2,1)S(1)} %get-tuple-element.388.refs_2_), channel_id=1, source_target_pairs={{0,1},{1,0},{2,3},{3,2},{4,5},{5,4},{6,7},{7,6},{8,9},{9,8},{10,11... | collective-permute-start | bytes 7077896 | tf_op jit(solution)/shard_map/ppermute | solution.py:586
  187.4 12.6 %collective-permute-start.43 = (bf16[4,27,16,128]{3,2,1,0:T(8,128)(2,1)S(1)}, bf16[4,27,16,128]{3,2,1,0:T(8,128)(2,1)S(1)}, u32[]{:S(2)}, u32[]{:S(2)}) collective-permute-start(bf16[4,27,16,128]{3,2,1,0:T(8,128)(2,1)S(1)} %get-tuple-element.383.refs_2_), channel_id=1, source_target_pairs={{0,2},{1,3},{2,0},{3,1},{4,6},{5,7},{6,4},{7,5},{8,10},{9,11},{10,... | collective-permute-start | bytes 1327112 | tf_op jit(solution)/shard_map/ppermute | solution.py:586
  188.9 9.1 %collective-permute-start.42 = (bf16[4,18,16,128]{3,2,1,0:T(8,128)(2,1)S(1)}, bf16[4,18,16,128]{3,2,1,0:T(8,128)(2,1)S(1)}, u32[]{:S(2)}, u32[]{:S(2)}) collective-permute-start(bf16[4,18,16,128]{3,2,1,0:T(8,128)(2,1)S(1)} %get-tuple-element.382.refs_1_), channel_id=1, source_target_pairs={{0,4},{1,5},{2,6},{3,7},{4,0},{5,1},{6,2},{7,3},{8,12},{9,13},{10,... | collective-permute-start | bytes 884744 | tf_op jit(solution)/shard_map/ppermute | solution.py:586
  189.4 8.3 %collective-permute-start.44 = (bf16[1,28,16,128]{3,2,1,0:T(8,128)(2,1)S(1)}, bf16[1,28,16,128]{3,2,1,0:T(8,128)(2,1)S(1)}, u32[]{:S(2)}, u32[]{:S(2)}) collective-permute-start(bf16[1,28,16,128]{3,2,1,0:T(8,128)(2,1)S(1)} %get-tuple-element.384.refs_5_), channel_id=1, source_target_pairs={{0,16},{1,17},{2,18},{3,19},{4,20},{5,21},{6,22},{7,23},{8,24},{9,... | collective-permute-start | bytes 344072 | tf_op jit(solution)/shard_map/ppermute | solution.py:586
  200.1 27.7 %collective-permute-start.51 = (bf16[8,27,16,128]{3,2,1,0:T(8,128)(2,1)S(1)}, bf16[8,27,16,128]{3,2,1,0:T(8,128)(2,1)S(1)}, u32[]{:S(2)}, u32[]{:S(2)}) collective-permute-start(bf16[8,27,16,128]{3,2,1,0:T(8,128)(2,1)S(1)} %get-tuple-element.398.refs_2_), channel_id=1, source_target_pairs={{0,4},{1,5},{2,6},{3,7},{4,0},{5,1},{6,2},{7,3},{8,12},{9,13},{10,... | collective-permute-start | bytes 2654216 | tf_op jit(solution)/shard_map/ppermute | solution.py:586
  201.0 16.1 %collective-permute-start.47 = (bf16[2,2,128,768]{3,2,1,0:T(8,128)(2,1)S(1)}, bf16[2,2,128,768]{3,2,1,0:T(8,128)(2,1)S(1)}, u32[]{:S(2)}, u32[]{:S(2)}) collective-permute-start(bf16[2,2,128,768]{3,2,1,0:T(8,128)(2,1)S(1)} %get-tuple-element.391), channel_id=1, source_target_pairs={{0,1},{1,0},{2,3},{3,2},{4,5},{5,4},{6,7},{7,6},{8,9},{9,8},{10,11... | collective-permute-start | bytes 2359304 | tf_op jit(solution)/shard_map/ppermute | solution.py:586
  201.0 26.7 %collective-permute-start.50 = (bf16[8,18,16,128]{3,2,1,0:T(8,128)(2,1)S(1)}, bf16[8,18,16,128]{3,2,1,0:T(8,128)(2,1)S(1)}, u32[]{:S(2)}, u32[]{:S(2)}) collective-permute-start(bf16[8,18,16,128]{3,2,1,0:T(8,128)(2,1)S(1)} %get-tuple-element.397.refs_1_), channel_id=1, source_target_pairs={{0,2},{1,3},{2,0},{3,1},{4,6},{5,7},{6,4},{7,5},{8,10},{9,11},{10,... | collective-permute-start | bytes 1769480 | tf_op jit(solution)/shard_map/ppermute | solution.py:586
  202.1 8.0 %collective-permute-start.45 = (bf16[2,28,16,128]{3,2,1,0:T(8,128)(2,1)S(1)}, bf16[2,28,16,128]{3,2,1,0:T(8,128)(2,1)S(1)}, u32[]{:S(2)}, u32[]{:S(2)}) collective-permute-start(bf16[2,28,16,128]{3,2,1,0:T(8,128)(2,1)S(1)} %get-tuple-element.386.refs_1_), channel_id=1, source_target_pairs={{0,8},{1,9},{2,10},{3,11},{4,12},{5,13},{6,14},{7,15},{8,0},{9,1},... | collective-permute-start | bytes 688136 | tf_op jit(solution)/shard_map/ppermute | solution.py:586
  210.1 17.5 %collective-permute-start.48 = (bf16[4,18,16,128]{3,2,1,0:T(8,128)(2,1)S(1)}, bf16[4,18,16,128]{3,2,1,0:T(8,128)(2,1)S(1)}, u32[]{:S(2)}, u32[]{:S(2)}) collective-permute-start(bf16[4,18,16,128]{3,2,1,0:T(8,128)(2,1)S(1)} %get-tuple-element.394.refs_1_), channel_id=1, source_target_pairs={{0,4},{1,5},{2,6},{3,7},{4,0},{5,1},{6,2},{7,3},{8,12},{9,13},{10,... | collective-permute-start | bytes 884744 | tf_op jit(solution)/shard_map/ppermute | solution.py:586
  211.5 8.7 %collective-permute-start.49 = (bf16[4,10,16,128]{3,2,1,0:T(8,128)(2,1)S(1)}, bf16[4,10,16,128]{3,2,1,0:T(8,128)(2,1)S(1)}, u32[]{:S(2)}, u32[]{:S(2)}) collective-permute-start(bf16[4,10,16,128]{3,2,1,0:T(8,128)(2,1)S(1)} %get-tuple-element.395.refs_2_), channel_id=1, source_target_pairs={{0,2},{1,3},{2,0},{3,1},{4,6},{5,7},{6,4},{7,5},{8,10},{9,11},{10,... | collective-permute-start | bytes 491528 | tf_op jit(solution)/shard_map/ppermute | solution.py:586
  227.9 5.4 %collective-permute-start.52 = (bf16[16,45,16,128]{3,2,1,0:T(8,128)(2,1)S(1)}, bf16[16,45,16,128]{3,2,1,0:T(8,128)(2,1)S(1)}, u32[]{:S(2)}, u32[]{:S(2)}) collective-permute-start(bf16[16,45,16,128]{3,2,1,0:T(8,128)(2,1)S(1)} %get-tuple-element.400.refs_2_), channel_id=1, source_target_pairs={{0,1},{1,0},{2,3},{3,2},{4,5},{5,4},{6,7},{7,6},{8,9},{9,8},{10,11... | collective-permute-start | bytes 8847368 | tf_op jit(solution)/shard_map/ppermute | solution.py:586
  228.0 15.7 %collective-permute-start.53 = (bf16[8,18,16,128]{3,2,1,0:T(8,128)(2,1)S(1)}, bf16[8,18,16,128]{3,2,1,0:T(8,128)(2,1)S(1)}, u32[]{:S(2)}, u32[]{:S(2)}) collective-permute-start(bf16[8,18,16,128]{3,2,1,0:T(8,128)(2,1)S(1)} %get-tuple-element.402.refs_1_), channel_id=1, source_target_pairs={{0,2},{1,3},{2,0},{3,1},{4,6},{5,7},{6,4},{7,5},{8,10},{9,11},{10,... | collective-permute-start | bytes 1769480 | tf_op jit(solution)/shard_map/ppermute | solution.py:586
  229.6 11.1 %collective-permute-start.54 = (bf16[8,10,16,128]{3,2,1,0:T(8,128)(2,1)S(1)}, bf16[8,10,16,128]{3,2,1,0:T(8,128)(2,1)S(1)}, u32[]{:S(2)}, u32[]{:S(2)}) collective-permute-start(bf16[8,10,16,128]{3,2,1,0:T(8,128)(2,1)S(1)} %get-tuple-element.403.refs_2_), channel_id=1, source_target_pairs={{0,4},{1,5},{2,6},{3,7},{4,0},{5,1},{6,2},{7,3},{8,12},{9,13},{10,... | collective-permute-start | bytes 983048 | tf_op jit(solution)/shard_map/ppermute | solution.py:586
  243.9 3.9 %collective-permute-start.55 = (bf16[16,28,16,128]{3,2,1,0:T(8,128)(2,1)S(1)}, bf16[16,28,16,128]{3,2,1,0:T(8,128)(2,1)S(1)}, u32[]{:S(2)}, u32[]{:S(2)}) collective-permute-start(bf16[16,28,16,128]{3,2,1,0:T(8,128)(2,1)S(1)} %get-tuple-element.405.refs_2_), channel_id=1, source_target_pairs={{0,1},{1,0},{2,3},{3,2},{4,5},{5,4},{6,7},{7,6},{8,9},{9,8},{10,11... | collective-permute-start | bytes 5505032 | tf_op jit(solution)/shard_map/ppermute | solution.py:586
  (45 other events, 295.0 us)
